TPU v7x, 32 devices: a whole 2x2x4 slice. The times are simulated.
32 devices in a mesh: blk: 4 (over x, core), dp: 8 (over z, y).
Axes of the slice: x: 2, y: 2, z: 4, core: 2. Of those that a mesh axis runs over, the one named last changes fastest.
Arguments:
- hidden_in: bfloat16 [8, 4, 320, 2048], P('dp', 'blk'), may hold values from -6 to 6
- cotangent: bfloat16 [8, 4, 320, 2048], P('dp', 'blk'), may hold values from -6 to 6
- seq_lengths: int32 [8, 2], P('dp'), may hold values from 128 to 1024, as said below
- block_order: int32 [2, 4], replicated, may hold values from 0 to 3, each once within a row
- w_qkv: bfloat16 [2048, 6144], P(('blk', 'dp')), may hold values from -0.1875 to 0.1875
- w_out: bfloat16 [2048, 2048], P(('blk', 'dp')), may hold values from -0.5 to 0.5
- w_up: bfloat16 [2048, 8192], P(('blk', 'dp')), may hold values from -0.125 to 0.125
- w_down: bfloat16 [8192, 2048], P(('blk', 'dp')), may hold values from -0.09375 to 0.09375
- norm_gains: float32 [2, 2048], replicated, may hold values from 0.5 to 1.5
- norm_biases: float32 [2, 2048], replicated, may hold values from -4 to 4
- hidden_bias: float32 [8192], replicated, may hold values from -6 to 6
Outputs:
- layer_out: bfloat16 [8, 4, 320, 2048], P('dp', 'blk')
- grad_input: bfloat16 [8, 4, 320, 2048], P('dp', 'blk')
- grad_w_qkv: float32 [2048, 6144], P(('blk', 'dp'))
- grad_w_out: float32 [2048, 2048], P(('blk', 'dp'))
- grad_w_up: float32 [2048, 8192], P(('blk', 'dp'))
- grad_w_down: float32 [8192, 2048], P(('blk', 'dp'))
- grad_norm_gains: float32 [2, 2048], P(None, ('blk', 'dp'))
- grad_norm_biases: float32 [2, 2048], P(None, ('blk', 'dp'))
- grad_hidden_bias: float32 [8192], P(('blk', 'dp'))
Inputs may be any that keep to these rules, and one draw needn't show every extreme that they name: `seq_lengths`: column 0 lies from 512 to 1024, column 1 from 128 to 256; in each row one of the two equals its bucket length, and column 0 does in at least one row. `block_order`: each row holds every block number once.
All inputs are finite; a program needn't handle non-finite values.
Results may differ from a plain program's by a relative error of at most 0.015.
Values may be sent and summed in bfloat16 or wider, within the bound.
No kernel may reach another device: no remote copies, remote signals or barrier semaphores. Data moves between devices by JAX's collectives and lax.ppermute only.
A program may use at most 768 MiB of HBM per device.

v0:
```python
from functools import partial

import jax
import jax.numpy as jnp
from jax import lax
from jax.sharding import PartitionSpec as P

HEADS = 16
HEAD = 128
BLK_A = 256
BLK_B = 64


EPSILON = 1e-05
NEGATIVE = -1e30


def shifted(block, axis, distance):
    devices = range(lax.axis_size(axis))
    route = [((i - distance) % len(devices), i) for i in devices]
    return lax.ppermute(block, axis, route)


def layer_norm(value, gain, bias):
    center = value - jnp.mean(value, axis=-1, keepdims=True)
    spread = jnp.mean(center * center, axis=-1, keepdims=True)
    return center * lax.rsqrt(spread + EPSILON) * gain + bias


def lookup(table_row, index):
    return jnp.sum(jnp.where(jnp.arange(table_row.shape[0]) == index, table_row, 0))


def block_places(block_id, count):
    return block_id * count + jnp.arange(count, dtype=jnp.int32)


def allowed_of(query_places, key_places, length):
    return (key_places[None, :] <= query_places[:, None]) & (key_places[None, :] < length)


def scores_of(queries, keys, allowed):
    scores = jnp.einsum(
        "qhd,khd->hqk", queries, keys, preferred_element_type=jnp.float32
    ) * HEAD ** (-0.5)
    return jnp.where(allowed[None], scores, NEGATIVE)


def contract_last(left, right):
    return lax.dot_general(
        left, right, (((1,), (1,)), ((), ())), preferred_element_type=jnp.float32
    )


def contract_first(left, right):
    return lax.dot_general(
        left, right, (((0,), (0,)), ((), ())), preferred_element_type=jnp.float32
    )


def fetch_forward(w_qkv, w_out, w_up, w_down):
    return (
        lax.all_gather(w_qkv, ("blk", "dp"), axis=0, tiled=True),
        lax.all_gather(w_out, ("blk", "dp"), axis=0, tiled=True),
        lax.all_gather(w_up, ("blk", "dp"), axis=0, tiled=True),
        lax.all_gather(w_down, ("blk", "dp"), axis=0, tiled=True),
    )


def fetch_backward(w_qkv, w_out, w_up, w_down):
    return (
        lax.all_gather(w_qkv, ("blk", "dp"), axis=0, tiled=True),
        lax.all_gather(w_out, ("blk", "dp"), axis=0, tiled=True),
        lax.all_gather(w_up, ("blk", "dp"), axis=0, tiled=True),
        lax.all_gather(w_down, ("blk", "dp"), axis=0, tiled=True),
    )


def attention_forward(queries, keys, values, order_row, length):
    count = queries.shape[0]
    cycle = lax.axis_size("blk")
    index = lax.axis_index("blk")
    query_places = block_places(lookup(order_row, index), count)
    peak = jnp.full((queries.shape[1], count), NEGATIVE, jnp.float32)
    total = jnp.zeros((queries.shape[1], count), jnp.float32)
    key_block = keys
    for turn_index in range(cycle):
        source = (index - turn_index) % cycle
        allowed = allowed_of(query_places, block_places(lookup(order_row, source), count), length)

        def gather_stats(state, key_block=key_block, allowed=allowed):
            running_peak, running_total = state
            scores = scores_of(queries, key_block, allowed)
            top = jnp.maximum(running_peak, jnp.max(scores, axis=-1))
            weights = jnp.where(allowed[None], jnp.exp(scores - top[..., None]), 0.0)
            return (top, running_total * jnp.exp(running_peak - top) + jnp.sum(weights, axis=-1))

        peak, total = gather_stats((peak, total))
        if turn_index + 1 < cycle:
            key_block = shifted(key_block, "blk", 1)
    log_total = peak + jnp.log(total)
    output = jnp.zeros(queries.shape, jnp.float32)
    key_block, value_block = (keys, values)
    for turn_index in range(cycle):
        source = (index - turn_index) % cycle
        allowed = allowed_of(query_places, block_places(lookup(order_row, source), count), length)

        def add_values(running, key_block=key_block, value_block=value_block, allowed=allowed):
            scores = scores_of(queries, key_block, allowed)
            probs = jnp.where(allowed[None], jnp.exp(scores - log_total[..., None]), 0.0).astype(
                jnp.bfloat16
            )
            return running + jnp.einsum(
                "hqk,khd->qhd", probs, value_block, preferred_element_type=jnp.float32
            )

        output = add_values(output)
        if turn_index + 1 < cycle:
            key_block, value_block = shifted((key_block, value_block), "blk", 1)
    return (output, log_total)


def attention_backward(queries, keys, values, grad_attended, delta, log_total, order_row, length):
    count = queries.shape[0]
    cycle = lax.axis_size("blk")
    index = lax.axis_index("blk")
    scale = HEAD ** (-0.5)
    query_places = block_places(lookup(order_row, index), count)
    grad_queries = jnp.zeros(queries.shape, jnp.float32)
    grad_keys = jnp.zeros(queries.shape, jnp.float32)
    grad_values = jnp.zeros(queries.shape, jnp.float32)
    key_block, value_block = (keys, values)
    for turn_index in range(cycle):
        source = (index - turn_index) % cycle
        allowed = allowed_of(query_places, block_places(lookup(order_row, source), count), length)

        def add_grads(state, key_block=key_block, value_block=value_block, allowed=allowed):
            held_queries, held_keys, held_values = state
            scores = scores_of(queries, key_block, allowed)
            probs = jnp.where(allowed[None], jnp.exp(scores - log_total[..., None]), 0.0)
            rounded = probs.astype(jnp.bfloat16)
            held_values = held_values + jnp.einsum(
                "hqk,qhd->khd", rounded, grad_attended, preferred_element_type=jnp.float32
            )
            grad_probs = jnp.einsum(
                "qhd,khd->hqk", grad_attended, value_block, preferred_element_type=jnp.float32
            )
            grad_scores = (probs * (grad_probs - delta[..., None])).astype(jnp.bfloat16)
            held_queries = held_queries + scale * jnp.einsum(
                "hqk,khd->qhd", grad_scores, key_block, preferred_element_type=jnp.float32
            )
            held_keys = held_keys + scale * jnp.einsum(
                "hqk,qhd->khd", grad_scores, queries, preferred_element_type=jnp.float32
            )
            return (held_queries, held_keys, held_values)

        grad_queries, grad_keys, grad_values = add_grads((grad_queries, grad_keys, grad_values))
        grad_keys, grad_values = (
            shifted(grad_keys.astype(jnp.bfloat16), "blk", 1).astype(grad_keys.dtype),
            shifted(grad_values.astype(jnp.bfloat16), "blk", 1).astype(grad_values.dtype),
        )
        if turn_index + 1 < cycle:
            key_block, value_block = shifted((key_block, value_block), "blk", 1)
    return (grad_queries, grad_keys, grad_values)


def forward_micro(rows_in, weights, gains, biases, hidden_bias, order_row, length):
    full_qkv, full_out, full_up, full_down = weights
    count = rows_in.shape[0]
    width = rows_in.shape[1]
    inputs = rows_in.astype(jnp.float32)
    normed, first_pull = jax.vjp(layer_norm, inputs, gains[0], biases[0])
    normed_low = normed.astype(jnp.bfloat16)
    projected = jnp.dot(normed_low, full_qkv, preferred_element_type=jnp.float32).astype(
        jnp.bfloat16
    )
    queries = projected[:, :width].reshape(count, HEADS, HEAD)
    keys = projected[:, width : 2 * width].reshape(count, HEADS, HEAD)
    values = projected[:, 2 * width :].reshape(count, HEADS, HEAD)
    attended, log_total = attention_forward(queries, keys, values, order_row, length)
    attended_low = attended.reshape(count, width).astype(jnp.bfloat16)
    mixed = inputs + jnp.dot(attended_low, full_out, preferred_element_type=jnp.float32)
    second, second_pull = jax.vjp(layer_norm, mixed, gains[1], biases[1])
    second_low = second.astype(jnp.bfloat16)
    hidden_pre = jnp.dot(second_low, full_up, preferred_element_type=jnp.float32) + hidden_bias
    activated, gelu_pull = jax.vjp(partial(jax.nn.gelu, approximate=True), hidden_pre)
    activated_low = activated.astype(jnp.bfloat16)
    result = mixed + jnp.dot(activated_low, full_down, preferred_element_type=jnp.float32)
    saved = (
        normed_low,
        queries,
        keys,
        values,
        attended,
        log_total,
        attended_low,
        second_low,
        activated_low,
        first_pull,
        second_pull,
        gelu_pull,
    )
    return (result.astype(jnp.bfloat16), saved)


def backward_micro(cot_rows, weights, saved, order_row, length):
    full_qkv, full_out, full_up, full_down = weights
    (
        normed_low,
        queries,
        keys,
        values,
        attended,
        log_total,
        attended_low,
        second_low,
        activated_low,
        first_pull,
        second_pull,
        gelu_pull,
    ) = saved
    count = cot_rows.shape[0]
    width = cot_rows.shape[1]
    grad_activated = contract_last(cot_rows, full_down)
    (grad_hidden,) = gelu_pull(grad_activated)
    grad_hidden_low = grad_hidden.astype(jnp.bfloat16)
    grad_second = contract_last(grad_hidden_low, full_up)
    grad_mixed_norm, grad_gain_two, grad_bias_two = second_pull(grad_second)
    grad_mixed = cot_rows.astype(jnp.float32) + grad_mixed_norm
    grad_mixed_low = grad_mixed.astype(jnp.bfloat16)
    grad_attended = (
        contract_last(grad_mixed_low, full_out).astype(jnp.bfloat16).reshape(count, HEADS, HEAD)
    )
    delta = jnp.einsum("qhd,qhd->hq", grad_attended.astype(jnp.float32), attended)
    grad_queries, grad_keys, grad_values = attention_backward(
        queries, keys, values, grad_attended, delta, log_total, order_row, length
    )
    grad_projected = jnp.concatenate(
        [
            grad_queries.reshape(count, width),
            grad_keys.reshape(count, width),
            grad_values.reshape(count, width),
        ],
        axis=1,
    ).astype(jnp.bfloat16)
    grad_normed = contract_last(grad_projected, full_qkv)
    grad_inputs_norm, grad_gain_one, grad_bias_one = first_pull(grad_normed)
    grad_inputs = grad_mixed + grad_inputs_norm
    gain_terms = jnp.stack([grad_gain_one, grad_gain_two])
    bias_terms = jnp.stack([grad_bias_one, grad_bias_two])
    hidden_term = jnp.sum(grad_hidden_low.astype(jnp.float32), axis=0)
    kept = (
        normed_low,
        grad_projected,
        attended_low,
        grad_mixed_low,
        second_low,
        grad_hidden_low,
        activated_low,
        cot_rows,
    )
    return (grad_inputs.astype(jnp.bfloat16), kept, gain_terms, bias_terms, hidden_term)


def body(
    hidden_in,
    cotangent,
    seq_lengths,
    block_order,
    w_qkv,
    w_out,
    w_up,
    w_down,
    norm_gains,
    norm_biases,
    hidden_bias,
):
    total_rows = hidden_in.shape[2]
    width = hidden_in.shape[3]
    rows_in = hidden_in.reshape(total_rows, width)
    cot_rows = cotangent.reshape(total_rows, width)
    splits = ((0, BLK_A, 0), (BLK_A, BLK_B, 1))
    fetched = fetch_forward(w_qkv, w_out, w_up, w_down)
    results = []
    saved_lists = []
    for first, block_rows, column in splits:
        order_row = block_order[column]
        length = seq_lengths[0, column]
        result, saved = forward_micro(
            rows_in[first : first + block_rows],
            fetched,
            norm_gains,
            norm_biases,
            hidden_bias,
            order_row,
            length,
        )
        results.append(result)
        saved_lists.append(saved)
    back_weights = fetch_backward(w_qkv, w_out, w_up, w_down)
    grad_rows_in = []
    kept_lists = []
    gain_sum = jnp.zeros((2, width), jnp.float32)
    bias_sum = jnp.zeros((2, width), jnp.float32)
    hidden_sum = jnp.zeros((hidden_bias.shape[0],), jnp.float32)
    for place_index in range(2):
        first, block_rows, column = splits[place_index]
        order_row = block_order[column]
        length = seq_lengths[0, column]
        grad_inputs, kept, gain_terms, bias_terms, hidden_term = backward_micro(
            cot_rows[first : first + block_rows],
            back_weights,
            saved_lists[place_index],
            order_row,
            length,
        )
        grad_rows_in.append(grad_inputs)
        kept_lists.append(kept)
        gain_sum = gain_sum + gain_terms
        bias_sum = bias_sum + bias_terms
        hidden_sum = hidden_sum + hidden_term
    joined = [
        jnp.concatenate([kept_lists[0][place], kept_lists[1][place]], axis=0) for place in range(8)
    ]
    (
        normed_all,
        grad_projected_all,
        attended_all,
        grad_mixed_all,
        second_all,
        grad_hidden_all,
        activated_all,
        cot_all,
    ) = joined
    first_term = contract_first(normed_all, grad_projected_all)
    second_term = contract_first(attended_all, grad_mixed_all)
    third_term = contract_first(second_all, grad_hidden_all)
    summed_rows = lax.psum_scatter(
        jnp.concatenate([first_term, second_term, third_term], axis=1),
        ("blk", "dp"),
        scatter_dimension=0,
        tiled=True,
    )
    grad_w_down = lax.psum_scatter(
        contract_first(
            lax.slice_in_dim(
                activated_all, 0, w_down.shape[0] * lax.axis_size(("blk", "dp")), axis=1
            ),
            cot_all,
        ),
        ("blk", "dp"),
        scatter_dimension=0,
        tiled=True,
    )
    grad_gains, grad_biases, grad_hidden_bias = (
        lax.psum_scatter(gain_sum, ("blk", "dp"), scatter_dimension=1, tiled=True),
        lax.psum_scatter(bias_sum, ("blk", "dp"), scatter_dimension=1, tiled=True),
        lax.psum_scatter(hidden_sum, ("blk", "dp"), scatter_dimension=0, tiled=True),
    )
    grad_w_qkv = summed_rows[:, : 3 * width]
    grad_w_out = summed_rows[:, 3 * width : 4 * width]
    grad_w_up = summed_rows[:, 4 * width :]
    layer_out = jnp.concatenate(results, axis=0).reshape(1, 1, total_rows, width)
    grad_input = jnp.concatenate(grad_rows_in, axis=0).reshape(1, 1, total_rows, width)
    return (
        layer_out,
        grad_input,
        grad_w_qkv,
        grad_w_out,
        grad_w_up,
        grad_w_down,
        grad_gains,
        grad_biases,
        grad_hidden_bias,
    )


def solution(mesh):
    return jax.shard_map(
        body,
        mesh=mesh,
        in_specs=(
            P("dp", "blk", None, None),
            P("dp", "blk", None, None),
            P("dp", None),
            P(),
            P(("blk", "dp"), None),
            P(("blk", "dp"), None),
            P(("blk", "dp"), None),
            P(("blk", "dp"), None),
            P(),
            P(),
            P(),
        ),
        out_specs=(
            P("dp", "blk", None, None),
            P("dp", "blk", None, None),
            P(("blk", "dp"), None),
            P(("blk", "dp"), None),
            P(("blk", "dp"), None),
            P(("blk", "dp"), None),
            P(None, ("blk", "dp")),
            P(None, ("blk", "dp")),
            P(("blk", "dp")),
        ),
        check_vma=False,
    )
```

profile of v0, /device:TPU:0, one launch (start us, length us, event | category | flops | bytes accessed | tf_op | source)
XLA Modules:
  0.0 4542.7 jit_solution(3084430910631044773)
XLA Ops:
  28.4 140.0 %all-gather.5.cloned.1.call-done = bf16[2048,6144]{1,0:T(8,128)(2,1)} async-done(((bf16[64,6144]{1,0:T(8,128)(2,1)}), bf16[2048,6144]{1,0:T(8,128)(2,1)}) %all-gather.5.cloned.1.call-update) | async-done | bytes 25165840 | tf_op jit(solution)/shard_map/all_gather | solution.py:63
  168.3 10.5 convolution_convert_fusion.1
  182.9 11.6 convolution_convert_fusion
  208.7 36.9 collective-permute-done.7
  248.5 11.6 collective-permute-start.11
  275.2 12.9 collective-permute-done.1
  301.7 29.0 collective-permute-done.2
  340.8 10.8 collective-permute-done.5
  359.9 107.9 %all-gather.9.cloned.1.call-done = bf16[2048,8192]{1,0:T(8,128)(2,1)} async-done(((bf16[64,8192]{1,0:T(8,128)(2,1)}), bf16[2048,8192]{1,0:T(8,128)(2,1)}) %all-gather.9.cloned.1.call-update) | async-done | bytes 33554448 | tf_op jit(solution)/shard_map/all_gather | solution.py:65
  467.7 18.5 multiply_convert_fusion.7
  486.2 177.3 %all-gather.11.cloned.1.call-done = bf16[8192,2048]{1,0:T(8,128)(2,1)} async-done(((bf16[256,2048]{1,0:T(8,128)(2,1)}), bf16[8192,2048]{1,0:T(8,128)(2,1)}) %all-gather.11.cloned.1.call-update) | async-done | bytes 33554448 | tf_op jit(solution)/shard_map/all_gather | solution.py:66
  663.6 16.4 convert_reduce_fusion.2
  680.0 16.6 multiply_reduce_fusion.3
  708.8 19.8 multiply_convert_fusion
  728.5 21.9 convert_reduce_fusion
  750.4 18.5 multiply_reduce_fusion
  803.4 29.3 fusion.7
  869.0 14.2 collective-permute-done.21
  892.2 11.1 collective-permute-done.17
  903.6 10.8 collective-permute-done.13
  920.2 11.2 collective-permute-done.18
  944.0 12.8 fusion.221
  965.2 14.5 fusion.220
  983.2 22.9 fusion.15
  1007.6 86.1 %pad_maximum_fusion = f32[2048,16384]{1,0:T(8,128)} fusion(f32[2048,8192]{1,0:T(8,128)} %fusion.7, f32[2048,2048]{1,0:T(8,128)} %fusion.66, f32[2048,6144]{1,0:T(8,128)} %fusion.15), kind=kLoop, calls=%fused_computation | loop fusion | flops 67108864 | bytes 268435456 | tf_op jit(solution)/shard_map/concatenate | solution.py:339
  1096.0 29.5 fusion.11
  1126.3 39.9 all-reduce.1
  1166.9 13.8 fusion.46
  1180.9 16.5 fusion.43
  1203.6 46.9 %reduce-scatter.12.cloned.1.call-done = f32[64,2]{1,0:T(8,128)} async-done(((f32[2048,2]{1,0:T(8,128)}), f32[64,2]{1,0:T(8,128)}) %reduce-scatter.12.cloned.1.call-update) | async-done | bytes 528
  1251.9 1878.9 %all-reduce.4.cloned.1.call-done = f32[2048,16384]{1,0:T(8,128)} async-done(((f32[2048,16384]{1,0:T(8,128)}), f32[2048,16384]{1,0:T(8,128)}) %all-reduce.4.cloned.1.call-update) | async-done | bytes 134217744
  3139.1 1396.6 %reduce-scatter.8.cloned.1.call-done = f32[256,2048]{1,0:T(8,128)} async-done(((f32[8192,2048]{1,0:T(8,128)}), f32[256,2048]{1,0:T(8,128)}) %reduce-scatter.8.cloned.1.call-update) | async-done | bytes 2097168 | tf_op jit(solution)/shard_map/reduce_scatter | solution.py:344
  (537 shorter events, 224.1 us)
Async XLA Ops:
  7.2 161.1 %all-gather.5.cloned.1.call-start = ((), (), s32[]{:S(2)}) async-start(), calls=%async_computation.3 | async-start | bytes 25952256 | tf_op jit(solution)/shard_map/all_gather | solution.py:63
  7.9 261.4 %all-gather.7.cloned.1.call-start = ((), (), s32[]{:S(2)}) async-start(), calls=%async_computation.4 | async-start | bytes 8650752 | tf_op jit(solution)/shard_map/all_gather | solution.py:64
  8.7 459.0 %all-gather.9.cloned.1.call-start = ((), (), s32[]{:S(2)}) async-start(), calls=%async_computation.5 | async-start | bytes 34603008 | tf_op jit(solution)/shard_map/all_gather | solution.py:65
  9.4 654.1 %all-gather.11.cloned.1.call-start = ((), (), s32[]{:S(2)}) async-start(), calls=%async_computation.6 | async-start | bytes 34603008 | tf_op jit(solution)/shard_map/all_gather | solution.py:66
  10.0 1192.2 %reduce-scatter.10.cloned.1.call-start = ((), (), s32[]{:S(2)}) async-start(), calls=%async_computation.8 | async-start | bytes 1081344
  181.3 21.3 collective-permute-start.6
  181.6 25.6 collective-permute-start.9
  201.8 67.5 %collective-permute-start = (bf16[256,16,128]{2,0,1:T(8,128)(2,1)}, bf16[256,16,128]{2,0,1:T(8,128)(2,1)}, u32[]{:S(2)}, u32[]{:S(2)}) collective-permute-start(bf16[256,16,128]{2,0,1:T(8,128)(2,1)} %bitcast.416), channel_id=1, source_target_pairs={{24,0},{0,8},{8,16},{16,24},{25,1},{1,9},{9,17},{17,25},{26,2},{2,... | collective-permute-start | bytes 3145736 | tf_op jit(solution)/shard_map/ppermute | solution.py:21
  202.1 72.6 %collective-permute-start.3 = (bf16[256,16,128]{0,2,1:T(8,128)(2,1)}, bf16[256,16,128]{0,2,1:T(8,128)(2,1)}, u32[]{:S(2)}, u32[]{:S(2)}) collective-permute-start(bf16[256,16,128]{0,2,1:T(8,128)(2,1)} %bitcast.437), channel_id=1, source_target_pairs={{24,0},{0,8},{8,16},{16,24},{25,1},{1,9},{9,17},{17,25},{26,2},{2,... | collective-permute-start | bytes 3145736 | tf_op jit(solution)/shard_map/ppermute | solution.py:21
  202.6 43.0 collective-permute-start.7
  207.2 41.3 collective-permute-start.10
  248.5 17.4 collective-permute-start.11
  269.3 18.8 collective-permute-start.1
  274.7 24.5 collective-permute-start.4
  288.0 42.7 collective-permute-start.2
  299.2 52.4 %collective-permute-start.5 = (bf16[256,16,128]{0,2,1:T(8,128)(2,1)S(1)}, bf16[256,16,128]{0,2,1:T(8,128)(2,1)S(1)}, u32[]{:S(2)}, u32[]{:S(2)}) collective-permute-start(bf16[256,16,128]{0,2,1:T(8,128)(2,1)S(1)} %collective-permute-done.4), channel_id=1, source_target_pairs={{24,0},{0,8},{8,16},{16,24},{25,1},{1,9},{9,17},{17,25},{26,2},{2,... | collective-permute-start | bytes 3145736 | tf_op jit(solution)/shard_map/ppermute | solution.py:21
  832.7 34.0 collective-permute-start.20
  833.0 34.2 collective-permute-start.24
  841.1 45.1 collective-permute-start.16
  866.2 22.3 collective-permute-start.12
  866.9 16.3 collective-permute-start.21
  867.5 18.6 collective-permute-start.25
  889.4 25.1 collective-permute-start.13
  889.8 27.5 collective-permute-start.23
  892.1 28.0 collective-permute-start.27
  903.6 27.8 collective-permute-start.18
  914.8 27.7 collective-permute-start.14
  932.6 26.7 collective-permute-start.19
  943.9 21.2 collective-permute-start.15
  982.7 267.8 %reduce-scatter.12.cloned.1.call-start = ((), (), s32[]{:S(2)}) async-start(), calls=%async_computation.9 | async-start | bytes 1081344
  1007.5 2123.3 %all-reduce.4.cloned.1.call-start = ((), (), s32[]{:S(2)}) async-start(), calls=%async_computation.10 | async-start | bytes 268435456
  1093.7 3442.0 %reduce-scatter.8.cloned.1.call-start = ((), (), s32[]{:S(2)}) async-start(), calls=%async_computation.7 | async-start | bytes 69206016 | tf_op jit(solution)/shard_map/reduce_scatter | solution.py:344
  (160 other events, 3945.6 us)
Sparse Core Ops, SparseCore 0:
  10.9 157.3 all-gather.4
  171.3 84.6 all-gather.6
  259.0 208.6 all-gather.8
  470.6 192.9 all-gather.10
  982.8 133.3 reduce-scatter.9
  1119.0 131.4 reduce-scatter.11
  1257.0 1873.8 all-reduce.3
  3133.8 1401.8 reduce-scatter.7
where the time goes:
time: 4550 us; the launch traced here: 4540 us
  waiting for transfers between devices  3920 us (86%)
  matrix products  366 us (8%)
  other arithmetic  122 us (3%)
    unnamed x11, waiting for transfers between devices  1930 us
    reduce_scatter x1, waiting for transfers between devices, body(): lax.psum_scatter(contract_first(lax.slice_in_dim(activated_all, 0, w_down...  1400 us
    all_gather x1, waiting for transfers between devices, fetch_forward(): lax.all_gather(w_down, ('blk', 'dp'), axis=0, tiled=True)  177 us
    ppermute x28, waiting for transfers between devices, shifted(): return lax.ppermute(block, axis, route)  173 us
    all_gather x1, waiting for transfers between devices, fetch_forward(): lax.all_gather(w_qkv, ('blk', 'dp'), axis=0, tiled=True)  140 us
    dot_general x8, matrix products, contract_last(): lax.dot_general(left, right, (((1,), (1,)), ((), ())), preferred_element_...  113 us
    all_gather x1, waiting for transfers between devices, fetch_forward(): lax.all_gather(w_up, ('blk', 'dp'), axis=0, tiled=True)  108 us
  transfers between devices with their start and end apart: 36, of which 23 were waited for; matrix products, arithmetic and copies ran while one was open for 7% of the time, Pallas kernels for 0%

commit v1 on v0

v1 whole, which is shorter than its diff:
```python
import jax
import jax.numpy as jnp
from jax import lax
from jax.sharding import PartitionSpec as P

HEAD = 128
BLK_A = 256
BLK_B = 64

EPSILON = 1e-05
NEGATIVE = -1e30
BF16 = jnp.bfloat16
F32 = jnp.float32


def inner_size(count):
    inner = 1
    while (inner * 2) ** 2 <= count:
        inner *= 2
    return inner


def layer_norm(value, gain, bias):
    center = value - jnp.mean(value, axis=-1, keepdims=True)
    spread = jnp.mean(center * center, axis=-1, keepdims=True)
    return center * lax.rsqrt(spread + EPSILON) * gain + bias


def contract_last(left, right):
    return lax.dot_general(
        left, right, (((1,), (1,)), ((), ())), preferred_element_type=F32
    )


def contract_first(left, right):
    return lax.dot_general(
        left, right, (((0,), (0,)), ((), ())), preferred_element_type=F32
    )


def flip(block, bits):
    count = lax.axis_size("blk")
    return lax.ppermute(block, "blk", [(i ^ bits, i) for i in range(count)])


def outer_shift(block, distance):
    count = lax.axis_size("dp")
    inner = inner_size(count)
    outer = count // inner
    route = [
        (z * inner + y, ((z + distance) % outer) * inner + y)
        for z in range(outer)
        for y in range(inner)
    ]
    return lax.ppermute(block, "dp", route)


def inner_shift(block, distance):
    count = lax.axis_size("dp")
    inner = inner_size(count)
    route = [
        (z * inner + y, z * inner + (y + distance) % inner)
        for z in range(count // inner)
        for y in range(inner)
    ]
    return lax.ppermute(block, "dp", route)


def pick(array, index, axis):
    return lax.dynamic_index_in_dim(array, index, axis, keepdims=False)


def place(whole, part, index, axis):
    return lax.dynamic_update_index_in_dim(whole, part, index, axis)


def exchange_blk(parts):
    count = lax.axis_size("blk")
    index = lax.axis_index("blk")
    out = parts
    for bits in range(1, count):
        out = place(out, flip(pick(parts, index ^ bits, 0), bits), index ^ bits, 0)
    return out


def gather_dp(part):
    count = lax.axis_size("dp")
    inner = inner_size(count)
    outer = count // inner
    index = lax.axis_index("dp")
    z, y = index // inner, index % inner
    groups, rows, columns = part.shape
    whole = jnp.zeros((groups, count, rows, columns), part.dtype)
    for far in range(outer):
        from_z = part if far == 0 else outer_shift(part, far)
        for near in range(inner):
            piece = from_z if near == 0 else inner_shift(from_z, near)
            source = ((z - far) % outer) * inner + (y - near) % inner
            whole = place(whole, piece, source, 1)
    return whole.reshape(groups * count * rows, columns)


def scatter_dp(total, groups):
    count = lax.axis_size("dp")
    inner = inner_size(count)
    outer = count // inner
    index = lax.axis_index("dp")
    z, y = index // inner, index % inner
    columns = total.shape[1]
    parts = total.astype(BF16).reshape(groups, outer, inner, -1, columns)
    held = pick(parts, y, 2).astype(F32)
    for near in range(1, inner):
        held = held + inner_shift(pick(parts, (y + near) % inner, 2), near).astype(F32)
    low = held.astype(BF16)
    out = pick(low, z, 1).astype(F32)
    for far in range(1, outer):
        out = out + outer_shift(pick(low, (z + far) % outer, 1), far).astype(F32)
    return out


def gather_blk(part):
    count = lax.axis_size("blk")
    index = lax.axis_index("blk")
    whole = jnp.zeros((count,) + part.shape, part.dtype)
    for far in range(0, count, 2):
        piece = part if far == 0 else flip(part, far)
        whole = place(whole, piece, index ^ far, 0)
        whole = place(whole, flip(piece, 1), index ^ far ^ 1, 0)
    return whole


def scatter_blk(total):
    count = lax.axis_size("blk")
    index = lax.axis_index("blk")
    far_index, core = index // 2, index % 2
    parts = total.astype(BF16).reshape((count // 2, 2) + total.shape[1:])
    held = pick(parts, core, 1).astype(F32) + flip(pick(parts, core ^ 1, 1), 1).astype(F32)
    low = held.astype(BF16)
    out = pick(low, far_index, 0).astype(F32)
    for far in range(1, count // 2):
        out = out + flip(pick(low, far_index ^ far, 0), far * 2).astype(F32)
    return out


def sum_small(total):
    blk, dp = lax.axis_size("blk"), lax.axis_size("dp")
    count, width = total.shape
    parts = total.reshape(count, blk, dp, -1).transpose(1, 2, 0, 3)
    got = jnp.sum(lax.all_to_all(parts, "blk", 0, 0), axis=0)
    return jnp.sum(lax.all_to_all(got, "dp", 0, 0), axis=0)


def allowed_of(places, length):
    return (places[None, :] <= places[:, None]) & (places[None, :] < length)


def scores_of(queries, keys, allowed):
    scores = jnp.einsum("qhd,khd->hqk", queries, keys, preferred_element_type=F32) * HEAD ** (-0.5)
    return jnp.where(allowed[None], scores, NEGATIVE)


def attention_forward(queries, keys, values, allowed):
    scores = scores_of(queries, keys, allowed)
    peak = jnp.max(scores, axis=-1, keepdims=True)
    log_total = peak + jnp.log(jnp.sum(jnp.exp(scores - peak), axis=-1, keepdims=True))
    probs = jnp.where(allowed[None], jnp.exp(scores - log_total), 0.0).astype(BF16)
    attended = jnp.einsum("hqk,khd->qhd", probs, values, preferred_element_type=F32)
    return attended, log_total


def attention_backward(queries, keys, values, attended, grad_attended, log_total, allowed):
    scale = HEAD ** (-0.5)
    delta = jnp.einsum("qhd,qhd->hq", grad_attended.astype(F32), attended)
    scores = scores_of(queries, keys, allowed)
    probs = jnp.where(allowed[None], jnp.exp(scores - log_total), 0.0)
    grad_values = jnp.einsum(
        "hqk,qhd->khd", probs.astype(BF16), grad_attended, preferred_element_type=F32
    )
    grad_probs = jnp.einsum("qhd,khd->hqk", grad_attended, values, preferred_element_type=F32)
    grad_scores = (probs * (grad_probs - delta[..., None])).astype(BF16)
    grad_queries = scale * jnp.einsum("hqk,khd->qhd", grad_scores, keys, preferred_element_type=F32)
    grad_keys = scale * jnp.einsum("hqk,qhd->khd", grad_scores, queries, preferred_element_type=F32)
    return grad_queries, grad_keys, grad_values


def body(
    hidden_in,
    cotangent,
    seq_lengths,
    block_order,
    w_qkv,
    w_out,
    w_up,
    w_down,
    norm_gains,
    norm_biases,
    hidden_bias,
):
    blk = lax.axis_size("blk")
    index = lax.axis_index("blk")
    rows, width = hidden_in.shape[2:]
    heads = width // HEAD // blk
    part = width // blk
    x = hidden_in.reshape(rows, width).astype(F32)
    cot_low = cotangent.reshape(rows, width)
    splits = ((0, BLK_A), (BLK_A, BLK_A + BLK_B))

    shard = w_qkv.shape[0]
    hidden = hidden_bias.shape[0] // blk
    out_full = gather_dp(w_out[None])
    qkv_part = exchange_blk(w_qkv.reshape(shard, 3, blk, part).transpose(2, 0, 1, 3).reshape(blk, shard, 3 * part))
    qkv_full = gather_dp(qkv_part)
    up_part = exchange_blk(w_up.reshape(shard, blk, hidden).transpose(1, 0, 2))
    up_full = gather_dp(up_part)
    down_full = gather_dp(w_down[None])

    normed, first_pull = jax.vjp(layer_norm, x, norm_gains[0], norm_biases[0])
    normed_all = gather_blk(normed.astype(BF16)).reshape(blk * rows, width)
    projected = jnp.dot(normed_all, qkv_full, preferred_element_type=F32).astype(BF16)
    projected = projected.reshape(blk, rows, 3, heads, HEAD)

    attended_parts, saved = [], []
    for column, (first, last) in enumerate(splits):
        count = last - first
        places = (
            block_order[column][:, None] * count + jnp.arange(count, dtype=jnp.int32)[None, :]
        ).reshape(blk * count)
        allowed = allowed_of(places, seq_lengths[0, column])
        mine = projected[:, first:last].reshape(blk * count, 3, heads, HEAD)
        queries, keys, values = mine[:, 0], mine[:, 1], mine[:, 2]
        attended, log_total = attention_forward(queries, keys, values, allowed)
        attended_parts.append(attended.astype(BF16).reshape(blk, count, part))
        saved.append((queries, keys, values, attended, log_total, allowed))
    attended_low = jnp.concatenate(attended_parts, axis=1).reshape(blk * rows, part)
    mixed = x + scatter_blk(
        jnp.dot(attended_low, out_full, preferred_element_type=F32).reshape(blk, rows, width)
    )
    second, second_pull = jax.vjp(layer_norm, mixed, norm_gains[1], norm_biases[1])
    second_all = gather_blk(second.astype(BF16)).reshape(blk * rows, width)
    bias_part = lax.dynamic_slice_in_dim(hidden_bias, index * hidden, hidden)
    hidden_pre = jnp.dot(second_all, up_full, preferred_element_type=F32) + bias_part
    activated, gelu_pull = jax.vjp(lambda v: jax.nn.gelu(v, approximate=True), hidden_pre)
    activated_low = activated.astype(BF16)
    result = mixed + scatter_blk(
        jnp.dot(activated_low, down_full, preferred_element_type=F32).reshape(blk, rows, width)
    )

    cot_all = gather_blk(cot_low).reshape(blk * rows, width)
    down_sum = scatter_dp(contract_first(activated_low, cot_all), 1)
    (grad_hidden,) = gelu_pull(contract_last(cot_all, down_full))
    grad_hidden_low = grad_hidden.astype(BF16)
    hidden_sum = jnp.sum(grad_hidden_low.astype(F32), axis=0)
    grad_second = scatter_blk(contract_last(grad_hidden_low, up_full).reshape(blk, rows, width))
    up_sum = scatter_dp(contract_first(second_all, grad_hidden_low), blk)
    grad_mixed_norm, gain_two, bias_two = second_pull(grad_second)
    grad_mixed = cot_low.astype(F32) + grad_mixed_norm
    mixed_all = gather_blk(grad_mixed.astype(BF16)).reshape(blk * rows, width)
    grad_attended = contract_last(mixed_all, out_full).astype(BF16).reshape(blk, rows, heads, HEAD)
    out_sum = scatter_dp(contract_first(attended_low, mixed_all), 1)
    grad_parts = []
    for (first, last), (queries, keys, values, attended, log_total, allowed) in zip(splits, saved):
        grads = attention_backward(
            queries,
            keys,
            values,
            attended,
            grad_attended[:, first:last].reshape(-1, heads, HEAD),
            log_total,
            allowed,
        )
        grads = jnp.concatenate([g.astype(BF16).reshape(-1, part) for g in grads], axis=1)
        grad_parts.append(grads.reshape(blk, last - first, 3 * part))
    grad_projected = jnp.concatenate(grad_parts, axis=1).reshape(blk * rows, 3 * part)
    qkv_sum = scatter_dp(contract_first(normed_all, grad_projected), blk)
    grad_normed = scatter_blk(contract_last(grad_projected, qkv_full).reshape(blk, rows, width))
    grad_input_norm, gain_one, bias_one = first_pull(grad_normed)
    grad_input = (grad_mixed + grad_input_norm).astype(BF16)

    grad_qkv = exchange_blk(qkv_sum.astype(BF16)).astype(F32)
    grad_qkv = grad_qkv.reshape(blk, shard, 3, part).transpose(1, 2, 0, 3).reshape(shard, 3 * width)
    grad_up = exchange_blk(up_sum.astype(BF16)).astype(F32).transpose(1, 0, 2).reshape(shard, -1)
    norms = sum_small(jnp.stack([gain_one, gain_two, bias_one, bias_two]))
    dp = lax.axis_size("dp")
    grad_hidden_bias = jnp.sum(lax.all_to_all(hidden_sum.reshape(dp, -1), "dp", 0, 0), axis=0)
    return (
        result.astype(BF16).reshape(1, 1, rows, width),
        grad_input.reshape(1, 1, rows, width),
        grad_qkv,
        out_sum[0],
        grad_up,
        down_sum[0],
        norms[:2],
        norms[2:],
        grad_hidden_bias,
    )


def solution(mesh):
    return jax.shard_map(
        body,
        mesh=mesh,
        in_specs=(
            P("dp", "blk", None, None),
            P("dp", "blk", None, None),
            P("dp", None),
            P(),
            P(("blk", "dp"), None),
            P(("blk", "dp"), None),
            P(("blk", "dp"), None),
            P(("blk", "dp"), None),
            P(),
            P(),
            P(),
        ),
        out_specs=(
            P("dp", "blk", None, None),
            P("dp", "blk", None, None),
            P(("blk", "dp"), None),
            P(("blk", "dp"), None),
            P(("blk", "dp"), None),
            P(("blk", "dp"), None),
            P(None, ("blk", "dp")),
            P(None, ("blk", "dp")),
            P(("blk", "dp")),
        ),
        check_vma=False,
    )
```

time: 4550 us -> 1250 us (0.27)
  waiting for transfers between devices: 3920 us -> 554 us
  local copies, waits for them, and re-layouts: 44.4 us -> 218 us
  starting transfers between devices: 23.8 us -> 189 us
  matrix products: 366 us -> 204 us
  other arithmetic: 122 us -> 71.7 us
    unnamed x11 -> x0, waiting for transfers between devices: 1930 us -> none
    reduce_scatter x1 -> x0, waiting for transfers between devices: 1400 us -> none  [body(): lax.psum_scatter(contract_first(lax.slice_in_dim(activated_all, 0, w_down...]
    all_gather x4 -> x0, waiting for transfers between devices: 425 us -> none  [the longest x1 177 us: fetch_forward(): lax.all_gather(w_down, ('blk', 'dp'), axis=0, tiled=True)]
    ppermute x28 -> x76, waiting for transfers between devices: 173 us -> 467 us  [the longest x20 263 us: inner_shift(): return lax.ppermute(block, 'dp', route)]
    ppermute x28 -> x76, starting transfers between devices: 23.1 us -> 163 us  [the longest x24 123 us: outer_shift(): return lax.ppermute(block, 'dp', route)]
    dynamic_update_slice x0 -> x56, local copies, waits for them, and re-layouts: none -> 97.8 us  [place(): return lax.dynamic_update_index_in_dim(whole, part, index, axis)]
    all_to_all x0 -> x3, waiting for transfers between devices: none -> 87.6 us  [the longest x1 86 us: body(): lax.all_to_all(hidden_sum.reshape(dp, -1), 'dp', 0, 0)]
    concatenate x1 -> x0, other arithmetic: 86.1 us -> none  [body(): jnp.concatenate([first_term, second_term, third_term], axis=1)]
  transfers between devices with their start and end apart: 36 -> 79, of which waited for: 23 -> 32; matrix products, arithmetic and copies ran while one was open for 7% -> 33% of each run, Pallas kernels for 0% -> 0%
where the time goes in v1:
time: 1250 us; the launch traced here: 1240 us
  waiting for transfers between devices  554 us (44%)
  local copies, waits for them, and re-layouts  218 us (17%)
  matrix products  204 us (16%)
  starting transfers between devices  189 us (15%)
  other arithmetic  71.7 us (6%)
    ppermute x20, waiting for transfers between devices, inner_shift(): return lax.ppermute(block, 'dp', route)  263 us
    ppermute x24, waiting for transfers between devices, outer_shift(): return lax.ppermute(block, 'dp', route)  126 us
    ppermute x24, starting transfers between devices, outer_shift(): return lax.ppermute(block, 'dp', route)  123 us
    dynamic_update_slice x56, local copies, waits for them, and re-layouts, place(): return lax.dynamic_update_index_in_dim(whole, part, index, axis)  97.8 us
    all_to_all x1, waiting for transfers between devices, body(): lax.all_to_all(hidden_sum.reshape(dp, -1), 'dp', 0, 0)  86 us
    ppermute x32, waiting for transfers between devices, flip(): return lax.ppermute(block, 'blk', [(i ^ bits, i) for i in range(count)])  77 us
    dot_general x4, matrix products, contract_last(): lax.dot_general(left, right, (((1,), (1,)), ((), ())), preferred_element_...  63.4 us
    dot_general x4, matrix products, contract_first(): lax.dot_general(left, right, (((0,), (0,)), ((), ())), preferred_element_...  51.1 us
  transfers between devices with their start and end apart: 79, of which 32 were waited for; matrix products, arithmetic and copies ran while one was open for 33% of the time, Pallas kernels for 0%

profile of v1, /device:TPU:0, one launch (start us, length us, event | category | flops | bytes accessed | tf_op | source)
XLA Modules:
  0.0 1240.3 jit_solution(17312899430659580510)
XLA Ops:
  122.5 23.5 %collective-permute-done.17 = bf16[1,64,2048]{2,1,0:T(8,128)(2,1)S(1)} collective-permute-done((bf16[1,64,2048]{2,1,0:T(8,128)(2,1)S(1)}, bf16[1,64,2048]{2,1,0:T(8,128)(2,1)S(1)}, u32[]{:S(2)}, u32[]{:S(2)}) %collective-permute-start.17) | collective-permute-done | bytes 262176 | tf_op jit(solution)/shard_map/ppermute | solution.py:66
  160.8 12.8 %collective-permute-done.6 = bf16[4,64,1536]{2,1,0:T(8,128)(2,1)S(1)} collective-permute-done((bf16[4,64,1536]{2,1,0:T(8,128)(2,1)S(1)}, bf16[4,64,1536]{2,1,0:T(8,128)(2,1)S(1)}, u32[]{:S(2)}, u32[]{:S(2)}) %collective-permute-start.6) | collective-permute-done | bytes 786464 | tf_op jit(solution)/shard_map/ppermute | solution.py:66
  173.6 21.2 %collective-permute-done.7 = bf16[4,64,1536]{2,1,0:T(8,128)(2,1)S(1)} collective-permute-done((bf16[4,64,1536]{2,1,0:T(8,128)(2,1)S(1)}, bf16[4,64,1536]{2,1,0:T(8,128)(2,1)S(1)}, u32[]{:S(2)}, u32[]{:S(2)}) %collective-permute-start.7) | collective-permute-done | bytes 786464 | tf_op jit(solution)/shard_map/ppermute | solution.py:55
  195.9 22.7 %collective-permute-start.9 = (bf16[4,64,1536]{2,1,0:T(8,128)(2,1)S(1)}, bf16[4,64,1536]{2,1,0:T(8,128)(2,1)S(1)}, u32[]{:S(2)}, u32[]{:S(2)}) collective-permute-start(bf16[4,64,1536]{2,1,0:T(8,128)(2,1)S(1)} %bitcast_dynamic-update-slice_fusion.52), channel_id=1, source_target_pairs={{0,4},{1,5},{2,6},{3,7},{4,0},{5,1},{6,2},{7,3},{8,12},{9,13},{10,... | collective-permute-start | bytes 2359304 | tf_op jit(solution)/shard_map/ppermute | solution.py:55
  230.2 20.9 %collective-permute-done.9 = bf16[4,64,1536]{2,1,0:T(8,128)(2,1)S(1)} collective-permute-done((bf16[4,64,1536]{2,1,0:T(8,128)(2,1)S(1)}, bf16[4,64,1536]{2,1,0:T(8,128)(2,1)S(1)}, u32[]{:S(2)}, u32[]{:S(2)}) %collective-permute-start.9) | collective-permute-done | bytes 786464 | tf_op jit(solution)/shard_map/ppermute | solution.py:55
  260.4 33.5 %collective-permute-done.10 = bf16[4,64,1536]{2,1,0:T(8,128)(2,1)S(1)} collective-permute-done((bf16[4,64,1536]{2,1,0:T(8,128)(2,1)S(1)}, bf16[4,64,1536]{2,1,0:T(8,128)(2,1)S(1)}, u32[]{:S(2)}, u32[]{:S(2)}) %collective-permute-start.10) | collective-permute-done | bytes 786464 | tf_op jit(solution)/shard_map/ppermute | solution.py:66
  294.8 15.1 %collective-permute-done.12 = bf16[4,64,1536]{2,1,0:T(8,128)(2,1)S(1)} collective-permute-done((bf16[4,64,1536]{2,1,0:T(8,128)(2,1)S(1)}, bf16[4,64,1536]{2,1,0:T(8,128)(2,1)S(1)}, u32[]{:S(2)}, u32[]{:S(2)}) %collective-permute-start.12) | collective-permute-done | bytes 786464 | tf_op jit(solution)/shard_map/ppermute | solution.py:66
  309.9 35.5 %collective-permute-start.29 = (bf16[4,64,2048]{2,0,1:T(4,128)(2,1)S(1)}, bf16[4,64,2048]{2,0,1:T(4,128)(2,1)}, u32[]{:S(2)}, u32[]{:S(2)}) collective-permute-start(bf16[4,64,2048]{2,0,1:T(4,128)(2,1)S(1)} %dynamic_update_slice.216), channel_id=1, source_target_pairs={{0,2},{1,3},{2,4},{3,5},{4,6},{5,7},{6,0},{7,1},{8,10},{9,11},{10,... | collective-permute-start | bytes 3145736 | tf_op jit(solution)/shard_map/ppermute | solution.py:55
  348.5 11.4 convolution_convert_fusion.2
  418.5 16.5 %collective-permute-done.39 = bf16[1,256,2048]{2,1,0:T(8,128)(2,1)S(1)} collective-permute-done((bf16[1,256,2048]{2,1,0:T(8,128)(2,1)}, bf16[1,256,2048]{2,1,0:T(8,128)(2,1)S(1)}, u32[]{:S(2)}, u32[]{:S(2)}) %collective-permute-start.39) | collective-permute-done | bytes 1048608 | tf_op jit(solution)/shard_map/ppermute | solution.py:66
  440.2 14.5 %collective-permute-done.31 = bf16[4,64,2048]{2,0,1:T(4,128)(2,1)S(1)} collective-permute-done((bf16[4,64,2048]{2,0,1:T(4,128)(2,1)S(1)}, bf16[4,64,2048]{2,0,1:T(4,128)(2,1)S(1)}, u32[]{:S(2)}, u32[]{:S(2)}) %collective-permute-start.31) | collective-permute-done | bytes 1048608 | tf_op jit(solution)/shard_map/ppermute | solution.py:55
  465.4 14.5 %collective-permute-done.30 = bf16[4,64,2048]{2,0,1:T(4,128)(2,1)S(1)} collective-permute-done((bf16[4,64,2048]{2,0,1:T(4,128)(2,1)}, bf16[4,64,2048]{2,0,1:T(4,128)(2,1)S(1)}, u32[]{:S(2)}, u32[]{:S(2)}) %collective-permute-start.30) | collective-permute-done | bytes 1048608 | tf_op jit(solution)/shard_map/ppermute | solution.py:66
  506.6 11.3 copy.374
  533.7 13.8 %fusion.94 = f32[1280,2048]{1,0:T(8,128)} fusion(bf16[1280,2048]{1,0:T(8,128)(2,1)S(1)} %bitcast.537, bf16[2048,2048]{1,0:T(8,128)(2,1)S(1)} %bitcast.515), kind=kOutput, calls=%fused_computation.276 | convolution fusion | flops 10737418240 | bytes 24117248 | tf_op jit(solution)/shard_map/dot_general | solution.py:241
  547.5 26.5 %convert_reduce_fusion = (f32[2048]{0:T(1024)}, bf16[1280,2048]{1,0:T(8,128)(2,1)}, bf16[1280,2048]{1,0:T(8,128)(2,1)}) fusion(f32[1280,2048]{1,0:T(8,128)} %fusion.94, f32[2048]{0:T(1024)S(1)} %dynamic-slice-done, bf16[1280,2048]{1,0:T(8,128)(2,1)} %bitcast.102, bf16[2048,2048]{1,0:T(8,128)(2,1)} %bitcast.89), kind=kOutput, calls=%fused_computation.16 | convolution fusion | flops 10802952192 | bytes 34619392 | tf_op jit(solution)/shard_map/dot_general | solution.py:30
  574.1 15.4 %convolution_convert_fusion.5 = bf16[4,320,2048]{2,1,0:T(8,128)(2,1)S(1)} fusion(bf16[4,320,2048]{2,1,0:T(8,128)(2,1)} %bitcast.573, bf16[2048,2048,1]{1,0,2:T(8,128)(2,1)} %bitcast.90), kind=kOutput, calls=%fused_computation.41 | convolution fusion | flops 10740039680 | bytes 18874368 | tf_op jit(solution)/shard_map/dot_general | solution.py:245
  593.4 13.6 %convolution_convert_fusion.1 = bf16[2048,2048]{1,0:T(8,128)(2,1)S(1)} fusion(bf16[1280,2048]{1,0:T(8,128)(2,1)S(1)} %bitcast.538, bf16[1280,2048]{1,0:T(8,128)(2,1)} %get-tuple-element.16), kind=kOutput, calls=%fused_computation.23 | convolution fusion | flops 10741612544 | bytes 18874368 | tf_op jit(solution)/shard_map/dot_general | solution.py:36
  607.0 15.4 %convolution_convert_fusion.4 = bf16[4,320,2048]{2,1,0:T(8,128)(2,1)S(1)} fusion(bf16[4,320,2048]{2,1,0:T(8,128)(2,1)} %bitcast.574, bf16[2048,2048,1]{1,0,2:T(8,128)(2,1)S(1)} %bitcast.518), kind=kOutput, calls=%fused_computation.40 | convolution fusion | flops 10740039680 | bytes 18874368 | tf_op jit(solution)/shard_map/dot_general | solution.py:30
  627.4 14.9 %convolution_convert_fusion = bf16[2048,2048]{1,0:T(8,128)(2,1)S(1)} fusion(bf16[1280,2048]{1,0:T(8,128)(2,1)} %get-tuple-element.25, bf16[1280,2048]{1,0:T(8,128)(2,1)} %bitcast.102), kind=kOutput, calls=%fused_computation.22 | convolution fusion | flops 10741612544 | bytes 18874368 | tf_op jit(solution)/shard_map/dot_general | solution.py:36
  657.3 25.3 %collective-permute-done.48 = bf16[320,2048]{1,0:T(8,128)(2,1)} collective-permute-done((bf16[320,2048]{1,0:T(8,128)(2,1)}, bf16[320,2048]{1,0:T(8,128)(2,1)}, u32[]{:S(2)}, u32[]{:S(2)}) %collective-permute-start.48) | collective-permute-done | bytes 1310752 | tf_op jit(solution)/shard_map/ppermute | solution.py:43
  685.5 23.6 %collective-permute-done.43 = bf16[320,2048]{1,0:T(8,128)(2,1)} collective-permute-done((bf16[320,2048]{1,0:T(8,128)(2,1)}, bf16[320,2048]{1,0:T(8,128)(2,1)}, u32[]{:S(2)}, u32[]{:S(2)}) %collective-permute-start.43) | collective-permute-done | bytes 1310752 | tf_op jit(solution)/shard_map/ppermute | solution.py:43
  726.1 17.5 %collective-permute-start.66 = (bf16[4,64,2048]{2,1,0:T(8,128)(2,1)S(1)}, bf16[4,64,2048]{2,1,0:T(8,128)(2,1)}, u32[]{:S(2)}, u32[]{:S(2)}) collective-permute-start(bf16[4,64,2048]{2,1,0:T(8,128)(2,1)S(1)} %get-tuple-element.31), channel_id=1, source_target_pairs={{0,2},{1,3},{2,4},{3,5},{4,6},{5,7},{6,0},{7,1},{8,10},{9,11},{10,... | collective-permute-start | bytes 3145736 | tf_op jit(solution)/shard_map/ppermute | solution.py:55
  751.6 56.7 %collective-permute-done.72 = bf16[1,4,256,2048]{3,2,1,0:T(8,128)(2,1)} collective-permute-done((bf16[1,4,256,2048]{3,2,1,0:T(8,128)(2,1)}, bf16[1,4,256,2048]{3,2,1,0:T(8,128)(2,1)}, u32[]{:S(2)}, u32[]{:S(2)}) %collective-permute-start.72) | collective-permute-done | bytes 4194336 | tf_op jit(solution)/shard_map/ppermute | solution.py:66
  816.1 17.5 %collective-permute-start.73 = (bf16[1,256,2048]{2,1,0:T(8,128)(2,1)}, bf16[1,256,2048]{2,1,0:T(8,128)(2,1)S(1)}, u32[]{:S(2)}, u32[]{:S(2)}) collective-permute-start(bf16[1,256,2048]{2,1,0:T(8,128)(2,1)} %get-tuple-element.28), channel_id=1, source_target_pairs={{0,2},{1,3},{2,4},{3,5},{4,6},{5,7},{6,0},{7,1},{8,10},{9,11},{10,... | collective-permute-start | bytes 3145736 | tf_op jit(solution)/shard_map/ppermute | solution.py:55
  841.9 86.0 %all-to-all-done.2 = f32[8,1,256]{2,1,0:T(1,128)S(1)} async-done(((f32[8,1,256]{2,1,0:T(1,128)}), f32[8,1,256]{2,1,0:T(1,128)S(1)}, u32[]{:S(2)}, u32[]{:S(2)}) %all-to-all-start.2) | async-done | bytes 8224 | tf_op jit(solution)/shard_map/all_to_all | solution.py:284
  1007.9 16.0 %bitcast_convert_fusion = bf16[2048,1536]{1,0:T(8,128)(2,1)S(1)} fusion(bf16[4,320,2048]{2,1,0:T(8,128)(2,1)} %bitcast_dynamic-update-slice_fusion.12, bf16[4,64,512]{2,1,0:T(8,128)(2,1)S(1)} %concatenate.34, bf16[4,64,512]{2,1,0:T(8,128)(2,1)S(1)} %concatenate.33, bf16[4,64,512]{2,1,0:T(8,128)(2,1)S(1)} %concatenate.32, bf16[4,256,512]{2,1,0:T(8,128)(2,1)} %copy.388, ...), kind=kOutput, calls=%fused_computation.7 | convolution fusion | flops 8079802368 | bytes 15466496 | tf_op jit(solution)/shard_map/dot_general | solution.py:36
  1023.9 17.0 %convolution_convert_fusion.3 = bf16[4,320,2048]{2,1,0:T(8,128)(2,1)} fusion(bf16[2048,1536,1]{1,0,2:T(8,128)(2,1)} %bitcast.521, bf16[4,64,512]{2,1,0:T(8,128)(2,1)S(1)} %concatenate.34, bf16[4,64,512]{2,1,0:T(8,128)(2,1)S(1)} %concatenate.33, bf16[4,64,512]{2,1,0:T(8,128)(2,1)S(1)} %concatenate.32, bf16[4,256,512]{2,1,0:T(8,128)(2,1)S(1)} %copy-done.43, ...), kind=kOutput, calls=%fused_computation.39 | convolution fusion | flops 8079278080 | bytes 15466496 | tf_op jit(solution)/shard_map/dot_general | solution.py:30
  1052.8 16.8 %collective-permute-done.61 = bf16[1,4,64,2048]{3,2,1,0:T(8,128)(2,1)S(1)} collective-permute-done((bf16[1,4,64,2048]{3,2,1,0:T(8,128)(2,1)S(1)}, bf16[1,4,64,2048]{3,2,1,0:T(8,128)(2,1)S(1)}, u32[]{:S(2)}, u32[]{:S(2)}) %collective-permute-start.61) | collective-permute-done | bytes 1048608 | tf_op jit(solution)/shard_map/ppermute | solution.py:66
  1091.2 45.1 %collective-permute-done.54 = bf16[4,4,64,1536]{3,2,0,1:T(8,128)(2,1)S(1)} collective-permute-done((bf16[4,4,64,1536]{3,2,0,1:T(8,128)(2,1)S(1)}, bf16[4,4,64,1536]{3,2,0,1:T(8,128)(2,1)S(1)}, u32[]{:S(2)}, u32[]{:S(2)}) %collective-permute-start.54) | collective-permute-done | bytes 3145760 | tf_op jit(solution)/shard_map/ppermute | solution.py:66
  1149.9 11.5 collective-permute-done.55
  1161.4 32.3 %collective-permute-done.56 = bf16[4,64,1536]{2,1,0:T(8,128)(2,1)} collective-permute-done((bf16[4,64,1536]{2,1,0:T(8,128)(2,1)}, bf16[4,64,1536]{2,1,0:T(8,128)(2,1)}, u32[]{:S(2)}, u32[]{:S(2)}) %collective-permute-start.56) | collective-permute-done | bytes 786464 | tf_op jit(solution)/shard_map/ppermute | solution.py:55
  1198.7 17.9 %all-to-all-start.1 = ((f32[8,1,256]{2,1,0:T(1,128)}), f32[8,1,256]{2,1,0:T(1,128)S(1)}, u32[]{:S(2)}, u32[]{:S(2)}) async-start(f32[8,1,256]{2,1,0:T(1,128)} %reshape.707), calls=%async_computation.1 | async-start | bytes 16384 | tf_op jit(solution)/shard_map/all_to_all | solution.py:150
  (521 shorter events, 501.4 us)
Async XLA Ops:
  9.3 186.6 %collective-permute-start = (bf16[320,2048]{1,0:T(8,128)(2,1)}, bf16[320,2048]{1,0:T(8,128)(2,1)}, u32[]{:S(2)}, u32[]{:S(2)}) collective-permute-start(bf16[320,2048]{1,0:T(8,128)(2,1)} %fusion.25), channel_id=1, source_target_pairs={{8,0},{0,8},{24,16},{16,24},{9,1},{1,9},{25,17},{17,25},{10,2},{2,... | collective-permute-start | bytes 3932168 | tf_op jit(solution)/shard_map/ppermute | solution.py:43
  9.8 211.4 %collective-permute-start.1 = (bf16[320,2048]{1,0:T(8,128)(2,1)}, bf16[320,2048]{1,0:T(8,128)(2,1)}, u32[]{:S(2)}, u32[]{:S(2)}) collective-permute-start(bf16[320,2048]{1,0:T(8,128)(2,1)} %fusion.25), channel_id=1, source_target_pairs={{16,0},{24,8},{0,16},{8,24},{17,1},{25,9},{1,17},{9,25},{18,2},{26... | collective-permute-start | bytes 3932168 | tf_op jit(solution)/shard_map/ppermute | solution.py:43
  57.6 54.3 %collective-permute-start.16 = (bf16[1,64,2048]{2,1,0:T(8,128)(2,1)}, bf16[1,64,2048]{2,1,0:T(8,128)(2,1)S(1)}, u32[]{:S(2)}, u32[]{:S(2)}) collective-permute-start(bf16[1,64,2048]{2,1,0:T(8,128)(2,1)} %bitcast.563), channel_id=1, source_target_pairs={{0,4},{1,5},{2,6},{3,7},{4,0},{5,1},{6,2},{7,3},{8,12},{9,13},{10,... | collective-permute-start | bytes 786440 | tf_op jit(solution)/shard_map/ppermute | solution.py:55
  153.5 251.9 %collective-permute-start.38 = (bf16[1,256,2048]{2,1,0:T(8,128)(2,1)}, bf16[1,256,2048]{2,1,0:T(8,128)(2,1)}, u32[]{:S(2)}, u32[]{:S(2)}) collective-permute-start(bf16[1,256,2048]{2,1,0:T(8,128)(2,1)} %bitcast.81), channel_id=1, source_target_pairs={{0,4},{1,5},{2,6},{3,7},{4,0},{5,1},{6,2},{7,3},{8,12},{9,13},{10,... | collective-permute-start | bytes 3145736 | tf_op jit(solution)/shard_map/ppermute | solution.py:55
  195.9 55.2 %collective-permute-start.9 = (bf16[4,64,1536]{2,1,0:T(8,128)(2,1)S(1)}, bf16[4,64,1536]{2,1,0:T(8,128)(2,1)S(1)}, u32[]{:S(2)}, u32[]{:S(2)}) collective-permute-start(bf16[4,64,1536]{2,1,0:T(8,128)(2,1)S(1)} %bitcast_dynamic-update-slice_fusion.52), channel_id=1, source_target_pairs={{0,4},{1,5},{2,6},{3,7},{4,0},{5,1},{6,2},{7,3},{8,12},{9,13},{10,... | collective-permute-start | bytes 2359304 | tf_op jit(solution)/shard_map/ppermute | solution.py:55
  226.6 186.5 %collective-permute-start.40 = (bf16[1,256,2048]{2,1,0:T(8,128)(2,1)}, bf16[1,256,2048]{2,1,0:T(8,128)(2,1)}, u32[]{:S(2)}, u32[]{:S(2)}) collective-permute-start(bf16[1,256,2048]{2,1,0:T(8,128)(2,1)} %bitcast.81), channel_id=1, source_target_pairs={{0,6},{1,7},{2,0},{3,1},{4,2},{5,3},{6,4},{7,5},{8,14},{9,15},{10,... | collective-permute-start | bytes 3145736 | tf_op jit(solution)/shard_map/ppermute | solution.py:55
  251.1 151.5 %collective-permute-start.28 = (bf16[4,64,2048]{2,0,1:T(4,128)(2,1)S(1)}, bf16[4,64,2048]{2,0,1:T(4,128)(2,1)}, u32[]{:S(2)}, u32[]{:S(2)}) collective-permute-start(bf16[4,64,2048]{2,0,1:T(4,128)(2,1)S(1)} %dynamic_update_slice.216), channel_id=1, source_target_pairs={{0,1},{1,0},{2,3},{3,2},{4,5},{5,4},{6,7},{7,6},{8,9},{9,8},{10,11... | collective-permute-start | bytes 3145736 | tf_op jit(solution)/shard_map/ppermute | solution.py:66
  294.0 51.4 %collective-permute-start.2 = (bf16[320,2048]{1,0:T(8,128)(2,1)}, bf16[320,2048]{1,0:T(8,128)(2,1)S(1)}, u32[]{:S(2)}, u32[]{:S(2)}) collective-permute-start(bf16[320,2048]{1,0:T(8,128)(2,1)} %collective-permute-done.1), channel_id=1, source_target_pairs={{8,0},{0,8},{24,16},{16,24},{9,1},{1,9},{25,17},{17,25},{10,2},{2,... | collective-permute-start | bytes 3932168 | tf_op jit(solution)/shard_map/ppermute | solution.py:43
  309.9 98.9 %collective-permute-start.29 = (bf16[4,64,2048]{2,0,1:T(4,128)(2,1)S(1)}, bf16[4,64,2048]{2,0,1:T(4,128)(2,1)}, u32[]{:S(2)}, u32[]{:S(2)}) collective-permute-start(bf16[4,64,2048]{2,0,1:T(4,128)(2,1)S(1)} %dynamic_update_slice.216), channel_id=1, source_target_pairs={{0,2},{1,3},{2,4},{3,5},{4,6},{5,7},{6,0},{7,1},{8,10},{9,11},{10,... | collective-permute-start | bytes 3145736 | tf_op jit(solution)/shard_map/ppermute | solution.py:55
  345.4 67.9 %collective-permute-start.37 = (bf16[1,256,2048]{2,1,0:T(8,128)(2,1)}, bf16[1,256,2048]{2,1,0:T(8,128)(2,1)}, u32[]{:S(2)}, u32[]{:S(2)}) collective-permute-start(bf16[1,256,2048]{2,1,0:T(8,128)(2,1)} %collective-permute-done.36), channel_id=1, source_target_pairs={{0,1},{1,0},{2,3},{3,2},{4,5},{5,4},{6,7},{7,6},{8,9},{9,8},{10,11... | collective-permute-start | bytes 3145736 | tf_op jit(solution)/shard_map/ppermute | solution.py:66
  402.6 58.6 %collective-permute-start.20 = (bf16[2,320,2048]{2,1,0:T(8,128)(2,1)S(1)}, bf16[2,320,2048]{2,1,0:T(8,128)(2,1)S(1)}, u32[]{:S(2)}, u32[]{:S(2)}) collective-permute-start(bf16[2,320,2048]{2,1,0:T(8,128)(2,1)S(1)} %dynamic-slice_bitcast_fusion.5), channel_id=1, source_target_pairs={{8,0},{0,8},{24,16},{16,24},{9,1},{1,9},{25,17},{17,25},{10,2},{2,... | collective-permute-start | bytes 7864328 | tf_op jit(solution)/shard_map/ppermute | solution.py:43
  413.4 50.8 %collective-permute-start.41 = (bf16[1,256,2048]{2,1,0:T(8,128)(2,1)}, bf16[1,256,2048]{2,1,0:T(8,128)(2,1)S(1)}, u32[]{:S(2)}, u32[]{:S(2)}) collective-permute-start(bf16[1,256,2048]{2,1,0:T(8,128)(2,1)} %collective-permute-done.40), channel_id=1, source_target_pairs={{0,1},{1,0},{2,3},{3,2},{4,5},{5,4},{6,7},{7,6},{8,9},{9,8},{10,11... | collective-permute-start | bytes 3145736 | tf_op jit(solution)/shard_map/ppermute | solution.py:66
  454.7 72.4 %collective-permute-start.46 = (bf16[320,2048]{1,0:T(8,128)(2,1)}, bf16[320,2048]{1,0:T(8,128)(2,1)}, u32[]{:S(2)}, u32[]{:S(2)}) collective-permute-start(bf16[320,2048]{1,0:T(8,128)(2,1)} %collective-permute-done.45), channel_id=1, source_target_pairs={{8,0},{0,8},{24,16},{16,24},{9,1},{1,9},{25,17},{17,25},{10,2},{2,... | collective-permute-start | bytes 3932168 | tf_op jit(solution)/shard_map/ppermute | solution.py:43
  461.2 63.1 %collective-permute-start.34 = (bf16[4,64,2048]{2,0,1:T(4,128)(2,1)}, bf16[4,64,2048]{2,0,1:T(4,128)(2,1)}, u32[]{:S(2)}, u32[]{:S(2)}) collective-permute-start(bf16[4,64,2048]{2,0,1:T(4,128)(2,1)} %collective-permute-done.33), channel_id=1, source_target_pairs={{0,1},{1,0},{2,3},{3,2},{4,5},{5,4},{6,7},{7,6},{8,9},{9,8},{10,11... | collective-permute-start | bytes 3145736 | tf_op jit(solution)/shard_map/ppermute | solution.py:66
  591.3 59.6 %collective-permute-start.42 = (bf16[2,320,2048]{2,1,0:T(8,128)(2,1)}, bf16[2,320,2048]{2,1,0:T(8,128)(2,1)}, u32[]{:S(2)}, u32[]{:S(2)}) collective-permute-start(bf16[2,320,2048]{2,1,0:T(8,128)(2,1)} %dynamic-slice_bitcast_fusion.4), channel_id=1, source_target_pairs={{8,0},{0,8},{24,16},{16,24},{9,1},{1,9},{25,17},{17,25},{10,2},{2,... | collective-permute-start | bytes 7864328 | tf_op jit(solution)/shard_map/ppermute | solution.py:43
  625.6 93.7 %collective-permute-start.65 = (bf16[4,4,64,2048]{3,2,1,0:T(8,128)(2,1)}, bf16[4,4,64,2048]{3,2,1,0:T(8,128)(2,1)}, u32[]{:S(2)}, u32[]{:S(2)}) collective-permute-start(bf16[4,4,64,2048]{3,2,1,0:T(8,128)(2,1)} %dynamic-slice_bitcast_fusion.1), channel_id=1, source_target_pairs={{0,1},{1,0},{2,3},{3,2},{4,5},{5,4},{6,7},{7,6},{8,9},{9,8},{10,11... | collective-permute-start | bytes 12582920 | tf_op jit(solution)/shard_map/ppermute | solution.py:66
  647.8 160.5 %collective-permute-start.72 = (bf16[1,4,256,2048]{3,2,1,0:T(8,128)(2,1)}, bf16[1,4,256,2048]{3,2,1,0:T(8,128)(2,1)}, u32[]{:S(2)}, u32[]{:S(2)}) collective-permute-start(bf16[1,4,256,2048]{3,2,1,0:T(8,128)(2,1)} %dynamic-slice_bitcast_fusion), channel_id=1, source_target_pairs={{0,1},{1,0},{2,3},{3,2},{4,5},{5,4},{6,7},{7,6},{8,9},{9,8},{10,11... | collective-permute-start | bytes 12582920 | tf_op jit(solution)/shard_map/ppermute | solution.py:66
  655.8 53.3 %collective-permute-start.43 = (bf16[320,2048]{1,0:T(8,128)(2,1)}, bf16[320,2048]{1,0:T(8,128)(2,1)}, u32[]{:S(2)}, u32[]{:S(2)}) collective-permute-start(bf16[320,2048]{1,0:T(8,128)(2,1)} %dynamic-slice_bitcast_fusion.8), channel_id=1, source_target_pairs={{16,0},{24,8},{0,16},{8,24},{17,1},{25,9},{1,17},{9,25},{18,2},{26... | collective-permute-start | bytes 3932168 | tf_op jit(solution)/shard_map/ppermute | solution.py:43
  726.1 107.5 %collective-permute-start.66 = (bf16[4,64,2048]{2,1,0:T(8,128)(2,1)S(1)}, bf16[4,64,2048]{2,1,0:T(8,128)(2,1)}, u32[]{:S(2)}, u32[]{:S(2)}) collective-permute-start(bf16[4,64,2048]{2,1,0:T(8,128)(2,1)S(1)} %get-tuple-element.31), channel_id=1, source_target_pairs={{0,2},{1,3},{2,4},{3,5},{4,6},{5,7},{6,0},{7,1},{8,10},{9,11},{10,... | collective-permute-start | bytes 3145736 | tf_op jit(solution)/shard_map/ppermute | solution.py:55
  743.7 93.4 %collective-permute-start.67 = (bf16[4,64,2048]{2,1,0:T(8,128)(2,1)S(1)}, bf16[4,64,2048]{2,1,0:T(8,128)(2,1)}, u32[]{:S(2)}, u32[]{:S(2)}) collective-permute-start(bf16[4,64,2048]{2,1,0:T(8,128)(2,1)S(1)} %get-tuple-element.33), channel_id=1, source_target_pairs={{0,4},{1,5},{2,6},{3,7},{4,0},{5,1},{6,2},{7,3},{8,12},{9,13},{10,... | collective-permute-start | bytes 3145736 | tf_op jit(solution)/shard_map/ppermute | solution.py:55
  749.2 184.5 %collective-permute-start.50 = (bf16[320,2048]{1,0:T(8,128)(2,1)}, bf16[320,2048]{1,0:T(8,128)(2,1)S(1)}, u32[]{:S(2)}, u32[]{:S(2)}) collective-permute-start(bf16[320,2048]{1,0:T(8,128)(2,1)} %get-tuple-element.18), channel_id=1, source_target_pairs={{16,0},{24,8},{0,16},{8,24},{17,1},{25,9},{1,17},{9,25},{18,2},{26... | collective-permute-start | bytes 3932168 | tf_op jit(solution)/shard_map/ppermute | solution.py:43
  749.5 179.1 %collective-permute-start.68 = (bf16[4,64,2048]{2,1,0:T(8,128)(2,1)}, bf16[4,64,2048]{2,1,0:T(8,128)(2,1)}, u32[]{:S(2)}, u32[]{:S(2)}) collective-permute-start(bf16[4,64,2048]{2,1,0:T(8,128)(2,1)} %get-tuple-element.32), channel_id=1, source_target_pairs={{0,6},{1,7},{2,0},{3,1},{4,2},{5,3},{6,4},{7,5},{8,14},{9,15},{10,... | collective-permute-start | bytes 3145736 | tf_op jit(solution)/shard_map/ppermute | solution.py:55
  816.1 118.5 %collective-permute-start.73 = (bf16[1,256,2048]{2,1,0:T(8,128)(2,1)}, bf16[1,256,2048]{2,1,0:T(8,128)(2,1)S(1)}, u32[]{:S(2)}, u32[]{:S(2)}) collective-permute-start(bf16[1,256,2048]{2,1,0:T(8,128)(2,1)} %get-tuple-element.28), channel_id=1, source_target_pairs={{0,2},{1,3},{2,4},{3,5},{4,6},{5,7},{6,0},{7,1},{8,10},{9,11},{10,... | collective-permute-start | bytes 3145736 | tf_op jit(solution)/shard_map/ppermute | solution.py:55
  833.7 101.0 %collective-permute-start.74 = (bf16[1,256,2048]{2,1,0:T(8,128)(2,1)}, bf16[1,256,2048]{2,1,0:T(8,128)(2,1)}, u32[]{:S(2)}, u32[]{:S(2)}) collective-permute-start(bf16[1,256,2048]{2,1,0:T(8,128)(2,1)} %get-tuple-element.30), channel_id=1, source_target_pairs={{0,4},{1,5},{2,6},{3,7},{4,0},{5,1},{6,2},{7,3},{8,12},{9,13},{10,... | collective-permute-start | bytes 3145736 | tf_op jit(solution)/shard_map/ppermute | solution.py:55
  837.1 97.6 %collective-permute-start.75 = (bf16[1,256,2048]{2,1,0:T(8,128)(2,1)}, bf16[1,256,2048]{2,1,0:T(8,128)(2,1)}, u32[]{:S(2)}, u32[]{:S(2)}) collective-permute-start(bf16[1,256,2048]{2,1,0:T(8,128)(2,1)} %get-tuple-element.29), channel_id=1, source_target_pairs={{0,6},{1,7},{2,0},{3,1},{4,2},{5,3},{6,4},{7,5},{8,14},{9,15},{10,... | collective-permute-start | bytes 3145736 | tf_op jit(solution)/shard_map/ppermute | solution.py:55
  837.1 90.8 %all-to-all-start.2 = ((f32[8,1,256]{2,1,0:T(1,128)}), f32[8,1,256]{2,1,0:T(1,128)S(1)}, u32[]{:S(2)}, u32[]{:S(2)}) async-start(f32[8,1,256]{2,1,0:T(1,128)} %bitcast.183), calls=%async_computation.2 | async-start | bytes 16384 | tf_op jit(solution)/shard_map/all_to_all | solution.py:284
  940.8 105.5 %collective-permute-start.70 = (bf16[64,2048]{1,0:T(8,128)(2,1)}, bf16[64,2048]{1,0:T(8,128)(2,1)}, u32[]{:S(2)}, u32[]{:S(2)}) collective-permute-start(bf16[64,2048]{1,0:T(8,128)(2,1)} %get-tuple-element.39), channel_id=1, source_target_pairs={{16,0},{24,8},{0,16},{8,24},{17,1},{25,9},{1,17},{9,25},{18,2},{26... | collective-permute-start | bytes 786440 | tf_op jit(solution)/shard_map/ppermute | solution.py:43
  941.4 106.6 %collective-permute-start.71 = (bf16[64,2048]{1,0:T(8,128)(2,1)}, bf16[64,2048]{1,0:T(8,128)(2,1)}, u32[]{:S(2)}, u32[]{:S(2)}) collective-permute-start(bf16[64,2048]{1,0:T(8,128)(2,1)} %get-tuple-element.38), channel_id=1, source_target_pairs={{24,0},{16,8},{8,16},{0,24},{25,1},{17,9},{9,17},{1,25},{26,2},{18... | collective-permute-start | bytes 786440 | tf_op jit(solution)/shard_map/ppermute | solution.py:43
  1044.7 91.6 %collective-permute-start.54 = (bf16[4,4,64,1536]{3,2,0,1:T(8,128)(2,1)S(1)}, bf16[4,4,64,1536]{3,2,0,1:T(8,128)(2,1)S(1)}, u32[]{:S(2)}, u32[]{:S(2)}) collective-permute-start(bf16[4,4,64,1536]{3,2,0,1:T(8,128)(2,1)S(1)} %bitcast.542), channel_id=1, source_target_pairs={{0,1},{1,0},{2,3},{3,2},{4,5},{5,4},{6,7},{7,6},{8,9},{9,8},{10,11... | collective-permute-start | bytes 9437192 | tf_op jit(solution)/shard_map/ppermute | solution.py:66
  1075.2 67.6 %collective-permute-start.53 = (bf16[320,2048]{1,0:T(8,128)(2,1)S(1)}, bf16[320,2048]{1,0:T(8,128)(2,1)S(1)}, u32[]{:S(2)}, u32[]{:S(2)}) collective-permute-start(bf16[320,2048]{1,0:T(8,128)(2,1)S(1)} %dynamic-slice_bitcast_fusion.6), channel_id=1, source_target_pairs={{16,0},{24,8},{0,16},{8,24},{17,1},{25,9},{1,17},{9,25},{18,2},{26... | collective-permute-start | bytes 3932168 | tf_op jit(solution)/shard_map/ppermute | solution.py:43
  1139.4 54.3 %collective-permute-start.56 = (bf16[4,64,1536]{2,1,0:T(8,128)(2,1)}, bf16[4,64,1536]{2,1,0:T(8,128)(2,1)}, u32[]{:S(2)}, u32[]{:S(2)}) collective-permute-start(bf16[4,64,1536]{2,1,0:T(8,128)(2,1)} %get-tuple-element.36), channel_id=1, source_target_pairs={{0,4},{1,5},{2,6},{3,7},{4,0},{5,1},{6,2},{7,3},{8,12},{9,13},{10,... | collective-permute-start | bytes 2359304 | tf_op jit(solution)/shard_map/ppermute | solution.py:55
  1139.4 54.3 %collective-permute-start.57 = (bf16[4,64,1536]{2,1,0:T(8,128)(2,1)}, bf16[4,64,1536]{2,1,0:T(8,128)(2,1)}, u32[]{:S(2)}, u32[]{:S(2)}) collective-permute-start(bf16[4,64,1536]{2,1,0:T(8,128)(2,1)} %get-tuple-element.35), channel_id=1, source_target_pairs={{0,6},{1,7},{2,0},{3,1},{4,2},{5,3},{6,4},{7,5},{8,14},{9,15},{10,... | collective-permute-start | bytes 2359304 | tf_op jit(solution)/shard_map/ppermute | solution.py:55
  (131 other events, 2972.4 us)

commit v2 on v1

v2 whole, which is shorter than its diff:
```python
import jax
import jax.numpy as jnp
from jax import lax
from jax.sharding import PartitionSpec as P

HEAD = 128
BLK_A = 256
BLK_B = 64

EPSILON = 1e-05
NEGATIVE = -1e30
BF16 = jnp.bfloat16
F32 = jnp.float32


def after(value, *others):
    return lax.optimization_barrier((value, others))[0]


def layer_norm(value, gain, bias):
    center = value - jnp.mean(value, axis=-1, keepdims=True)
    spread = jnp.mean(center * center, axis=-1, keepdims=True)
    return center * lax.rsqrt(spread + EPSILON) * gain + bias


def contract_last(left, right):
    return lax.dot_general(
        left, right, (((1,), (1,)), ((), ())), preferred_element_type=F32
    )


def contract_first(left, right):
    return lax.dot_general(
        left, right, (((0,), (0,)), ((), ())), preferred_element_type=F32
    )


def flip(axis, bits, block):
    count = lax.axis_size(axis)
    return lax.ppermute(block, axis, [(i ^ bits, i) for i in range(count)])


def flip_core(block):
    return flip("blk", 1, block)


def flip_x(block):
    return flip("blk", 2, block)


def flip_y(block):
    return flip("dp", 1, block)


def lines():
    count = lax.axis_size("dp")
    return [[z * 2 + y for z in range(count // 2)] for y in range(2)]


def gather_z(part, axis):
    return lax.all_gather(part, "dp", axis_index_groups=lines(), axis=axis, tiled=True)


def scatter_z(total, axis):
    return lax.psum_scatter(
        total, "dp", axis_index_groups=lines(), scatter_dimension=axis, tiled=True
    )


def by_y(own, other):
    y = lax.axis_index("dp") % 2
    return jnp.where(y == 0, own, other), jnp.where(y == 0, other, own)


def exchange(cut):
    y = lax.axis_index("dp") % 2
    other = flip_y(cut(1 - y))
    both = jnp.stack(by_y(cut(y), other), axis=1)
    return lax.all_to_all(both, "blk", 0, 0)


def gather_plane(part):
    half = part.shape[0] // 2
    from_x, from_y, from_core = flip_x(part), flip_y(part), flip_core(part)
    diagonal = jnp.concatenate([flip_y(from_x[:half]), flip_x(from_y[half:])], axis=0)
    mine = [part, from_x, from_y, diagonal]
    return jnp.concatenate(
        mine + [from_core] + [flip_core(piece) for piece in mine[1:]], axis=0
    )


def scatter_plane(product, rows):
    half = rows // 2
    got = flip_core(product(4, 8).astype(BF16))
    held = product(0, 4) + got.astype(F32)
    own, to_x, to_y, across = [held[i * rows : (i + 1) * rows] for i in range(4)]
    across = across.astype(BF16)
    x_across, y_across = flip_x(across[:half]), flip_y(across[half:])
    x_top = flip_x(to_x[:half].astype(BF16))
    y_bottom = flip_y(to_y[half:].astype(BF16))
    y_top = flip_y((to_y[:half] + x_across.astype(F32)).astype(BF16))
    x_bottom = flip_x((to_x[half:] + y_across.astype(F32)).astype(BF16))
    top = own[:half] + x_top.astype(F32) + y_top.astype(F32)
    bottom = own[half:] + x_bottom.astype(F32) + y_bottom.astype(F32)
    return jnp.concatenate([top, bottom], axis=0)


def sum_over(total, axis, bits):
    while bits < lax.axis_size(axis):
        total = total + flip(axis, bits, total)
        bits *= 2
    return total


def allowed_of(places, length):
    return (places[None, :] <= places[:, None]) & (places[None, :] < length)


def scores_of(queries, keys, allowed):
    scores = jnp.einsum("qhd,khd->hqk", queries, keys, preferred_element_type=F32) * HEAD ** (-0.5)
    return jnp.where(allowed[None], scores, NEGATIVE)


def attention_forward(queries, keys, values, allowed):
    scores = scores_of(queries, keys, allowed)
    peak = jnp.max(scores, axis=-1, keepdims=True)
    log_total = peak + jnp.log(jnp.sum(jnp.exp(scores - peak), axis=-1, keepdims=True))
    probs = jnp.where(allowed[None], jnp.exp(scores - log_total), 0.0).astype(BF16)
    attended = jnp.einsum("hqk,khd->qhd", probs, values, preferred_element_type=F32)
    return attended, log_total


def attention_backward(queries, keys, values, attended, grad_attended, log_total, allowed):
    scale = HEAD ** (-0.5)
    delta = jnp.einsum("qhd,qhd->hq", grad_attended.astype(F32), attended)
    scores = scores_of(queries, keys, allowed)
    probs = jnp.where(allowed[None], jnp.exp(scores - log_total), 0.0)
    grad_values = jnp.einsum(
        "hqk,qhd->khd", probs.astype(BF16), grad_attended, preferred_element_type=F32
    )
    grad_probs = jnp.einsum("qhd,khd->hqk", grad_attended, values, preferred_element_type=F32)
    grad_scores = (probs * (grad_probs - delta[..., None])).astype(BF16)
    grad_queries = scale * jnp.einsum("hqk,khd->qhd", grad_scores, keys, preferred_element_type=F32)
    grad_keys = scale * jnp.einsum("hqk,qhd->khd", grad_scores, queries, preferred_element_type=F32)
    return grad_queries, grad_keys, grad_values


def body(
    hidden_in,
    cotangent,
    seq_lengths,
    block_order,
    w_qkv,
    w_out,
    w_up,
    w_down,
    norm_gains,
    norm_biases,
    hidden_bias,
):
    blk, dp = lax.axis_size("blk"), lax.axis_size("dp")
    lanes = dp // 2
    b, d = lax.axis_index("blk"), lax.axis_index("dp")
    z, y = d // 2, d % 2
    rows, width = hidden_in.shape[2:]
    pairs = width // HEAD // blk // 2
    part = pairs * HEAD
    shard = w_qkv.shape[0]
    units = w_down.shape[0]
    x = hidden_in.reshape(rows, width).astype(F32)
    cot_low = cotangent.reshape(rows, width)
    splits = ((0, BLK_A), (BLK_A, BLK_A + BLK_B))

    def cut_qkv(to_y):
        view = w_qkv.reshape(shard, 3, blk, pairs, 2, HEAD)
        view = lax.dynamic_index_in_dim(view, to_y, 4, keepdims=False)
        return view.transpose(2, 0, 1, 3, 4).reshape(blk, shard, 3 * part)

    def cut_up(to_y):
        view = w_up.reshape(shard, blk, lanes, 2, units)
        view = lax.dynamic_index_in_dim(view, to_y, 3, keepdims=False)
        return view.transpose(1, 0, 2, 3).reshape(blk, shard, lanes * units)

    pieces = [[p for p in range(dp) if (p * shard // HEAD) % 2 == to_y] for to_y in range(2)]
    route = [(pieces[to_y][lane], lane * 2 + to_y) for to_y in range(2) for lane in range(lanes)]

    out_full = gather_z(lax.ppermute(w_out, "dp", route), 0)
    qkv_part = exchange(cut_qkv).reshape(blk, 2 * shard, 3 * part)
    qkv_full = gather_z(qkv_part, 1).reshape(width, 3 * part)
    up_part = exchange(cut_up).reshape(blk, 2 * shard, lanes * units)
    up_full = gather_z(up_part, 1).reshape(width, lanes * units)
    down_full = gather_z(w_down, 0)

    normed, first_pull = jax.vjp(layer_norm, x, norm_gains[0], norm_biases[0])
    normed_all = gather_plane(normed.astype(BF16))
    cot_all = gather_plane(after(cot_low, normed_all))
    projected = jnp.dot(normed_all, qkv_full, preferred_element_type=F32).astype(BF16)
    held = projected.reshape(2, 2, 2, rows, 3, pairs, HEAD)
    lengths = [seq_lengths, flip_y(seq_lengths)]

    def sequences(array, select):
        return [select(array[:, s, :, first:last]) for first, last in splits for s in range(2)]

    def back(parts):
        joined = []
        for column, (first, last) in enumerate(splits):
            pair = [p.reshape(2, 2, last - first, -1) for p in parts[2 * column : 2 * column + 2]]
            joined.append(jnp.stack(pair, axis=1))
        return jnp.concatenate(joined, axis=3).reshape(8 * rows, -1)

    states = []
    for index, mine in enumerate(sequences(held, lambda v: v.reshape(-1, 3, pairs, HEAD))):
        column, s = index // 2, index % 2
        count = splits[column][1] - splits[column][0]
        blocks = jnp.stack(
            [
                lax.dynamic_index_in_dim(block_order[column], b ^ (far * 2 + core), 0, keepdims=False)
                for core in range(2)
                for far in range(2)
            ]
        )
        places = (
            blocks[:, None] * count + jnp.arange(count, dtype=jnp.int32)[None, :]
        ).reshape(4 * count)
        allowed = allowed_of(places, lengths[s][0, column])
        queries, keys, values = mine[:, 0], mine[:, 1], mine[:, 2]
        attended, log_total = attention_forward(queries, keys, values, allowed)
        states.append((queries, keys, values, attended, log_total, allowed))
    attended_low = back([state[3].astype(BF16).reshape(-1, part) for state in states])

    def times(left, right):
        return lambda first, last: jnp.dot(
            left[first * rows : last * rows], right, preferred_element_type=F32
        )

    def times_transposed(left, right):
        return lambda first, last: contract_last(left[first * rows : last * rows], right)

    mixed = x + scatter_plane(times(attended_low, out_full), rows)
    second, second_pull = jax.vjp(layer_norm, mixed, norm_gains[1], norm_biases[1])
    second_all = gather_plane(second.astype(BF16))
    bias_part = lax.dynamic_slice_in_dim(
        hidden_bias.reshape(blk, lanes, 2, units), b, 1, 0
    )
    bias_part = lax.dynamic_index_in_dim(bias_part, y, 2, keepdims=False).reshape(-1)
    hidden_pre = jnp.dot(second_all, up_full, preferred_element_type=F32) + bias_part
    activated, gelu_pull = jax.vjp(lambda v: jax.nn.gelu(v, approximate=True), hidden_pre)
    activated_low = activated.astype(BF16)

    down_sum = scatter_z(contract_first(activated_low, cot_all).astype(BF16), 0)
    (grad_hidden,) = gelu_pull(contract_last(cot_all, down_full))
    grad_hidden_low = grad_hidden.astype(BF16)
    hidden_sum = jnp.sum(grad_hidden_low.astype(F32), axis=0)
    grad_second = scatter_plane(times_transposed(grad_hidden_low, up_full), rows)
    up_sum = contract_first(second_all, grad_hidden_low).astype(BF16)
    up_sum = scatter_z(up_sum.reshape(blk, -1, lanes * units), 1)
    grad_mixed_norm, gain_two, bias_two = second_pull(grad_second)
    grad_mixed = cot_low.astype(F32) + grad_mixed_norm
    mixed_all = gather_plane(grad_mixed.astype(BF16))
    result = mixed + scatter_plane(times(after(activated_low, mixed_all), down_full), rows)
    grad_attended = contract_last(mixed_all, out_full).astype(BF16)
    out_sum = contract_first(attended_low, mixed_all).astype(BF16)
    grad_parts = []
    grad_views = sequences(
        grad_attended.reshape(2, 2, 2, rows, pairs, HEAD), lambda v: v.reshape(-1, pairs, HEAD)
    )
    for grad_view, (queries, keys, values, attended, log_total, allowed) in zip(grad_views, states):
        grads = attention_backward(
            queries, keys, values, attended, grad_view, log_total, allowed
        )
        grad_parts.append(
            jnp.concatenate([g.astype(BF16).reshape(-1, part) for g in grads], axis=1)
        )
    grad_projected = back(grad_parts)
    qkv_sum = contract_first(normed_all, grad_projected).astype(BF16)
    qkv_sum = scatter_z(qkv_sum.reshape(blk, -1, 3 * part), 1)
    out_sum = scatter_z(out_sum, 0)
    grad_normed = scatter_plane(times_transposed(grad_projected, qkv_full), rows)
    grad_input_norm, gain_one, bias_one = first_pull(grad_normed)
    grad_input = (grad_mixed + grad_input_norm).astype(BF16)

    def give_back(total):
        parts = total.reshape(blk, 2, shard, -1)
        return exchange(lambda to_y: lax.dynamic_index_in_dim(parts, to_y, 1, keepdims=False))

    grad_up = give_back(up_sum).reshape(blk, 2, shard, lanes, units).astype(F32)
    grad_up = grad_up.transpose(2, 0, 3, 1, 4).reshape(shard, -1)
    grad_qkv = give_back(qkv_sum).reshape(blk, 2, shard, 3, pairs, HEAD).astype(F32)
    grad_qkv = grad_qkv.transpose(2, 3, 0, 4, 1, 5).reshape(shard, -1)
    grad_out = lax.ppermute(out_sum, "dp", [(j, i) for i, j in route]).astype(F32)
    small = jnp.concatenate([gain_one, gain_two, bias_one, bias_two, hidden_sum])
    small = sum_over(small, "dp", 2)
    norms = small[: 4 * width].reshape(4, width)
    norms = sum_over(norms + flip_y(norms), "blk", 1)
    norms = lax.dynamic_slice_in_dim(norms, (b * dp + d) * shard, shard, 1)
    grad_hidden_bias = lax.dynamic_slice_in_dim(small, 4 * width + z * units, units)
    return (
        result.astype(BF16).reshape(1, 1, rows, width),
        grad_input.reshape(1, 1, rows, width),
        grad_qkv,
        grad_out,
        grad_up,
        down_sum.astype(F32),
        norms[:2],
        norms[2:],
        grad_hidden_bias,
    )


def solution(mesh):
    return jax.shard_map(
        body,
        mesh=mesh,
        in_specs=(
            P("dp", "blk", None, None),
            P("dp", "blk", None, None),
            P("dp", None),
            P(),
            P(("blk", "dp"), None),
            P(("blk", "dp"), None),
            P(("blk", "dp"), None),
            P(("blk", "dp"), None),
            P(),
            P(),
            P(),
        ),
        out_specs=(
            P("dp", "blk", None, None),
            P("dp", "blk", None, None),
            P(("blk", "dp"), None),
            P(("blk", "dp"), None),
            P(("blk", "dp"), None),
            P(("blk", "dp"), None),
            P(None, ("blk", "dp")),
            P(None, ("blk", "dp")),
            P(("blk", "dp")),
        ),
        check_vma=False,
    )
```

time: 1250 us -> 887 us (0.71)
  waiting for transfers between devices: 554 us -> 294 us
  starting transfers between devices: 189 us -> 81.5 us
  local copies, waits for them, and re-layouts: 218 us -> 133 us
  matrix products: 204 us -> 240 us
  blocking collectives: 0 us -> 32.6 us
  between operations: 2.56 us -> 16.6 us
    ppermute x76 -> x72, waiting for transfers between devices: 467 us -> 287 us  [the longest x70 287 us: flip(): return lax.ppermute(block, axis, [(i ^ bits, i) for i in range(count)])]
    dynamic_update_slice x56 -> x0, local copies, waits for them, and re-layouts: 97.8 us -> none  [place(): return lax.dynamic_update_index_in_dim(whole, part, index, axis)]
    ppermute x76 -> x72, starting transfers between devices: 163 us -> 73.4 us  [the longest x70 68.2 us: flip(): return lax.ppermute(block, axis, [(i ^ bits, i) for i in range(count)])]
    all_to_all x3 -> x2, waiting for transfers between devices: 87.6 us -> 7.09 us  [exchange(): return lax.all_to_all(both, 'blk', 0, 0)]
    all_to_all x0 -> x2, blocking collectives: none -> 32.6 us  [exchange(): return lax.all_to_all(both, 'blk', 0, 0)]
    squeeze x21 -> x2, local copies, waits for them, and re-layouts: 24.1 us -> 2.86 us  [give_back(): lax.dynamic_index_in_dim(parts, to_y, 1, keepdims=False)]
    broadcast_in_dim x7 -> x0, local copies, waits for them, and re-layouts: 18.8 us -> none  [the longest x4 14.3 us: gather_dp(): whole = jnp.zeros((groups, count, rows, columns), part.dtype)]
    all_to_all x3 -> x2, starting transfers between devices: 26 us -> 7.18 us  [exchange(): return lax.all_to_all(both, 'blk', 0, 0)]
  transfers between devices with their start and end apart: 79 -> 82, of which waited for: 32 -> 32; matrix products, arithmetic and copies ran while one was open for 33% -> 43% of each run, Pallas kernels for 0% -> 0%
where the time goes in v2:
time: 887 us; the launch traced here: 877 us
  waiting for transfers between devices  294 us (33%)
  matrix products  240 us (27%)
  local copies, waits for them, and re-layouts  133 us (15%)
  starting transfers between devices  81.5 us (9%)
  other arithmetic  78.8 us (9%)
  blocking collectives  32.6 us (4%)
  between operations  16.6 us (2%)
    ppermute x70, waiting for transfers between devices, flip(): return lax.ppermute(block, axis, [(i ^ bits, i) for i in range(count)])  287 us
    ppermute x70, starting transfers between devices, flip(): return lax.ppermute(block, axis, [(i ^ bits, i) for i in range(count)])  68.2 us
    dot_general x6, matrix products, contract_last(): lax.dot_general(left, right, (((1,), (1,)), ((), ())), preferred_element_...  66.9 us
    dot_general x4, matrix products, contract_first(): lax.dot_general(left, right, (((0,), (0,)), ((), ())), preferred_element_...  46.5 us
    unnamed x233, local copies, waits for them, and re-layouts  42.1 us
    all_to_all x2, blocking collectives, exchange(): return lax.all_to_all(both, 'blk', 0, 0)  32.6 us
    dot_general x4, matrix products, times(): jnp.dot(left[first * rows:last * rows], right, preferred_element_type=F32)  29.1 us
    concatenate x18, local copies, waits for them, and re-layouts, body(): jnp.concatenate([g.astype(BF16).reshape(-1, part) for g in grads], axis=1)  17.8 us
  transfers between devices with their start and end apart: 82, of which 32 were waited for; matrix products, arithmetic and copies ran while one was open for 43% of the time, Pallas kernels for 0%

profile of v2, /device:TPU:0, one launch (start us, length us, event | category | flops | bytes accessed | tf_op | source)
XLA Modules:
  0.0 876.6 jit_solution(9581353177938904191)
XLA Ops:
  16.0 8.5 collective-permute-done.8
  24.8 14.9 %all_to_all.20 = bf16[4,2,64,768]{3,2,1,0:T(8,128)(2,1)} all-to-all(bf16[4,2,64,768]{3,2,1,0:T(8,128)(2,1)S(1)} %copy.222), channel_id=1, replica_groups=mesh['blk'=4,'dp'=8] {'blk'}, dimensions={0} | all-to-all | bytes 1572864 | tf_op jit(solution)/shard_map/all_to_all | solution.py:79
  57.3 23.1 %collective-permute-done.9 = s32[1,2]{1,0:T(1,128)S(1)} collective-permute-done((s32[1,2]{1,0:T(1,128)S(1)}, s32[1,2]{1,0:T(1,128)S(1)}, u32[]{:S(2)}, u32[]{:S(2)}) %collective-permute-start.9) | collective-permute-done | bytes 40 | tf_op jit(solution)/shard_map/ppermute | solution.py:40
  116.4 13.6 %convolution_convert_fusion.4 = bf16[2560,768]{1,0:T(8,128)(2,1)} fusion(bf16[2560,2048]{1,0:T(8,128)(2,1)} %constant_dynamic-update-slice_fusion, bf16[2048,768]{1,0:T(8,128)(2,1)} %bitcast.429), kind=kOutput, calls=%fused_computation.33 | convolution fusion | flops 8055029760 | bytes 17563648 | tf_op jit(solution)/shard_map/dot_general | solution.py:197
  130.0 8.3 reshape.772
  167.4 7.6 bitcast_convert_fusion.1
  192.5 12.1 %collective-permute-done.26 = bf16[4,64,1024]{2,1,0:T(8,128)(2,1)S(1)} collective-permute-done((bf16[4,64,1024]{2,1,0:T(8,128)(2,1)S(1)}, bf16[4,64,1024]{2,1,0:T(8,128)(2,1)S(1)}, u32[]{:S(2)}, u32[]{:S(2)}) %collective-permute-start.26) | collective-permute-done | bytes 524320 | tf_op jit(solution)/shard_map/ppermute | solution.py:40
  204.9 17.7 %all_to_all.21 = bf16[4,2,64,1024]{3,2,1,0:T(8,128)(2,1)} all-to-all(bf16[4,2,64,1024]{3,2,1,0:T(8,128)(2,1)S(1)} %copy.244), channel_id=1, replica_groups=mesh['blk'=4,'dp'=8] {'blk'}, dimensions={0} | all-to-all | bytes 2097152 | tf_op jit(solution)/shard_map/all_to_all | solution.py:79
  230.8 13.9 %collective-permute-done.13 = bf16[160,2048]{1,0:T(8,128)(2,1)S(1)} collective-permute-done((bf16[160,2048]{1,0:T(8,128)(2,1)S(1)}, bf16[160,2048]{1,0:T(8,128)(2,1)S(1)}, u32[]{:S(2)}, u32[]{:S(2)}) %collective-permute-start.13) | collective-permute-done | bytes 655392 | tf_op jit(solution)/shard_map/ppermute | solution.py:40
  247.2 11.5 %collective-permute-done.12 = bf16[160,2048]{1,0:T(8,128)(2,1)S(1)} collective-permute-done((bf16[160,2048]{1,0:T(8,128)(2,1)S(1)}, bf16[160,2048]{1,0:T(8,128)(2,1)S(1)}, u32[]{:S(2)}, u32[]{:S(2)}) %collective-permute-start.12) | collective-permute-done | bytes 655392 | tf_op jit(solution)/shard_map/ppermute | solution.py:40
  265.9 24.9 %collective-permute-done.28 = bf16[320,2048]{1,0:T(8,128)(2,1)} collective-permute-done((bf16[320,2048]{1,0:T(8,128)(2,1)}, bf16[320,2048]{1,0:T(8,128)(2,1)}, u32[]{:S(2)}, u32[]{:S(2)}) %collective-permute-start.28) | collective-permute-done | bytes 1310752 | tf_op jit(solution)/shard_map/ppermute | solution.py:40
  296.6 8.2 collective-permute-done.17
  318.4 24.5 %collective-permute-done.19 = bf16[320,2048]{1,0:T(8,128)(2,1)S(1)} collective-permute-done((bf16[320,2048]{1,0:T(8,128)(2,1)S(1)}, bf16[320,2048]{1,0:T(8,128)(2,1)S(1)}, u32[]{:S(2)}, u32[]{:S(2)}) %collective-permute-start.19) | collective-permute-done | bytes 1310752 | tf_op jit(solution)/shard_map/ppermute | solution.py:40
  348.7 9.3 %collective-permute-done.21 = bf16[160,2048]{1,0:T(8,128)(2,1)S(1)} collective-permute-done((bf16[160,2048]{1,0:T(8,128)(2,1)S(1)}, bf16[160,2048]{1,0:T(8,128)(2,1)S(1)}, u32[]{:S(2)}, u32[]{:S(2)}) %collective-permute-start.21) | collective-permute-done | bytes 655392 | tf_op jit(solution)/shard_map/ppermute | solution.py:40
  367.2 16.6 %fusion.154 = f32[2560,1024]{1,0:T(8,128)} fusion(bf16[2560,2048]{1,0:T(8,128)(2,1)} %constant_dynamic-update-slice_fusion.9, bf16[2048,1024]{1,0:T(8,128)(2,1)} %bitcast.426), kind=kOutput, calls=%fused_computation.341 | convolution fusion | flops 10737418240 | bytes 25165824 | tf_op jit(solution)/shard_map/dot_general | solution.py:246
  383.9 26.5 %convert_reduce_fusion = (f32[1024]{0:T(1024)}, bf16[2560,1024]{1,0:T(8,128)(2,1)}, bf16[2560,1024]{1,0:T(8,128)(2,1)}) fusion(f32[2560,1024]{1,0:T(8,128)} %fusion.154, f32[1024]{0:T(1024)S(1)} %bitcast.425, bf16[2560,2048]{1,0:T(8,128)(2,1)} %copy-done.57, bf16[1024,2048]{1,0:T(8,128)(2,1)} %all-gather.11.cloned.1.call-done), kind=kOutput, calls=%fused_computation.9 | convolution fusion | flops 10802953216 | bytes 35659776 | tf_op jit(solution)/shard_map/dot_general | solution.py:27
  410.4 8.0 convolution_convert_fusion.2
  418.9 8.4 collective-permute-done.35
  427.3 9.6 %fusion.152 = (bf16[1280,2048]{1,0:T(8,128)(2,1)S(1)}, f32[1280,2048]{1,0:T(8,128)S(1)}) fusion(bf16[1280,2048]{1,0:T(8,128)(2,1)} %collective-permute-done.35, bf16[2048,1024]{1,0:T(8,128)(2,1)} %bitcast.427, bf16[2560,1024]{1,0:T(8,128)(2,1)} %get-tuple-element.18), kind=kOutput, calls=%fused_computation.339 | convolution fusion | flops 5376573440 | bytes 27787264 | tf_op jit(solution)/shard_map/dot_general | solution.py:27
  441.1 13.8 %collective-permute-done.37 = bf16[160,2048]{1,0:T(8,128)(2,1)S(1)} collective-permute-done((bf16[160,2048]{1,0:T(8,128)(2,1)S(1)}, bf16[160,2048]{1,0:T(8,128)(2,1)S(1)}, u32[]{:S(2)}, u32[]{:S(2)}) %collective-permute-start.37) | collective-permute-done | bytes 655392 | tf_op jit(solution)/shard_map/ppermute | solution.py:40
  457.6 15.4 %convolution_convert_fusion.7 = bf16[2048,1024]{1,0:T(8,128)(2,1)} fusion(bf16[2560,2048]{1,0:T(8,128)(2,1)} %constant_dynamic-update-slice_fusion.9, bf16[2560,1024]{1,0:T(8,128)(2,1)S(1)} %copy-done.94), kind=kOutput, calls=%fused_computation.45 | convolution fusion | flops 10739515392 | bytes 19922944 | tf_op jit(solution)/shard_map/dot_general | solution.py:33
  478.0 10.7 %collective-permute-done.41 = bf16[160,2048]{1,0:T(8,128)(2,1)S(1)} collective-permute-done((bf16[160,2048]{1,0:T(8,128)(2,1)S(1)}, bf16[160,2048]{1,0:T(8,128)(2,1)S(1)}, u32[]{:S(2)}, u32[]{:S(2)}) %collective-permute-start.41) | collective-permute-done | bytes 655392 | tf_op jit(solution)/shard_map/ppermute | solution.py:40
  500.4 26.0 %collective-permute-done.43 = bf16[320,2048]{1,0:T(8,128)(2,1)S(1)} collective-permute-done((bf16[320,2048]{1,0:T(8,128)(2,1)S(1)}, bf16[320,2048]{1,0:T(8,128)(2,1)S(1)}, u32[]{:S(2)}, u32[]{:S(2)}) %collective-permute-start.43) | collective-permute-done | bytes 1310752 | tf_op jit(solution)/shard_map/ppermute | solution.py:40
  530.4 11.4 %collective-permute-done.45 = bf16[160,2048]{1,0:T(8,128)(2,1)S(1)} collective-permute-done((bf16[160,2048]{1,0:T(8,128)(2,1)S(1)}, bf16[160,2048]{1,0:T(8,128)(2,1)S(1)}, u32[]{:S(2)}, u32[]{:S(2)}) %collective-permute-start.45) | collective-permute-done | bytes 655392 | tf_op jit(solution)/shard_map/ppermute | solution.py:40
  553.0 16.9 %convolution_convert_fusion.6 = bf16[1024,2048]{1,0:T(8,128)(2,1)} fusion(bf16[2560,1024]{1,0:T(8,128)(2,1)} %get-tuple-element.12, bf16[2560,2048]{1,0:T(8,128)(2,1)} %copy-done.57), kind=kOutput, calls=%fused_computation.44 | convolution fusion | flops 10739515392 | bytes 19922944 | tf_op jit(solution)/shard_map/dot_general | solution.py:33
  678.4 9.3 %convolution_convert_fusion.1 = bf16[1280,2048]{1,0:T(8,128)(2,1)} fusion(bf16[1024,2048]{1,0:T(8,128)(2,1)S(1)} %copy-done.90, bf16[2560,1024]{1,0:T(8,128)(2,1)} %get-tuple-element.12), kind=kOutput, calls=%fused_computation.24 | convolution fusion | flops 5371330560 | bytes 12058624 | tf_op jit(solution)/shard_map/dot_general | solution.py:232
  688.2 10.3 %convolution_convert_fusion.8 = bf16[2048,768]{1,0:T(8,128)(2,1)} fusion(bf16[2560,2048]{1,0:T(8,128)(2,1)S(1)} %bitcast.420, bf16[2560,768]{1,0:T(8,128)(2,1)S(1)} %bitcast.362), kind=kOutput, calls=%fused_computation.46 | convolution fusion | flops 8054636544 | bytes 17563648 | tf_op jit(solution)/shard_map/dot_general | solution.py:33
  699.9 13.7 %collective-permute-done.66 = bf16[4,64,1024]{2,1,0:T(8,128)(2,1)S(1)} collective-permute-done((bf16[4,64,1024]{2,1,0:T(8,128)(2,1)S(1)}, bf16[4,64,1024]{2,1,0:T(8,128)(2,1)S(1)}, u32[]{:S(2)}, u32[]{:S(2)}) %collective-permute-start.66) | collective-permute-done | bytes 524320 | tf_op jit(solution)/shard_map/ppermute | solution.py:40
  719.4 9.6 %fusion.128 = (bf16[1280,2048]{1,0:T(8,128)(2,1)S(1)}, f32[1280,2048]{1,0:T(8,128)}) fusion(bf16[1280,2048]{1,0:T(8,128)(2,1)} %collective-permute-done.57, bf16[1280,768]{1,0:T(8,128)(2,1)S(1)} %bitcast.388, bf16[2048,768]{1,0:T(8,128)(2,1)} %bitcast.430), kind=kOutput, calls=%fused_computation.317 | convolution fusion | flops 4034396160 | bytes 26083328 | tf_op jit(solution)/shard_map/dot_general | solution.py:27
  732.6 10.7 %fusion.153 = (bf16[1280,2048]{1,0:T(8,128)(2,1)S(1)}, f32[1280,2048]{1,0:T(8,128)}) fusion(bf16[1280,2048]{1,0:T(8,128)(2,1)} %collective-permute-done.50, bf16[1024,2048]{1,0:T(8,128)(2,1)S(1)} %copy-done.91, bf16[2560,1024]{1,0:T(8,128)(2,1)} %get-tuple-element.12), kind=kOutput, calls=%fused_computation.340 | convolution fusion | flops 5376573440 | bytes 27787264 | tf_op jit(solution)/shard_map/dot_general | solution.py:232
  805.5 8.9 %collective-permute-done.54 = bf16[160,2048]{1,0:T(8,128)(2,1)S(1)} collective-permute-done((bf16[160,2048]{1,0:T(8,128)(2,1)S(1)}, bf16[160,2048]{1,0:T(8,128)(2,1)S(1)}, u32[]{:S(2)}, u32[]{:S(2)}) %collective-permute-start.54) | collective-permute-done | bytes 655392 | tf_op jit(solution)/shard_map/ppermute | solution.py:40
  814.4 14.1 %collective-permute-done.53 = bf16[160,2048]{1,0:T(8,128)(2,1)S(1)} collective-permute-done((bf16[160,2048]{1,0:T(8,128)(2,1)}, bf16[160,2048]{1,0:T(8,128)(2,1)S(1)}, u32[]{:S(2)}, u32[]{:S(2)}) %collective-permute-start.53) | collective-permute-done | bytes 655392 | tf_op jit(solution)/shard_map/ppermute | solution.py:40
  (592 shorter events, 422.0 us)
Async XLA Ops:
  7.2 109.2 %all-gather.5.cloned.1.call-start = ((), (), s32[]{:S(2)}) async-start(), calls=%async_computation.8 | async-start | bytes 3932160 | tf_op jit(solution)/shard_map/all_gather | solution.py:61
  39.7 139.4 %all-gather.7.cloned.1.call-start = ((), (), s32[]{:S(2)}) async-start(), calls=%async_computation.9 | async-start | bytes 1310720 | tf_op jit(solution)/shard_map/all_gather | solution.py:61
  43.9 66.3 %collective-permute-start.4 = (bf16[320,2048]{1,0:T(8,128)(2,1)}, bf16[320,2048]{1,0:T(8,128)(2,1)}, u32[]{:S(2)}, u32[]{:S(2)}) collective-permute-start(bf16[320,2048]{1,0:T(8,128)(2,1)} %get-tuple-element.38), channel_id=1, source_target_pairs={{8,0},{0,8},{24,16},{16,24},{9,1},{1,9},{25,17},{17,25},{10,2},{2,... | collective-permute-start | bytes 3932168 | tf_op jit(solution)/shard_map/ppermute | solution.py:40
  44.0 40.7 %collective-permute-start.1 = (bf16[320,2048]{1,0:T(8,128)(2,1)}, bf16[320,2048]{1,0:T(8,128)(2,1)S(1)}, u32[]{:S(2)}, u32[]{:S(2)}) collective-permute-start(bf16[320,2048]{1,0:T(8,128)(2,1)} %get-tuple-element.38), channel_id=1, source_target_pairs={{1,0},{0,1},{3,2},{2,3},{5,4},{4,5},{7,6},{6,7},{9,8},{8,9},{11,10... | collective-permute-start | bytes 3932168 | tf_op jit(solution)/shard_map/ppermute | solution.py:40
  45.8 40.0 %collective-permute-start = (bf16[320,2048]{1,0:T(8,128)(2,1)}, bf16[320,2048]{1,0:T(8,128)(2,1)}, u32[]{:S(2)}, u32[]{:S(2)}) collective-permute-start(bf16[320,2048]{1,0:T(8,128)(2,1)} %get-tuple-element.38), channel_id=1, source_target_pairs={{16,0},{24,8},{0,16},{8,24},{17,1},{25,9},{1,17},{9,25},{18,2},{26... | collective-permute-start | bytes 3932168 | tf_op jit(solution)/shard_map/ppermute | solution.py:40
  46.2 34.2 %collective-permute-start.9 = (s32[1,2]{1,0:T(1,128)S(1)}, s32[1,2]{1,0:T(1,128)S(1)}, u32[]{:S(2)}, u32[]{:S(2)}) collective-permute-start(s32[1,2]{1,0:T(1,128)S(1)} %copy-done.88), channel_id=1, source_target_pairs={{1,0},{0,1},{3,2},{2,3},{5,4},{4,5},{7,6},{6,7},{9,8},{8,9},{11,10... | collective-permute-start | bytes 32 | tf_op jit(solution)/shard_map/ppermute | solution.py:40
  46.4 45.3 %collective-permute-start.10 = (bf16[64,2048]{1,0:T(8,128)(2,1)}, bf16[64,2048]{1,0:T(8,128)(2,1)}, u32[]{:S(2)}, u32[]{:S(2)}) collective-permute-start(bf16[64,2048]{1,0:T(8,128)(2,1)} %param.16), channel_id=1, source_target_pairs={{0,0},{1,2},{4,4},{5,6},{2,1},{3,3},{6,5},{7,7},{8,8},{9,10},{12,1... | collective-permute-start | bytes 786440 | tf_op jit(solution)/shard_map/ppermute | solution.py:187
  91.8 275.4 %all-gather.9.cloned.1.call-start = ((), (), s32[]{:S(2)}) async-start(), calls=%async_computation.10 | async-start | bytes 5242880 | tf_op jit(solution)/shard_map/all_gather | solution.py:61
  184.3 38.4 %collective-permute-start.11 = (bf16[1280,2048]{1,0:T(8,128)(2,1)}, bf16[1280,2048]{1,0:T(8,128)(2,1)}, u32[]{:S(2)}, u32[]{:S(2)}) collective-permute-start(bf16[1280,2048]{1,0:T(8,128)(2,1)} %convolution_convert_fusion.3), channel_id=1, source_target_pairs={{8,0},{0,8},{24,16},{16,24},{9,1},{1,9},{25,17},{17,25},{10,2},{2,... | collective-permute-start | bytes 15728648 | tf_op jit(solution)/shard_map/ppermute | solution.py:40
  222.6 161.2 %all-gather.11.cloned.1.call-start = ((), (), s32[]{:S(2)}) async-start(), calls=%async_computation.11 | async-start | bytes 5242880 | tf_op jit(solution)/shard_map/all_gather | solution.py:61
  246.6 44.1 %collective-permute-start.28 = (bf16[320,2048]{1,0:T(8,128)(2,1)}, bf16[320,2048]{1,0:T(8,128)(2,1)}, u32[]{:S(2)}, u32[]{:S(2)}) collective-permute-start(bf16[320,2048]{1,0:T(8,128)(2,1)} %bitcast.66), channel_id=1, source_target_pairs={{1,0},{0,1},{3,2},{2,3},{5,4},{4,5},{7,6},{6,7},{9,8},{8,9},{11,10... | collective-permute-start | bytes 3932168 | tf_op jit(solution)/shard_map/ppermute | solution.py:40
  246.9 45.3 %collective-permute-start.27 = (bf16[320,2048]{1,0:T(8,128)(2,1)}, bf16[320,2048]{1,0:T(8,128)(2,1)}, u32[]{:S(2)}, u32[]{:S(2)}) collective-permute-start(bf16[320,2048]{1,0:T(8,128)(2,1)} %bitcast.66), channel_id=1, source_target_pairs={{16,0},{24,8},{0,16},{8,24},{17,1},{25,9},{1,17},{9,25},{18,2},{26... | collective-permute-start | bytes 3932168 | tf_op jit(solution)/shard_map/ppermute | solution.py:40
  258.7 46.1 %collective-permute-start.17 = (bf16[160,2048]{1,0:T(8,128)(2,1)S(1)}, bf16[160,2048]{1,0:T(8,128)(2,1)}, u32[]{:S(2)}, u32[]{:S(2)}) collective-permute-start(bf16[160,2048]{1,0:T(8,128)(2,1)S(1)} %get-tuple-element.62), channel_id=1, source_target_pairs={{1,0},{0,1},{3,2},{2,3},{5,4},{4,5},{7,6},{6,7},{9,8},{8,9},{11,10... | collective-permute-start | bytes 1966088 | tf_op jit(solution)/shard_map/ppermute | solution.py:40
  264.0 40.8 %collective-permute-start.16 = (bf16[160,2048]{1,0:T(8,128)(2,1)}, bf16[160,2048]{1,0:T(8,128)(2,1)}, u32[]{:S(2)}, u32[]{:S(2)}) collective-permute-start(bf16[160,2048]{1,0:T(8,128)(2,1)} %get-tuple-element.48), channel_id=1, source_target_pairs={{16,0},{24,8},{0,16},{8,24},{17,1},{25,9},{1,17},{9,25},{18,2},{26... | collective-permute-start | bytes 1966088 | tf_op jit(solution)/shard_map/ppermute | solution.py:40
  264.3 434.2 %reduce-scatter.9.cloned.1.call-start = ((), (), s32[]{:S(2)}) async-start(), calls=%async_computation.14 | async-start | bytes 5242880 | tf_op jit(solution)/shard_map/reduce_scatter | solution.py:65
  264.4 52.0 %collective-permute-start.31 = (bf16[320,2048]{1,0:T(8,128)(2,1)}, bf16[320,2048]{1,0:T(8,128)(2,1)S(1)}, u32[]{:S(2)}, u32[]{:S(2)}) collective-permute-start(bf16[320,2048]{1,0:T(8,128)(2,1)} %bitcast.66), channel_id=1, source_target_pairs={{8,0},{0,8},{24,16},{16,24},{9,1},{1,9},{25,17},{17,25},{10,2},{2,... | collective-permute-start | bytes 3932168 | tf_op jit(solution)/shard_map/ppermute | solution.py:40
  304.8 41.3 %collective-permute-start.33 = (bf16[320,2048]{1,0:T(8,128)(2,1)}, bf16[320,2048]{1,0:T(8,128)(2,1)S(1)}, u32[]{:S(2)}, u32[]{:S(2)}) collective-permute-start(bf16[320,2048]{1,0:T(8,128)(2,1)} %collective-permute-done.28), channel_id=1, source_target_pairs={{8,0},{0,8},{24,16},{16,24},{9,1},{1,9},{25,17},{17,25},{10,2},{2,... | collective-permute-start | bytes 3932168 | tf_op jit(solution)/shard_map/ppermute | solution.py:40
  438.7 34.9 %collective-permute-start.36 = (bf16[160,2048]{1,0:T(8,128)(2,1)S(1)}, bf16[160,2048]{1,0:T(8,128)(2,1)S(1)}, u32[]{:S(2)}, u32[]{:S(2)}) collective-permute-start(bf16[160,2048]{1,0:T(8,128)(2,1)S(1)} %get-tuple-element.57), channel_id=1, source_target_pairs={{16,0},{24,8},{0,16},{8,24},{17,1},{25,9},{1,17},{9,25},{18,2},{26... | collective-permute-start | bytes 1966088 | tf_op jit(solution)/shard_map/ppermute | solution.py:40
  439.3 34.3 %collective-permute-start.39 = (bf16[160,2048]{1,0:T(8,128)(2,1)S(1)}, bf16[160,2048]{1,0:T(8,128)(2,1)S(1)}, u32[]{:S(2)}, u32[]{:S(2)}) collective-permute-start(bf16[160,2048]{1,0:T(8,128)(2,1)S(1)} %get-tuple-element.59), channel_id=1, source_target_pairs={{1,0},{0,1},{3,2},{2,3},{5,4},{4,5},{7,6},{6,7},{9,8},{8,9},{11,10... | collective-permute-start | bytes 1966088 | tf_op jit(solution)/shard_map/ppermute | solution.py:40
  473.0 273.1 %reduce-scatter.7.cloned.1.call-start = ((), (), s32[]{:S(2)}) async-start(), calls=%async_computation.13 | async-start | bytes 1310720 | tf_op jit(solution)/shard_map/reduce_scatter | solution.py:65
  553.0 202.6 %reduce-scatter.11.cloned.1.call-start = ((), (), s32[]{:S(2)}) async-start(), calls=%async_computation.15 | async-start | bytes 5242880 | tf_op jit(solution)/shard_map/reduce_scatter | solution.py:65
  569.9 201.9 %reduce-scatter.5.cloned.1.call-start = ((), (), s32[]{:S(2)}) async-start(), calls=%async_computation.12 | async-start | bytes 3932160 | tf_op jit(solution)/shard_map/reduce_scatter | solution.py:65
  678.3 41.1 %collective-permute-start.57 = (bf16[1280,2048]{1,0:T(8,128)(2,1)}, bf16[1280,2048]{1,0:T(8,128)(2,1)}, u32[]{:S(2)}, u32[]{:S(2)}) collective-permute-start(bf16[1280,2048]{1,0:T(8,128)(2,1)} %convolution_convert_fusion), channel_id=1, source_target_pairs={{8,0},{0,8},{24,16},{16,24},{9,1},{1,9},{25,17},{17,25},{10,2},{2,... | collective-permute-start | bytes 15728648 | tf_op jit(solution)/shard_map/ppermute | solution.py:40
  687.7 44.9 %collective-permute-start.50 = (bf16[1280,2048]{1,0:T(8,128)(2,1)}, bf16[1280,2048]{1,0:T(8,128)(2,1)}, u32[]{:S(2)}, u32[]{:S(2)}) collective-permute-start(bf16[1280,2048]{1,0:T(8,128)(2,1)} %convolution_convert_fusion.1), channel_id=1, source_target_pairs={{8,0},{0,8},{24,16},{16,24},{9,1},{1,9},{25,17},{17,25},{10,2},{2,... | collective-permute-start | bytes 15728648 | tf_op jit(solution)/shard_map/ppermute | solution.py:40
  715.9 42.4 %all-to-all-start.3 = ((bf16[4,2,64,1024]{3,2,1,0:T(8,128)(2,1)}), bf16[4,2,64,1024]{3,2,1,0:T(8,128)(2,1)S(1)}, u32[]{:S(2)}, u32[]{:S(2)}) async-start(bf16[4,2,64,1024]{3,2,1,0:T(8,128)(2,1)} %copy.296), calls=%async_computation.6 | async-start | bytes 2097152 | tf_op jit(solution)/shard_map/all_to_all | solution.py:79
  748.6 33.2 %collective-permute-start.63 = (bf16[160,2048]{1,0:T(8,128)(2,1)}, bf16[160,2048]{1,0:T(8,128)(2,1)}, u32[]{:S(2)}, u32[]{:S(2)}) collective-permute-start(bf16[160,2048]{1,0:T(8,128)(2,1)} %get-tuple-element.50), channel_id=1, source_target_pairs={{1,0},{0,1},{3,2},{2,3},{5,4},{4,5},{7,6},{6,7},{9,8},{8,9},{11,10... | collective-permute-start | bytes 1966088 | tf_op jit(solution)/shard_map/ppermute | solution.py:40
  755.3 35.7 %collective-permute-start.62 = (bf16[160,2048]{1,0:T(8,128)(2,1)}, bf16[160,2048]{1,0:T(8,128)(2,1)}, u32[]{:S(2)}, u32[]{:S(2)}) collective-permute-start(bf16[160,2048]{1,0:T(8,128)(2,1)} %get-tuple-element.43), channel_id=1, source_target_pairs={{16,0},{24,8},{0,16},{8,24},{17,1},{25,9},{1,17},{9,25},{18,2},{26... | collective-permute-start | bytes 1966088 | tf_op jit(solution)/shard_map/ppermute | solution.py:40
  767.4 36.8 %collective-permute-start.51 = (bf16[160,2048]{1,0:T(8,128)(2,1)}, bf16[160,2048]{1,0:T(8,128)(2,1)}, u32[]{:S(2)}, u32[]{:S(2)}) collective-permute-start(bf16[160,2048]{1,0:T(8,128)(2,1)} %get-tuple-element.53), channel_id=1, source_target_pairs={{16,0},{24,8},{0,16},{8,24},{17,1},{25,9},{1,17},{9,25},{18,2},{26... | collective-permute-start | bytes 1966088 | tf_op jit(solution)/shard_map/ppermute | solution.py:40
  777.0 77.3 %collective-permute-start.56 = (bf16[160,2048]{1,0:T(8,128)(2,1)}, bf16[160,2048]{1,0:T(8,128)(2,1)}, u32[]{:S(2)}, u32[]{:S(2)}) collective-permute-start(bf16[160,2048]{1,0:T(8,128)(2,1)} %get-tuple-element.54), channel_id=1, source_target_pairs={{1,0},{0,1},{3,2},{2,3},{5,4},{4,5},{7,6},{6,7},{9,8},{8,9},{11,10... | collective-permute-start | bytes 1966088 | tf_op jit(solution)/shard_map/ppermute | solution.py:40
  781.8 32.6 %collective-permute-start.54 = (bf16[160,2048]{1,0:T(8,128)(2,1)S(1)}, bf16[160,2048]{1,0:T(8,128)(2,1)S(1)}, u32[]{:S(2)}, u32[]{:S(2)}) collective-permute-start(bf16[160,2048]{1,0:T(8,128)(2,1)S(1)} %copy-done.47), channel_id=1, source_target_pairs={{1,0},{0,1},{3,2},{2,3},{5,4},{4,5},{7,6},{6,7},{9,8},{8,9},{11,10... | collective-permute-start | bytes 1966088 | tf_op jit(solution)/shard_map/ppermute | solution.py:40
  786.4 42.1 %collective-permute-start.53 = (bf16[160,2048]{1,0:T(8,128)(2,1)}, bf16[160,2048]{1,0:T(8,128)(2,1)S(1)}, u32[]{:S(2)}, u32[]{:S(2)}) collective-permute-start(bf16[160,2048]{1,0:T(8,128)(2,1)} %fusion.51), channel_id=1, source_target_pairs={{1,0},{0,1},{3,2},{2,3},{5,4},{4,5},{7,6},{6,7},{9,8},{8,9},{11,10... | collective-permute-start | bytes 1966088 | tf_op jit(solution)/shard_map/ppermute | solution.py:40
  791.0 55.4 %collective-permute-start.64 = (bf16[4,64,768]{2,1,0:T(8,128)(2,1)}, bf16[4,64,768]{2,1,0:T(8,128)(2,1)}, u32[]{:S(2)}, u32[]{:S(2)}) collective-permute-start(bf16[4,64,768]{2,1,0:T(8,128)(2,1)} %dynamic-slice_bitcast_fusion.1), channel_id=1, source_target_pairs={{1,0},{0,1},{3,2},{2,3},{5,4},{4,5},{7,6},{6,7},{9,8},{8,9},{11,10... | collective-permute-start | bytes 1179656 | tf_op jit(solution)/shard_map/ppermute | solution.py:40
  (148 other events, 2799.6 us)
Sparse Core Ops, SparseCore 0:
  39.8 67.7 all-gather.4
  109.2 27.8 all-gather.6
  222.7 80.3 all-gather.8
  304.5 79.2 all-gather.10
  473.2 76.0 reduce-scatter.8
  553.1 26.4 reduce-scatter.6
  581.9 75.4 reduce-scatter.10
  698.6 63.5 reduce-scatter.4

commit v3 on v2

v3 whole, which is shorter than its diff:
```python
import jax
import jax.numpy as jnp
from jax import lax
from jax.experimental import pallas as pl
from jax.experimental.pallas import tpu as pltpu
from jax.sharding import PartitionSpec as P

HEAD = 128
BLK_A = 256
BLK_B = 64
SPLITS = ((0, BLK_A), (BLK_A, BLK_A + BLK_B))

EPSILON = 1e-05
NEGATIVE = -1e30
SCALE = HEAD ** (-0.5)
BF16 = jnp.bfloat16
F32 = jnp.float32


def after(value, *others):
    return lax.optimization_barrier((value, others))[0]


def layer_norm(value, gain, bias):
    center = value - jnp.mean(value, axis=-1, keepdims=True)
    spread = jnp.mean(center * center, axis=-1, keepdims=True)
    return center * lax.rsqrt(spread + EPSILON) * gain + bias


def contract_last(left, right):
    return lax.dot_general(
        left, right, (((1,), (1,)), ((), ())), preferred_element_type=F32
    )


def contract_first(left, right):
    return lax.dot_general(
        left, right, (((0,), (0,)), ((), ())), preferred_element_type=F32
    )


def flip(axis, bits, block):
    count = lax.axis_size(axis)
    return lax.ppermute(block, axis, [(i ^ bits, i) for i in range(count)])


def flip_core(block):
    return flip("blk", 1, block)


def flip_x(block):
    return flip("blk", 2, block)


def flip_y(block):
    return flip("dp", 1, block)


def lines():
    count = lax.axis_size("dp")
    return [[z * 2 + y for z in range(count // 2)] for y in range(2)]


def gather_z(part, axis):
    return lax.all_gather(part, "dp", axis_index_groups=lines(), axis=axis, tiled=True)


def scatter_z(total, axis):
    return lax.psum_scatter(
        total, "dp", axis_index_groups=lines(), scatter_dimension=axis, tiled=True
    )


def by_y(own, other):
    y = lax.axis_index("dp") % 2
    return jnp.where(y == 0, own, other), jnp.where(y == 0, other, own)


def exchange(cut):
    y = lax.axis_index("dp") % 2
    other = flip_y(cut(1 - y))
    both = jnp.stack(by_y(cut(y), other), axis=1)
    return lax.all_to_all(both, "blk", 0, 0)


def gather_plane(part):
    half = part.shape[0] // 2
    from_x, from_y, from_core = flip_x(part), flip_y(part), flip_core(part)
    diagonal = jnp.concatenate([flip_y(from_x[:half]), flip_x(from_y[half:])], axis=0)
    mine = [part, from_x, from_y, diagonal]
    return jnp.concatenate(
        mine + [from_core] + [flip_core(piece) for piece in mine[1:]], axis=0
    )


def scatter_plane(product, rows):
    half = rows // 2
    got = flip_core(product(4, 8).astype(BF16))
    held = product(0, 4).astype(F32) + got.astype(F32)
    own, to_x, to_y, across = [held[i * rows : (i + 1) * rows] for i in range(4)]
    across = across.astype(BF16)
    x_across, y_across = flip_x(across[:half]), flip_y(across[half:])
    x_top = flip_x(to_x[:half].astype(BF16))
    y_bottom = flip_y(to_y[half:].astype(BF16))
    sent = [
        (to_y[:half] + x_across.astype(F32)).astype(BF16),
        (to_x[half:] + y_across.astype(F32)).astype(BF16),
    ]
    y_top = flip_y(sent[0])
    x_bottom = flip_x(sent[1])
    top = own[:half] + x_top.astype(F32) + y_top.astype(F32)
    bottom = own[half:] + x_bottom.astype(F32) + y_bottom.astype(F32)
    return jnp.concatenate([top, bottom], axis=0), sent


def sum_over(total, axis, bits):
    while bits < lax.axis_size(axis):
        total = total + flip(axis, bits, total)
        bits *= 2
    return total


def part_of(slots_ref, column, block):
    slot = slots_ref[column, block]
    first, last = SPLITS[column]
    return slot // 2, 0, slot % 2, slice(first, last)


def scores_of(queries, keys, first, length):
    scores = contract_last(queries, keys) * SCALE
    key_places = lax.broadcasted_iota(jnp.int32, scores.shape, 1)
    query_places = first + lax.broadcasted_iota(jnp.int32, scores.shape, 0)
    allowed = (key_places <= query_places) & (key_places < length)
    return jnp.where(allowed, scores, NEGATIVE)


def attention_steps():
    for column, (first, last) in enumerate(SPLITS):
        size = last - first
        step = 1 if size * 4 > 512 else 4
        yield column, size, [(p, step, (p + step) * size) for p in range(0, 4, step)]


def attention_forward_kernel(slots_ref, lengths_ref, in_ref, out_ref, log_ref, q_ref, k_ref, v_ref):
    sequence = pl.program_id(0)
    heads = in_ref.shape[-1] // (3 * HEAD)
    for column, size, runs in attention_steps():
        length = lengths_ref[sequence, column]
        for head in range(heads):
            for third, ref in enumerate((q_ref, k_ref, v_ref)):
                lanes = slice((third * heads + head) * HEAD, (third * heads + head + 1) * HEAD)
                for block in range(4):
                    ref[block * size : (block + 1) * size] = in_ref[
                        (*part_of(slots_ref, column, block), lanes)
                    ]
            lanes = slice(head * HEAD, (head + 1) * HEAD)
            for start, step, keys in runs:
                rows = slice(start * size, (start + step) * size)
                scores = scores_of(q_ref[rows], k_ref[:keys], start * size, length)
                peak = jnp.max(scores, axis=-1, keepdims=True)
                weights = jnp.exp(scores - peak)
                total = jnp.sum(weights, axis=-1, keepdims=True)
                attended = jnp.dot(weights.astype(BF16), v_ref[:keys], preferred_element_type=F32)
                attended = (attended / total).astype(BF16)
                log_total = jnp.broadcast_to(peak + jnp.log(total), (step * size, HEAD))
                for i in range(step):
                    where = part_of(slots_ref, column, start + i)
                    out_ref[(*where, lanes)] = attended[i * size : (i + 1) * size]
                    log_ref[(*where, lanes)] = log_total[i * size : (i + 1) * size]


def attention_backward_kernel(
    slots_ref, lengths_ref, in_ref, grad_ref, log_ref, out_ref, q_ref, k_ref, v_ref, g_ref, dk_ref, dv_ref
):
    sequence = pl.program_id(0)
    heads = in_ref.shape[-1] // (3 * HEAD)
    for column, size, runs in attention_steps():
        length = lengths_ref[sequence, column]
        for head in range(heads):
            columns = [
                slice((third * heads + head) * HEAD, (third * heads + head + 1) * HEAD)
                for third in range(3)
            ]
            lanes = slice(head * HEAD, (head + 1) * HEAD)
            for block in range(4):
                here = slice(block * size, (block + 1) * size)
                where = part_of(slots_ref, column, block)
                q_ref[here] = in_ref[(*where, columns[0])]
                k_ref[here] = in_ref[(*where, columns[1])]
                v_ref[here] = in_ref[(*where, columns[2])]
                g_ref[here] = grad_ref[(*where, lanes)]
            dk_ref[...] = jnp.zeros_like(dk_ref)
            dv_ref[...] = jnp.zeros_like(dv_ref)
            for start, step, keys in runs:
                rows = slice(start * size, (start + step) * size)
                queries, grads = q_ref[rows], g_ref[rows]
                log_total = jnp.concatenate(
                    [
                        log_ref[(*part_of(slots_ref, column, start + i), lanes)][:, :1]
                        for i in range(step)
                    ],
                    axis=0,
                )
                scores = scores_of(queries, k_ref[:keys], start * size, length)
                probs = jnp.exp(scores - log_total)
                grad_probs = contract_last(grads, v_ref[:keys])
                delta = jnp.sum(probs * grad_probs, axis=-1, keepdims=True)
                grad_scores = (probs * (grad_probs - delta)).astype(BF16)
                dv_ref[:keys] += contract_first(probs.astype(BF16), grads)
                dk_ref[:keys] += contract_first(grad_scores, queries)
                dq = jnp.dot(grad_scores, k_ref[:keys], preferred_element_type=F32) * SCALE
                dq = dq.astype(BF16)
                for i in range(step):
                    where = part_of(slots_ref, column, start + i)
                    out_ref[(*where, columns[0])] = dq[i * size : (i + 1) * size]
            for block in range(4):
                here = slice(block * size, (block + 1) * size)
                where = part_of(slots_ref, column, block)
                out_ref[(*where, columns[1])] = (dk_ref[here] * SCALE).astype(BF16)
                out_ref[(*where, columns[2])] = dv_ref[here].astype(BF16)


def attention_call(kernel, arrays, outs, scratch, slots, lengths, matmuls):
    count = 4 * BLK_A
    rows = arrays[0].shape[0] // 8

    def spec(columns):
        return pl.BlockSpec((2, 1, 2, rows, columns), lambda s, *_: (0, s, 0, 0, 0))

    heads = arrays[0].shape[1] // (3 * HEAD)
    results = pl.pallas_call(
        kernel,
        grid_spec=pltpu.PrefetchScalarGridSpec(
            num_scalar_prefetch=2,
            grid=(2,),
            in_specs=[spec(a.shape[1]) for a in arrays],
            out_specs=[spec(columns) for columns, _ in outs],
            scratch_shapes=[pltpu.VMEM((count, HEAD), dtype) for dtype in scratch],
        ),
        out_shape=[jax.ShapeDtypeStruct((2, 2, 2, rows, c), dtype) for c, dtype in outs],
        compiler_params=pltpu.CompilerParams(vmem_limit_bytes=48 * 2**20),
        cost_estimate=pl.CostEstimate(
            flops=matmuls * 2 * heads * count * count * HEAD * 2,
            bytes_accessed=8 * rows * HEAD * heads * 2 * 4,
            transcendentals=2 * heads * count * count,
        ),
    )(slots, lengths, *[a.reshape(2, 2, 2, rows, -1) for a in arrays])
    return [r.reshape(8 * rows, -1) for r in results]


def body(
    hidden_in,
    cotangent,
    seq_lengths,
    block_order,
    w_qkv,
    w_out,
    w_up,
    w_down,
    norm_gains,
    norm_biases,
    hidden_bias,
):
    blk, dp = lax.axis_size("blk"), lax.axis_size("dp")
    lanes = dp // 2
    b, d = lax.axis_index("blk"), lax.axis_index("dp")
    z, y = d // 2, d % 2
    rows, width = hidden_in.shape[2:]
    pairs = width // HEAD // blk // 2
    part = pairs * HEAD
    shard = w_qkv.shape[0]
    units = w_down.shape[0]
    x = hidden_in.reshape(rows, width).astype(F32)
    cot_low = cotangent.reshape(rows, width)

    def cut_qkv(to_y):
        view = w_qkv.reshape(shard, 3, blk, pairs, 2, HEAD)
        view = lax.dynamic_index_in_dim(view, to_y, 4, keepdims=False)
        return view.transpose(2, 0, 1, 3, 4).reshape(blk, shard, 3 * part)

    def cut_up(to_y):
        view = late_up.reshape(shard, blk, lanes, 2, units)
        view = lax.dynamic_index_in_dim(view, to_y, 3, keepdims=False)
        return view.transpose(1, 0, 2, 3).reshape(blk, shard, lanes * units)

    pieces = [[p for p in range(dp) if (p * shard // HEAD) % 2 == to_y] for to_y in range(2)]
    route = [(pieces[to_y][lane], lane * 2 + to_y) for to_y in range(2) for lane in range(lanes)]

    holders = jnp.stack(
        [jnp.take(block_order, b ^ (far * 2 + core), axis=1) for core in range(2) for far in range(2)],
        axis=1,
    )
    found = holders[:, None, :] == jnp.arange(4, dtype=jnp.int32)[None, :, None]
    slots = jnp.sum(jnp.where(found, jnp.arange(4, dtype=jnp.int32), 0), axis=2)
    lengths = jnp.concatenate([seq_lengths, flip_y(seq_lengths)], axis=0)

    out_full = gather_z(lax.ppermute(w_out, "dp", route), 0)
    qkv_part = exchange(cut_qkv).reshape(blk, 2 * shard, 3 * part)
    qkv_full = gather_z(after(qkv_part, out_full), 1).reshape(width, 3 * part)

    normed, first_pull = jax.vjp(layer_norm, x, norm_gains[0], norm_biases[0])
    normed_all = gather_plane(after(normed.astype(BF16), qkv_part))
    late_up = after(w_up, normed_all)
    up_part = exchange(cut_up).reshape(blk, 2 * shard, lanes * units)
    up_full = gather_z(up_part, 1).reshape(width, lanes * units)
    down_full = gather_z(after(w_down, up_part), 0)
    cot_all = gather_plane(after(cot_low, up_part))
    projected = jnp.dot(normed_all, qkv_full, preferred_element_type=F32).astype(BF16)
    attended_low, log_total = attention_call(
        attention_forward_kernel,
        [projected],
        [(part, BF16), (part, F32)],
        [BF16] * 3,
        slots,
        lengths,
        2,
    )

    def times(left, right):
        return lambda first, last: jnp.dot(
            left[first * rows : last * rows], right, preferred_element_type=F32
        )

    def times_transposed(left, right):
        return lambda first, last: contract_last(left[first * rows : last * rows], right)

    mixed = x + scatter_plane(times(attended_low, out_full), rows)[0]
    second, second_pull = jax.vjp(layer_norm, mixed, norm_gains[1], norm_biases[1])
    second_all = gather_plane(second.astype(BF16))
    bias_part = lax.dynamic_slice_in_dim(
        hidden_bias.reshape(blk, lanes, 2, units), b, 1, 0
    )
    bias_part = lax.dynamic_index_in_dim(bias_part, y, 2, keepdims=False).reshape(-1)
    hidden_pre = jnp.dot(second_all, up_full, preferred_element_type=F32) + bias_part
    activated, gelu_pull = jax.vjp(lambda v: jax.nn.gelu(v, approximate=True), hidden_pre)
    activated_low = activated.astype(BF16)

    down_sum = contract_first(activated_low, cot_all).astype(BF16)
    down_full = after(down_full, down_sum)
    down_sum = scatter_z(down_sum, 0)
    (grad_hidden,) = gelu_pull(contract_last(cot_all, down_full))
    grad_hidden_low = grad_hidden.astype(BF16)
    hidden_sum = jnp.sum(grad_hidden_low.astype(F32), axis=0)
    grad_second, sent = scatter_plane(times_transposed(grad_hidden_low, up_full), rows)
    up_sum = contract_first(second_all, after(grad_hidden_low, *sent)).astype(BF16)
    up_sum = scatter_z(up_sum.reshape(blk, -1, lanes * units), 1)
    grad_mixed_norm, gain_two, bias_two = second_pull(grad_second)
    grad_mixed = cot_low.astype(F32) + grad_mixed_norm
    mixed_low = grad_mixed.astype(BF16)
    mixed_all = gather_plane(mixed_low)
    product = jnp.dot(
        after(activated_low, mixed_low), down_full, preferred_element_type=F32
    ).astype(BF16)
    product = after(product, mixed_all)
    result = mixed + scatter_plane(lambda first, last: product[first * rows : last * rows], rows)[0]
    grad_attended = contract_last(mixed_all, out_full).astype(BF16)
    (grad_projected,) = attention_call(
        attention_backward_kernel,
        [projected, grad_attended, log_total],
        [(3 * part, BF16)],
        [BF16] * 4 + [F32] * 2,
        slots,
        lengths,
        5,
    )
    qkv_sum = contract_first(normed_all, grad_projected).astype(BF16)
    grad_projected = after(grad_projected, qkv_sum)
    qkv_sum = scatter_z(qkv_sum.reshape(blk, -1, 3 * part), 1)
    grad_normed, sent = scatter_plane(times_transposed(grad_projected, qkv_full), rows)
    out_sum = contract_first(after(attended_low, *sent), mixed_all).astype(BF16)
    out_sum = scatter_z(after(out_sum, qkv_sum), 0)
    grad_input_norm, gain_one, bias_one = first_pull(grad_normed)
    grad_input = (grad_mixed + grad_input_norm).astype(BF16)

    def give_back(total):
        parts = total.reshape(blk, 2, shard, -1)
        return exchange(lambda to_y: lax.dynamic_index_in_dim(parts, to_y, 1, keepdims=False))

    grad_up = give_back(up_sum).reshape(blk, 2, shard, lanes, units).astype(F32)
    grad_up = grad_up.transpose(2, 0, 3, 1, 4).reshape(shard, -1)
    grad_qkv = give_back(qkv_sum).reshape(blk, 2, shard, 3, pairs, HEAD).astype(F32)
    grad_qkv = grad_qkv.transpose(2, 3, 0, 4, 1, 5).reshape(shard, -1)
    grad_out = lax.ppermute(out_sum, "dp", [(j, i) for i, j in route]).astype(F32)
    small = jnp.concatenate([gain_one, gain_two, bias_one, bias_two, hidden_sum])
    small = sum_over(small, "dp", 2)
    norms = small[: 4 * width].reshape(4, width)
    norms = sum_over(norms + flip_y(norms), "blk", 1)
    norms = lax.dynamic_slice_in_dim(norms, (b * dp + d) * shard, shard, 1)
    grad_hidden_bias = lax.dynamic_slice_in_dim(small, 4 * width + z * units, units)
    return (
        result.astype(BF16).reshape(1, 1, rows, width),
        grad_input.reshape(1, 1, rows, width),
        grad_qkv,
        grad_out,
        grad_up,
        down_sum.astype(F32),
        norms[:2],
        norms[2:],
        grad_hidden_bias,
    )


def solution(mesh):
    return jax.shard_map(
        body,
        mesh=mesh,
        in_specs=(
            P("dp", "blk", None, None),
            P("dp", "blk", None, None),
            P("dp", None),
            P(),
            P(("blk", "dp"), None),
            P(("blk", "dp"), None),
            P(("blk", "dp"), None),
            P(("blk", "dp"), None),
            P(),
            P(),
            P(),
        ),
        out_specs=(
            P("dp", "blk", None, None),
            P("dp", "blk", None, None),
            P(("blk", "dp"), None),
            P(("blk", "dp"), None),
            P(("blk", "dp"), None),
            P(("blk", "dp"), None),
            P(None, ("blk", "dp")),
            P(None, ("blk", "dp")),
            P(("blk", "dp")),
        ),
        check_vma=False,
    )
```

time: 887 us -> 815 us (0.919)
  matrix products: 240 us -> 175 us
  waiting for transfers between devices: 294 us -> 336 us
  local copies, waits for them, and re-layouts: 133 us -> 97.6 us
  Pallas kernels: 0 us -> 27.5 us
  other arithmetic: 78.8 us -> 60.1 us
  blocking collectives: 32.6 us -> 17.6 us
  starting transfers between devices: 81.5 us -> 72.3 us
    dot_general x24 -> x1, matrix products: 67.2 us -> 13 us  [body(): jnp.dot(after(activated_low, mixed_low), down_full, preferred_element_typ...]
    pallas_call x0 -> x2, Pallas kernels: none -> 27.5 us  [attention_call(): pl.pallas_call(kernel, grid_spec=pltpu.PrefetchScalarGridSpec(num_scalar_...]
    ppermute x70, waiting for transfers between devices: 287 us -> 309 us  [flip(): return lax.ppermute(block, axis, [(i ^ bits, i) for i in range(count)])]
    dot_general x4 -> x2, matrix products: 29.1 us -> 8.33 us  [times(): jnp.dot(left[first * rows:last * rows], right, preferred_element_type=F32)]
    concatenate x18 -> x0, local copies, waits for them, and re-layouts: 17.8 us -> none  [body(): jnp.concatenate([g.astype(BF16).reshape(-1, part) for g in grads], axis=1)]
    all_to_all x2 -> x1, blocking collectives: 32.6 us -> 17.6 us  [exchange(): return lax.all_to_all(both, 'blk', 0, 0)]
    another operation x0 -> x2, other arithmetic: none -> 12.9 us
    all_gather x4, waiting for transfers between devices: 0.05 us -> 12.7 us  [gather_z(): lax.all_gather(part, 'dp', axis_index_groups=lines(), axis=axis, tiled=True)]
  transfers between devices with their start and end apart: 82 -> 83, of which waited for: 32 -> 36; matrix products, arithmetic and copies ran while one was open for 43% -> 30% of each run, Pallas kernels for 0% -> 2%
where the time goes in v3:
time: 815 us; the launch traced here: 802 us
  waiting for transfers between devices  336 us (41%)
  matrix products  175 us (21%)
  local copies, waits for them, and re-layouts  97.6 us (12%)
  starting transfers between devices  72.3 us (9%)
  other arithmetic  60.1 us (7%)
  Pallas kernels  27.5 us (3%)
  blocking collectives  17.6 us (2%)
  between operations  15.6 us (2%)
    ppermute x70, waiting for transfers between devices, flip(): return lax.ppermute(block, axis, [(i ^ bits, i) for i in range(count)])  309 us
    dot_general x6, matrix products, contract_last(): lax.dot_general(left, right, (((1,), (1,)), ((), ())), preferred_element_...  69 us
    ppermute x70, starting transfers between devices, flip(): return lax.ppermute(block, axis, [(i ^ bits, i) for i in range(count)])  57.6 us
    dot_general x4, matrix products, contract_first(): lax.dot_general(left, right, (((0,), (0,)), ((), ())), preferred_element_...  52.6 us
    unnamed x136, local copies, waits for them, and re-layouts  45.8 us
    pallas_call x2, Pallas kernels, attention_call(): pl.pallas_call(kernel, grid_spec=pltpu.PrefetchScalarGridSpec(num_scalar_...  27.5 us
    dot_general x1, matrix products, body(): jnp.dot(second_all, up_full, preferred_element_type=F32) + bias_part  18.6 us
    all_to_all x1, blocking collectives, exchange(): return lax.all_to_all(both, 'blk', 0, 0)  17.6 us
  transfers between devices with their start and end apart: 83, of which 36 were waited for; matrix products, arithmetic and copies ran while one was open for 30% of the time, Pallas kernels for 2%

profile of v3, /device:TPU:0, one launch (start us, length us, event | category | flops | bytes accessed | tf_op | source)
XLA Modules:
  0.0 801.9 jit_solution(6426864159390780256)
XLA Ops:
  32.9 11.0 %all-to-all-done = bf16[4,2,64,768]{3,2,1,0:T(8,128)(2,1)S(1)} async-done(((bf16[4,2,64,768]{3,2,1,0:T(8,128)(2,1)}), bf16[4,2,64,768]{3,2,1,0:T(8,128)(2,1)S(1)}, u32[]{:S(2)}, u32[]{:S(2)}) %all-to-all-start) | async-done | bytes 786464 | tf_op jit(solution)/shard_map/all_to_all | solution.py:83
  53.7 26.6 %collective-permute-done.3 = bf16[320,2048]{1,0:T(8,128)(2,1)S(1)} collective-permute-done((bf16[320,2048]{1,0:T(8,128)(2,1)S(1)}, bf16[320,2048]{1,0:T(8,128)(2,1)S(1)}, u32[]{:S(2)}, u32[]{:S(2)}) %collective-permute-start.3) | collective-permute-done | bytes 1310752 | tf_op jit(solution)/shard_map/ppermute | solution.py:44
  114.0 13.3 %convolution_convert_fusion.4 = bf16[2560,768]{1,0:T(8,128)(2,1)} fusion(bf16[2560,2048]{1,0:T(8,128)(2,1)} %constant_dynamic-update-slice_fusion, bf16[2048,768]{1,0:T(8,128)(2,1)} %bitcast.210), kind=kOutput, calls=%fused_computation.19 | convolution fusion | flops 8055029760 | bytes 17563648 | tf_op jit(solution)/shard_map/dot_general | solution.py:308
  127.3 10.2 %shard_map.178 = (bf16[2,2,2,320,256]{4,3,2,1,0:T(8,128)(2,1)S(1)}, f32[2,2,2,320,256]{4,3,2,1,0:T(8,128)S(1)}) custom-call(s32[2,4]{1,0:T(2,128)S(1)} %select_reduce_fusion.slots_ref, s32[2,2]{1,0:T(2,128)S(1)} %pad_add_fusion.1.lengths_ref, bf16[2,2,2,320,768]{4,3,2,1,0:T(8,128)(2,1)} %bitcast.213), custom_call_target="tpu_custom_call" | custom-call | flops 2147483648 | bytes 5242880 | tf_op jit(solution)/shard_map/pallas_call | solution.py:231
  153.1 12.2 %collective-permute-done.26 = bf16[4,64,1024]{2,1,0:T(8,128)(2,1)S(1)} collective-permute-done((bf16[4,64,1024]{2,1,0:T(8,128)(2,1)S(1)}, bf16[4,64,1024]{2,1,0:T(8,128)(2,1)S(1)}, u32[]{:S(2)}, u32[]{:S(2)}) %collective-permute-start.26) | collective-permute-done | bytes 524320 | tf_op jit(solution)/shard_map/ppermute | solution.py:44
  165.6 17.6 %all_to_all.20 = bf16[4,2,64,1024]{3,2,1,0:T(8,128)(2,1)} all-to-all(bf16[4,2,64,1024]{3,2,1,0:T(8,128)(2,1)S(1)} %copy.82), channel_id=1, replica_groups=mesh['blk'=4,'dp'=8] {'blk'}, dimensions={0} | all-to-all | bytes 2097152 | tf_op jit(solution)/shard_map/all_to_all | solution.py:83
  191.6 14.2 %collective-permute-done.13 = bf16[160,2048]{1,0:T(8,128)(2,1)S(1)} collective-permute-done((bf16[160,2048]{1,0:T(8,128)(2,1)S(1)}, bf16[160,2048]{1,0:T(8,128)(2,1)S(1)}, u32[]{:S(2)}, u32[]{:S(2)}) %collective-permute-start.13) | collective-permute-done | bytes 655392 | tf_op jit(solution)/shard_map/ppermute | solution.py:44
  208.3 11.5 %collective-permute-done.12 = bf16[160,2048]{1,0:T(8,128)(2,1)S(1)} collective-permute-done((bf16[160,2048]{1,0:T(8,128)(2,1)S(1)}, bf16[160,2048]{1,0:T(8,128)(2,1)S(1)}, u32[]{:S(2)}, u32[]{:S(2)}) %collective-permute-start.12) | collective-permute-done | bytes 655392 | tf_op jit(solution)/shard_map/ppermute | solution.py:44
  227.4 24.5 %collective-permute-done.28 = bf16[320,2048]{1,0:T(8,128)(2,1)} collective-permute-done((bf16[320,2048]{1,0:T(8,128)(2,1)}, bf16[320,2048]{1,0:T(8,128)(2,1)}, u32[]{:S(2)}, u32[]{:S(2)}) %collective-permute-start.28) | collective-permute-done | bytes 1310752 | tf_op jit(solution)/shard_map/ppermute | solution.py:44
  257.5 8.4 %collective-permute-done.17 = bf16[160,2048]{1,0:T(8,128)(2,1)} collective-permute-done((bf16[160,2048]{1,0:T(8,128)(2,1)S(1)}, bf16[160,2048]{1,0:T(8,128)(2,1)}, u32[]{:S(2)}, u32[]{:S(2)}) %collective-permute-start.17) | collective-permute-done | bytes 655392 | tf_op jit(solution)/shard_map/ppermute | solution.py:44
  280.8 23.2 %collective-permute-done.19 = bf16[320,2048]{1,0:T(8,128)(2,1)S(1)} collective-permute-done((bf16[320,2048]{1,0:T(8,128)(2,1)S(1)}, bf16[320,2048]{1,0:T(8,128)(2,1)S(1)}, u32[]{:S(2)}, u32[]{:S(2)}) %collective-permute-start.19) | collective-permute-done | bytes 1310752 | tf_op jit(solution)/shard_map/ppermute | solution.py:44
  309.5 9.4 %collective-permute-done.21 = bf16[160,2048]{1,0:T(8,128)(2,1)S(1)} collective-permute-done((bf16[160,2048]{1,0:T(8,128)(2,1)S(1)}, bf16[160,2048]{1,0:T(8,128)(2,1)S(1)}, u32[]{:S(2)}, u32[]{:S(2)}) %collective-permute-start.21) | collective-permute-done | bytes 655392 | tf_op jit(solution)/shard_map/ppermute | solution.py:44
  328.4 18.6 %multiply_convert_fusion = (bf16[2560,1024]{1,0:T(8,128)(2,1)S(1)}, f32[2560,1024]{1,0:T(8,128)}) fusion(f32[1024]{0:T(1024)S(1)} %bitcast.201, bf16[2560,2048]{1,0:T(8,128)(2,1)} %constant_dynamic-update-slice_fusion.9, bf16[2048,1024]{1,0:T(8,128)(2,1)} %bitcast.207), kind=kOutput, calls=%fused_computation.14 | convolution fusion | flops 10763632640 | bytes 30412800 | tf_op jit(solution)/shard_map/dot_general | solution.py:334
  349.3 15.6 %convolution_convert_fusion.6 = bf16[1024,2048]{1,0:T(8,128)(2,1)} fusion(bf16[2560,1024]{1,0:T(8,128)(2,1)S(1)} %get-tuple-element.31, bf16[2560,2048]{1,0:T(8,128)(2,1)} %copy-done.32), kind=kOutput, calls=%fused_computation.29 | convolution fusion | flops 10739515392 | bytes 19922944 | tf_op jit(solution)/shard_map/dot_general | solution.py:37
  364.9 25.5 %convert_reduce_fusion = (f32[1024]{0:T(1024)}, bf16[2560,1024]{1,0:T(8,128)(2,1)}) fusion(f32[2560,1024]{1,0:T(8,128)} %get-tuple-element.124, f32[1024]{0:T(1024)S(1)} %bitcast.202, bf16[2560,2048]{1,0:T(8,128)(2,1)} %copy-done.32, bf16[1024,2048]{1,0:T(8,128)(2,1)} %all-gather.11.cloned.1.call-done), kind=kOutput, calls=%fused_computation.10 | convolution fusion | flops 10797710336 | bytes 30416896 | tf_op jit(solution)/shard_map/dot_general | solution.py:31
  398.7 8.4 %collective-permute-done.35 = bf16[1280,2048]{1,0:T(8,128)(2,1)} collective-permute-done((bf16[1280,2048]{1,0:T(8,128)(2,1)S(1)}, bf16[1280,2048]{1,0:T(8,128)(2,1)}, u32[]{:S(2)}, u32[]{:S(2)}) %collective-permute-start.35) | collective-permute-done | bytes 5242912 | tf_op jit(solution)/shard_map/ppermute | solution.py:44
  407.1 10.1 %fusion.95 = (bf16[1280,2048]{1,0:T(8,128)(2,1)S(1)}, f32[1280,2048]{1,0:T(8,128)S(1)}) fusion(bf16[1280,2048]{1,0:T(8,128)(2,1)} %collective-permute-done.35, bf16[2048,1024]{1,0:T(8,128)(2,1)} %bitcast.208, bf16[2560,1024]{1,0:T(8,128)(2,1)} %get-tuple-element.37), kind=kOutput, calls=%fused_computation.223 | convolution fusion | flops 5376573440 | bytes 27787264 | tf_op jit(solution)/shard_map/dot_general | solution.py:31
  421.1 14.1 %collective-permute-done.37 = bf16[160,2048]{1,0:T(8,128)(2,1)S(1)} collective-permute-done((bf16[160,2048]{1,0:T(8,128)(2,1)S(1)}, bf16[160,2048]{1,0:T(8,128)(2,1)S(1)}, u32[]{:S(2)}, u32[]{:S(2)}) %collective-permute-start.37) | collective-permute-done | bytes 655392 | tf_op jit(solution)/shard_map/ppermute | solution.py:44
  436.8 11.8 %collective-permute-done.36 = bf16[160,2048]{1,0:T(8,128)(2,1)S(1)} collective-permute-done((bf16[160,2048]{1,0:T(8,128)(2,1)S(1)}, bf16[160,2048]{1,0:T(8,128)(2,1)S(1)}, u32[]{:S(2)}, u32[]{:S(2)}) %collective-permute-start.36) | collective-permute-done | bytes 655392 | tf_op jit(solution)/shard_map/ppermute | solution.py:44
  452.7 15.5 %convolution_convert_fusion.7 = bf16[2048,1024]{1,0:T(8,128)(2,1)} fusion(bf16[2560,2048]{1,0:T(8,128)(2,1)} %constant_dynamic-update-slice_fusion.9, bf16[2560,1024]{1,0:T(8,128)(2,1)S(1)} %bitcast.219), kind=kOutput, calls=%fused_computation.30 | convolution fusion | flops 10739515392 | bytes 19922944 | tf_op jit(solution)/shard_map/dot_general | solution.py:37
  470.2 12.9 %collective-permute-done.41 = bf16[160,2048]{1,0:T(8,128)(2,1)S(1)} collective-permute-done((bf16[160,2048]{1,0:T(8,128)(2,1)S(1)}, bf16[160,2048]{1,0:T(8,128)(2,1)S(1)}, u32[]{:S(2)}, u32[]{:S(2)}) %collective-permute-start.41) | collective-permute-done | bytes 655392 | tf_op jit(solution)/shard_map/ppermute | solution.py:44
  492.0 27.0 %collective-permute-done.43 = bf16[320,2048]{1,0:T(8,128)(2,1)S(1)} collective-permute-done((bf16[320,2048]{1,0:T(8,128)(2,1)}, bf16[320,2048]{1,0:T(8,128)(2,1)S(1)}, u32[]{:S(2)}, u32[]{:S(2)}) %collective-permute-start.43) | collective-permute-done | bytes 1310752 | tf_op jit(solution)/shard_map/ppermute | solution.py:44
  554.8 17.4 %shard_map.179 = bf16[2,2,2,320,768]{4,3,2,1,0:T(8,128)(2,1)} custom-call(s32[2,4]{1,0:T(2,128)S(1)} %select_reduce_fusion.slots_ref, s32[2,2]{1,0:T(2,128)S(1)} %pad_add_fusion.1.lengths_ref, bf16[2,2,2,320,768]{4,3,2,1,0:T(8,128)(2,1)} %bitcast.214, bf16[2,2,2,320,256]{4,3,2,1,0:T(8,128)(2,1)S(1)} %bitcast.166, ...), custom_call_target="tpu_custom_call" | custom-call | flops 5368709120 | bytes 5242880 | tf_op jit(solution)/shard_map/pallas_call | solution.py:231
  572.2 13.7 %convolution_convert_fusion.8 = bf16[2048,768]{1,0:T(8,128)(2,1)} fusion(bf16[2560,2048]{1,0:T(8,128)(2,1)} %constant_dynamic-update-slice_fusion, bf16[2560,768]{1,0:T(8,128)(2,1)} %bitcast.215), kind=kOutput, calls=%fused_computation.31 | convolution fusion | flops 8054636544 | bytes 17563648 | tf_op jit(solution)/shard_map/dot_general | solution.py:37
  593.1 13.0 %convolution_convert_fusion = bf16[2560,2048]{1,0:T(8,128)(2,1)S(1)} fusion(bf16[2560,1024]{1,0:T(8,128)(2,1)} %copy-done.49, bf16[1024,2048]{1,0:T(8,128)(2,1)S(1)} %copy-done.45), kind=kOutput, calls=%fused_computation.2 | convolution fusion | flops 10742661120 | bytes 19922944 | tf_op jit(solution)/shard_map/dot_general | solution.py:351
  613.3 13.9 %collective-permute-done.66 = bf16[4,64,1024]{2,1,0:T(8,128)(2,1)S(1)} collective-permute-done((bf16[4,64,1024]{2,1,0:T(8,128)(2,1)S(1)}, bf16[4,64,1024]{2,1,0:T(8,128)(2,1)S(1)}, u32[]{:S(2)}, u32[]{:S(2)}) %collective-permute-start.66) | collective-permute-done | bytes 524320 | tf_op jit(solution)/shard_map/ppermute | solution.py:44
  633.1 12.3 %fusion.96 = (bf16[1280,2048]{1,0:T(8,128)(2,1)S(1)}, f32[1280,2048]{1,0:T(8,128)}) fusion(bf16[1280,2048]{1,0:T(8,128)(2,1)} %collective-permute-done.57, bf16[2048,768]{1,0:T(8,128)(2,1)} %bitcast.211, bf16[2560,768]{1,0:T(8,128)(2,1)} %bitcast.216), kind=kOutput, calls=%fused_computation.224 | convolution fusion | flops 4034396160 | bytes 26083328 | tf_op jit(solution)/shard_map/dot_general | solution.py:31
  648.9 12.8 %fusion.73 = (bf16[1280,2048]{1,0:T(8,128)(2,1)}, f32[1280,2048]{1,0:T(8,128)}) fusion(bf16[1280,2048]{1,0:T(8,128)(2,1)} %collective-permute-done.50, bf16[2560,2048]{1,0:T(8,128)(2,1)} %copy-done.15), kind=kLoop, calls=%fused_computation.207 | loop fusion | flops 10485760 | bytes 26214400 | tf_op jit(solution)/shard_map/convert.11
  689.3 20.5 %collective-permute-done.58 = bf16[160,2048]{1,0:T(8,128)(2,1)} collective-permute-done((bf16[160,2048]{1,0:T(8,128)(2,1)S(1)}, bf16[160,2048]{1,0:T(8,128)(2,1)}, u32[]{:S(2)}, u32[]{:S(2)}) %collective-permute-start.58) | collective-permute-done | bytes 655392 | tf_op jit(solution)/shard_map/ppermute | solution.py:44
  711.9 13.1 %collective-permute-done.60 = bf16[160,2048]{1,0:T(8,128)(2,1)} collective-permute-done((bf16[160,2048]{1,0:T(8,128)(2,1)}, bf16[160,2048]{1,0:T(8,128)(2,1)}, u32[]{:S(2)}, u32[]{:S(2)}) %collective-permute-start.60) | collective-permute-done | bytes 655392 | tf_op jit(solution)/shard_map/ppermute | solution.py:44
  730.6 7.8 convolution_convert_fusion.9
  738.8 14.3 %collective-permute-done.53 = bf16[160,2048]{1,0:T(8,128)(2,1)} collective-permute-done((bf16[160,2048]{1,0:T(8,128)(2,1)S(1)}, bf16[160,2048]{1,0:T(8,128)(2,1)}, u32[]{:S(2)}, u32[]{:S(2)}) %collective-permute-start.53) | collective-permute-done | bytes 655392 | tf_op jit(solution)/shard_map/ppermute | solution.py:44
  (408 shorter events, 305.9 us)
Async XLA Ops:
  7.2 41.7 %all-gather.5.cloned.1.call-start = ((), (), s32[]{:S(2)}) async-start(), calls=%async_computation.8 | async-start | bytes 1310720 | tf_op jit(solution)/shard_map/all_gather | solution.py:65
  32.3 81.7 %all-gather.7.cloned.1.call-start = ((), (), s32[]{:S(2)}) async-start(), calls=%async_computation.9 | async-start | bytes 3932160 | tf_op jit(solution)/shard_map/all_gather | solution.py:65
  48.9 279.5 %all-gather.9.cloned.1.call-start = ((), (), s32[]{:S(2)}) async-start(), calls=%async_computation.10 | async-start | bytes 5242880 | tf_op jit(solution)/shard_map/all_gather | solution.py:65
  49.8 30.5 %collective-permute-start.3 = (bf16[320,2048]{1,0:T(8,128)(2,1)S(1)}, bf16[320,2048]{1,0:T(8,128)(2,1)S(1)}, u32[]{:S(2)}, u32[]{:S(2)}) collective-permute-start(bf16[320,2048]{1,0:T(8,128)(2,1)S(1)} %fusion.16), channel_id=1, source_target_pairs={{1,0},{0,1},{3,2},{2,3},{5,4},{4,5},{7,6},{6,7},{9,8},{8,9},{11,10... | collective-permute-start | bytes 3932168 | tf_op jit(solution)/shard_map/ppermute | solution.py:44
  51.3 30.5 %collective-permute-start.2 = (bf16[320,2048]{1,0:T(8,128)(2,1)S(1)}, bf16[320,2048]{1,0:T(8,128)(2,1)}, u32[]{:S(2)}, u32[]{:S(2)}) collective-permute-start(bf16[320,2048]{1,0:T(8,128)(2,1)S(1)} %fusion.16), channel_id=1, source_target_pairs={{16,0},{24,8},{0,16},{8,24},{17,1},{25,9},{1,17},{9,25},{18,2},{26... | collective-permute-start | bytes 3932168 | tf_op jit(solution)/shard_map/ppermute | solution.py:44
  52.8 31.9 %collective-permute-start = (s32[1,2]{1,0:T(1,128)S(1)}, s32[1,2]{1,0:T(1,128)S(1)}, u32[]{:S(2)}, u32[]{:S(2)}) collective-permute-start(s32[1,2]{1,0:T(1,128)S(1)} %copy-done.44), channel_id=1, source_target_pairs={{1,0},{0,1},{3,2},{2,3},{5,4},{4,5},{7,6},{6,7},{9,8},{8,9},{11,10... | collective-permute-start | bytes 32 | tf_op jit(solution)/shard_map/ppermute | solution.py:44
  143.1 40.3 %collective-permute-start.11 = (bf16[1280,2048]{1,0:T(8,128)(2,1)}, bf16[1280,2048]{1,0:T(8,128)(2,1)}, u32[]{:S(2)}, u32[]{:S(2)}) collective-permute-start(bf16[1280,2048]{1,0:T(8,128)(2,1)} %convolution_convert_fusion.3), channel_id=1, source_target_pairs={{8,0},{0,8},{24,16},{16,24},{9,1},{1,9},{25,17},{17,25},{10,2},{2,... | collective-permute-start | bytes 15728648 | tf_op jit(solution)/shard_map/ppermute | solution.py:44
  183.3 181.7 %all-gather.11.cloned.1.call-start = ((), (), s32[]{:S(2)}) async-start(), calls=%async_computation.11 | async-start | bytes 5242880 | tf_op jit(solution)/shard_map/all_gather | solution.py:65
  188.5 31.4 %collective-permute-start.12 = (bf16[160,2048]{1,0:T(8,128)(2,1)S(1)}, bf16[160,2048]{1,0:T(8,128)(2,1)S(1)}, u32[]{:S(2)}, u32[]{:S(2)}) collective-permute-start(bf16[160,2048]{1,0:T(8,128)(2,1)S(1)} %get-tuple-element.97), channel_id=1, source_target_pairs={{16,0},{24,8},{0,16},{8,24},{17,1},{25,9},{1,17},{9,25},{18,2},{26... | collective-permute-start | bytes 1966088 | tf_op jit(solution)/shard_map/ppermute | solution.py:44
  190.1 31.2 %collective-permute-start.15 = (bf16[160,2048]{1,0:T(8,128)(2,1)S(1)}, bf16[160,2048]{1,0:T(8,128)(2,1)S(1)}, u32[]{:S(2)}, u32[]{:S(2)}) collective-permute-start(bf16[160,2048]{1,0:T(8,128)(2,1)S(1)} %get-tuple-element.99), channel_id=1, source_target_pairs={{1,0},{0,1},{3,2},{2,3},{5,4},{4,5},{7,6},{6,7},{9,8},{8,9},{11,10... | collective-permute-start | bytes 1966088 | tf_op jit(solution)/shard_map/ppermute | solution.py:44
  207.5 44.4 %collective-permute-start.28 = (bf16[320,2048]{1,0:T(8,128)(2,1)}, bf16[320,2048]{1,0:T(8,128)(2,1)}, u32[]{:S(2)}, u32[]{:S(2)}) collective-permute-start(bf16[320,2048]{1,0:T(8,128)(2,1)} %bitcast.27), channel_id=1, source_target_pairs={{1,0},{0,1},{3,2},{2,3},{5,4},{4,5},{7,6},{6,7},{9,8},{8,9},{11,10... | collective-permute-start | bytes 3932168 | tf_op jit(solution)/shard_map/ppermute | solution.py:44
  208.0 45.3 %collective-permute-start.27 = (bf16[320,2048]{1,0:T(8,128)(2,1)}, bf16[320,2048]{1,0:T(8,128)(2,1)}, u32[]{:S(2)}, u32[]{:S(2)}) collective-permute-start(bf16[320,2048]{1,0:T(8,128)(2,1)} %bitcast.27), channel_id=1, source_target_pairs={{16,0},{24,8},{0,16},{8,24},{17,1},{25,9},{1,17},{9,25},{18,2},{26... | collective-permute-start | bytes 3932168 | tf_op jit(solution)/shard_map/ppermute | solution.py:44
  219.8 46.1 %collective-permute-start.17 = (bf16[160,2048]{1,0:T(8,128)(2,1)S(1)}, bf16[160,2048]{1,0:T(8,128)(2,1)}, u32[]{:S(2)}, u32[]{:S(2)}) collective-permute-start(bf16[160,2048]{1,0:T(8,128)(2,1)S(1)} %get-tuple-element.98), channel_id=1, source_target_pairs={{1,0},{0,1},{3,2},{2,3},{5,4},{4,5},{7,6},{6,7},{9,8},{8,9},{11,10... | collective-permute-start | bytes 1966088 | tf_op jit(solution)/shard_map/ppermute | solution.py:44
  225.5 40.4 %collective-permute-start.16 = (bf16[160,2048]{1,0:T(8,128)(2,1)}, bf16[160,2048]{1,0:T(8,128)(2,1)}, u32[]{:S(2)}, u32[]{:S(2)}) collective-permute-start(bf16[160,2048]{1,0:T(8,128)(2,1)} %get-tuple-element.84), channel_id=1, source_target_pairs={{16,0},{24,8},{0,16},{8,24},{17,1},{25,9},{1,17},{9,25},{18,2},{26... | collective-permute-start | bytes 1966088 | tf_op jit(solution)/shard_map/ppermute | solution.py:44
  225.8 51.7 %collective-permute-start.31 = (bf16[320,2048]{1,0:T(8,128)(2,1)}, bf16[320,2048]{1,0:T(8,128)(2,1)}, u32[]{:S(2)}, u32[]{:S(2)}) collective-permute-start(bf16[320,2048]{1,0:T(8,128)(2,1)} %bitcast.27), channel_id=1, source_target_pairs={{8,0},{0,8},{24,16},{16,24},{9,1},{1,9},{25,17},{17,25},{10,2},{2,... | collective-permute-start | bytes 3932168 | tf_op jit(solution)/shard_map/ppermute | solution.py:44
  225.9 385.8 %reduce-scatter.9.cloned.1.call-start = ((), (), s32[]{:S(2)}) async-start(), calls=%async_computation.14 | async-start | bytes 5242880 | tf_op jit(solution)/shard_map/reduce_scatter | solution.py:69
  265.9 41.1 %collective-permute-start.33 = (bf16[320,2048]{1,0:T(8,128)(2,1)}, bf16[320,2048]{1,0:T(8,128)(2,1)S(1)}, u32[]{:S(2)}, u32[]{:S(2)}) collective-permute-start(bf16[320,2048]{1,0:T(8,128)(2,1)} %collective-permute-done.28), channel_id=1, source_target_pairs={{8,0},{0,8},{24,16},{16,24},{9,1},{1,9},{25,17},{17,25},{10,2},{2,... | collective-permute-start | bytes 3932168 | tf_op jit(solution)/shard_map/ppermute | solution.py:44
  417.9 30.7 %collective-permute-start.36 = (bf16[160,2048]{1,0:T(8,128)(2,1)S(1)}, bf16[160,2048]{1,0:T(8,128)(2,1)S(1)}, u32[]{:S(2)}, u32[]{:S(2)}) collective-permute-start(bf16[160,2048]{1,0:T(8,128)(2,1)S(1)} %get-tuple-element.93), channel_id=1, source_target_pairs={{16,0},{24,8},{0,16},{8,24},{17,1},{25,9},{1,17},{9,25},{18,2},{26... | collective-permute-start | bytes 1966088 | tf_op jit(solution)/shard_map/ppermute | solution.py:44
  468.2 197.2 %reduce-scatter.11.cloned.1.call-start = ((), (), s32[]{:S(2)}) async-start(), calls=%async_computation.15 | async-start | bytes 5242880 | tf_op jit(solution)/shard_map/reduce_scatter | solution.py:69
  491.7 29.7 %collective-permute-start.42 = (bf16[320,2048]{1,0:T(8,128)(2,1)}, bf16[320,2048]{1,0:T(8,128)(2,1)S(1)}, u32[]{:S(2)}, u32[]{:S(2)}) collective-permute-start(bf16[320,2048]{1,0:T(8,128)(2,1)} %get-tuple-element.68), channel_id=1, source_target_pairs={{16,0},{24,8},{0,16},{8,24},{17,1},{25,9},{1,17},{9,25},{18,2},{26... | collective-permute-start | bytes 3932168 | tf_op jit(solution)/shard_map/ppermute | solution.py:44
  523.9 163.7 %reduce-scatter.5.cloned.1.call-start = ((), (), s32[]{:S(2)}) async-start(), calls=%async_computation.12 | async-start | bytes 3932160 | tf_op jit(solution)/shard_map/reduce_scatter | solution.py:69
  592.4 40.7 %collective-permute-start.57 = (bf16[1280,2048]{1,0:T(8,128)(2,1)}, bf16[1280,2048]{1,0:T(8,128)(2,1)}, u32[]{:S(2)}, u32[]{:S(2)}) collective-permute-start(bf16[1280,2048]{1,0:T(8,128)(2,1)} %convolution_convert_fusion.1), channel_id=1, source_target_pairs={{8,0},{0,8},{24,16},{16,24},{9,1},{1,9},{25,17},{17,25},{10,2},{2,... | collective-permute-start | bytes 15728648 | tf_op jit(solution)/shard_map/ppermute | solution.py:44
  611.7 37.2 %collective-permute-start.50 = (bf16[1280,2048]{1,0:T(8,128)(2,1)}, bf16[1280,2048]{1,0:T(8,128)(2,1)}, u32[]{:S(2)}, u32[]{:S(2)}) collective-permute-start(bf16[1280,2048]{1,0:T(8,128)(2,1)} %slice.266), channel_id=1, source_target_pairs={{8,0},{0,8},{24,16},{16,24},{9,1},{1,9},{25,17},{17,25},{10,2},{2,... | collective-permute-start | bytes 15728648 | tf_op jit(solution)/shard_map/ppermute | solution.py:44
  629.5 42.3 %all-to-all-start.3 = ((bf16[4,2,64,1024]{3,2,1,0:T(8,128)(2,1)}), bf16[4,2,64,1024]{3,2,1,0:T(8,128)(2,1)S(1)}, u32[]{:S(2)}, u32[]{:S(2)}) async-start(bf16[4,2,64,1024]{3,2,1,0:T(8,128)(2,1)} %copy.89), calls=%async_computation.6 | async-start | bytes 2097152 | tf_op jit(solution)/shard_map/all_to_all | solution.py:83
  633.1 158.7 %reduce-scatter.7.cloned.1.call-start = ((), (), s32[]{:S(2)}) async-start(), calls=%async_computation.13 | async-start | bytes 1310720 | tf_op jit(solution)/shard_map/reduce_scatter | solution.py:69
  646.9 33.0 %collective-permute-start.59 = (bf16[160,2048]{1,0:T(8,128)(2,1)}, bf16[160,2048]{1,0:T(8,128)(2,1)}, u32[]{:S(2)}, u32[]{:S(2)}) collective-permute-start(bf16[160,2048]{1,0:T(8,128)(2,1)} %get-tuple-element.88), channel_id=1, source_target_pairs={{16,0},{24,8},{0,16},{8,24},{17,1},{25,9},{1,17},{9,25},{18,2},{26... | collective-permute-start | bytes 1966088 | tf_op jit(solution)/shard_map/ppermute | solution.py:44
  668.2 60.5 %collective-permute-start.51 = (bf16[160,2048]{1,0:T(8,128)(2,1)}, bf16[160,2048]{1,0:T(8,128)(2,1)}, u32[]{:S(2)}, u32[]{:S(2)}) collective-permute-start(bf16[160,2048]{1,0:T(8,128)(2,1)} %get-tuple-element.89), channel_id=1, source_target_pairs={{16,0},{24,8},{0,16},{8,24},{17,1},{25,9},{1,17},{9,25},{18,2},{26... | collective-permute-start | bytes 1966088 | tf_op jit(solution)/shard_map/ppermute | solution.py:44
  670.0 68.4 %collective-permute-start.56 = (bf16[160,2048]{1,0:T(8,128)(2,1)}, bf16[160,2048]{1,0:T(8,128)(2,1)}, u32[]{:S(2)}, u32[]{:S(2)}) collective-permute-start(bf16[160,2048]{1,0:T(8,128)(2,1)} %get-tuple-element.90), channel_id=1, source_target_pairs={{1,0},{0,1},{3,2},{2,3},{5,4},{4,5},{7,6},{6,7},{9,8},{8,9},{11,10... | collective-permute-start | bytes 1966088 | tf_op jit(solution)/shard_map/ppermute | solution.py:44
  679.9 30.0 %collective-permute-start.58 = (bf16[160,2048]{1,0:T(8,128)(2,1)S(1)}, bf16[160,2048]{1,0:T(8,128)(2,1)}, u32[]{:S(2)}, u32[]{:S(2)}) collective-permute-start(bf16[160,2048]{1,0:T(8,128)(2,1)S(1)} %copy-done.28), channel_id=1, source_target_pairs={{16,0},{24,8},{0,16},{8,24},{17,1},{25,9},{1,17},{9,25},{18,2},{26... | collective-permute-start | bytes 1966088 | tf_op jit(solution)/shard_map/ppermute | solution.py:44
  683.2 41.8 %collective-permute-start.60 = (bf16[160,2048]{1,0:T(8,128)(2,1)}, bf16[160,2048]{1,0:T(8,128)(2,1)}, u32[]{:S(2)}, u32[]{:S(2)}) collective-permute-start(bf16[160,2048]{1,0:T(8,128)(2,1)} %fusion.42), channel_id=1, source_target_pairs={{1,0},{0,1},{3,2},{2,3},{5,4},{4,5},{7,6},{6,7},{9,8},{8,9},{11,10... | collective-permute-start | bytes 1966088 | tf_op jit(solution)/shard_map/ppermute | solution.py:44
  709.9 46.3 %collective-permute-start.63 = (bf16[160,2048]{1,0:T(8,128)(2,1)S(1)}, bf16[160,2048]{1,0:T(8,128)(2,1)}, u32[]{:S(2)}, u32[]{:S(2)}) collective-permute-start(bf16[160,2048]{1,0:T(8,128)(2,1)S(1)} %copy-done.26), channel_id=1, source_target_pairs={{1,0},{0,1},{3,2},{2,3},{5,4},{4,5},{7,6},{6,7},{9,8},{8,9},{11,10... | collective-permute-start | bytes 1966088 | tf_op jit(solution)/shard_map/ppermute | solution.py:44
  711.6 41.5 %collective-permute-start.53 = (bf16[160,2048]{1,0:T(8,128)(2,1)S(1)}, bf16[160,2048]{1,0:T(8,128)(2,1)}, u32[]{:S(2)}, u32[]{:S(2)}) collective-permute-start(bf16[160,2048]{1,0:T(8,128)(2,1)S(1)} %get-tuple-element.80), channel_id=1, source_target_pairs={{1,0},{0,1},{3,2},{2,3},{5,4},{4,5},{7,6},{6,7},{9,8},{8,9},{11,10... | collective-permute-start | bytes 1966088 | tf_op jit(solution)/shard_map/ppermute | solution.py:44
  (103 other events, 1406.7 us)
Sparse Core Ops, SparseCore 0:
  20.0 28.7 all-gather.4
  51.0 62.9 all-gather.6
  183.4 78.5 all-gather.8
  263.4 79.2 all-gather.10
  468.4 74.5 reduce-scatter.8
  545.2 77.2 reduce-scatter.10
  624.8 60.7 reduce-scatter.4
  738.6 24.4 reduce-scatter.6

commit v4 on v3

v4 whole, which is shorter than its diff:
```python
import jax
import jax.numpy as jnp
from jax import lax
from jax.experimental import pallas as pl
from jax.experimental.pallas import tpu as pltpu
from jax.sharding import PartitionSpec as P

HEAD = 128
BLK_A = 256
BLK_B = 64
SPLITS = ((0, BLK_A), (BLK_A, BLK_A + BLK_B))
BLOCK_HALF = (BLK_A + BLK_B) // 2

EPSILON = 1e-05
NEGATIVE = -1e30
SCALE = HEAD ** (-0.5)
BF16 = jnp.bfloat16
F32 = jnp.float32


def after(value, *others):
    return lax.optimization_barrier((value, others))[0]


def layer_norm(value, gain, bias):
    center = value - jnp.mean(value, axis=-1, keepdims=True)
    spread = jnp.mean(center * center, axis=-1, keepdims=True)
    return center * lax.rsqrt(spread + EPSILON) * gain + bias


def gelu(v):
    rate = (2.0 / 3.141592653589793) ** 0.5
    squared = v * v
    bend = jnp.tanh(rate * v * (1.0 + 0.044715 * squared))
    rise = 0.5 * (1.0 + bend)
    slope = rise + 0.5 * v * (1.0 - bend * bend) * rate * (1.0 + 3 * 0.044715 * squared)
    return v * rise, slope


def contract_last(left, right):
    return lax.dot_general(
        left, right, (((1,), (1,)), ((), ())), preferred_element_type=F32
    )


def contract_first(left, right):
    return lax.dot_general(
        left, right, (((0,), (0,)), ((), ())), preferred_element_type=F32
    )


def flip(axis, bits, block):
    count = lax.axis_size(axis)
    return lax.ppermute(block, axis, [(i ^ bits, i) for i in range(count)])


def flip_core(block):
    return flip("blk", 1, block)


def flip_x(block):
    return flip("blk", 2, block)


def flip_y(block):
    return flip("dp", 1, block)


def lines():
    count = lax.axis_size("dp")
    return [[z * 2 + y for z in range(count // 2)] for y in range(2)]


def gather_z(part, axis):
    return lax.all_gather(part, "dp", axis_index_groups=lines(), axis=axis, tiled=True)


def scatter_z(total, axis):
    return lax.psum_scatter(
        total, "dp", axis_index_groups=lines(), scatter_dimension=axis, tiled=True
    )


def column(groups, blk, runs, width, group, b, run, y):
    return (((group * blk + b) * runs + run) * 2 + y) * width


def split_columns(shard, groups, blk, runs, width):
    rows = shard.shape[0]
    count = groups * runs * width

    def kernel(y_ref, in_ref, out_ref):
        b = pl.program_id(1)
        y = jnp.where(pl.program_id(0) == 0, 1 - y_ref[0], y_ref[0])
        for group in range(groups):
            for run in range(runs):
                start = column(groups, blk, runs, width, group, b, run, y)
                to = (group * runs + run) * width
                out_ref[0, 0, :, to : to + width] = in_ref[:, pl.ds(pl.multiple_of(start, 128), width)]

    return pl.pallas_call(
        kernel,
        grid_spec=pltpu.PrefetchScalarGridSpec(
            num_scalar_prefetch=1,
            grid=(2, blk),
            in_specs=[pl.BlockSpec(shard.shape, lambda i, j, *_: (0, 0))],
            out_specs=pl.BlockSpec((1, 1, rows, count), lambda i, j, *_: (i, j, 0, 0)),
        ),
        out_shape=jax.ShapeDtypeStruct((2, blk, rows, count), shard.dtype),
        compiler_params=pltpu.CompilerParams(vmem_limit_bytes=16 * 2**20),
        cost_estimate=pl.CostEstimate(flops=0, bytes_accessed=4 * shard.size, transcendentals=0),
    )((lax.axis_index("dp") % 2).reshape(1), shard)


def join_y(own, other):
    blk, rows, count = own.shape

    def kernel(y_ref, own_ref, other_ref, out_ref):
        out_ref[0, y_ref[0]] = own_ref[0]
        out_ref[0, 1 - y_ref[0]] = other_ref[0]

    piece = pl.BlockSpec((1, rows, count), lambda i, *_: (i, 0, 0))
    return pl.pallas_call(
        kernel,
        grid_spec=pltpu.PrefetchScalarGridSpec(
            num_scalar_prefetch=1,
            grid=(blk,),
            in_specs=[piece, piece],
            out_specs=pl.BlockSpec((1, 2, rows, count), lambda i, *_: (i, 0, 0, 0)),
        ),
        out_shape=jax.ShapeDtypeStruct((blk, 2, rows, count), own.dtype),
        compiler_params=pltpu.CompilerParams(vmem_limit_bytes=16 * 2**20),
        cost_estimate=pl.CostEstimate(flops=0, bytes_accessed=8 * own.size, transcendentals=0),
    )((lax.axis_index("dp") % 2).reshape(1), own, other)


def merge_columns(parts, groups, blk, runs, width):
    _, _, rows, count = parts.shape

    def kernel(in_ref, out_ref):
        b = pl.program_id(0)
        for y in range(2):
            for group in range(groups):
                for run in range(runs):
                    start = column(groups, blk, runs, width, group, b, run, y)
                    at = (group * runs + run) * width
                    out_ref[:, pl.ds(pl.multiple_of(start, 128), width)] = in_ref[
                        0, y, :, at : at + width
                    ].astype(F32)

    return pl.pallas_call(
        kernel,
        grid=(blk,),
        in_specs=[pl.BlockSpec((1, 2, rows, count), lambda i: (i, 0, 0, 0))],
        out_specs=pl.BlockSpec((rows, blk * 2 * count), lambda i: (0, 0)),
        out_shape=jax.ShapeDtypeStruct((rows, blk * 2 * count), F32),
        compiler_params=pltpu.CompilerParams(vmem_limit_bytes=16 * 2**20),
        cost_estimate=pl.CostEstimate(flops=0, bytes_accessed=6 * parts.size, transcendentals=0),
    )(parts)


def exchange(own, other):
    return lax.all_to_all(join_y(own, other), "blk", 0, 0)


TOPS = ((0, 5), (3, 4))
BOTTOMS = ((1, 2), (7, 6))


def gather_first(part, y_others=(), x_others=()):
    return part, flip_x(after(part, x_others)), flip_y(after(part, y_others)), flip_core(after(part, x_others))


def gather_second(part, from_x, from_y, from_core):
    half = part.shape[0] // 2
    diagonal = [flip_y(from_x[:half]), flip_x(from_y[half:])]
    return [part, from_x, from_y], diagonal, [from_core, flip_core(from_x), flip_core(from_y)]


def gather_third(mine, diagonal, others):
    most = assemble([*mine, *others], [(0, 0, 2, 0), (1, 0, 1, 5), (1, 1, 1, 2), (2, 0, 1, 3), (2, 1, 1, 7)])
    diagonal = after(diagonal, most)
    both = [*diagonal, *[flip_core(piece) for piece in diagonal]]
    return assemble(both, [(0, 0, 1, 4), (1, 0, 1, 6)], most)


def assemble(pieces, runs, whole=None):
    half = BLOCK_HALF
    columns = pieces[0].shape[1]
    side_pieces = len(pieces) // 2
    copies, total = [], 0
    for side in range(2):
        for piece, start, count, to in runs:
            copies.append(
                (side * side_pieces + piece, start * half, count * half, (side * 8 + to) * half, total)
            )
            total += count * half

    def kernel(*refs):
        out_ref, held_ref, in_sems, out_sems = refs[-4:]
        reads, writes = [], []
        for i, (piece, start, count, to, at) in enumerate(copies):
            there = held_ref.at[pl.ds(at, count)]
            source = refs[piece].at[pl.ds(start, count)]
            reads.append(pltpu.make_async_copy(source, there, in_sems.at[i]))
            writes.append(pltpu.make_async_copy(there, out_ref.at[pl.ds(to, count)], out_sems.at[i]))
        for read in reads:
            read.start()
        for read, write in zip(reads, writes):
            read.wait()
            write.start()
        for write in writes:
            write.wait()

    inputs = [*pieces] if whole is None else [*pieces, whole]
    return pl.pallas_call(
        kernel,
        in_specs=[pl.BlockSpec(memory_space=pl.ANY)] * len(inputs),
        out_specs=pl.BlockSpec(memory_space=pltpu.HBM),
        out_shape=jax.ShapeDtypeStruct((16 * half, columns), pieces[0].dtype),
        input_output_aliases={} if whole is None else {len(inputs) - 1: 0},
        scratch_shapes=[pltpu.VMEM((total, columns), pieces[0].dtype)]
        + [pltpu.SemaphoreType.DMA((len(copies),))] * 2,
        compiler_params=pltpu.CompilerParams(vmem_limit_bytes=56 * 2**20),
        cost_estimate=pl.CostEstimate(flops=0, bytes_accessed=4 * total * columns, transcendentals=0),
    )(*inputs)


def scatter_core(product):
    far, near = product(12, 16).astype(BF16), product(8, 12).astype(BF16)
    return scatter_pair(product, flip_core(far), flip_core(near))


def scatter_pair(product, far, near):
    middle = far.shape[0] // 2
    to_x = (product(4, 6).astype(F32) + far[:middle].astype(F32)).astype(BF16)
    to_y = (product(6, 8).astype(F32) + far[middle:].astype(F32)).astype(BF16)
    return (to_x, to_y), (product(0, 4, to_x, to_y), near)


def scatter_first(held, *others):
    to_x, to_y = held[0]
    return flip_x(after(to_x, *others)), flip_y(after(to_y, *others))


def scatter_second(held, from_x, from_y):
    half = from_x.shape[0] // 2
    product, got = held[1]
    to_x = product[2 * half : 3 * half].astype(F32) + got[2 * half : 3 * half].astype(F32)
    to_y = product[3 * half :].astype(F32) + got[3 * half :].astype(F32)
    to_x = (to_x + from_y[:half].astype(F32)).astype(BF16)
    to_y = (to_y + from_x[:half].astype(F32)).astype(BF16)
    return to_x, to_y


def scatter_third(held, from_x, from_y, to_x, to_y):
    half = from_x.shape[0] // 2
    product, got = held[1]
    own = product[: 2 * half].astype(F32) + got[: 2 * half].astype(F32)
    top = from_x[half:].astype(F32) + flip_y(to_y).astype(F32)
    bottom = from_y[half:].astype(F32) + flip_x(to_x).astype(F32)
    return own + jnp.concatenate([top, bottom], axis=0)


def sum_small(norms, hidden):
    blk, dp = lax.axis_size("blk"), lax.axis_size("dp")
    count = norms.shape[0]
    parts = norms.reshape(count, blk, -1).transpose(1, 0, 2)
    parts = jnp.sum(lax.all_to_all(parts, "blk", 0, 0), axis=0)
    parts = parts.reshape(count, dp, -1).transpose(1, 0, 2)
    share = parts.shape[2]
    hidden = jnp.repeat(hidden.reshape(dp // 2, -1), 2, axis=0)
    both = jnp.concatenate([parts.reshape(dp, -1), hidden], axis=1)
    both = lax.all_to_all(both, "dp", 0, 0)
    mine = jnp.arange(dp) % 2 == lax.axis_index("dp") % 2
    return (
        jnp.sum(both[:, : count * share], axis=0).reshape(count, share),
        jnp.sum(jnp.where(mine[:, None], both[:, count * share :], 0.0), axis=0),
    )


def runs_of(places_ref, sequence, column, block, half):
    first, last = SPLITS[column]
    if first < half:
        top = min(last, half)
        yield places_ref[sequence, column, block], slice(first, top), slice(0, top - first)
    if last > half:
        start = max(first, half)
        yield (
            places_ref[sequence, column, 4 + block],
            slice(start - half, last - half),
            slice(start - first, last - first),
        )


def load_block(places_ref, sequence, column, block, ref, lanes, to_ref, row):
    for which, here, there in runs_of(places_ref, sequence, column, block, ref.shape[1]):
        to_ref[row + there.start : row + there.stop] = ref[which, here, lanes]


def store_block(places_ref, sequence, column, block, ref, lanes, value):
    for which, here, there in runs_of(places_ref, sequence, column, block, ref.shape[1]):
        ref[which, here, lanes] = value[there]


def scores_of(queries, keys, first, length):
    scores = contract_last(queries, keys) * SCALE
    key_places = lax.broadcasted_iota(jnp.int32, scores.shape, 1)
    query_places = first + lax.broadcasted_iota(jnp.int32, scores.shape, 0)
    allowed = (key_places <= query_places) & (key_places < length)
    return jnp.where(allowed, scores, NEGATIVE)


def attention_steps():
    for column, (first, last) in enumerate(SPLITS):
        size = last - first
        step = 1 if size * 4 > 512 else 4
        yield column, size, [(p, step, (p + step) * size) for p in range(0, 4, step)]


def attention_forward_kernel(places_ref, lengths_ref, in_ref, out_ref, log_ref, q_ref, k_ref, v_ref):
    sequence = pl.program_id(0)
    heads = in_ref.shape[-1] // (3 * HEAD)
    for column, size, runs in attention_steps():
        length = lengths_ref[sequence, column]
        for head in range(heads):
            for third, ref in enumerate((q_ref, k_ref, v_ref)):
                lanes = slice((third * heads + head) * HEAD, (third * heads + head + 1) * HEAD)
                for block in range(4):
                    load_block(places_ref, sequence, column, block, in_ref, lanes, ref, block * size)
            lanes = slice(head * HEAD, (head + 1) * HEAD)
            for start, step, keys in runs:
                rows = slice(start * size, (start + step) * size)
                scores = scores_of(q_ref[rows], k_ref[:keys], start * size, length)
                peak = jnp.max(scores, axis=-1, keepdims=True)
                weights = jnp.exp(scores - peak)
                total = jnp.sum(weights, axis=-1, keepdims=True)
                attended = jnp.dot(weights.astype(BF16), v_ref[:keys], preferred_element_type=F32)
                attended = (attended / total).astype(BF16)
                log_total = jnp.broadcast_to(peak + jnp.log(total), (step * size, HEAD))
                for i in range(step):
                    here = slice(i * size, (i + 1) * size)
                    at = (places_ref, sequence, column, start + i)
                    store_block(*at, out_ref, lanes, attended[here])
                    store_block(*at, log_ref, lanes, log_total[here])


def attention_backward_kernel(
    places_ref,
    lengths_ref,
    in_ref,
    grad_ref,
    log_ref,
    out_ref,
    q_ref,
    k_ref,
    v_ref,
    g_ref,
    log_rows_ref,
    dk_ref,
    dv_ref,
):
    sequence = pl.program_id(0)
    heads = in_ref.shape[-1] // (3 * HEAD)
    for column, size, runs in attention_steps():
        length = lengths_ref[sequence, column]
        for head in range(heads):
            columns = [
                slice((third * heads + head) * HEAD, (third * heads + head + 1) * HEAD)
                for third in range(3)
            ]
            lanes = slice(head * HEAD, (head + 1) * HEAD)
            for block in range(4):
                at = (places_ref, sequence, column, block)
                load_block(*at, in_ref, columns[0], q_ref, block * size)
                load_block(*at, in_ref, columns[1], k_ref, block * size)
                load_block(*at, in_ref, columns[2], v_ref, block * size)
                load_block(*at, grad_ref, lanes, g_ref, block * size)
                load_block(*at, log_ref, lanes, log_rows_ref, block * size)
            dk_ref[...] = jnp.zeros_like(dk_ref)
            dv_ref[...] = jnp.zeros_like(dv_ref)
            for start, step, keys in runs:
                rows = slice(start * size, (start + step) * size)
                queries, grads = q_ref[rows], g_ref[rows]
                scores = scores_of(queries, k_ref[:keys], start * size, length)
                probs = jnp.exp(scores - log_rows_ref[rows, :1])
                grad_probs = contract_last(grads, v_ref[:keys])
                delta = jnp.sum(probs * grad_probs, axis=-1, keepdims=True)
                grad_scores = (probs * (grad_probs - delta)).astype(BF16)
                dv_ref[:keys] += contract_first(probs.astype(BF16), grads)
                dk_ref[:keys] += contract_first(grad_scores, queries)
                dq = jnp.dot(grad_scores, k_ref[:keys], preferred_element_type=F32) * SCALE
                dq = dq.astype(BF16)
                for i in range(step):
                    at = (places_ref, sequence, column, start + i)
                    store_block(*at, out_ref, columns[0], dq[i * size : (i + 1) * size])
            for block in range(4):
                here = slice(block * size, (block + 1) * size)
                at = (places_ref, sequence, column, block)
                store_block(*at, out_ref, columns[1], (dk_ref[here] * SCALE).astype(BF16))
                store_block(*at, out_ref, columns[2], dv_ref[here].astype(BF16))


def attention_call(kernel, arrays, outs, scratch, places, lengths, matmuls):
    count = 4 * BLK_A
    half = arrays[0].shape[0] // 16

    def spec(columns):
        return pl.BlockSpec((16, half, columns), lambda s, *_: (0, 0, 0))

    heads = arrays[0].shape[1] // (3 * HEAD)
    results = pl.pallas_call(
        kernel,
        grid_spec=pltpu.PrefetchScalarGridSpec(
            num_scalar_prefetch=2,
            grid=(2,),
            in_specs=[spec(a.shape[1]) for a in arrays],
            out_specs=[spec(columns) for columns, _ in outs],
            scratch_shapes=[pltpu.VMEM((count, HEAD), dtype) for dtype in scratch],
        ),
        out_shape=[jax.ShapeDtypeStruct((16, half, c), dtype) for c, dtype in outs],
        compiler_params=pltpu.CompilerParams(vmem_limit_bytes=48 * 2**20),
        cost_estimate=pl.CostEstimate(
            flops=matmuls * 2 * heads * count * count * HEAD * 2,
            bytes_accessed=16 * half * HEAD * heads * 2 * 4,
            transcendentals=2 * heads * count * count,
        ),
    )(places, lengths, *[a.reshape(16, half, -1) for a in arrays])
    return [r.reshape(16 * half, -1) for r in results]


def body(
    hidden_in,
    cotangent,
    seq_lengths,
    block_order,
    w_qkv,
    w_out,
    w_up,
    w_down,
    norm_gains,
    norm_biases,
    hidden_bias,
):
    blk, dp = lax.axis_size("blk"), lax.axis_size("dp")
    lanes = dp // 2
    b, d = lax.axis_index("blk"), lax.axis_index("dp")
    z, y = d // 2, d % 2
    rows, width = hidden_in.shape[2:]
    pairs = width // HEAD // blk // 2
    part = pairs * HEAD
    half = rows // 2
    shard = w_qkv.shape[0]
    units = w_down.shape[0]
    x = hidden_in.reshape(rows, width).astype(F32)
    cot_low = cotangent.reshape(rows, width)

    qkv_cut = (3, blk, pairs, HEAD)
    up_cut = (1, blk, lanes, units)

    pieces = [[p for p in range(dp) if (p * shard // HEAD) % 2 == to_y] for to_y in range(2)]
    route = [(pieces[to_y][lane], lane * 2 + to_y) for to_y in range(2) for lane in range(lanes)]

    near = [(core, far) for core in range(2) for far in range(2)]
    holders = jnp.stack(
        [jnp.take(block_order, b ^ (far * 2 + core), axis=1) for core, far in near], axis=1
    )
    found = holders[:, None, :] == jnp.arange(4, dtype=jnp.int32)[None, :, None]
    tables = jnp.array(
        [[[core * 8 + t[s][far] for core, far in near] for t in (TOPS, BOTTOMS)] for s in range(2)],
        jnp.int32,
    )
    places = jnp.sum(jnp.where(found[None, :, None], tables[:, None, :, None], 0), axis=-1)
    places = places.reshape(2, 2, 8)

    out_full = gather_z(lax.ppermute(w_out, "dp", route), 0)
    normed, first_pull = jax.vjp(layer_norm, x, norm_gains[0], norm_biases[0])
    lengths = jnp.concatenate([seq_lengths, flip_y(seq_lengths)], axis=0)
    qkv_pair = split_columns(w_qkv, *qkv_cut)
    qkv_other = flip_y(after(qkv_pair[0], lengths))
    steps = gather_first(normed.astype(BF16))
    qkv_part = exchange(after(qkv_pair[1], steps), qkv_other).reshape(blk, 2 * shard, 3 * part)
    qkv_full = gather_z(after(qkv_part, out_full), 1).reshape(width, 3 * part)
    down_full = gather_z(after(w_down, qkv_part), 0)
    steps = gather_second(*after(steps, qkv_part))
    cot_low = after(cot_low, qkv_part)
    cot_steps = gather_second(*gather_first(cot_low))
    normed_all = gather_third(*steps)
    up_pair = split_columns(after(w_up, qkv_part), *up_cut)
    up_other = flip_y(after(up_pair[0], cot_steps[1]))
    up_part = exchange(up_pair[1], up_other).reshape(blk, 2 * shard, lanes * units)
    up_full = gather_z(after(up_part, qkv_full), 1).reshape(width, lanes * units)

    def split_sum(total):
        parts = total.reshape(blk, 2, shard, -1)
        other = flip_y(lax.dynamic_index_in_dim(parts, 1 - y, 1, keepdims=False))
        return lax.dynamic_index_in_dim(parts, y, 1, keepdims=False), other

    def times(left, right):
        return lambda first, last, *others: jnp.dot(
            after(left, *others)[first * half : last * half], right, preferred_element_type=F32
        )

    def times_transposed(left, right):
        return lambda first, last, *others: contract_last(
            after(left, *others)[first * half : last * half], right
        )

    projected = jnp.dot(
        after(normed_all, up_other), qkv_full, preferred_element_type=F32
    ).astype(BF16)
    attended_low, log_total = attention_call(
        attention_forward_kernel,
        [projected],
        [(part, BF16), (part, F32)],
        [BF16] * 3,
        places,
        lengths,
        2,
    )
    attended_low = after(attended_low, up_part)
    held = scatter_core(times(attended_low, out_full))
    got = scatter_first(held)
    cot_all = gather_third(*after(cot_steps, held))
    mixed = x + scatter_third(held, *got, *scatter_second(held, *got))
    second, second_pull = jax.vjp(layer_norm, mixed, norm_gains[1], norm_biases[1])
    second_low = second.astype(BF16)
    steps = gather_first(second_low)
    grad_activated = contract_last(after(cot_all, second_low), down_full)
    steps = gather_second(*after(steps, grad_activated))
    second_all = gather_third(*steps)
    bias_part = lax.dynamic_slice_in_dim(
        hidden_bias.reshape(blk, lanes, 2, units), b, 1, 0
    )
    bias_part = lax.dynamic_index_in_dim(bias_part, y, 2, keepdims=False).reshape(-1)
    hidden_pre = jnp.dot(second_all, up_full, preferred_element_type=F32) + bias_part
    activated, slope = gelu(hidden_pre)
    activated_low = activated.astype(BF16)
    grad_hidden_low = (grad_activated * slope).astype(BF16)

    held = scatter_core(times_transposed(grad_hidden_low, up_full))
    got = scatter_first(held)
    down_term = contract_first(after(activated_low, held), cot_all).astype(BF16)
    down_sum = scatter_z(down_term, 0)
    hidden_sum = jnp.sum(after(grad_hidden_low, down_term).astype(F32), axis=0)
    last = scatter_second(held, *after(got, hidden_sum))
    product = times(after(activated_low, last), down_full)
    result_high = product(12, 16).astype(BF16), product(8, 12).astype(BF16)
    grad_second = scatter_third(held, *got, *last)
    grad_mixed_norm, gain_two, bias_two = second_pull(grad_second)
    grad_mixed = cot_low.astype(F32) + grad_mixed_norm
    mixed_low = grad_mixed.astype(BF16)
    steps = gather_first(mixed_low)
    up_term = contract_first(second_all, after(grad_hidden_low, mixed_low)).astype(BF16)
    up_sum = scatter_z(up_term.reshape(blk, -1, lanes * units), 1)
    steps = gather_second(*after(steps, up_term))
    product = times(after(activated_low, up_term), down_full)
    result_low = product(0, 8).astype(BF16)
    mixed_all = gather_third(*after(steps, result_low))
    result_held = scatter_pair(
        lambda first, last, *others: result_low[first * half : last * half],
        *[flip_core(piece) for piece in result_high],
    )
    grad_attended = contract_last(mixed_all, out_full).astype(BF16)
    result_got = scatter_first(result_held, mixed_all)
    (grad_projected,) = attention_call(
        attention_backward_kernel,
        [projected, grad_attended, log_total],
        [(3 * part, BF16)],
        [BF16] * 4 + [F32] * 3,
        places,
        lengths,
        5,
    )
    result_last = scatter_second(result_held, *after(result_got, grad_projected))
    qkv_term = contract_first(
        normed_all, after(grad_projected, up_sum, down_sum, *result_last)
    ).astype(BF16)
    qkv_sum = scatter_z(qkv_term.reshape(blk, -1, 3 * part), 1)
    result = mixed + scatter_third(result_held, *after(result_got, qkv_term), *result_last)
    up_pair = split_sum(after(up_sum, *result_last))
    held = scatter_core(times_transposed(after(grad_projected, qkv_term, result), qkv_full))
    got = scatter_first(held, up_pair)
    out_term = contract_first(after(attended_low, held), mixed_all).astype(BF16)
    grad_normed = scatter_third(held, *got, *scatter_second(held, *got))
    grad_input_norm, gain_one, bias_one = first_pull(grad_normed)
    qkv_pair = split_sum(qkv_sum)
    grad_input = (grad_mixed + grad_input_norm).astype(BF16)

    qkv_got = exchange(*qkv_pair)
    up_got = exchange(up_pair[0], after(up_pair[1], gain_one))
    grad_up = merge_columns(up_got, *up_cut)
    grad_qkv = merge_columns(qkv_got, *qkv_cut)
    norms, hidden_sum = sum_small(
        after(jnp.stack([gain_one, gain_two, bias_one, bias_two]), qkv_got), hidden_sum
    )
    out_sum = after(scatter_z(out_term, 0), norms)
    grad_out = lax.ppermute(out_sum, "dp", [(j, i) for i, j in route]).astype(F32)
    return (
        result.astype(BF16).reshape(1, 1, rows, width),
        grad_input.reshape(1, 1, rows, width),
        grad_qkv,
        grad_out,
        grad_up,
        down_sum.astype(F32),
        norms[:2],
        norms[2:],
        hidden_sum,
    )


def solution(mesh):
    return jax.shard_map(
        body,
        mesh=mesh,
        in_specs=(
            P("dp", "blk", None, None),
            P("dp", "blk", None, None),
            P("dp", None),
            P(),
            P(("blk", "dp"), None),
            P(("blk", "dp"), None),
            P(("blk", "dp"), None),
            P(("blk", "dp"), None),
            P(),
            P(),
            P(),
        ),
        out_specs=(
            P("dp", "blk", None, None),
            P("dp", "blk", None, None),
            P(("blk", "dp"), None),
            P(("blk", "dp"), None),
            P(("blk", "dp"), None),
            P(("blk", "dp"), None),
            P(None, ("blk", "dp")),
            P(None, ("blk", "dp")),
            P(("blk", "dp")),
        ),
        check_vma=False,
    )
```

time: 815 us -> 725 us (0.89)
  waiting for transfers between devices: 336 us -> 252 us
  local copies, waits for them, and re-layouts: 97.6 us -> 30.9 us
  Pallas kernels: 27.5 us -> 75.4 us
  starting transfers between devices: 72.3 us -> 91.7 us
  blocking collectives: 17.6 us -> 0 us
  other arithmetic: 60.1 us -> 70.1 us
    ppermute x70 -> x65, waiting for transfers between devices: 309 us -> 228 us  [flip(): return lax.ppermute(block, axis, [(i ^ bits, i) for i in range(count)])]
    pallas_call x0 -> x16, Pallas kernels: none -> 45.9 us  [the longest x8 36.3 us: assemble(): pl.pallas_call(kernel, in_specs=[pl.BlockSpec(memory_space=pl.ANY)] * len...]
    unnamed x136 -> x183, local copies, waits for them, and re-layouts: 45.8 us -> 17.4 us
    reshape x13 -> x5, local copies, waits for them, and re-layouts: 18.5 us -> 0.27 us  [the longest x1 0.08 us: body(): places = places.reshape(2, 2, 8)]
    all_to_all x1 -> x0, blocking collectives: 17.6 us -> none  [exchange(): return lax.all_to_all(both, 'blk', 0, 0)]
    another operation x10 -> x2, other arithmetic: 14.5 us -> 0.67 us  [the longest x1 0.65 us: body(): jnp.stack([gain_one, gain_two, bias_one, bias_two])]
    add x7 -> x9, other arithmetic: 3.81 us -> 15.5 us  [the longest x4 6.62 us: scatter_third(): top = from_x[half:].astype(F32) + flip_y(to_y).astype(F32)]
    all_gather x4, waiting for transfers between devices: 12.7 us -> 2.36 us  [gather_z(): lax.all_gather(part, 'dp', axis_index_groups=lines(), axis=axis, tiled=True)]
  transfers between devices with their start and end apart: 83 -> 81, of which waited for: 36 -> 38; matrix products, arithmetic and copies ran while one was open for 30% -> 31% of each run, Pallas kernels for 2% -> 11%
where the time goes in v4:
time: 725 us; the launch traced here: 715 us
  waiting for transfers between devices  252 us (35%)
  matrix products  179 us (25%)
  starting transfers between devices  91.7 us (13%)
  Pallas kernels  75.4 us (10%)
  other arithmetic  70.1 us (10%)
  local copies, waits for them, and re-layouts  30.9 us (4%)
  between operations  15.9 us (2%)
    ppermute x65, waiting for transfers between devices, flip(): return lax.ppermute(block, axis, [(i ^ bits, i) for i in range(count)])  228 us
    ppermute x65, starting transfers between devices, flip(): return lax.ppermute(block, axis, [(i ^ bits, i) for i in range(count)])  66.4 us
    dot_general x12, matrix products, contract_last(): lax.dot_general(left, right, (((1,), (1,)), ((), ())), preferred_element_...  65.6 us
    dot_general x4, matrix products, contract_first(): lax.dot_general(left, right, (((0,), (0,)), ((), ())), preferred_element_...  44.6 us
    pallas_call x8, Pallas kernels, assemble(): pl.pallas_call(kernel, in_specs=[pl.BlockSpec(memory_space=pl.ANY)] * len...  36.3 us
    pallas_call x2, Pallas kernels, attention_call(): pl.pallas_call(kernel, grid_spec=pltpu.PrefetchScalarGridSpec(num_scalar_...  29.5 us
    dot_general x8, matrix products, times(): jnp.dot(after(left, *others)[first * half:last * half], right, preferred_...  28.7 us
    dot_general x1, matrix products, body(): jnp.dot(second_all, up_full, preferred_element_type=F32) + bias_part  26.8 us
  transfers between devices with their start and end apart: 81, of which 38 were waited for; matrix products, arithmetic and copies ran while one was open for 31% of the time, Pallas kernels for 11%

profile of v4, /device:TPU:0, one launch (start us, length us, event | category | flops | bytes accessed | tf_op | source)
XLA Modules:
  0.0 715.2 jit_solution(4022900174166957913)
XLA Ops:
  19.6 11.5 %collective-permute-start = (s32[1,2]{1,0:T(1,128)S(1)}, s32[1,2]{1,0:T(1,128)S(1)}, u32[]{:S(2)}, u32[]{:S(2)}) collective-permute-start(s32[1,2]{1,0:T(1,128)S(1)} %copy-done.71), channel_id=1, source_target_pairs={{1,0},{0,1},{3,2},{2,3},{5,4},{4,5},{7,6},{6,7},{9,8},{8,9},{11,10... | collective-permute-start | bytes 32 | tf_op jit(solution)/shard_map/ppermute | solution.py:54
  31.5 20.1 %collective-permute-done = s32[1,2]{1,0:T(1,128)S(1)} collective-permute-done((s32[1,2]{1,0:T(1,128)S(1)}, s32[1,2]{1,0:T(1,128)S(1)}, u32[]{:S(2)}, u32[]{:S(2)}) %collective-permute-start) | collective-permute-done | bytes 40 | tf_op jit(solution)/shard_map/ppermute | solution.py:54
  54.2 7.9 %collective-permute-done.4.other_ref = bf16[4,64,768]{2,1,0:T(8,128)(2,1)S(1)} collective-permute-done((bf16[4,64,768]{2,1,0:T(8,128)(2,1)S(1)}, bf16[4,64,768]{2,1,0:T(8,128)(2,1)S(1)}, u32[]{:S(2)}, u32[]{:S(2)}) %collective-permute-start.4) | collective-permute-done | bytes 393248 | tf_op jit(solution)/shard_map/ppermute | solution.py:54
  67.1 11.5 %all-to-all-done = bf16[4,2,64,768]{3,2,1,0:T(8,128)(2,1)S(1)} async-done(((bf16[4,2,64,768]{3,2,1,0:T(8,128)(2,1)}), bf16[4,2,64,768]{3,2,1,0:T(8,128)(2,1)S(1)}, u32[]{:S(2)}, u32[]{:S(2)}) %all-to-all-start) | async-done | bytes 786464 | tf_op jit(solution)/shard_map/all_to_all | solution.py:163
  85.8 24.2 %collective-permute-done.11.refs_1_ = bf16[320,2048]{1,0:T(8,128)(2,1)S(1)} collective-permute-done((bf16[320,2048]{1,0:T(8,128)(2,1)S(1)}, bf16[320,2048]{1,0:T(8,128)(2,1)S(1)}, u32[]{:S(2)}, u32[]{:S(2)}) %collective-permute-start.11) | collective-permute-done | bytes 1310752 | tf_op jit(solution)/shard_map/ppermute | solution.py:54
  117.6 6.4 shard_map.189.refs_4_
  129.1 9.4 %collective-permute-done.12.refs_0_ = bf16[160,2048]{1,0:T(8,128)(2,1)S(1)} collective-permute-done((bf16[160,2048]{1,0:T(8,128)(2,1)}, bf16[160,2048]{1,0:T(8,128)(2,1)S(1)}, u32[]{:S(2)}, u32[]{:S(2)}) %collective-permute-start.12) | collective-permute-done | bytes 655392 | tf_op jit(solution)/shard_map/ppermute | solution.py:54
  146.3 6.7 collective-permute-done.15.other_ref
  158.2 13.2 %convolution_convert_fusion.1 = bf16[2560,768]{1,0:T(8,128)(2,1)} fusion(bf16[2560,2048]{1,0:T(8,128)(2,1)} %shard_map.190, bf16[2048,768]{1,0:T(8,128)(2,1)} %bitcast.180), kind=kOutput, calls=%fused_computation.6 | convolution fusion | flops 8055029760 | bytes 17563648 | tf_op jit(solution)/shard_map/dot_general | solution.py:509
  171.4 10.8 %shard_map.192 = (bf16[16,160,256]{2,1,0:T(8,128)(2,1)S(1)}, f32[16,160,256]{2,1,0:T(8,128)S(1)}) custom-call(s32[2,2,8]{2,1,0:T(2,128)S(1)} %reshape.203.places_ref, s32[2,2]{1,0:T(2,128)S(1)} %pad_add_fusion.1.lengths_ref, bf16[16,160,768]{2,1,0:T(8,128)(2,1)} %bitcast.186), custom_call_target="tpu_custom_call" | custom-call | flops 2147483648 | bytes 5242880 | tf_op jit(solution)/shard_map/pallas_call | solution.py:412
  201.7 6.4 shard_map.194.refs_4_
  208.8 13.8 %collective-permute-done.19 = bf16[320,2048]{1,0:T(8,128)(2,1)} collective-permute-done((bf16[320,2048]{1,0:T(8,128)(2,1)}, bf16[320,2048]{1,0:T(8,128)(2,1)}, u32[]{:S(2)}, u32[]{:S(2)}) %collective-permute-start.19) | collective-permute-done | bytes 1310752 | tf_op jit(solution)/shard_map/ppermute | solution.py:54
  236.1 9.7 %collective-permute-done.22 = bf16[160,2048]{1,0:T(8,128)(2,1)} collective-permute-done((bf16[160,2048]{1,0:T(8,128)(2,1)}, bf16[160,2048]{1,0:T(8,128)(2,1)}, u32[]{:S(2)}, u32[]{:S(2)}) %collective-permute-start.22) | collective-permute-done | bytes 655392 | tf_op jit(solution)/shard_map/ppermute | solution.py:54
  256.4 17.0 %fusion.87 = f32[2560,1024]{1,0:T(8,128)} fusion(bf16[2560,2048]{1,0:T(8,128)(2,1)} %shard_map.195, bf16[1024,2048]{1,0:T(8,128)(2,1)} %all-gather.9.cloned.1.call-done), kind=kOutput, calls=%fused_computation.166 | convolution fusion | flops 10737418240 | bytes 25165824 | tf_op jit(solution)/shard_map/dot_general | solution.py:41
  273.4 9.2 %collective-permute-done.23.refs_1_ = bf16[320,2048]{1,0:T(8,128)(2,1)} collective-permute-done((bf16[320,2048]{1,0:T(8,128)(2,1)}, bf16[320,2048]{1,0:T(8,128)(2,1)}, u32[]{:S(2)}, u32[]{:S(2)}) %collective-permute-start.23) | collective-permute-done | bytes 1310752 | tf_op jit(solution)/shard_map/ppermute | solution.py:54
  313.3 26.8 %multiply_convert_fusion = (bf16[2560,1024]{1,0:T(8,128)(2,1)S(1)}, bf16[2560,1024]{1,0:T(8,128)(2,1)}) fusion(f32[2560,1024]{1,0:T(8,128)} %fusion.87, f32[1024]{0:T(1024)S(1)} %bitcast.169, bf16[2560,2048]{1,0:T(8,128)(2,1)} %shard_map.197, bf16[2048,1024]{1,0:T(8,128)(2,1)} %bitcast.174), kind=kOutput, calls=%fused_computation.1 | convolution fusion | flops 10792468480 | bytes 35655680 | tf_op jit(solution)/shard_map/dot_general | solution.py:536
  361.4 13.5 %convolution_convert_fusion.3 = bf16[1024,2048]{1,0:T(8,128)(2,1)} fusion(bf16[2560,1024]{1,0:T(8,128)(2,1)S(1)} %bitcast.195, bf16[2560,2048]{1,0:T(8,128)(2,1)S(1)} %bitcast.136), kind=kOutput, calls=%fused_computation.10 | convolution fusion | flops 10739515392 | bytes 19922944 | tf_op jit(solution)/shard_map/dot_general | solution.py:47
  390.5 13.6 %collective-permute-done.42 = bf16[160,2048]{1,0:T(8,128)(2,1)S(1)} collective-permute-done((bf16[160,2048]{1,0:T(8,128)(2,1)S(1)}, bf16[160,2048]{1,0:T(8,128)(2,1)S(1)}, u32[]{:S(2)}, u32[]{:S(2)}) %collective-permute-start.42) | collective-permute-done | bytes 655392 | tf_op jit(solution)/shard_map/ppermute | solution.py:54
  414.6 13.4 %convolution_convert_fusion.4 = bf16[2048,1024]{1,0:T(8,128)(2,1)} fusion(bf16[2560,2048]{1,0:T(8,128)(2,1)S(1)} %bitcast.138, bf16[2560,1024]{1,0:T(8,128)(2,1)S(1)} %bitcast.146), kind=kOutput, calls=%fused_computation.11 | convolution fusion | flops 10739515392 | bytes 19922944 | tf_op jit(solution)/shard_map/dot_general | solution.py:47
  430.0 7.0 convolution_convert_fusion.10
  437.5 19.4 %collective-permute-done.45.refs_1_ = bf16[320,2048]{1,0:T(8,128)(2,1)S(1)} collective-permute-done((bf16[320,2048]{1,0:T(8,128)(2,1)}, bf16[320,2048]{1,0:T(8,128)(2,1)S(1)}, u32[]{:S(2)}, u32[]{:S(2)}) %collective-permute-start.45) | collective-permute-done | bytes 1310752 | tf_op jit(solution)/shard_map/ppermute | solution.py:54
  459.1 6.5 convolution_convert_fusion.11
  465.7 8.9 %collective-permute-done.48.refs_0_ = bf16[160,2048]{1,0:T(8,128)(2,1)S(1)} collective-permute-done((bf16[160,2048]{1,0:T(8,128)(2,1)S(1)}, bf16[160,2048]{1,0:T(8,128)(2,1)S(1)}, u32[]{:S(2)}, u32[]{:S(2)}) %collective-permute-start.48) | collective-permute-done | bytes 655392 | tf_op jit(solution)/shard_map/ppermute | solution.py:54
  475.9 7.2 %convolution_convert_fusion = bf16[1280,2048]{1,0:T(8,128)(2,1)} fusion(bf16[1024,2048]{1,0:T(8,128)(2,1)S(1)} %copy-done.72, bf16[2560,1024]{1,0:T(8,128)(2,1)S(1)} %bitcast.197), kind=kOutput, calls=%fused_computation.5 | convolution fusion | flops 5371330560 | bytes 12058624 | tf_op jit(solution)/shard_map/dot_general | solution.py:500
  483.2 7.8 %collective-permute-done.49.refs_1_ = bf16[160,2048]{1,0:T(8,128)(2,1)S(1)} collective-permute-done((bf16[160,2048]{1,0:T(8,128)(2,1)S(1)}, bf16[160,2048]{1,0:T(8,128)(2,1)S(1)}, u32[]{:S(2)}, u32[]{:S(2)}) %collective-permute-start.49) | collective-permute-done | bytes 655392 | tf_op jit(solution)/shard_map/ppermute | solution.py:54
  511.6 6.9 convolution_convert_fusion.2
  518.5 18.7 %shard_map.200 = bf16[16,160,768]{2,1,0:T(8,128)(2,1)} custom-call(s32[2,2,8]{2,1,0:T(2,128)S(1)} %reshape.203.places_ref, s32[2,2]{1,0:T(2,128)S(1)} %pad_add_fusion.1.lengths_ref, bf16[16,160,768]{2,1,0:T(8,128)(2,1)} %bitcast.187, bf16[16,160,256]{2,1,0:T(8,128)(2,1)S(1)} %bitcast.132, f32[16,160,256]{2,1,0:T(8,128)S(1)} %copy-done.5), custom_call_target="tpu_custom_call" | custom-call | flops 5368709120 | bytes 5242880 | tf_op jit(solution)/shard_map/pallas_call | solution.py:412
  546.7 13.8 %convolution_convert_fusion.5 = bf16[2048,768]{1,0:T(8,128)(2,1)} fusion(bf16[2560,2048]{1,0:T(8,128)(2,1)} %shard_map.190, bf16[2560,768]{1,0:T(8,128)(2,1)} %bitcast.188), kind=kOutput, calls=%fused_computation.12 | convolution fusion | flops 8054636544 | bytes 17563648 | tf_op jit(solution)/shard_map/dot_general | solution.py:47
  580.4 7.1 collective-permute-done.60.other_ref
  614.0 21.1 %collective-permute-done.61 = bf16[320,2048]{1,0:T(8,128)(2,1)S(1)} collective-permute-done((bf16[320,2048]{1,0:T(8,128)(2,1)}, bf16[320,2048]{1,0:T(8,128)(2,1)S(1)}, u32[]{:S(2)}, u32[]{:S(2)}) %collective-permute-start.61) | collective-permute-done | bytes 1310752 | tf_op jit(solution)/shard_map/ppermute | solution.py:54
  643.9 11.1 %collective-permute-done.64 = bf16[160,2048]{1,0:T(8,128)(2,1)S(1)} collective-permute-done((bf16[160,2048]{1,0:T(8,128)(2,1)}, bf16[160,2048]{1,0:T(8,128)(2,1)S(1)}, u32[]{:S(2)}, u32[]{:S(2)}) %collective-permute-start.64) | collective-permute-done | bytes 655392 | tf_op jit(solution)/shard_map/ppermute | solution.py:54
  678.9 7.9 %all-to-all-done.2.in_ref = bf16[4,2,64,768]{3,2,1,0:T(8,128)(2,1)S(1)} async-done(((bf16[4,2,64,768]{3,2,1,0:T(8,128)(2,1)}), bf16[4,2,64,768]{3,2,1,0:T(8,128)(2,1)S(1)}, u32[]{:S(2)}, u32[]{:S(2)}) %all-to-all-start.2) | async-done | bytes 786464 | tf_op jit(solution)/shard_map/all_to_all | solution.py:163
  (446 shorter events, 310.7 us)
Async XLA Ops:
  7.2 59.9 %all-gather.5.cloned.1.call-start = ((), (), s32[]{:S(2)}) async-start(), calls=%async_computation.10 | async-start | bytes 1310720 | tf_op jit(solution)/shard_map/all_gather | solution.py:75
  13.6 40.6 %collective-permute-start.1 = (bf16[320,2048]{1,0:T(8,128)(2,1)S(1)}, bf16[320,2048]{1,0:T(8,128)(2,1)}, u32[]{:S(2)}, u32[]{:S(2)}) collective-permute-start(bf16[320,2048]{1,0:T(8,128)(2,1)S(1)} %fusion.11.refs_0_), channel_id=1, source_target_pairs={{16,0},{24,8},{0,16},{8,24},{17,1},{25,9},{1,17},{9,25},{18,2},{26... | collective-permute-start | bytes 3932168 | tf_op jit(solution)/shard_map/ppermute | solution.py:54
  16.6 37.6 %collective-permute-start.2 = (bf16[320,2048]{1,0:T(8,128)(2,1)S(1)}, bf16[320,2048]{1,0:T(8,128)(2,1)}, u32[]{:S(2)}, u32[]{:S(2)}) collective-permute-start(bf16[320,2048]{1,0:T(8,128)(2,1)S(1)} %fusion.11.refs_0_), channel_id=1, source_target_pairs={{1,0},{0,1},{3,2},{2,3},{5,4},{4,5},{7,6},{6,7},{9,8},{8,9},{11,10... | collective-permute-start | bytes 3932168 | tf_op jit(solution)/shard_map/ppermute | solution.py:54
  18.1 36.0 %collective-permute-start.3 = (bf16[320,2048]{1,0:T(8,128)(2,1)S(1)}, bf16[320,2048]{1,0:T(8,128)(2,1)}, u32[]{:S(2)}, u32[]{:S(2)}) collective-permute-start(bf16[320,2048]{1,0:T(8,128)(2,1)S(1)} %fusion.11.refs_0_), channel_id=1, source_target_pairs={{8,0},{0,8},{24,16},{16,24},{9,1},{1,9},{25,17},{17,25},{10,2},{2,... | collective-permute-start | bytes 3932168 | tf_op jit(solution)/shard_map/ppermute | solution.py:54
  19.6 32.0 %collective-permute-start = (s32[1,2]{1,0:T(1,128)S(1)}, s32[1,2]{1,0:T(1,128)S(1)}, u32[]{:S(2)}, u32[]{:S(2)}) collective-permute-start(s32[1,2]{1,0:T(1,128)S(1)} %copy-done.71), channel_id=1, source_target_pairs={{1,0},{0,1},{3,2},{2,3},{5,4},{4,5},{7,6},{6,7},{9,8},{8,9},{11,10... | collective-permute-start | bytes 32 | tf_op jit(solution)/shard_map/ppermute | solution.py:54
  67.0 91.1 %all-gather.7.cloned.1.call-start = ((), (), s32[]{:S(2)}) async-start(), calls=%async_computation.11 | async-start | bytes 3932160 | tf_op jit(solution)/shard_map/all_gather | solution.py:75
  79.6 176.8 %all-gather.9.cloned.1.call-start = ((), (), s32[]{:S(2)}) async-start(), calls=%async_computation.12 | async-start | bytes 5242880 | tf_op jit(solution)/shard_map/all_gather | solution.py:75
  79.7 30.4 %collective-permute-start.11 = (bf16[320,2048]{1,0:T(8,128)(2,1)S(1)}, bf16[320,2048]{1,0:T(8,128)(2,1)S(1)}, u32[]{:S(2)}, u32[]{:S(2)}) collective-permute-start(bf16[320,2048]{1,0:T(8,128)(2,1)S(1)} %bitcast.140), channel_id=1, source_target_pairs={{16,0},{24,8},{0,16},{8,24},{17,1},{25,9},{1,17},{9,25},{18,2},{26... | collective-permute-start | bytes 3932168 | tf_op jit(solution)/shard_map/ppermute | solution.py:54
  80.1 31.7 %collective-permute-start.13 = (bf16[320,2048]{1,0:T(8,128)(2,1)S(1)}, bf16[320,2048]{1,0:T(8,128)(2,1)S(1)}, u32[]{:S(2)}, u32[]{:S(2)}) collective-permute-start(bf16[320,2048]{1,0:T(8,128)(2,1)S(1)} %bitcast.141), channel_id=1, source_target_pairs={{1,0},{0,1},{3,2},{2,3},{5,4},{4,5},{7,6},{6,7},{9,8},{8,9},{11,10... | collective-permute-start | bytes 3932168 | tf_op jit(solution)/shard_map/ppermute | solution.py:54
  81.8 32.6 %collective-permute-start.7 = (bf16[320,2048]{1,0:T(8,128)(2,1)}, bf16[320,2048]{1,0:T(8,128)(2,1)S(1)}, u32[]{:S(2)}, u32[]{:S(2)}) collective-permute-start(bf16[320,2048]{1,0:T(8,128)(2,1)} %collective-permute-done.1.refs_1_), channel_id=1, source_target_pairs={{8,0},{0,8},{24,16},{16,24},{9,1},{1,9},{25,17},{17,25},{10,2},{2,... | collective-permute-start | bytes 3932168 | tf_op jit(solution)/shard_map/ppermute | solution.py:54
  81.8 34.7 %collective-permute-start.8 = (bf16[320,2048]{1,0:T(8,128)(2,1)}, bf16[320,2048]{1,0:T(8,128)(2,1)S(1)}, u32[]{:S(2)}, u32[]{:S(2)}) collective-permute-start(bf16[320,2048]{1,0:T(8,128)(2,1)} %collective-permute-done.2.refs_2_), channel_id=1, source_target_pairs={{8,0},{0,8},{24,16},{16,24},{9,1},{1,9},{25,17},{17,25},{10,2},{2,... | collective-permute-start | bytes 3932168 | tf_op jit(solution)/shard_map/ppermute | solution.py:54
  85.5 40.4 %collective-permute-start.5 = (bf16[160,2048]{1,0:T(8,128)(2,1)}, bf16[160,2048]{1,0:T(8,128)(2,1)S(1)}, u32[]{:S(2)}, u32[]{:S(2)}) collective-permute-start(bf16[160,2048]{1,0:T(8,128)(2,1)} %slice.294), channel_id=1, source_target_pairs={{1,0},{0,1},{3,2},{2,3},{5,4},{4,5},{7,6},{6,7},{9,8},{8,9},{11,10... | collective-permute-start | bytes 1966088 | tf_op jit(solution)/shard_map/ppermute | solution.py:54
  154.6 29.1 %all-to-all-start.1 = ((bf16[4,2,64,1024]{3,2,1,0:T(8,128)(2,1)}), bf16[4,2,64,1024]{3,2,1,0:T(8,128)(2,1)S(1)}, u32[]{:S(2)}, u32[]{:S(2)}) async-start(bf16[4,2,64,1024]{3,2,1,0:T(8,128)(2,1)} %shard_map.193), calls=%async_computation.1 | async-start | bytes 2097152 | tf_op jit(solution)/shard_map/all_to_all | solution.py:163
  158.1 155.2 %all-gather.11.cloned.1.call-start = ((), (), s32[]{:S(2)}) async-start(), calls=%async_computation.13 | async-start | bytes 5242880 | tf_op jit(solution)/shard_map/all_gather | solution.py:75
  191.2 31.4 %collective-permute-start.19 = (bf16[320,2048]{1,0:T(8,128)(2,1)}, bf16[320,2048]{1,0:T(8,128)(2,1)}, u32[]{:S(2)}, u32[]{:S(2)}) collective-permute-start(bf16[320,2048]{1,0:T(8,128)(2,1)} %fusion.8), channel_id=1, source_target_pairs={{16,0},{24,8},{0,16},{8,24},{17,1},{25,9},{1,17},{9,25},{18,2},{26... | collective-permute-start | bytes 3932168 | tf_op jit(solution)/shard_map/ppermute | solution.py:54
  194.6 30.8 %collective-permute-start.21 = (bf16[320,2048]{1,0:T(8,128)(2,1)}, bf16[320,2048]{1,0:T(8,128)(2,1)S(1)}, u32[]{:S(2)}, u32[]{:S(2)}) collective-permute-start(bf16[320,2048]{1,0:T(8,128)(2,1)} %fusion.9), channel_id=1, source_target_pairs={{1,0},{0,1},{3,2},{2,3},{5,4},{4,5},{7,6},{6,7},{9,8},{8,9},{11,10... | collective-permute-start | bytes 3932168 | tf_op jit(solution)/shard_map/ppermute | solution.py:54
  232.5 314.1 %reduce-scatter.7.cloned.1.call-start = ((), (), s32[]{:S(2)}) async-start(), calls=%async_computation.15 | async-start | bytes 5242880 | tf_op jit(solution)/shard_map/reduce_scatter | solution.py:79
  254.7 29.2 %collective-permute-start.24 = (bf16[320,2048]{1,0:T(8,128)(2,1)}, bf16[320,2048]{1,0:T(8,128)(2,1)}, u32[]{:S(2)}, u32[]{:S(2)}) collective-permute-start(bf16[320,2048]{1,0:T(8,128)(2,1)} %add_convert_fusion.7.refs_0_), channel_id=1, source_target_pairs={{1,0},{0,1},{3,2},{2,3},{5,4},{4,5},{7,6},{6,7},{9,8},{8,9},{11,10... | collective-permute-start | bytes 3932168 | tf_op jit(solution)/shard_map/ppermute | solution.py:54
  353.7 31.1 %collective-permute-start.39 = (bf16[320,2048]{1,0:T(8,128)(2,1)}, bf16[320,2048]{1,0:T(8,128)(2,1)}, u32[]{:S(2)}, u32[]{:S(2)}) collective-permute-start(bf16[320,2048]{1,0:T(8,128)(2,1)} %add_convert_fusion.6), channel_id=1, source_target_pairs={{16,0},{24,8},{0,16},{8,24},{17,1},{25,9},{1,17},{9,25},{18,2},{26... | collective-permute-start | bytes 3932168 | tf_op jit(solution)/shard_map/ppermute | solution.py:54
  355.2 30.9 %collective-permute-start.40 = (bf16[320,2048]{1,0:T(8,128)(2,1)}, bf16[320,2048]{1,0:T(8,128)(2,1)}, u32[]{:S(2)}, u32[]{:S(2)}) collective-permute-start(bf16[320,2048]{1,0:T(8,128)(2,1)} %add_convert_fusion.5), channel_id=1, source_target_pairs={{1,0},{0,1},{3,2},{2,3},{5,4},{4,5},{7,6},{6,7},{9,8},{8,9},{11,10... | collective-permute-start | bytes 3932168 | tf_op jit(solution)/shard_map/ppermute | solution.py:54
  374.9 171.8 %reduce-scatter.5.cloned.1.call-start = ((), (), s32[]{:S(2)}) async-start(), calls=%async_computation.14 | async-start | bytes 5242880 | tf_op jit(solution)/shard_map/reduce_scatter | solution.py:79
  428.0 231.0 %reduce-scatter.9.cloned.1.call-start = ((), (), s32[]{:S(2)}) async-start(), calls=%async_computation.16 | async-start | bytes 3932160 | tf_op jit(solution)/shard_map/reduce_scatter | solution.py:79
  437.0 62.1 %collective-permute-start.44 = (bf16[640,2048]{1,0:T(8,128)(2,1)}, bf16[640,2048]{1,0:T(8,128)(2,1)}, u32[]{:S(2)}, u32[]{:S(2)}) collective-permute-start(bf16[640,2048]{1,0:T(8,128)(2,1)} %convolution_convert_fusion.10), channel_id=1, source_target_pairs={{8,0},{0,8},{24,16},{16,24},{9,1},{1,9},{25,17},{17,25},{10,2},{2,... | collective-permute-start | bytes 7864328 | tf_op jit(solution)/shard_map/ppermute | solution.py:54
  457.3 33.6 %collective-permute-start.50 = (bf16[320,2048]{1,0:T(8,128)(2,1)S(1)}, bf16[320,2048]{1,0:T(8,128)(2,1)S(1)}, u32[]{:S(2)}, u32[]{:S(2)}) collective-permute-start(bf16[320,2048]{1,0:T(8,128)(2,1)S(1)} %collective-permute-done.45.refs_1_), channel_id=1, source_target_pairs={{8,0},{0,8},{24,16},{16,24},{9,1},{1,9},{25,17},{17,25},{10,2},{2,... | collective-permute-start | bytes 3932168 | tf_op jit(solution)/shard_map/ppermute | solution.py:54
  458.9 33.1 %collective-permute-start.51 = (bf16[320,2048]{1,0:T(8,128)(2,1)S(1)}, bf16[320,2048]{1,0:T(8,128)(2,1)}, u32[]{:S(2)}, u32[]{:S(2)}) collective-permute-start(bf16[320,2048]{1,0:T(8,128)(2,1)S(1)} %collective-permute-done.46.refs_2_), channel_id=1, source_target_pairs={{8,0},{0,8},{24,16},{16,24},{9,1},{1,9},{25,17},{17,25},{10,2},{2,... | collective-permute-start | bytes 3932168 | tf_op jit(solution)/shard_map/ppermute | solution.py:54
  465.6 75.2 %collective-permute-start.43 = (bf16[640,2048]{1,0:T(8,128)(2,1)}, bf16[640,2048]{1,0:T(8,128)(2,1)}, u32[]{:S(2)}, u32[]{:S(2)}) collective-permute-start(bf16[640,2048]{1,0:T(8,128)(2,1)} %convolution_convert_fusion.11), channel_id=1, source_target_pairs={{8,0},{0,8},{24,16},{16,24},{9,1},{1,9},{25,17},{17,25},{10,2},{2,... | collective-permute-start | bytes 7864328 | tf_op jit(solution)/shard_map/ppermute | solution.py:54
  508.7 31.0 %collective-permute-start.54 = (bf16[320,2048]{1,0:T(8,128)(2,1)}, bf16[320,2048]{1,0:T(8,128)(2,1)S(1)}, u32[]{:S(2)}, u32[]{:S(2)}) collective-permute-start(bf16[320,2048]{1,0:T(8,128)(2,1)} %get-tuple-element.139), channel_id=1, source_target_pairs={{16,0},{24,8},{0,16},{8,24},{17,1},{25,9},{1,17},{9,25},{18,2},{26... | collective-permute-start | bytes 3932168 | tf_op jit(solution)/shard_map/ppermute | solution.py:54
  510.1 30.7 %collective-permute-start.55 = (bf16[320,2048]{1,0:T(8,128)(2,1)}, bf16[320,2048]{1,0:T(8,128)(2,1)S(1)}, u32[]{:S(2)}, u32[]{:S(2)}) collective-permute-start(bf16[320,2048]{1,0:T(8,128)(2,1)} %get-tuple-element.140), channel_id=1, source_target_pairs={{1,0},{0,1},{3,2},{2,3},{5,4},{4,5},{7,6},{6,7},{9,8},{8,9},{11,10... | collective-permute-start | bytes 3932168 | tf_op jit(solution)/shard_map/ppermute | solution.py:54
  580.2 33.8 %collective-permute-start.59 = (bf16[640,2048]{1,0:T(8,128)(2,1)}, bf16[640,2048]{1,0:T(8,128)(2,1)}, u32[]{:S(2)}, u32[]{:S(2)}) collective-permute-start(bf16[640,2048]{1,0:T(8,128)(2,1)} %convolution_convert_fusion.6), channel_id=1, source_target_pairs={{8,0},{0,8},{24,16},{16,24},{9,1},{1,9},{25,17},{17,25},{10,2},{2,... | collective-permute-start | bytes 7864328 | tf_op jit(solution)/shard_map/ppermute | solution.py:54
  592.6 97.5 %reduce-scatter.11.cloned.1.call-start = ((), (), s32[]{:S(2)}) async-start(), calls=%async_computation.17 | async-start | bytes 1310720 | tf_op jit(solution)/shard_map/reduce_scatter | solution.py:79
  597.5 37.6 %collective-permute-start.61 = (bf16[320,2048]{1,0:T(8,128)(2,1)}, bf16[320,2048]{1,0:T(8,128)(2,1)S(1)}, u32[]{:S(2)}, u32[]{:S(2)}) collective-permute-start(bf16[320,2048]{1,0:T(8,128)(2,1)} %add_convert_fusion.2), channel_id=1, source_target_pairs={{16,0},{24,8},{0,16},{8,24},{17,1},{25,9},{1,17},{9,25},{18,2},{26... | collective-permute-start | bytes 3932168 | tf_op jit(solution)/shard_map/ppermute | solution.py:54
  603.2 31.9 %collective-permute-start.63 = (bf16[320,2048]{1,0:T(8,128)(2,1)}, bf16[320,2048]{1,0:T(8,128)(2,1)}, u32[]{:S(2)}, u32[]{:S(2)}) collective-permute-start(bf16[320,2048]{1,0:T(8,128)(2,1)} %add_convert_fusion.1), channel_id=1, source_target_pairs={{1,0},{0,1},{3,2},{2,3},{5,4},{4,5},{7,6},{6,7},{9,8},{8,9},{11,10... | collective-permute-start | bytes 3932168 | tf_op jit(solution)/shard_map/ppermute | solution.py:54
  (140 other events, 1707.6 us)
Sparse Core Ops, SparseCore 0:
  19.7 38.2 all-gather.4
  79.7 63.0 all-gather.6
  144.4 79.4 all-gather.8
  232.6 80.6 all-gather.10
  375.0 73.4 reduce-scatter.6
  450.8 77.2 reduce-scatter.4
  567.1 57.9 reduce-scatter.8
  644.0 25.3 reduce-scatter.10

commit v5 on v4

--- a/solution.py
+++ b/solution.py
@@ -104,9 +104,9 @@
             num_scalar_prefetch=1,
             grid=(2, blk),
             in_specs=[pl.BlockSpec(shard.shape, lambda i, j, *_: (0, 0))],
-            out_specs=pl.BlockSpec((1, 1, rows, count), lambda i, j, *_: (i, j, 0, 0)),
+            out_specs=pl.BlockSpec((1, 1, rows, count), lambda i, j, *_: (j, i, 0, 0)),
         ),
-        out_shape=jax.ShapeDtypeStruct((2, blk, rows, count), shard.dtype),
+        out_shape=jax.ShapeDtypeStruct((blk, 2, rows, count), shard.dtype),
         compiler_params=pltpu.CompilerParams(vmem_limit_bytes=16 * 2**20),
         cost_estimate=pl.CostEstimate(flops=0, bytes_accessed=4 * shard.size, transcendentals=0),
     )((lax.axis_index("dp") % 2).reshape(1), shard)
@@ -167,21 +167,13 @@
 BOTTOMS = ((1, 2), (7, 6))
 
 
-def gather_first(part, y_others=(), x_others=()):
-    return part, flip_x(after(part, x_others)), flip_y(after(part, y_others)), flip_core(after(part, x_others))
-
-
-def gather_second(part, from_x, from_y, from_core):
-    half = part.shape[0] // 2
-    diagonal = [flip_y(from_x[:half]), flip_x(from_y[half:])]
-    return [part, from_x, from_y], diagonal, [from_core, flip_core(from_x), flip_core(from_y)]
-
-
-def gather_third(mine, diagonal, others):
-    most = assemble([*mine, *others], [(0, 0, 2, 0), (1, 0, 1, 5), (1, 1, 1, 2), (2, 0, 1, 3), (2, 1, 1, 7)])
-    diagonal = after(diagonal, most)
-    both = [*diagonal, *[flip_core(piece) for piece in diagonal]]
-    return assemble(both, [(0, 0, 1, 4), (1, 0, 1, 6)], most)
+MOST = ((0, 0, 2, 0), (1, 0, 1, 5), (1, 1, 1, 2), (2, 0, 1, 3), (2, 1, 1, 7))
+REST = ((0, 0, 1, 4), (1, 0, 1, 6))
+
+
+def diagonal_of(from_x, from_y):
+    half = from_x.shape[0] // 2
+    return flip_y(from_x[:half]), flip_x(from_y[half:])
 
 
 def assemble(pieces, runs, whole=None):
@@ -226,47 +218,34 @@
     )(*inputs)
 
 
-def scatter_core(product):
-    far, near = product(12, 16).astype(BF16), product(8, 12).astype(BF16)
-    return scatter_pair(product, flip_core(far), flip_core(near))
-
-
-def scatter_pair(product, far, near):
-    middle = far.shape[0] // 2
-    to_x = (product(4, 6).astype(F32) + far[:middle].astype(F32)).astype(BF16)
-    to_y = (product(6, 8).astype(F32) + far[middle:].astype(F32)).astype(BF16)
-    return (to_x, to_y), (product(0, 4, to_x, to_y), near)
-
-
-def scatter_first(held, *others):
-    to_x, to_y = held[0]
-    return flip_x(after(to_x, *others)), flip_y(after(to_y, *others))
-
-
-def scatter_second(held, from_x, from_y):
-    half = from_x.shape[0] // 2
-    product, got = held[1]
-    to_x = product[2 * half : 3 * half].astype(F32) + got[2 * half : 3 * half].astype(F32)
-    to_y = product[3 * half :].astype(F32) + got[3 * half :].astype(F32)
+def last_sends(near, got, from_x, from_y):
+    half = near.shape[0] // 4
+    to_x = near[2 * half : 3 * half].astype(F32) + got[2 * half : 3 * half].astype(F32)
+    to_y = near[3 * half :].astype(F32) + got[3 * half :].astype(F32)
     to_x = (to_x + from_y[:half].astype(F32)).astype(BF16)
     to_y = (to_y + from_x[:half].astype(F32)).astype(BF16)
     return to_x, to_y
 
 
-def scatter_third(held, from_x, from_y, to_x, to_y):
-    half = from_x.shape[0] // 2
-    product, got = held[1]
-    own = product[: 2 * half].astype(F32) + got[: 2 * half].astype(F32)
-    top = from_x[half:].astype(F32) + flip_y(to_y).astype(F32)
-    bottom = from_y[half:].astype(F32) + flip_x(to_x).astype(F32)
-    return own + jnp.concatenate([top, bottom], axis=0)
-
-
-def sum_small(norms, hidden):
-    blk, dp = lax.axis_size("blk"), lax.axis_size("dp")
-    count = norms.shape[0]
-    parts = norms.reshape(count, blk, -1).transpose(1, 0, 2)
-    parts = jnp.sum(lax.all_to_all(parts, "blk", 0, 0), axis=0)
+def own_rows(near, got, from_x, from_y):
+    half = near.shape[0] // 4
+    own = near[: 2 * half].astype(F32) + got[: 2 * half].astype(F32)
+    return own + jnp.concatenate([from_x[half:], from_y[half:]], axis=0).astype(F32)
+
+
+def add_last(own, last_x, last_y):
+    return own + jnp.concatenate([last_y, last_x], axis=0).astype(F32)
+
+
+def sum_blk(norms):
+    blk = lax.axis_size("blk")
+    parts = norms.reshape(norms.shape[0], blk, -1).transpose(1, 0, 2)
+    return jnp.sum(lax.all_to_all(parts, "blk", 0, 0), axis=0)
+
+
+def sum_dp(parts, hidden):
+    dp = lax.axis_size("dp")
+    count = parts.shape[0]
     parts = parts.reshape(count, dp, -1).transpose(1, 0, 2)
     share = parts.shape[2]
     hidden = jnp.repeat(hidden.reshape(dp // 2, -1), 2, axis=0)
@@ -473,42 +452,62 @@
     places = jnp.sum(jnp.where(found[None, :, None], tables[:, None, :, None], 0), axis=-1)
     places = places.reshape(2, 2, 8)
 
+    gate = [seq_lengths]
+
+    def seal(*values):
+        gate[0], values = lax.optimization_barrier((gate[0], values))
+        return values if len(values) > 1 else values[0]
+
+    def enter(*values):
+        values = lax.optimization_barrier((values, gate[0]))[0]
+        return values if len(values) > 1 else values[0]
+
+    def rows_of(array, first, last):
+        return array[first * half : last * half]
+
+    def times(left, right):
+        return jnp.dot(left, right, preferred_element_type=F32)
+
     out_full = gather_z(lax.ppermute(w_out, "dp", route), 0)
     normed, first_pull = jax.vjp(layer_norm, x, norm_gains[0], norm_biases[0])
-    lengths = jnp.concatenate([seq_lengths, flip_y(seq_lengths)], axis=0)
-    qkv_pair = split_columns(w_qkv, *qkv_cut)
-    qkv_other = flip_y(after(qkv_pair[0], lengths))
-    steps = gather_first(normed.astype(BF16))
-    qkv_part = exchange(after(qkv_pair[1], steps), qkv_other).reshape(blk, 2 * shard, 3 * part)
+    normed_low = normed.astype(BF16)
+    qkv_pair = lax.all_to_all(split_columns(w_qkv, *qkv_cut), "blk", 0, 0)
+    qkv_pair, a_x, a_y, a_core, lengths = seal(
+        qkv_pair,
+        flip_x(normed_low),
+        flip_y(normed_low),
+        flip_core(normed_low),
+        flip_y(after(seq_lengths, normed_low)),
+    )
+    lengths = jnp.concatenate([seq_lengths, lengths], axis=0)
+
+    normed_low, qkv_pair, a_x, a_y, a_core = enter(normed_low, qkv_pair, a_x, a_y, a_core)
+    qkv_part = join_y(qkv_pair[:, 1], flip_y(qkv_pair[:, 0])).reshape(blk, 2 * shard, 3 * part)
     qkv_full = gather_z(after(qkv_part, out_full), 1).reshape(width, 3 * part)
     down_full = gather_z(after(w_down, qkv_part), 0)
-    steps = gather_second(*after(steps, qkv_part))
-    cot_low = after(cot_low, qkv_part)
-    cot_steps = gather_second(*gather_first(cot_low))
-    normed_all = gather_third(*steps)
-    up_pair = split_columns(after(w_up, qkv_part), *up_cut)
-    up_other = flip_y(after(up_pair[0], cot_steps[1]))
-    up_part = exchange(up_pair[1], up_other).reshape(blk, 2 * shard, lanes * units)
-    up_full = gather_z(after(up_part, qkv_full), 1).reshape(width, lanes * units)
-
-    def split_sum(total):
-        parts = total.reshape(blk, 2, shard, -1)
-        other = flip_y(lax.dynamic_index_in_dim(parts, 1 - y, 1, keepdims=False))
-        return lax.dynamic_index_in_dim(parts, y, 1, keepdims=False), other
-
-    def times(left, right):
-        return lambda first, last, *others: jnp.dot(
-            after(left, *others)[first * half : last * half], right, preferred_element_type=F32
-        )
-
-    def times_transposed(left, right):
-        return lambda first, last, *others: contract_last(
-            after(left, *others)[first * half : last * half], right
-        )
-
-    projected = jnp.dot(
-        after(normed_all, up_other), qkv_full, preferred_element_type=F32
-    ).astype(BF16)
+    a_across = diagonal_of(a_x, a_y)
+    a_others = a_core, flip_core(a_x), flip_core(a_y)
+    normed_all = assemble([normed_low, a_x, a_y, *a_others], MOST)
+    a_across, normed_all, up_pair, _ = seal(
+        a_across, normed_all, split_columns(enter(w_up), *up_cut), qkv_part
+    )
+
+    cot_low, normed_all, a_across = enter(cot_low, normed_all, a_across)
+    cot_x, cot_y, cot_core = flip_x(cot_low), flip_y(cot_low), flip_core(cot_low)
+    normed_all = assemble([*a_across, *[flip_core(piece) for piece in a_across]], REST, normed_all)
+    cot_x, cot_y, cot_core, normed_all = seal(cot_x, cot_y, cot_core, normed_all)
+
+    cot_x, cot_y, cot_core = enter(cot_x, cot_y, cot_core)
+    cot_across = diagonal_of(cot_x, cot_y)
+    cot_others = cot_core, flip_core(cot_x), flip_core(cot_y)
+    cot_across, cot_others, qkv_full = seal(cot_across, cot_others, qkv_full)
+
+    normed_all, up_pair, cot_across = enter(normed_all, up_pair, cot_across)
+    projected, up_pair = seal(
+        times(normed_all, qkv_full).astype(BF16), lax.all_to_all(up_pair, "blk", 0, 0)
+    )
+    projected, up_pair = enter(projected, up_pair)
+    up_own, up_other = up_pair[:, 1], flip_y(up_pair[:, 0])
     attended_low, log_total = attention_call(
         attention_forward_kernel,
         [projected],
@@ -518,51 +517,99 @@
         lengths,
         2,
     )
-    attended_low = after(attended_low, up_part)
-    held = scatter_core(times(attended_low, out_full))
-    got = scatter_first(held)
-    cot_all = gather_third(*after(cot_steps, held))
-    mixed = x + scatter_third(held, *got, *scatter_second(held, *got))
+    cot_others = [*cot_others, *[flip_core(piece) for piece in cot_across]]
+    attended_low, up_other, cot_others = seal(attended_low, up_other, cot_others)
+    up_part = join_y(*enter(up_own, up_other)).reshape(blk, 2 * shard, lanes * units)
+    up_full = gather_z(after(up_part, qkv_full), 1).reshape(width, lanes * units)
+
+    def start_sum(left, multiply, *beside):
+        left = enter(left)
+        far, near = [
+            flip_core(multiply(rows_of(left, *run)).astype(BF16)) for run in ((12, 16), (8, 12))
+        ]
+        middle = far.shape[0] // 2
+        to_x = (multiply(rows_of(left, 4, 6)) + far[:middle].astype(F32)).astype(BF16)
+        to_y = (multiply(rows_of(left, 6, 8)) + far[middle:].astype(F32)).astype(BF16)
+        to_x, to_y, near, beside = seal(to_x, to_y, near, beside)
+        return enter(to_x), enter(to_y), near, beside
+
+    to_x, to_y, near, _ = start_sum(attended_low, lambda v: times(v, out_full))
+    own = times(rows_of(enter(attended_low), 0, 4), out_full)
+    cot_all = assemble(enter(*[cot_low, cot_x, cot_y, *cot_others[:3]]), MOST)
+    cot_all = assemble(enter(*[*cot_across, *cot_others[3:]]), REST, cot_all)
+    from_x, from_y, own, cot_all = seal(flip_x(to_x), flip_y(to_y), own, cot_all)
+    sums = enter(own, near, from_x, from_y)
+    to_x, to_y = last_sends(*sums)
+    last_x, last_y, own, down_full = seal(
+        flip_x(to_x), flip_y(to_y), own_rows(*after(sums, to_x, to_y)), down_full
+    )
+    mixed = x + add_last(*enter(own, last_x, last_y))
     second, second_pull = jax.vjp(layer_norm, mixed, norm_gains[1], norm_biases[1])
-    second_low = second.astype(BF16)
-    steps = gather_first(second_low)
-    grad_activated = contract_last(after(cot_all, second_low), down_full)
-    steps = gather_second(*after(steps, grad_activated))
-    second_all = gather_third(*steps)
-    bias_part = lax.dynamic_slice_in_dim(
-        hidden_bias.reshape(blk, lanes, 2, units), b, 1, 0
-    )
+    second_low = seal(second.astype(BF16))
+
+    def gather_rows(part_low, beside, also):
+        part_low = enter(part_low)
+        from_x, from_y, from_core = flip_x(part_low), flip_y(part_low), flip_core(part_low)
+        from_x, from_y, from_core, beside = seal(from_x, from_y, from_core, beside())
+        part_low, from_x, from_y, from_core = enter(part_low, from_x, from_y, from_core)
+        across = diagonal_of(from_x, from_y)
+        others = from_core, flip_core(from_x), flip_core(from_y)
+        across, whole, also = seal(
+            across, assemble([part_low, from_x, from_y, *others], MOST), also(beside)
+        )
+        across, whole = enter(across, whole)
+        whole = assemble([*across, *[flip_core(piece) for piece in across]], REST, whole)
+        return seal(whole), beside, also
+
+    second_all, grad_activated, up_full = gather_rows(
+        second_low, lambda: contract_last(enter(cot_all), down_full), lambda beside: up_full
+    )
+    bias_part = lax.dynamic_slice_in_dim(hidden_bias.reshape(blk, lanes, 2, units), b, 1, 0)
     bias_part = lax.dynamic_index_in_dim(bias_part, y, 2, keepdims=False).reshape(-1)
-    hidden_pre = jnp.dot(second_all, up_full, preferred_element_type=F32) + bias_part
+    hidden_pre = times(enter(second_all), up_full) + bias_part
     activated, slope = gelu(hidden_pre)
-    activated_low = activated.astype(BF16)
-    grad_hidden_low = (grad_activated * slope).astype(BF16)
-
-    held = scatter_core(times_transposed(grad_hidden_low, up_full))
-    got = scatter_first(held)
-    down_term = contract_first(after(activated_low, held), cot_all).astype(BF16)
+    activated_low, grad_hidden_low = seal(
+        activated.astype(BF16), (grad_activated * slope).astype(BF16)
+    )
+
+    to_x, to_y, near, _ = start_sum(grad_hidden_low, lambda v: contract_last(v, up_full))
+    down_term = contract_first(enter(activated_low), cot_all).astype(BF16)
     down_sum = scatter_z(down_term, 0)
-    hidden_sum = jnp.sum(after(grad_hidden_low, down_term).astype(F32), axis=0)
-    last = scatter_second(held, *after(got, hidden_sum))
-    product = times(after(activated_low, last), down_full)
-    result_high = product(12, 16).astype(BF16), product(8, 12).astype(BF16)
-    grad_second = scatter_third(held, *got, *last)
-    grad_mixed_norm, gain_two, bias_two = second_pull(grad_second)
+    own = contract_last(rows_of(enter(grad_hidden_low), 0, 4), up_full)
+    from_x, from_y, own, down_term = seal(flip_x(to_x), flip_y(to_y), own, down_term)
+    sums = enter(own, near, from_x, from_y)
+    to_x, to_y = last_sends(*sums)
+    result_low = times(rows_of(enter(activated_low), 0, 8), down_full).astype(BF16)
+    last_x, last_y, own, result_low = seal(
+        flip_x(to_x), flip_y(to_y), own_rows(*after(sums, to_x, to_y)), result_low
+    )
+    grad_mixed_norm, gain_two, bias_two = second_pull(add_last(*enter(own, last_x, last_y)))
     grad_mixed = cot_low.astype(F32) + grad_mixed_norm
-    mixed_low = grad_mixed.astype(BF16)
-    steps = gather_first(mixed_low)
-    up_term = contract_first(second_all, after(grad_hidden_low, mixed_low)).astype(BF16)
+    mixed_low, gain_two, bias_two = seal(grad_mixed.astype(BF16), gain_two, bias_two)
+
+    def beside_gather():
+        up_term = contract_first(second_all, enter(grad_hidden_low)).astype(BF16)
+        result_near = times(rows_of(enter(activated_low), 8, 12), down_full).astype(BF16)
+        return up_term, result_near
+
+    def beside_second(beside):
+        far = times(rows_of(enter(activated_low), 12, 16), down_full).astype(BF16)
+        return far, flip_core(enter(beside[1])), down_sum
+
+    mixed_all, (up_term, _), (result_far, got_near, down_sum) = gather_rows(
+        mixed_low, beside_gather, beside_second
+    )
     up_sum = scatter_z(up_term.reshape(blk, -1, lanes * units), 1)
-    steps = gather_second(*after(steps, up_term))
-    product = times(after(activated_low, up_term), down_full)
-    result_low = product(0, 8).astype(BF16)
-    mixed_all = gather_third(*after(steps, result_low))
-    result_held = scatter_pair(
-        lambda first, last, *others: result_low[first * half : last * half],
-        *[flip_core(piece) for piece in result_high],
-    )
-    grad_attended = contract_last(mixed_all, out_full).astype(BF16)
-    result_got = scatter_first(result_held, mixed_all)
+    mixed_all, result_far = enter(mixed_all, result_far)
+    got_far, grad_attended = seal(
+        flip_core(result_far), contract_last(mixed_all, out_full).astype(BF16)
+    )
+    got_far, grad_attended = enter(got_far, grad_attended)
+    to_x = rows_of(result_low, 4, 6).astype(F32) + got_far[: 2 * half].astype(F32)
+    to_y = rows_of(result_low, 6, 8).astype(F32) + got_far[2 * half :].astype(F32)
+    to_x, to_y = to_x.astype(BF16), to_y.astype(BF16)
+    from_x, from_y = flip_x(to_x), flip_y(to_y)
+    grad_attended = after(grad_attended, to_x, to_y)
     (grad_projected,) = attention_call(
         attention_backward_kernel,
         [projected, grad_attended, log_total],
@@ -572,32 +619,59 @@
         lengths,
         5,
     )
-    result_last = scatter_second(result_held, *after(result_got, grad_projected))
-    qkv_term = contract_first(
-        normed_all, after(grad_projected, up_sum, down_sum, *result_last)
-    ).astype(BF16)
+    qkv_term = contract_first(normed_all, grad_projected).astype(BF16)
+    from_x, from_y, grad_projected, qkv_term = seal(from_x, from_y, grad_projected, qkv_term)
+
+    def split_sum(total):
+        parts = total.reshape(blk, 2, shard, -1)
+        other = flip_y(lax.dynamic_index_in_dim(parts, 1 - y, 1, keepdims=False))
+        return lax.dynamic_index_in_dim(parts, y, 1, keepdims=False), other
+
     qkv_sum = scatter_z(qkv_term.reshape(blk, -1, 3 * part), 1)
-    result = mixed + scatter_third(result_held, *after(result_got, qkv_term), *result_last)
-    up_pair = split_sum(after(up_sum, *result_last))
-    held = scatter_core(times_transposed(after(grad_projected, qkv_term, result), qkv_full))
-    got = scatter_first(held, up_pair)
-    out_term = contract_first(after(attended_low, held), mixed_all).astype(BF16)
-    grad_normed = scatter_third(held, *got, *scatter_second(held, *got))
-    grad_input_norm, gain_one, bias_one = first_pull(grad_normed)
-    qkv_pair = split_sum(qkv_sum)
+    result_sums = enter(rows_of(result_low, 0, 4), got_near, from_x, from_y)
+    to_x, to_y = last_sends(*result_sums)
+    left = after(grad_projected, to_x, to_y)
+    far, near = [
+        contract_last(rows_of(left, *run), qkv_full).astype(BF16) for run in ((12, 16), (8, 12))
+    ]
+    far, near, last_x, last_y = seal(far, near, flip_x(to_x), flip_y(to_y))
+    left, far, near = enter(grad_projected, far, near)
+    far, near = flip_core(far), flip_core(near)
+    up_pair = split_sum(enter(up_sum))
+    to_x = contract_last(rows_of(left, 4, 6), qkv_full) + far[: 2 * half].astype(F32)
+    to_y = contract_last(rows_of(left, 6, 8), qkv_full) + far[2 * half :].astype(F32)
+    to_x, to_y, up_pair = seal(to_x.astype(BF16), to_y.astype(BF16), up_pair)
+    to_x, to_y = enter(to_x, to_y)
+    hidden_sum = jnp.sum(enter(grad_hidden_low).astype(F32), axis=0)
+    own = contract_last(rows_of(enter(grad_projected), 0, 4), qkv_full)
+    result = mixed + add_last(own_rows(*enter(*result_sums)), last_x, last_y)
+    out_term = contract_first(enter(attended_low), mixed_all).astype(BF16)
+    from_x, from_y, own, result, out_term, hidden_sum = seal(
+        flip_x(to_x), flip_y(to_y), own, result, out_term, hidden_sum
+    )
+    sums = enter(own, near, from_x, from_y)
+    to_x, to_y = last_sends(*sums)
+    last_x, last_y, own = seal(flip_x(to_x), flip_y(to_y), own_rows(*after(sums, to_x, to_y)))
+
+    grad_input_norm, gain_one, bias_one = first_pull(add_last(*enter(own, last_x, last_y)))
     grad_input = (grad_mixed + grad_input_norm).astype(BF16)
-
-    qkv_got = exchange(*qkv_pair)
-    up_got = exchange(up_pair[0], after(up_pair[1], gain_one))
-    grad_up = merge_columns(up_got, *up_cut)
-    grad_qkv = merge_columns(qkv_got, *qkv_cut)
-    norms, hidden_sum = sum_small(
-        after(jnp.stack([gain_one, gain_two, bias_one, bias_two]), qkv_got), hidden_sum
-    )
-    out_sum = after(scatter_z(out_term, 0), norms)
+    up_got = exchange(*enter(*up_pair))
+    qkv_pair = split_sum(enter(qkv_sum))
+    up_got, qkv_pair, gain_one, bias_one, grad_input, result = seal(
+        up_got, qkv_pair, gain_one, bias_one, grad_input, result.astype(BF16)
+    )
+
+    norms = sum_blk(enter(jnp.stack([gain_one, gain_two, bias_one, bias_two])))
+    qkv_got = exchange(*enter(*qkv_pair))
+    out_sum = scatter_z(after(out_term, qkv_sum), 0)
+    grad_up = merge_columns(enter(up_got), *up_cut)
+    norms, qkv_got, grad_up = seal(norms, qkv_got, grad_up)
+    norms, hidden_sum = sum_dp(enter(norms), hidden_sum)
+    grad_qkv = merge_columns(enter(qkv_got), *qkv_cut)
+    out_sum = after(out_sum, norms)
     grad_out = lax.ppermute(out_sum, "dp", [(j, i) for i, j in route]).astype(F32)
     return (
-        result.astype(BF16).reshape(1, 1, rows, width),
+        result.reshape(1, 1, rows, width),
         grad_input.reshape(1, 1, rows, width),
         grad_qkv,
         grad_out,

time: 725 us -> 672 us (0.927)
  waiting for transfers between devices: 252 us -> 219 us
  other arithmetic: 70.1 us -> 58.7 us
  matrix products: 179 us -> 169 us
    ppermute x65, waiting for transfers between devices: 228 us -> 178 us  [flip(): return lax.ppermute(block, axis, [(i ^ bits, i) for i in range(count)])]
    dot_general x10, matrix products: 68.8 us -> 56.1 us  [times(): return jnp.dot(left, right, preferred_element_type=F32)]
    all_gather x4, waiting for transfers between devices: 2.36 us -> 14.1 us  [gather_z(): lax.all_gather(part, 'dp', axis_index_groups=lines(), axis=axis, tiled=True)]
    all_to_all x4 -> x2, waiting for transfers between devices: 21 us -> 10.6 us  [exchange(): return lax.all_to_all(join_y(own, other), 'blk', 0, 0)]
    all_to_all x2 -> x4, starting transfers between devices: 6.54 us -> 15.5 us  [the longest x1 5.19 us: sum_dp(): both = lax.all_to_all(both, 'dp', 0, 0)]
    all_to_all x2 -> x4, waiting for transfers between devices: 0.29 us -> 8.77 us  [the longest x1 3.69 us: sum_dp(): both = lax.all_to_all(both, 'dp', 0, 0)]
    slice x8 -> x18, local copies, waits for them, and re-layouts: 7.33 us -> 14.6 us  [the longest x8 6.48 us: diagonal_of(): return (flip_y(from_x[:half]), flip_x(from_y[half:]))]
    add x9 -> x4, other arithmetic: 15.5 us -> 9.59 us  [the longest x3 6.04 us: own_rows(): own + jnp.concatenate([from_x[half:], from_y[half:]], axis=0).astype(F32)]
  transfers between devices with their start and end apart: 81 -> 81, of which waited for: 38 -> 48; matrix products, arithmetic and copies ran while one was open for 31% -> 32% of each run, Pallas kernels for 11% -> 11%
where the time goes in v5:
time: 672 us; the launch traced here: 664 us
  waiting for transfers between devices  219 us (33%)
  matrix products  169 us (25%)
  starting transfers between devices  88.7 us (13%)
  Pallas kernels  80 us (12%)
  other arithmetic  58.7 us (9%)
  local copies, waits for them, and re-layouts  32.3 us (5%)
  between operations  15.9 us (2%)
    ppermute x65, waiting for transfers between devices, flip(): return lax.ppermute(block, axis, [(i ^ bits, i) for i in range(count)])  178 us
    dot_general x12, matrix products, contract_last(): lax.dot_general(left, right, (((1,), (1,)), ((), ())), preferred_element_...  68 us
    ppermute x65, starting transfers between devices, flip(): return lax.ppermute(block, axis, [(i ^ bits, i) for i in range(count)])  60.1 us
    dot_general x10, matrix products, times(): return jnp.dot(left, right, preferred_element_type=F32)  56.1 us
    dot_general x4, matrix products, contract_first(): lax.dot_general(left, right, (((0,), (0,)), ((), ())), preferred_element_...  45.1 us
    pallas_call x8, Pallas kernels, assemble(): pl.pallas_call(kernel, in_specs=[pl.BlockSpec(memory_space=pl.ANY)] * len...  36.5 us
    pallas_call x2, Pallas kernels, attention_call(): pl.pallas_call(kernel, grid_spec=pltpu.PrefetchScalarGridSpec(num_scalar_...  29.1 us
    all_gather x4, waiting for transfers between devices, gather_z(): lax.all_gather(part, 'dp', axis_index_groups=lines(), axis=axis, tiled=True)  14.1 us
  transfers between devices with their start and end apart: 81, of which 48 were waited for; matrix products, arithmetic and copies ran while one was open for 32% of the time, Pallas kernels for 11%

profile of v5, /device:TPU:0, one launch (start us, length us, event | category | flops | bytes accessed | tf_op | source)
XLA Modules:
  0.0 663.5 jit_solution(1824995689108661023)
XLA Ops:
  26.5 8.9 %collective-permute-start.3 = (s32[1,2]{1,0:T(1,128)S(1)}, s32[1,2]{1,0:T(1,128)S(1)}, u32[]{:S(2)}, u32[]{:S(2)}) collective-permute-start(s32[1,2]{1,0:T(1,128)S(1)} %copy-done.78), channel_id=1, source_target_pairs={{1,0},{0,1},{3,2},{2,3},{5,4},{4,5},{7,6},{6,7},{9,8},{8,9},{11,10... | collective-permute-start | bytes 32 | tf_op jit(solution)/shard_map/ppermute | solution.py:54
  35.4 14.6 %collective-permute-done.3 = s32[1,2]{1,0:T(1,128)S(1)} collective-permute-done((s32[1,2]{1,0:T(1,128)S(1)}, s32[1,2]{1,0:T(1,128)S(1)}, u32[]{:S(2)}, u32[]{:S(2)}) %collective-permute-start.3) | collective-permute-done | bytes 40 | tf_op jit(solution)/shard_map/ppermute | solution.py:54
  55.2 8.6 %collective-permute-done.8.other_ref = bf16[4,64,768]{2,1,0:T(8,128)(2,1)S(1)} collective-permute-done((bf16[4,64,768]{2,1,0:T(8,128)(2,1)S(1)}, bf16[4,64,768]{2,1,0:T(8,128)(2,1)S(1)}, u32[]{:S(2)}, u32[]{:S(2)}) %collective-permute-start.8) | collective-permute-done | bytes 393248 | tf_op jit(solution)/shard_map/ppermute | solution.py:54
  76.1 6.4 shard_map.188.refs_4_
  95.2 20.6 %collective-permute-done.10.refs_2_ = bf16[320,2048]{1,0:T(8,128)(2,1)S(1)} collective-permute-done((bf16[320,2048]{1,0:T(8,128)(2,1)S(1)}, bf16[320,2048]{1,0:T(8,128)(2,1)S(1)}, u32[]{:S(2)}, u32[]{:S(2)}) %collective-permute-start.10) | collective-permute-done | bytes 1310752 | tf_op jit(solution)/shard_map/ppermute | solution.py:54
  122.8 13.7 %collective-permute-done.14.refs_0_ = bf16[160,2048]{1,0:T(8,128)(2,1)} collective-permute-done((bf16[160,2048]{1,0:T(8,128)(2,1)}, bf16[160,2048]{1,0:T(8,128)(2,1)}, u32[]{:S(2)}, u32[]{:S(2)}) %collective-permute-start.14) | collective-permute-done | bytes 655392 | tf_op jit(solution)/shard_map/ppermute | solution.py:54
  141.9 13.2 %convolution_convert_fusion.1 = bf16[2560,768]{1,0:T(8,128)(2,1)} fusion(bf16[2560,2048]{1,0:T(8,128)(2,1)} %shard_map.191, bf16[2048,768]{1,0:T(8,128)(2,1)} %bitcast.184), kind=kOutput, calls=%fused_computation.6 | convolution fusion | flops 8055029760 | bytes 17563648 | tf_op jit(solution)/shard_map/dot_general | solution.py:469
  157.3 10.5 %shard_map.192 = (bf16[16,160,256]{2,1,0:T(8,128)(2,1)S(1)}, f32[16,160,256]{2,1,0:T(8,128)S(1)}) custom-call(s32[2,2,8]{2,1,0:T(2,128)S(1)} %reshape.198.places_ref, s32[2,2]{1,0:T(2,128)S(1)} %pad_add_fusion.1.lengths_ref, bf16[16,160,768]{2,1,0:T(8,128)(2,1)} %bitcast.190), custom_call_target="tpu_custom_call" | custom-call | flops 2147483648 | bytes 5242880 | tf_op jit(solution)/shard_map/pallas_call | solution.py:391
  194.2 16.9 %collective-permute-done.25 = bf16[320,2048]{1,0:T(8,128)(2,1)} collective-permute-done((bf16[320,2048]{1,0:T(8,128)(2,1)}, bf16[320,2048]{1,0:T(8,128)(2,1)}, u32[]{:S(2)}, u32[]{:S(2)}) %collective-permute-start.25) | collective-permute-done | bytes 1310752 | tf_op jit(solution)/shard_map/ppermute | solution.py:54
  221.7 8.3 %collective-permute-done.26 = bf16[160,2048]{1,0:T(8,128)(2,1)S(1)} collective-permute-done((bf16[160,2048]{1,0:T(8,128)(2,1)}, bf16[160,2048]{1,0:T(8,128)(2,1)S(1)}, u32[]{:S(2)}, u32[]{:S(2)}) %collective-permute-start.26) | collective-permute-done | bytes 655392 | tf_op jit(solution)/shard_map/ppermute | solution.py:54
  237.1 15.4 %fusion.62 = f32[2560,1024]{1,0:T(8,128)} fusion(bf16[2560,2048]{1,0:T(8,128)(2,1)} %shard_map.194, bf16[1024,2048]{1,0:T(8,128)(2,1)S(1)} %copy-done.79), kind=kOutput, calls=%fused_computation.144 | convolution fusion | flops 10737418240 | bytes 25165824 | tf_op jit(solution)/shard_map/dot_general | solution.py:41
  252.5 11.0 %collective-permute-done.28.refs_1_ = bf16[320,2048]{1,0:T(8,128)(2,1)S(1)} collective-permute-done((bf16[320,2048]{1,0:T(8,128)(2,1)S(1)}, bf16[320,2048]{1,0:T(8,128)(2,1)S(1)}, u32[]{:S(2)}, u32[]{:S(2)}) %collective-permute-start.28) | collective-permute-done | bytes 1310752 | tf_op jit(solution)/shard_map/ppermute | solution.py:54
  271.4 6.4 shard_map.195.refs_4_
  277.9 14.1 %all-gather.11.cloned.1.call-done = bf16[4,512,1024]{2,1,0:T(8,128)(2,1)} async-done(((bf16[4,128,1024]{2,1,0:T(8,128)(2,1)}), bf16[4,512,1024]{2,1,0:T(8,128)(2,1)}) %all-gather.11.cloned.1.call-update) | async-done | bytes 4194320 | tf_op jit(solution)/shard_map/all_gather | solution.py:75
  298.9 15.3 %fusion.63 = f32[2560,1024]{1,0:T(8,128)S(1)} fusion(bf16[2560,2048]{1,0:T(8,128)(2,1)} %shard_map.197, bf16[2048,1024]{1,0:T(8,128)(2,1)} %bitcast.178), kind=kOutput, calls=%fused_computation.145 | convolution fusion | flops 10737418240 | bytes 25165824 | tf_op jit(solution)/shard_map/dot_general | solution.py:469
  314.3 8.5 %multiply_convert_fusion = (bf16[2560,1024]{1,0:T(8,128)(2,1)S(1)}, bf16[2560,1024]{1,0:T(8,128)(2,1)}) fusion(f32[2560,1024]{1,0:T(8,128)S(1)} %bitcast.147, f32[2560,1024]{1,0:T(8,128)S(1)} %fusion.63, f32[1024]{0:T(1024)S(1)} %bitcast.173), kind=kLoop, calls=%fused_computation.1 | loop fusion | flops 55050240 | bytes 31461376 | tf_op jit(solution)/shard_map/convert_element_type | solution.py:572
  322.8 7.6 %convolution_convert_fusion.13 = bf16[640,2048]{1,0:T(8,128)(2,1)S(1)} fusion(bf16[2048,1024]{1,0:T(8,128)(2,1)} %bitcast.179, bf16[2560,1024]{1,0:T(8,128)(2,1)S(1)} %get-tuple-element.504), kind=kOutput, calls=%fused_computation.28 | convolution fusion | flops 2685665280 | bytes 8126464 | tf_op jit(solution)/shard_map/dot_general | solution.py:41
  343.7 13.4 %convolution_convert_fusion.3 = bf16[1024,2048]{1,0:T(8,128)(2,1)} fusion(bf16[2560,1024]{1,0:T(8,128)(2,1)S(1)} %bitcast.151, bf16[2560,2048]{1,0:T(8,128)(2,1)S(1)} %bitcast.135), kind=kOutput, calls=%fused_computation.10 | convolution fusion | flops 10739515392 | bytes 19922944 | tf_op jit(solution)/shard_map/dot_general | solution.py:47
  362.4 9.4 %collective-permute-done.40 = bf16[320,2048]{1,0:T(8,128)(2,1)} collective-permute-done((bf16[320,2048]{1,0:T(8,128)(2,1)}, bf16[320,2048]{1,0:T(8,128)(2,1)}, u32[]{:S(2)}, u32[]{:S(2)}) %collective-permute-start.40) | collective-permute-done | bytes 1310752 | tf_op jit(solution)/shard_map/ppermute | solution.py:54
  377.0 9.1 %convolution_convert_fusion = bf16[1280,2048]{1,0:T(8,128)(2,1)} fusion(bf16[1024,2048]{1,0:T(8,128)(2,1)S(1)} %copy-done.80, bf16[2560,1024]{1,0:T(8,128)(2,1)} %get-tuple-element.451), kind=kOutput, calls=%fused_computation.5 | convolution fusion | flops 5371330560 | bytes 12058624 | tf_op jit(solution)/shard_map/dot_general | solution.py:469
  397.3 13.7 %convolution_convert_fusion.4 = bf16[2048,1024]{1,0:T(8,128)(2,1)} fusion(bf16[2560,2048]{1,0:T(8,128)(2,1)S(1)} %bitcast.133, bf16[2560,1024]{1,0:T(8,128)(2,1)S(1)} %bitcast.137), kind=kOutput, calls=%fused_computation.11 | convolution fusion | flops 10739515392 | bytes 19922944 | tf_op jit(solution)/shard_map/dot_general | solution.py:47
  411.0 7.2 %convolution_convert_fusion.11 = bf16[640,2048]{1,0:T(8,128)(2,1)} fusion(bf16[1024,2048]{1,0:T(8,128)(2,1)} %all-gather.9.cloned.1.call-done, bf16[2560,1024]{1,0:T(8,128)(2,1)} %get-tuple-element.451), kind=kOutput, calls=%fused_computation.26 | convolution fusion | flops 2685665280 | bytes 8126464 | tf_op jit(solution)/shard_map/dot_general | solution.py:469
  418.2 6.5 collective-permute-done.43.refs_1_
  435.6 6.4 shard_map.198.refs_4_
  453.6 8.7 %convolution_convert_fusion.2 = bf16[2560,256]{1,0:T(8,128)(2,1)S(1)} fusion(bf16[2560,2048]{1,0:T(8,128)(2,1)} %shard_map.199, bf16[256,2048]{1,0:T(8,128)(2,1)S(1)} %copy-done.16), kind=kOutput, calls=%fused_computation.9 | convolution fusion | flops 2685009920 | bytes 12845056 | tf_op jit(solution)/shard_map/dot_general | solution.py:41
  469.1 18.7 %shard_map.200 = bf16[16,160,768]{2,1,0:T(8,128)(2,1)} custom-call(s32[2,2,8]{2,1,0:T(2,128)S(1)} %reshape.198.places_ref, s32[2,2]{1,0:T(2,128)S(1)} %copy-done.5, bf16[16,160,768]{2,1,0:T(8,128)(2,1)} %bitcast.191, bf16[16,160,256]{2,1,0:T(8,128)(2,1)S(1)} %bitcast.129, f32[16,160,256]{2,1,0:T(8,128)S(1)} %copy-done.7), custom_call_target="tpu_custom_call" | custom-call | flops 5368709120 | bytes 5242880 | tf_op jit(solution)/shard_map/pallas_call | solution.py:391
  487.8 14.1 %convolution_convert_fusion.5 = bf16[2048,768]{1,0:T(8,128)(2,1)} fusion(bf16[2560,2048]{1,0:T(8,128)(2,1)} %shard_map.191, bf16[2560,768]{1,0:T(8,128)(2,1)} %bitcast.192), kind=kOutput, calls=%fused_computation.12 | convolution fusion | flops 8054636544 | bytes 17563648 | tf_op jit(solution)/shard_map/dot_general | solution.py:47
  511.8 7.6 %collective-permute-done.56 = bf16[160,2048]{1,0:T(8,128)(2,1)S(1)} collective-permute-done((bf16[160,2048]{1,0:T(8,128)(2,1)S(1)}, bf16[160,2048]{1,0:T(8,128)(2,1)S(1)}, u32[]{:S(2)}, u32[]{:S(2)}) %collective-permute-start.56) | collective-permute-done | bytes 655392 | tf_op jit(solution)/shard_map/ppermute | solution.py:54
  519.7 6.9 %reduce-scatter.7.cloned.1.call-done = bf16[4,128,1024]{2,1,0:T(8,128)(2,1)} async-done(((bf16[4,512,1024]{2,1,0:T(8,128)(2,1)}), bf16[4,128,1024]{2,1,0:T(8,128)(2,1)}) %reduce-scatter.7.cloned.1.call-update) | async-done | bytes 1048592 | tf_op jit(solution)/shard_map/reduce_scatter | solution.py:79
  558.3 13.7 %collective-permute-done.60 = bf16[320,2048]{1,0:T(8,128)(2,1)} collective-permute-done((bf16[320,2048]{1,0:T(8,128)(2,1)}, bf16[320,2048]{1,0:T(8,128)(2,1)}, u32[]{:S(2)}, u32[]{:S(2)}) %collective-permute-start.60) | collective-permute-done | bytes 1310752 | tf_op jit(solution)/shard_map/ppermute | solution.py:54
  583.4 8.1 %collective-permute-done.63 = bf16[160,2048]{1,0:T(8,128)(2,1)S(1)} collective-permute-done((bf16[160,2048]{1,0:T(8,128)(2,1)S(1)}, bf16[160,2048]{1,0:T(8,128)(2,1)S(1)}, u32[]{:S(2)}, u32[]{:S(2)}) %collective-permute-start.63) | collective-permute-done | bytes 655392 | tf_op jit(solution)/shard_map/ppermute | solution.py:54
  629.4 10.0 %all-to-all-done.4.in_ref = bf16[4,2,64,768]{3,2,1,0:T(8,128)(2,1)S(1)} async-done(((bf16[4,2,64,768]{3,2,1,0:T(8,128)(2,1)}), bf16[4,2,64,768]{3,2,1,0:T(8,128)(2,1)S(1)}, u32[]{:S(2)}, u32[]{:S(2)}) %all-to-all-start.4) | async-done | bytes 786464 | tf_op jit(solution)/shard_map/all_to_all | solution.py:163
  (486 shorter events, 294.2 us)
Async XLA Ops:
  7.2 58.1 %all-gather.5.cloned.1.call-start = ((), (), s32[]{:S(2)}) async-start(), calls=%async_computation.10 | async-start | bytes 1310720 | tf_op jit(solution)/shard_map/all_gather | solution.py:75
  12.0 40.2 %collective-permute-start = (bf16[320,2048]{1,0:T(8,128)(2,1)S(1)}, bf16[320,2048]{1,0:T(8,128)(2,1)S(1)}, u32[]{:S(2)}, u32[]{:S(2)}) collective-permute-start(bf16[320,2048]{1,0:T(8,128)(2,1)S(1)} %fusion.15.refs_0_), channel_id=1, source_target_pairs={{16,0},{24,8},{0,16},{8,24},{17,1},{25,9},{1,17},{9,25},{18,2},{26... | collective-permute-start | bytes 3932168 | tf_op jit(solution)/shard_map/ppermute | solution.py:54
  15.0 37.2 %collective-permute-start.1 = (bf16[320,2048]{1,0:T(8,128)(2,1)S(1)}, bf16[320,2048]{1,0:T(8,128)(2,1)}, u32[]{:S(2)}, u32[]{:S(2)}) collective-permute-start(bf16[320,2048]{1,0:T(8,128)(2,1)S(1)} %fusion.15.refs_0_), channel_id=1, source_target_pairs={{1,0},{0,1},{3,2},{2,3},{5,4},{4,5},{7,6},{6,7},{9,8},{8,9},{11,10... | collective-permute-start | bytes 3932168 | tf_op jit(solution)/shard_map/ppermute | solution.py:54
  16.5 35.7 %collective-permute-start.2 = (bf16[320,2048]{1,0:T(8,128)(2,1)S(1)}, bf16[320,2048]{1,0:T(8,128)(2,1)}, u32[]{:S(2)}, u32[]{:S(2)}) collective-permute-start(bf16[320,2048]{1,0:T(8,128)(2,1)S(1)} %fusion.15.refs_0_), channel_id=1, source_target_pairs={{8,0},{0,8},{24,16},{16,24},{9,1},{1,9},{25,17},{17,25},{10,2},{2,... | collective-permute-start | bytes 3932168 | tf_op jit(solution)/shard_map/ppermute | solution.py:54
  22.9 29.3 %all-to-all-start = ((bf16[4,2,64,768]{3,2,1,0:T(8,128)(2,1)}), bf16[4,2,64,768]{3,2,1,0:T(8,128)(2,1)S(1)}, u32[]{:S(2)}, u32[]{:S(2)}) async-start(bf16[4,2,64,768]{3,2,1,0:T(8,128)(2,1)} %shard_map.187), calls=%async_computation | async-start | bytes 1572864 | tf_op jit(solution)/shard_map/all_to_all | solution.py:474
  26.4 111.0 %all-gather.7.cloned.1.call-start = ((), (), s32[]{:S(2)}) async-start(), calls=%async_computation.11 | async-start | bytes 3932160 | tf_op jit(solution)/shard_map/all_gather | solution.py:75
  65.3 156.4 %all-gather.9.cloned.1.call-start = ((), (), s32[]{:S(2)}) async-start(), calls=%async_computation.12 | async-start | bytes 5242880 | tf_op jit(solution)/shard_map/all_gather | solution.py:75
  86.2 29.7 %collective-permute-start.10 = (bf16[320,2048]{1,0:T(8,128)(2,1)S(1)}, bf16[320,2048]{1,0:T(8,128)(2,1)S(1)}, u32[]{:S(2)}, u32[]{:S(2)}) collective-permute-start(bf16[320,2048]{1,0:T(8,128)(2,1)S(1)} %bitcast.142), channel_id=1, source_target_pairs={{1,0},{0,1},{3,2},{2,3},{5,4},{4,5},{7,6},{6,7},{9,8},{8,9},{11,10... | collective-permute-start | bytes 3932168 | tf_op jit(solution)/shard_map/ppermute | solution.py:54
  86.7 29.1 %collective-permute-start.11 = (bf16[320,2048]{1,0:T(8,128)(2,1)S(1)}, bf16[320,2048]{1,0:T(8,128)(2,1)S(1)}, u32[]{:S(2)}, u32[]{:S(2)}) collective-permute-start(bf16[320,2048]{1,0:T(8,128)(2,1)S(1)} %bitcast.143), channel_id=1, source_target_pairs={{8,0},{0,8},{24,16},{16,24},{9,1},{1,9},{25,17},{17,25},{10,2},{2,... | collective-permute-start | bytes 3932168 | tf_op jit(solution)/shard_map/ppermute | solution.py:54
  86.7 31.2 %collective-permute-start.9 = (bf16[320,2048]{1,0:T(8,128)(2,1)S(1)}, bf16[320,2048]{1,0:T(8,128)(2,1)S(1)}, u32[]{:S(2)}, u32[]{:S(2)}) collective-permute-start(bf16[320,2048]{1,0:T(8,128)(2,1)S(1)} %bitcast.144), channel_id=1, source_target_pairs={{16,0},{24,8},{0,16},{8,24},{17,1},{25,9},{1,17},{9,25},{18,2},{26... | collective-permute-start | bytes 3932168 | tf_op jit(solution)/shard_map/ppermute | solution.py:54
  141.1 150.9 %all-gather.11.cloned.1.call-start = ((), (), s32[]{:S(2)}) async-start(), calls=%async_computation.13 | async-start | bytes 5242880 | tf_op jit(solution)/shard_map/all_gather | solution.py:75
  141.3 26.5 %collective-permute-start.20 = (bf16[160,2048]{1,0:T(8,128)(2,1)}, bf16[160,2048]{1,0:T(8,128)(2,1)}, u32[]{:S(2)}, u32[]{:S(2)}) collective-permute-start(bf16[160,2048]{1,0:T(8,128)(2,1)} %collective-permute-done.14.refs_0_), channel_id=1, source_target_pairs={{8,0},{0,8},{24,16},{16,24},{9,1},{1,9},{25,17},{17,25},{10,2},{2,... | collective-permute-start | bytes 1966088 | tf_op jit(solution)/shard_map/ppermute | solution.py:54
  141.8 26.0 %collective-permute-start.21 = (bf16[160,2048]{1,0:T(8,128)(2,1)}, bf16[160,2048]{1,0:T(8,128)(2,1)}, u32[]{:S(2)}, u32[]{:S(2)}) collective-permute-start(bf16[160,2048]{1,0:T(8,128)(2,1)} %collective-permute-done.15.refs_1_), channel_id=1, source_target_pairs={{8,0},{0,8},{24,16},{16,24},{9,1},{1,9},{25,17},{17,25},{10,2},{2,... | collective-permute-start | bytes 1966088 | tf_op jit(solution)/shard_map/ppermute | solution.py:54
  180.0 31.1 %collective-permute-start.25 = (bf16[320,2048]{1,0:T(8,128)(2,1)}, bf16[320,2048]{1,0:T(8,128)(2,1)}, u32[]{:S(2)}, u32[]{:S(2)}) collective-permute-start(bf16[320,2048]{1,0:T(8,128)(2,1)} %fusion.13), channel_id=1, source_target_pairs={{1,0},{0,1},{3,2},{2,3},{5,4},{4,5},{7,6},{6,7},{9,8},{8,9},{11,10... | collective-permute-start | bytes 3932168 | tf_op jit(solution)/shard_map/ppermute | solution.py:54
  180.6 30.9 %collective-permute-start.24 = (bf16[320,2048]{1,0:T(8,128)(2,1)}, bf16[320,2048]{1,0:T(8,128)(2,1)}, u32[]{:S(2)}, u32[]{:S(2)}) collective-permute-start(bf16[320,2048]{1,0:T(8,128)(2,1)} %fusion.12), channel_id=1, source_target_pairs={{16,0},{24,8},{0,16},{8,24},{17,1},{25,9},{1,17},{9,25},{18,2},{26... | collective-permute-start | bytes 3932168 | tf_op jit(solution)/shard_map/ppermute | solution.py:54
  183.8 260.4 %reduce-scatter.5.cloned.1.call-start = ((), (), s32[]{:S(2)}) async-start(), calls=%async_computation.14 | async-start | bytes 5242880 | tf_op jit(solution)/shard_map/reduce_scatter | solution.py:79
  235.0 28.6 %collective-permute-start.28 = (bf16[320,2048]{1,0:T(8,128)(2,1)S(1)}, bf16[320,2048]{1,0:T(8,128)(2,1)S(1)}, u32[]{:S(2)}, u32[]{:S(2)}) collective-permute-start(bf16[320,2048]{1,0:T(8,128)(2,1)S(1)} %add_convert_fusion.3.refs_0_), channel_id=1, source_target_pairs={{16,0},{24,8},{0,16},{8,24},{17,1},{25,9},{1,17},{9,25},{18,2},{26... | collective-permute-start | bytes 3932168 | tf_op jit(solution)/shard_map/ppermute | solution.py:54
  235.5 28.6 %collective-permute-start.29 = (bf16[320,2048]{1,0:T(8,128)(2,1)S(1)}, bf16[320,2048]{1,0:T(8,128)(2,1)S(1)}, u32[]{:S(2)}, u32[]{:S(2)}) collective-permute-start(bf16[320,2048]{1,0:T(8,128)(2,1)S(1)} %add_convert_fusion.3.refs_0_), channel_id=1, source_target_pairs={{1,0},{0,1},{3,2},{2,3},{5,4},{4,5},{7,6},{6,7},{9,8},{8,9},{11,10... | collective-permute-start | bytes 3932168 | tf_op jit(solution)/shard_map/ppermute | solution.py:54
  236.9 27.1 %collective-permute-start.30 = (bf16[320,2048]{1,0:T(8,128)(2,1)S(1)}, bf16[320,2048]{1,0:T(8,128)(2,1)S(1)}, u32[]{:S(2)}, u32[]{:S(2)}) collective-permute-start(bf16[320,2048]{1,0:T(8,128)(2,1)S(1)} %add_convert_fusion.3.refs_0_), channel_id=1, source_target_pairs={{8,0},{0,8},{24,16},{16,24},{9,1},{1,9},{25,17},{17,25},{10,2},{2,... | collective-permute-start | bytes 3932168 | tf_op jit(solution)/shard_map/ppermute | solution.py:54
  340.7 31.1 %collective-permute-start.40 = (bf16[320,2048]{1,0:T(8,128)(2,1)}, bf16[320,2048]{1,0:T(8,128)(2,1)}, u32[]{:S(2)}, u32[]{:S(2)}) collective-permute-start(bf16[320,2048]{1,0:T(8,128)(2,1)} %fusion.9), channel_id=1, source_target_pairs={{1,0},{0,1},{3,2},{2,3},{5,4},{4,5},{7,6},{6,7},{9,8},{8,9},{11,10... | collective-permute-start | bytes 3932168 | tf_op jit(solution)/shard_map/ppermute | solution.py:54
  342.2 30.8 %collective-permute-start.39 = (bf16[320,2048]{1,0:T(8,128)(2,1)}, bf16[320,2048]{1,0:T(8,128)(2,1)}, u32[]{:S(2)}, u32[]{:S(2)}) collective-permute-start(bf16[320,2048]{1,0:T(8,128)(2,1)} %fusion.8), channel_id=1, source_target_pairs={{16,0},{24,8},{0,16},{8,24},{17,1},{25,9},{1,17},{9,25},{18,2},{26... | collective-permute-start | bytes 3932168 | tf_op jit(solution)/shard_map/ppermute | solution.py:54
  357.0 169.6 %reduce-scatter.7.cloned.1.call-start = ((), (), s32[]{:S(2)}) async-start(), calls=%async_computation.15 | async-start | bytes 5242880 | tf_op jit(solution)/shard_map/reduce_scatter | solution.py:79
  396.1 28.6 %collective-permute-start.43 = (bf16[320,2048]{1,0:T(8,128)(2,1)S(1)}, bf16[320,2048]{1,0:T(8,128)(2,1)S(1)}, u32[]{:S(2)}, u32[]{:S(2)}) collective-permute-start(bf16[320,2048]{1,0:T(8,128)(2,1)S(1)} %fusion.20.refs_0_), channel_id=1, source_target_pairs={{16,0},{24,8},{0,16},{8,24},{17,1},{25,9},{1,17},{9,25},{18,2},{26... | collective-permute-start | bytes 3932168 | tf_op jit(solution)/shard_map/ppermute | solution.py:54
  396.6 28.3 %collective-permute-start.44 = (bf16[320,2048]{1,0:T(8,128)(2,1)S(1)}, bf16[320,2048]{1,0:T(8,128)(2,1)S(1)}, u32[]{:S(2)}, u32[]{:S(2)}) collective-permute-start(bf16[320,2048]{1,0:T(8,128)(2,1)S(1)} %fusion.20.refs_0_), channel_id=1, source_target_pairs={{1,0},{0,1},{3,2},{2,3},{5,4},{4,5},{7,6},{6,7},{9,8},{8,9},{11,10... | collective-permute-start | bytes 3932168 | tf_op jit(solution)/shard_map/ppermute | solution.py:54
  397.2 27.8 %collective-permute-start.45 = (bf16[320,2048]{1,0:T(8,128)(2,1)S(1)}, bf16[320,2048]{1,0:T(8,128)(2,1)S(1)}, u32[]{:S(2)}, u32[]{:S(2)}) collective-permute-start(bf16[320,2048]{1,0:T(8,128)(2,1)S(1)} %fusion.20.refs_0_), channel_id=1, source_target_pairs={{8,0},{0,8},{24,16},{16,24},{9,1},{1,9},{25,17},{17,25},{10,2},{2,... | collective-permute-start | bytes 3932168 | tf_op jit(solution)/shard_map/ppermute | solution.py:54
  451.3 151.7 %reduce-scatter.9.cloned.1.call-start = ((), (), s32[]{:S(2)}) async-start(), calls=%async_computation.16 | async-start | bytes 3932160 | tf_op jit(solution)/shard_map/reduce_scatter | solution.py:79
  466.2 35.6 %collective-permute-start.54 = (bf16[320,2048]{1,0:T(8,128)(2,1)}, bf16[320,2048]{1,0:T(8,128)(2,1)S(1)}, u32[]{:S(2)}, u32[]{:S(2)}) collective-permute-start(bf16[320,2048]{1,0:T(8,128)(2,1)} %get-tuple-element.588), channel_id=1, source_target_pairs={{16,0},{24,8},{0,16},{8,24},{17,1},{25,9},{1,17},{9,25},{18,2},{26... | collective-permute-start | bytes 3932168 | tf_op jit(solution)/shard_map/ppermute | solution.py:54
  467.8 34.1 %collective-permute-start.55 = (bf16[320,2048]{1,0:T(8,128)(2,1)S(1)}, bf16[320,2048]{1,0:T(8,128)(2,1)S(1)}, u32[]{:S(2)}, u32[]{:S(2)}) collective-permute-start(bf16[320,2048]{1,0:T(8,128)(2,1)S(1)} %get-tuple-element.587), channel_id=1, source_target_pairs={{1,0},{0,1},{3,2},{2,3},{5,4},{4,5},{7,6},{6,7},{9,8},{8,9},{11,10... | collective-permute-start | bytes 3932168 | tf_op jit(solution)/shard_map/ppermute | solution.py:54
  529.5 43.6 %collective-permute-start.62 = (bf16[640,2048]{1,0:T(8,128)(2,1)}, bf16[640,2048]{1,0:T(8,128)(2,1)}, u32[]{:S(2)}, u32[]{:S(2)}) collective-permute-start(bf16[640,2048]{1,0:T(8,128)(2,1)} %convolution_convert_fusion.6), channel_id=1, source_target_pairs={{8,0},{0,8},{24,16},{16,24},{9,1},{1,9},{25,17},{17,25},{10,2},{2,... | collective-permute-start | bytes 7864328 | tf_op jit(solution)/shard_map/ppermute | solution.py:54
  541.9 30.2 %collective-permute-start.60 = (bf16[320,2048]{1,0:T(8,128)(2,1)}, bf16[320,2048]{1,0:T(8,128)(2,1)}, u32[]{:S(2)}, u32[]{:S(2)}) collective-permute-start(bf16[320,2048]{1,0:T(8,128)(2,1)} %fusion.10), channel_id=1, source_target_pairs={{16,0},{24,8},{0,16},{8,24},{17,1},{25,9},{1,17},{9,25},{18,2},{26... | collective-permute-start | bytes 3932168 | tf_op jit(solution)/shard_map/ppermute | solution.py:54
  543.4 29.7 %collective-permute-start.61 = (bf16[320,2048]{1,0:T(8,128)(2,1)}, bf16[320,2048]{1,0:T(8,128)(2,1)S(1)}, u32[]{:S(2)}, u32[]{:S(2)}) collective-permute-start(bf16[320,2048]{1,0:T(8,128)(2,1)} %fusion.11), channel_id=1, source_target_pairs={{1,0},{0,1},{3,2},{2,3},{5,4},{4,5},{7,6},{6,7},{9,8},{8,9},{11,10... | collective-permute-start | bytes 3932168 | tf_op jit(solution)/shard_map/ppermute | solution.py:54
  597.0 55.1 %reduce-scatter.11.cloned.1.call-start = ((), (), s32[]{:S(2)}) async-start(), calls=%async_computation.17 | async-start | bytes 1310720 | tf_op jit(solution)/shard_map/reduce_scatter | solution.py:79
  (157 other events, 1567.2 us)
Sparse Core Ops, SparseCore 0:
  20.3 35.6 all-gather.4
  65.4 64.6 all-gather.6
  131.7 79.4 all-gather.8
  212.6 79.2 all-gather.10
  357.2 73.5 reduce-scatter.4
  451.4 75.2 reduce-scatter.6
  528.9 60.7 reduce-scatter.8
  603.1 28.1 reduce-scatter.10

commit v6 on v5

--- a/solution.py
+++ b/solution.py
@@ -238,9 +238,11 @@
 
 
 def sum_blk(norms):
-    blk = lax.axis_size("blk")
-    parts = norms.reshape(norms.shape[0], blk, -1).transpose(1, 0, 2)
-    return jnp.sum(lax.all_to_all(parts, "blk", 0, 0), axis=0)
+    blk, b = lax.axis_size("blk"), lax.axis_index("blk")
+    norms = norms + flip_core(norms)
+    for bits in range(2, blk, 2):
+        norms = norms + flip("blk", bits, norms)
+    return lax.dynamic_slice_in_dim(norms, b * (norms.shape[1] // blk), norms.shape[1] // blk, 1)
 
 
 def sum_dp(parts, hidden):
@@ -408,6 +410,41 @@
     return [r.reshape(16 * half, -1) for r in results]
 
 
+def hidden_call(second_all, up_full, bias, grad_activated):
+    count, width = second_all.shape
+    units = up_full.shape[1]
+    step, lanes = 256, 256
+
+    def kernel(second_ref, up_ref, bias_ref, grad_ref, activated_ref, hidden_ref):
+        second = second_ref[...]
+        for first in range(0, units, lanes):
+            at = slice(first, first + lanes)
+            value = jnp.dot(second, up_ref[:, at], preferred_element_type=F32) + bias_ref[:, at]
+            activated, slope = gelu(value)
+            activated_ref[:, at] = activated.astype(BF16)
+            hidden_ref[:, at] = (grad_ref[:, at] * slope).astype(BF16)
+
+    def rows(columns):
+        return pl.BlockSpec((step, columns), lambda i: (i, 0))
+
+    def whole(*shape):
+        return pl.BlockSpec(shape, lambda i: (0, 0))
+
+    return pl.pallas_call(
+        kernel,
+        grid=(count // step,),
+        in_specs=[rows(width), whole(width, units), whole(1, units), rows(units)],
+        out_specs=[rows(units)] * 2,
+        out_shape=[jax.ShapeDtypeStruct((count, units), BF16)] * 2,
+        compiler_params=pltpu.CompilerParams(vmem_limit_bytes=40 * 2**20),
+        cost_estimate=pl.CostEstimate(
+            flops=2 * count * width * units,
+            bytes_accessed=2 * count * width + 2 * width * units + 8 * count * units,
+            transcendentals=count * units,
+        ),
+    )(second_all, up_full, bias.reshape(1, units), grad_activated)
+
+
 def body(
     hidden_in,
     cotangent,
@@ -468,46 +505,48 @@
     def times(left, right):
         return jnp.dot(left, right, preferred_element_type=F32)
 
-    out_full = gather_z(lax.ppermute(w_out, "dp", route), 0)
     normed, first_pull = jax.vjp(layer_norm, x, norm_gains[0], norm_biases[0])
     normed_low = normed.astype(BF16)
     qkv_pair = lax.all_to_all(split_columns(w_qkv, *qkv_cut), "blk", 0, 0)
-    qkv_pair, a_x, a_y, a_core, lengths = seal(
-        qkv_pair,
-        flip_x(normed_low),
-        flip_y(normed_low),
-        flip_core(normed_low),
-        flip_y(after(seq_lengths, normed_low)),
-    )
-    lengths = jnp.concatenate([seq_lengths, lengths], axis=0)
-
-    normed_low, qkv_pair, a_x, a_y, a_core = enter(normed_low, qkv_pair, a_x, a_y, a_core)
+    qkv_pair, normed_low, up_pair, out_piece = seal(
+        qkv_pair, normed_low, split_columns(w_up, *up_cut), lax.ppermute(w_out, "dp", route)
+    )
+
+    normed_low, qkv_pair, up_pair = enter(normed_low, qkv_pair, up_pair)
     qkv_part = join_y(qkv_pair[:, 1], flip_y(qkv_pair[:, 0])).reshape(blk, 2 * shard, 3 * part)
-    qkv_full = gather_z(after(qkv_part, out_full), 1).reshape(width, 3 * part)
+    qkv_full = gather_z(qkv_part, 1).reshape(width, 3 * part)
     down_full = gather_z(after(w_down, qkv_part), 0)
+    a_x, a_y, a_core, _ = seal(
+        flip_x(normed_low), flip_y(normed_low), flip_core(normed_low), qkv_part
+    )
+
+    normed_low, a_x, a_y, a_core = enter(normed_low, a_x, a_y, a_core)
     a_across = diagonal_of(a_x, a_y)
     a_others = a_core, flip_core(a_x), flip_core(a_y)
     normed_all = assemble([normed_low, a_x, a_y, *a_others], MOST)
-    a_across, normed_all, up_pair, _ = seal(
-        a_across, normed_all, split_columns(enter(w_up), *up_cut), qkv_part
-    )
+    a_across, normed_all = seal(a_across, normed_all)
 
     cot_low, normed_all, a_across = enter(cot_low, normed_all, a_across)
     cot_x, cot_y, cot_core = flip_x(cot_low), flip_y(cot_low), flip_core(cot_low)
     normed_all = assemble([*a_across, *[flip_core(piece) for piece in a_across]], REST, normed_all)
-    cot_x, cot_y, cot_core, normed_all = seal(cot_x, cot_y, cot_core, normed_all)
-
-    cot_x, cot_y, cot_core = enter(cot_x, cot_y, cot_core)
+    out_full = jnp.broadcast_to(enter(out_piece)[None], (lanes, *out_piece.shape))
+    out_full = lax.all_to_all(out_full, "dp", 0, 0, axis_index_groups=lines())
+    cot_x, cot_y, cot_core, normed_all, qkv_full, out_full = seal(
+        cot_x, cot_y, cot_core, normed_all, qkv_full, out_full
+    )
+    out_full = out_full.reshape(part, width)
+
+    cot_x, cot_y, cot_core, normed_all = enter(cot_x, cot_y, cot_core, normed_all)
     cot_across = diagonal_of(cot_x, cot_y)
     cot_others = cot_core, flip_core(cot_x), flip_core(cot_y)
-    cot_across, cot_others, qkv_full = seal(cot_across, cot_others, qkv_full)
-
-    normed_all, up_pair, cot_across = enter(normed_all, up_pair, cot_across)
-    projected, up_pair = seal(
-        times(normed_all, qkv_full).astype(BF16), lax.all_to_all(up_pair, "blk", 0, 0)
-    )
-    projected, up_pair = enter(projected, up_pair)
-    up_own, up_other = up_pair[:, 1], flip_y(up_pair[:, 0])
+    projected = times(normed_all, qkv_full).astype(BF16)
+    cot_across, cot_others, projected, lengths = seal(
+        cot_across, cot_others, projected, flip_y(enter(seq_lengths))
+    )
+    lengths = jnp.concatenate([seq_lengths, lengths], axis=0)
+
+    projected, up_pair, cot_across = enter(projected, up_pair, cot_across)
+    up_pair = lax.all_to_all(up_pair, "blk", 0, 0)
     attended_low, log_total = attention_call(
         attention_forward_kernel,
         [projected],
@@ -518,9 +557,8 @@
         2,
     )
     cot_others = [*cot_others, *[flip_core(piece) for piece in cot_across]]
-    attended_low, up_other, cot_others = seal(attended_low, up_other, cot_others)
-    up_part = join_y(*enter(up_own, up_other)).reshape(blk, 2 * shard, lanes * units)
-    up_full = gather_z(after(up_part, qkv_full), 1).reshape(width, lanes * units)
+    attended_low, up_pair, cot_others = seal(attended_low, up_pair, cot_others)
+    up_pair = enter(up_pair)
 
     def start_sum(left, multiply, *beside):
         left = enter(left)
@@ -533,16 +571,20 @@
         to_x, to_y, near, beside = seal(to_x, to_y, near, beside)
         return enter(to_x), enter(to_y), near, beside
 
-    to_x, to_y, near, _ = start_sum(attended_low, lambda v: times(v, out_full))
+    to_x, to_y, near, (up_other,) = start_sum(
+        attended_low, lambda v: times(v, out_full), flip_y(up_pair[:, 0])
+    )
+    up_part = join_y(*enter(up_pair[:, 1], up_other)).reshape(blk, 2 * shard, lanes * units)
+    up_full = gather_z(after(up_part, qkv_full), 1).reshape(width, lanes * units)
     own = times(rows_of(enter(attended_low), 0, 4), out_full)
     cot_all = assemble(enter(*[cot_low, cot_x, cot_y, *cot_others[:3]]), MOST)
     cot_all = assemble(enter(*[*cot_across, *cot_others[3:]]), REST, cot_all)
-    from_x, from_y, own, cot_all = seal(flip_x(to_x), flip_y(to_y), own, cot_all)
+    from_x, from_y, own, cot_all, down_full = seal(
+        flip_x(to_x), flip_y(to_y), own, cot_all, down_full
+    )
     sums = enter(own, near, from_x, from_y)
     to_x, to_y = last_sends(*sums)
-    last_x, last_y, own, down_full = seal(
-        flip_x(to_x), flip_y(to_y), own_rows(*after(sums, to_x, to_y)), down_full
-    )
+    last_x, last_y, own = seal(flip_x(to_x), flip_y(to_y), own_rows(*after(sums, to_x, to_y)))
     mixed = x + add_last(*enter(own, last_x, last_y))
     second, second_pull = jax.vjp(layer_norm, mixed, norm_gains[1], norm_biases[1])
     second_low = seal(second.astype(BF16))
@@ -566,10 +608,8 @@
     )
     bias_part = lax.dynamic_slice_in_dim(hidden_bias.reshape(blk, lanes, 2, units), b, 1, 0)
     bias_part = lax.dynamic_index_in_dim(bias_part, y, 2, keepdims=False).reshape(-1)
-    hidden_pre = times(enter(second_all), up_full) + bias_part
-    activated, slope = gelu(hidden_pre)
     activated_low, grad_hidden_low = seal(
-        activated.astype(BF16), (grad_activated * slope).astype(BF16)
+        *hidden_call(enter(second_all), up_full, bias_part, grad_activated)
     )
 
     to_x, to_y, near, _ = start_sum(grad_hidden_low, lambda v: contract_last(v, up_full))
@@ -651,7 +691,9 @@
     )
     sums = enter(own, near, from_x, from_y)
     to_x, to_y = last_sends(*sums)
-    last_x, last_y, own = seal(flip_x(to_x), flip_y(to_y), own_rows(*after(sums, to_x, to_y)))
+    last_x, last_y, own, qkv_sum = seal(
+        flip_x(to_x), flip_y(to_y), own_rows(*after(sums, to_x, to_y)), qkv_sum
+    )
 
     grad_input_norm, gain_one, bias_one = first_pull(add_last(*enter(own, last_x, last_y)))
     grad_input = (grad_mixed + grad_input_norm).astype(BF16)

time: 672 us -> 652 us (0.970)
  Pallas kernels: 80 us -> 102 us
  matrix products: 169 us -> 148 us
  other arithmetic: 58.7 us -> 41.2 us
    ppermute x65 -> x67, waiting for transfers between devices: 178 us -> 206 us  [flip(): return lax.ppermute(block, axis, [(i ^ bits, i) for i in range(count)])]
    pallas_call x0 -> x1, Pallas kernels: none -> 21.3 us  [hidden_call(): pl.pallas_call(kernel, grid=(count // step,), in_specs=[rows(width), whol...]
    dot_general x10 -> x9, matrix products: 56.1 us -> 37 us  [times(): return jnp.dot(left, right, preferred_element_type=F32)]
    all_gather x4 -> x3, waiting for transfers between devices: 14.1 us -> 0.01 us  [gather_z(): lax.all_gather(part, 'dp', axis_index_groups=lines(), axis=axis, tiled=True)]
    all_to_all x2, waiting for transfers between devices: 10.6 us -> 0.01 us  [exchange(): return lax.all_to_all(join_y(own, other), 'blk', 0, 0)]
    convert_element_type x1 -> x0, other arithmetic: 8.48 us -> none  [body(): (grad_activated * slope).astype(BF16)]
    ppermute x65 -> x67, starting transfers between devices: 60.1 us -> 53.5 us  [flip(): return lax.ppermute(block, axis, [(i ^ bits, i) for i in range(count)])]
  transfers between devices with their start and end apart: 81 -> 82, of which waited for: 48 -> 50; matrix products, arithmetic and copies ran while one was open for 32% -> 32% of each run, Pallas kernels for 11% -> 11%
where the time goes in v6:
time: 652 us; the launch traced here: 642 us
  waiting for transfers between devices  220 us (34%)
  matrix products  148 us (23%)
  Pallas kernels  102 us (16%)
  starting transfers between devices  83.7 us (13%)
  other arithmetic  41.2 us (6%)
  local copies, waits for them, and re-layouts  30.6 us (5%)
  between operations  15.9 us (2%)
    ppermute x67, waiting for transfers between devices, flip(): return lax.ppermute(block, axis, [(i ^ bits, i) for i in range(count)])  206 us
    dot_general x12, matrix products, contract_last(): lax.dot_general(left, right, (((1,), (1,)), ((), ())), preferred_element_...  63.9 us
    ppermute x67, starting transfers between devices, flip(): return lax.ppermute(block, axis, [(i ^ bits, i) for i in range(count)])  53.5 us
    dot_general x4, matrix products, contract_first(): lax.dot_general(left, right, (((0,), (0,)), ((), ())), preferred_element_...  47 us
    pallas_call x8, Pallas kernels, assemble(): pl.pallas_call(kernel, in_specs=[pl.BlockSpec(memory_space=pl.ANY)] * len...  37.1 us
    dot_general x9, matrix products, times(): return jnp.dot(left, right, preferred_element_type=F32)  37 us
    pallas_call x2, Pallas kernels, attention_call(): pl.pallas_call(kernel, grid_spec=pltpu.PrefetchScalarGridSpec(num_scalar_...  29.1 us
    pallas_call x1, Pallas kernels, hidden_call(): pl.pallas_call(kernel, grid=(count // step,), in_specs=[rows(width), whol...  21.3 us
  transfers between devices with their start and end apart: 82, of which 50 were waited for; matrix products, arithmetic and copies ran while one was open for 32% of the time, Pallas kernels for 11%

profile of v6, /device:TPU:0, one launch (start us, length us, event | category | flops | bytes accessed | tf_op | source)
XLA Modules:
  0.0 641.6 jit_solution(17969887551055976141)
XLA Ops:
  29.5 8.9 %collective-permute-done.4.other_ref = bf16[4,64,768]{2,1,0:T(8,128)(2,1)S(1)} collective-permute-done((bf16[4,64,768]{2,1,0:T(8,128)(2,1)S(1)}, bf16[4,64,768]{2,1,0:T(8,128)(2,1)S(1)}, u32[]{:S(2)}, u32[]{:S(2)}) %collective-permute-start.4) | collective-permute-done | bytes 393248 | tf_op jit(solution)/shard_map/ppermute | solution.py:54
  43.1 26.7 %collective-permute-done.1.refs_1_ = bf16[320,2048]{1,0:T(8,128)(2,1)S(1)} collective-permute-done((bf16[320,2048]{1,0:T(8,128)(2,1)S(1)}, bf16[320,2048]{1,0:T(8,128)(2,1)S(1)}, u32[]{:S(2)}, u32[]{:S(2)}) %collective-permute-start.1) | collective-permute-done | bytes 1310752 | tf_op jit(solution)/shard_map/ppermute | solution.py:54
  76.6 6.4 %shard_map.190.refs_4_ = bf16[2560,2048]{1,0:T(8,128)(2,1)} custom-call(bf16[320,2048]{1,0:T(8,128)(2,1)} %copy-done.28, bf16[320,2048]{1,0:T(8,128)(2,1)} %copy-done.36, bf16[320,2048]{1,0:T(8,128)(2,1)} %copy-done.38, bf16[320,2048]{1,0:T(8,128)(2,1)} %copy-done.45, bf16[320,2048]{1,0:T(8,128)(2,1)} %copy-done.47, ...), custom_call_target="tpu_custom_call" | custom-call | bytes 15728640 | tf_op jit(solution)/shard_map/pallas_call | solution.py:208
  83.0 6.7 %collective-permute-done.5.refs_0_ = bf16[160,2048]{1,0:T(8,128)(2,1)S(1)} collective-permute-done((bf16[160,2048]{1,0:T(8,128)(2,1)}, bf16[160,2048]{1,0:T(8,128)(2,1)S(1)}, u32[]{:S(2)}, u32[]{:S(2)}) %collective-permute-start.5) | collective-permute-done | bytes 655392 | tf_op jit(solution)/shard_map/ppermute | solution.py:54
  106.4 20.5 %collective-permute-done.10.refs_2_ = bf16[320,2048]{1,0:T(8,128)(2,1)} collective-permute-done((bf16[320,2048]{1,0:T(8,128)(2,1)S(1)}, bf16[320,2048]{1,0:T(8,128)(2,1)}, u32[]{:S(2)}, u32[]{:S(2)}) %collective-permute-start.10) | collective-permute-done | bytes 1310752 | tf_op jit(solution)/shard_map/ppermute | solution.py:54
  140.5 13.3 %convolution_convert_fusion.1 = bf16[2560,768]{1,0:T(8,128)(2,1)} fusion(bf16[2560,2048]{1,0:T(8,128)(2,1)} %shard_map.191, bf16[2048,768]{1,0:T(8,128)(2,1)} %bitcast.182), kind=kOutput, calls=%fused_computation.2 | convolution fusion | flops 8055029760 | bytes 17563648 | tf_op jit(solution)/shard_map/dot_general | solution.py:506
  160.1 10.5 %shard_map.192 = (bf16[16,160,256]{2,1,0:T(8,128)(2,1)S(1)}, f32[16,160,256]{2,1,0:T(8,128)S(1)}) custom-call(s32[2,2,8]{2,1,0:T(2,128)S(1)} %reshape.198.places_ref, s32[2,2]{1,0:T(2,128)S(1)} %pad_add_fusion.1.lengths_ref, bf16[16,160,768]{2,1,0:T(8,128)(2,1)} %bitcast.188), custom_call_target="tpu_custom_call" | custom-call | flops 2147483648 | bytes 5242880 | tf_op jit(solution)/shard_map/pallas_call | solution.py:393
  182.0 7.4 %collective-permute-done.23.other_ref = bf16[4,64,1024]{2,1,0:T(8,128)(2,1)S(1)} collective-permute-done((bf16[4,64,1024]{2,1,0:T(8,128)(2,1)S(1)}, bf16[4,64,1024]{2,1,0:T(8,128)(2,1)S(1)}, u32[]{:S(2)}, u32[]{:S(2)}) %collective-permute-start.23) | collective-permute-done | bytes 524320 | tf_op jit(solution)/shard_map/ppermute | solution.py:54
  192.5 6.4 %shard_map.193.refs_4_ = bf16[2560,2048]{1,0:T(8,128)(2,1)} custom-call(bf16[320,2048]{1,0:T(8,128)(2,1)} %bitcast.147, bf16[320,2048]{1,0:T(8,128)(2,1)} %collective-permute-done.9.refs_1_, bf16[320,2048]{1,0:T(8,128)(2,1)} %collective-permute-done.10.refs_2_, bf16[320,2048]{1,0:T(8,128)(2,1)} %collective-permute-done.11.refs_3_, ...), custom_call_target="tpu_custom_call" | custom-call | bytes 15728640 | tf_op jit(solution)/shard_map/pallas_call | solution.py:208
  204.8 14.8 %collective-permute-done.25 = bf16[320,2048]{1,0:T(8,128)(2,1)} collective-permute-done((bf16[320,2048]{1,0:T(8,128)(2,1)}, bf16[320,2048]{1,0:T(8,128)(2,1)}, u32[]{:S(2)}, u32[]{:S(2)}) %collective-permute-start.25) | collective-permute-done | bytes 1310752 | tf_op jit(solution)/shard_map/ppermute | solution.py:54
  229.1 8.9 %collective-permute-done.26 = bf16[160,2048]{1,0:T(8,128)(2,1)S(1)} collective-permute-done((bf16[160,2048]{1,0:T(8,128)(2,1)S(1)}, bf16[160,2048]{1,0:T(8,128)(2,1)S(1)}, u32[]{:S(2)}, u32[]{:S(2)}) %collective-permute-start.26) | collective-permute-done | bytes 655392 | tf_op jit(solution)/shard_map/ppermute | solution.py:54
  243.5 14.5 %fusion.62.grad_ref = f32[2560,1024]{1,0:T(8,128)} fusion(bf16[2560,2048]{1,0:T(8,128)(2,1)S(1)} %bitcast.138, bf16[1024,2048]{1,0:T(8,128)(2,1)S(1)} %copy-done.71), kind=kOutput, calls=%fused_computation.141 | convolution fusion | flops 10737418240 | bytes 25165824 | tf_op jit(solution)/shard_map/dot_general | solution.py:41
  258.1 10.9 %collective-permute-done.28.refs_1_ = bf16[320,2048]{1,0:T(8,128)(2,1)S(1)} collective-permute-done((bf16[320,2048]{1,0:T(8,128)(2,1)S(1)}, bf16[320,2048]{1,0:T(8,128)(2,1)S(1)}, u32[]{:S(2)}, u32[]{:S(2)}) %collective-permute-start.28) | collective-permute-done | bytes 1310752 | tf_op jit(solution)/shard_map/ppermute | solution.py:54
  274.9 6.4 shard_map.195.refs_4_
  281.3 6.5 %collective-permute-done.31.refs_0_ = bf16[160,2048]{1,0:T(8,128)(2,1)S(1)} collective-permute-done((bf16[160,2048]{1,0:T(8,128)(2,1)}, bf16[160,2048]{1,0:T(8,128)(2,1)S(1)}, u32[]{:S(2)}, u32[]{:S(2)}) %collective-permute-start.31) | collective-permute-done | bytes 655392 | tf_op jit(solution)/shard_map/ppermute | solution.py:54
  294.8 21.3 %shard_map.198 = (bf16[2560,1024]{1,0:T(8,128)(2,1)S(1)}, bf16[2560,1024]{1,0:T(8,128)(2,1)}) custom-call(bf16[2560,2048]{1,0:T(8,128)(2,1)} %shard_map.197.second_ref, bf16[2048,1024]{1,0:T(8,128)(2,1)S(1)} %bitcast.127, f32[1,1024]{1,0:T(1,128)S(1)} %bitcast.125, f32[2560,1024]{1,0:T(8,128)} %fusion.62.grad_ref), custom_call_target="tpu_custom_call" | custom-call | flops 10737418240 | bytes 35651584 | tf_op jit(solution)/shard_map/pallas_call | solution.py:433
  316.1 5.6 convolution_convert_fusion.13
  334.2 12.8 %convolution_convert_fusion.3 = bf16[1024,2048]{1,0:T(8,128)(2,1)} fusion(bf16[2560,1024]{1,0:T(8,128)(2,1)S(1)} %get-tuple-element.464, bf16[2560,2048]{1,0:T(8,128)(2,1)S(1)} %bitcast.140), kind=kOutput, calls=%fused_computation.6 | convolution fusion | flops 10739515392 | bytes 19922944 | tf_op jit(solution)/shard_map/dot_general | solution.py:47
  347.1 5.5 fusion.23
  352.6 10.6 %collective-permute-done.40 = bf16[320,2048]{1,0:T(8,128)(2,1)} collective-permute-done((bf16[320,2048]{1,0:T(8,128)(2,1)}, bf16[320,2048]{1,0:T(8,128)(2,1)}, u32[]{:S(2)}, u32[]{:S(2)}) %collective-permute-start.40) | collective-permute-done | bytes 1310752 | tf_op jit(solution)/shard_map/ppermute | solution.py:54
  368.8 7.3 %convolution_convert_fusion = bf16[1280,2048]{1,0:T(8,128)(2,1)} fusion(bf16[1024,2048]{1,0:T(8,128)(2,1)S(1)} %copy-done.72, bf16[2560,1024]{1,0:T(8,128)(2,1)S(1)} %copy-done.10), kind=kOutput, calls=%fused_computation.1 | convolution fusion | flops 5371330560 | bytes 12058624 | tf_op jit(solution)/shard_map/dot_general | solution.py:506
  388.4 15.4 %convolution_convert_fusion.4 = bf16[2048,1024]{1,0:T(8,128)(2,1)} fusion(bf16[2560,2048]{1,0:T(8,128)(2,1)S(1)} %bitcast.136, bf16[2560,1024]{1,0:T(8,128)(2,1)} %get-tuple-element.517), kind=kOutput, calls=%fused_computation.7 | convolution fusion | flops 10739515392 | bytes 19922944 | tf_op jit(solution)/shard_map/dot_general | solution.py:47
  408.0 7.1 %collective-permute-done.43.refs_1_ = bf16[320,2048]{1,0:T(8,128)(2,1)S(1)} collective-permute-done((bf16[320,2048]{1,0:T(8,128)(2,1)S(1)}, bf16[320,2048]{1,0:T(8,128)(2,1)S(1)}, u32[]{:S(2)}, u32[]{:S(2)}) %collective-permute-start.43) | collective-permute-done | bytes 1310752 | tf_op jit(solution)/shard_map/ppermute | solution.py:54
  425.2 6.4 %shard_map.199.refs_4_ = bf16[2560,2048]{1,0:T(8,128)(2,1)} custom-call(bf16[320,2048]{1,0:T(8,128)(2,1)} %copy-done.30, bf16[320,2048]{1,0:T(8,128)(2,1)} %copy-done.33, bf16[320,2048]{1,0:T(8,128)(2,1)} %copy-done.34, bf16[320,2048]{1,0:T(8,128)(2,1)} %copy-done.43, bf16[320,2048]{1,0:T(8,128)(2,1)} %copy-done.46, ...), custom_call_target="tpu_custom_call" | custom-call | bytes 15728640 | tf_op jit(solution)/shard_map/pallas_call | solution.py:208
  444.6 7.9 %convolution_convert_fusion.2 = bf16[2560,256]{1,0:T(8,128)(2,1)S(1)} fusion(bf16[2560,2048]{1,0:T(8,128)(2,1)} %shard_map.200, bf16[256,2048]{1,0:T(8,128)(2,1)S(1)} %bitcast.146), kind=kOutput, calls=%fused_computation.5 | convolution fusion | flops 2685009920 | bytes 12845056 | tf_op jit(solution)/shard_map/dot_general | solution.py:41
  456.2 18.7 %shard_map.201 = bf16[16,160,768]{2,1,0:T(8,128)(2,1)} custom-call(s32[2,2,8]{2,1,0:T(2,128)S(1)} %reshape.198.places_ref, s32[2,2]{1,0:T(2,128)S(1)} %copy-done.5, bf16[16,160,768]{2,1,0:T(8,128)(2,1)} %bitcast.189, bf16[16,160,256]{2,1,0:T(8,128)(2,1)S(1)} %bitcast.132, f32[16,160,256]{2,1,0:T(8,128)S(1)} %copy-done.8), custom_call_target="tpu_custom_call" | custom-call | flops 5368709120 | bytes 5242880 | tf_op jit(solution)/shard_map/pallas_call | solution.py:393
  474.9 15.0 %convolution_convert_fusion.5 = bf16[2048,768]{1,0:T(8,128)(2,1)} fusion(bf16[2560,2048]{1,0:T(8,128)(2,1)} %shard_map.191, bf16[2560,768]{1,0:T(8,128)(2,1)} %bitcast.190), kind=kOutput, calls=%fused_computation.8 | convolution fusion | flops 8054636544 | bytes 17563648 | tf_op jit(solution)/shard_map/dot_general | solution.py:47
  501.4 6.5 %collective-permute-done.56 = bf16[160,2048]{1,0:T(8,128)(2,1)S(1)} collective-permute-done((bf16[160,2048]{1,0:T(8,128)(2,1)S(1)}, bf16[160,2048]{1,0:T(8,128)(2,1)S(1)}, u32[]{:S(2)}, u32[]{:S(2)}) %collective-permute-start.56) | collective-permute-done | bytes 655392 | tf_op jit(solution)/shard_map/ppermute | solution.py:54
  542.0 13.8 %collective-permute-done.60 = bf16[320,2048]{1,0:T(8,128)(2,1)S(1)} collective-permute-done((bf16[320,2048]{1,0:T(8,128)(2,1)}, bf16[320,2048]{1,0:T(8,128)(2,1)S(1)}, u32[]{:S(2)}, u32[]{:S(2)}) %collective-permute-start.60) | collective-permute-done | bytes 1310752 | tf_op jit(solution)/shard_map/ppermute | solution.py:54
  567.1 7.8 %collective-permute-done.63 = bf16[160,2048]{1,0:T(8,128)(2,1)S(1)} collective-permute-done((bf16[160,2048]{1,0:T(8,128)(2,1)S(1)}, bf16[160,2048]{1,0:T(8,128)(2,1)S(1)}, u32[]{:S(2)}, u32[]{:S(2)}) %collective-permute-start.63) | collective-permute-done | bytes 655392 | tf_op jit(solution)/shard_map/ppermute | solution.py:54
  593.8 6.2 collective-permute-done.65.other_ref
  610.0 7.4 %collective-permute-done.67 = f32[4,2048]{1,0:T(4,128)S(1)} collective-permute-done((f32[4,2048]{1,0:T(4,128)S(1)}, f32[4,2048]{1,0:T(4,128)S(1)}, u32[]{:S(2)}, u32[]{:S(2)}) %collective-permute-start.67) | collective-permute-done | bytes 32800 | tf_op jit(solution)/shard_map/ppermute | solution.py:54
  (457 shorter events, 281.6 us)
Async XLA Ops:
  15.3 118.1 %all-gather.4.cloned.1.call-start = ((), (), s32[]{:S(2)}) async-start(), calls=%async_computation.10 | async-start | bytes 3932160 | tf_op jit(solution)/shard_map/all_gather | solution.py:75
  39.9 29.8 %collective-permute-start.1 = (bf16[320,2048]{1,0:T(8,128)(2,1)S(1)}, bf16[320,2048]{1,0:T(8,128)(2,1)S(1)}, u32[]{:S(2)}, u32[]{:S(2)}) collective-permute-start(bf16[320,2048]{1,0:T(8,128)(2,1)S(1)} %fusion.15.refs_0_), channel_id=1, source_target_pairs={{16,0},{24,8},{0,16},{8,24},{17,1},{25,9},{1,17},{9,25},{18,2},{26... | collective-permute-start | bytes 3932168 | tf_op jit(solution)/shard_map/ppermute | solution.py:54
  41.3 29.1 %collective-permute-start.2 = (bf16[320,2048]{1,0:T(8,128)(2,1)S(1)}, bf16[320,2048]{1,0:T(8,128)(2,1)S(1)}, u32[]{:S(2)}, u32[]{:S(2)}) collective-permute-start(bf16[320,2048]{1,0:T(8,128)(2,1)S(1)} %fusion.15.refs_0_), channel_id=1, source_target_pairs={{1,0},{0,1},{3,2},{2,3},{5,4},{4,5},{7,6},{6,7},{9,8},{8,9},{11,10... | collective-permute-start | bytes 3932168 | tf_op jit(solution)/shard_map/ppermute | solution.py:54
  43.0 27.4 %collective-permute-start.3 = (bf16[320,2048]{1,0:T(8,128)(2,1)S(1)}, bf16[320,2048]{1,0:T(8,128)(2,1)S(1)}, u32[]{:S(2)}, u32[]{:S(2)}) collective-permute-start(bf16[320,2048]{1,0:T(8,128)(2,1)S(1)} %fusion.15.refs_0_), channel_id=1, source_target_pairs={{8,0},{0,8},{24,16},{16,24},{9,1},{1,9},{25,17},{17,25},{10,2},{2,... | collective-permute-start | bytes 3932168 | tf_op jit(solution)/shard_map/ppermute | solution.py:54
  93.0 40.4 %all-to-all-start.1 = ((bf16[4,64,2048]{2,1,0:T(8,128)(2,1)}), bf16[4,64,2048]{2,1,0:T(8,128)(2,1)S(1)}, u32[]{:S(2)}, u32[]{:S(2)}) async-start(bf16[4,64,2048]{2,1,0:T(8,128)(2,1)} %broadcast_in_dim.68), calls=%async_computation.1 | async-start | bytes 2097152 | tf_op jit(solution)/shard_map/all_to_all | solution.py:533
  97.7 107.1 %all-gather.6.cloned.1.call-start = ((), (), s32[]{:S(2)}) async-start(), calls=%async_computation.11 | async-start | bytes 5242880 | tf_op jit(solution)/shard_map/all_gather | solution.py:75
  97.7 29.2 %collective-permute-start.10 = (bf16[320,2048]{1,0:T(8,128)(2,1)S(1)}, bf16[320,2048]{1,0:T(8,128)(2,1)}, u32[]{:S(2)}, u32[]{:S(2)}) collective-permute-start(bf16[320,2048]{1,0:T(8,128)(2,1)S(1)} %bitcast.148), channel_id=1, source_target_pairs={{1,0},{0,1},{3,2},{2,3},{5,4},{4,5},{7,6},{6,7},{9,8},{8,9},{11,10... | collective-permute-start | bytes 3932168 | tf_op jit(solution)/shard_map/ppermute | solution.py:54
  98.5 28.4 %collective-permute-start.11 = (bf16[320,2048]{1,0:T(8,128)(2,1)S(1)}, bf16[320,2048]{1,0:T(8,128)(2,1)}, u32[]{:S(2)}, u32[]{:S(2)}) collective-permute-start(bf16[320,2048]{1,0:T(8,128)(2,1)S(1)} %bitcast.149), channel_id=1, source_target_pairs={{8,0},{0,8},{24,16},{16,24},{9,1},{1,9},{25,17},{17,25},{10,2},{2,... | collective-permute-start | bytes 3932168 | tf_op jit(solution)/shard_map/ppermute | solution.py:54
  98.5 31.3 %collective-permute-start.9 = (bf16[320,2048]{1,0:T(8,128)(2,1)S(1)}, bf16[320,2048]{1,0:T(8,128)(2,1)}, u32[]{:S(2)}, u32[]{:S(2)}) collective-permute-start(bf16[320,2048]{1,0:T(8,128)(2,1)S(1)} %bitcast.150), channel_id=1, source_target_pairs={{16,0},{24,8},{0,16},{8,24},{17,1},{25,9},{1,17},{9,25},{18,2},{26... | collective-permute-start | bytes 3932168 | tf_op jit(solution)/shard_map/ppermute | solution.py:54
  134.9 20.1 %collective-permute-start.16 = (bf16[320,2048]{1,0:T(8,128)(2,1)}, bf16[320,2048]{1,0:T(8,128)(2,1)}, u32[]{:S(2)}, u32[]{:S(2)}) collective-permute-start(bf16[320,2048]{1,0:T(8,128)(2,1)} %collective-permute-done.9.refs_1_), channel_id=1, source_target_pairs={{8,0},{0,8},{24,16},{16,24},{9,1},{1,9},{25,17},{17,25},{10,2},{2,... | collective-permute-start | bytes 3932168 | tf_op jit(solution)/shard_map/ppermute | solution.py:54
  158.6 130.1 %all-gather.8.cloned.1.call-start = ((), (), s32[]{:S(2)}) async-start(), calls=%async_computation.12 | async-start | bytes 5242880 | tf_op jit(solution)/shard_map/all_gather | solution.py:75
  189.3 30.3 %collective-permute-start.25 = (bf16[320,2048]{1,0:T(8,128)(2,1)}, bf16[320,2048]{1,0:T(8,128)(2,1)}, u32[]{:S(2)}, u32[]{:S(2)}) collective-permute-start(bf16[320,2048]{1,0:T(8,128)(2,1)} %fusion.13), channel_id=1, source_target_pairs={{1,0},{0,1},{3,2},{2,3},{5,4},{4,5},{7,6},{6,7},{9,8},{8,9},{11,10... | collective-permute-start | bytes 3932168 | tf_op jit(solution)/shard_map/ppermute | solution.py:54
  189.7 30.0 %collective-permute-start.24 = (bf16[320,2048]{1,0:T(8,128)(2,1)}, bf16[320,2048]{1,0:T(8,128)(2,1)}, u32[]{:S(2)}, u32[]{:S(2)}) collective-permute-start(bf16[320,2048]{1,0:T(8,128)(2,1)} %fusion.12), channel_id=1, source_target_pairs={{16,0},{24,8},{0,16},{8,24},{17,1},{25,9},{1,17},{9,25},{18,2},{26... | collective-permute-start | bytes 3932168 | tf_op jit(solution)/shard_map/ppermute | solution.py:54
  192.5 242.8 %reduce-scatter.5.cloned.1.call-start = ((), (), s32[]{:S(2)}) async-start(), calls=%async_computation.13 | async-start | bytes 5242880 | tf_op jit(solution)/shard_map/reduce_scatter | solution.py:79
  240.9 28.1 %collective-permute-start.28 = (bf16[320,2048]{1,0:T(8,128)(2,1)S(1)}, bf16[320,2048]{1,0:T(8,128)(2,1)S(1)}, u32[]{:S(2)}, u32[]{:S(2)}) collective-permute-start(bf16[320,2048]{1,0:T(8,128)(2,1)S(1)} %add_convert_fusion.3.refs_0_), channel_id=1, source_target_pairs={{16,0},{24,8},{0,16},{8,24},{17,1},{25,9},{1,17},{9,25},{18,2},{26... | collective-permute-start | bytes 3932168 | tf_op jit(solution)/shard_map/ppermute | solution.py:54
  241.5 27.8 %collective-permute-start.29 = (bf16[320,2048]{1,0:T(8,128)(2,1)S(1)}, bf16[320,2048]{1,0:T(8,128)(2,1)S(1)}, u32[]{:S(2)}, u32[]{:S(2)}) collective-permute-start(bf16[320,2048]{1,0:T(8,128)(2,1)S(1)} %add_convert_fusion.3.refs_0_), channel_id=1, source_target_pairs={{1,0},{0,1},{3,2},{2,3},{5,4},{4,5},{7,6},{6,7},{9,8},{8,9},{11,10... | collective-permute-start | bytes 3932168 | tf_op jit(solution)/shard_map/ppermute | solution.py:54
  242.9 26.3 %collective-permute-start.30 = (bf16[320,2048]{1,0:T(8,128)(2,1)S(1)}, bf16[320,2048]{1,0:T(8,128)(2,1)S(1)}, u32[]{:S(2)}, u32[]{:S(2)}) collective-permute-start(bf16[320,2048]{1,0:T(8,128)(2,1)S(1)} %add_convert_fusion.3.refs_0_), channel_id=1, source_target_pairs={{8,0},{0,8},{24,16},{16,24},{9,1},{1,9},{25,17},{17,25},{10,2},{2,... | collective-permute-start | bytes 3932168 | tf_op jit(solution)/shard_map/ppermute | solution.py:54
  332.0 31.1 %collective-permute-start.40 = (bf16[320,2048]{1,0:T(8,128)(2,1)}, bf16[320,2048]{1,0:T(8,128)(2,1)}, u32[]{:S(2)}, u32[]{:S(2)}) collective-permute-start(bf16[320,2048]{1,0:T(8,128)(2,1)} %fusion.9), channel_id=1, source_target_pairs={{1,0},{0,1},{3,2},{2,3},{5,4},{4,5},{7,6},{6,7},{9,8},{8,9},{11,10... | collective-permute-start | bytes 3932168 | tf_op jit(solution)/shard_map/ppermute | solution.py:54
  332.8 30.8 %collective-permute-start.39 = (bf16[320,2048]{1,0:T(8,128)(2,1)}, bf16[320,2048]{1,0:T(8,128)(2,1)}, u32[]{:S(2)}, u32[]{:S(2)}) collective-permute-start(bf16[320,2048]{1,0:T(8,128)(2,1)} %fusion.8), channel_id=1, source_target_pairs={{16,0},{24,8},{0,16},{8,24},{17,1},{25,9},{1,17},{9,25},{18,2},{26... | collective-permute-start | bytes 3932168 | tf_op jit(solution)/shard_map/ppermute | solution.py:54
  347.0 163.4 %reduce-scatter.7.cloned.1.call-start = ((), (), s32[]{:S(2)}) async-start(), calls=%async_computation.14 | async-start | bytes 5242880 | tf_op jit(solution)/shard_map/reduce_scatter | solution.py:79
  386.6 28.6 %collective-permute-start.43 = (bf16[320,2048]{1,0:T(8,128)(2,1)S(1)}, bf16[320,2048]{1,0:T(8,128)(2,1)S(1)}, u32[]{:S(2)}, u32[]{:S(2)}) collective-permute-start(bf16[320,2048]{1,0:T(8,128)(2,1)S(1)} %fusion.20.refs_0_), channel_id=1, source_target_pairs={{16,0},{24,8},{0,16},{8,24},{17,1},{25,9},{1,17},{9,25},{18,2},{26... | collective-permute-start | bytes 3932168 | tf_op jit(solution)/shard_map/ppermute | solution.py:54
  387.1 28.3 %collective-permute-start.44 = (bf16[320,2048]{1,0:T(8,128)(2,1)S(1)}, bf16[320,2048]{1,0:T(8,128)(2,1)S(1)}, u32[]{:S(2)}, u32[]{:S(2)}) collective-permute-start(bf16[320,2048]{1,0:T(8,128)(2,1)S(1)} %fusion.20.refs_0_), channel_id=1, source_target_pairs={{1,0},{0,1},{3,2},{2,3},{5,4},{4,5},{7,6},{6,7},{9,8},{8,9},{11,10... | collective-permute-start | bytes 3932168 | tf_op jit(solution)/shard_map/ppermute | solution.py:54
  388.4 27.1 %collective-permute-start.45 = (bf16[320,2048]{1,0:T(8,128)(2,1)S(1)}, bf16[320,2048]{1,0:T(8,128)(2,1)S(1)}, u32[]{:S(2)}, u32[]{:S(2)}) collective-permute-start(bf16[320,2048]{1,0:T(8,128)(2,1)S(1)} %fusion.20.refs_0_), channel_id=1, source_target_pairs={{8,0},{0,8},{24,16},{16,24},{9,1},{1,9},{25,17},{17,25},{10,2},{2,... | collective-permute-start | bytes 3932168 | tf_op jit(solution)/shard_map/ppermute | solution.py:54
  415.5 19.8 %collective-permute-start.50 = (bf16[640,2048]{1,0:T(8,128)(2,1)}, bf16[640,2048]{1,0:T(8,128)(2,1)S(1)}, u32[]{:S(2)}, u32[]{:S(2)}) collective-permute-start(bf16[640,2048]{1,0:T(8,128)(2,1)} %convolution_convert_fusion.11), channel_id=1, source_target_pairs={{8,0},{0,8},{24,16},{16,24},{9,1},{1,9},{25,17},{17,25},{10,2},{2,... | collective-permute-start | bytes 7864328 | tf_op jit(solution)/shard_map/ppermute | solution.py:54
  435.9 139.5 %reduce-scatter.9.cloned.1.call-start = ((), (), s32[]{:S(2)}) async-start(), calls=%async_computation.15 | async-start | bytes 3932160 | tf_op jit(solution)/shard_map/reduce_scatter | solution.py:79
  454.7 35.3 %collective-permute-start.54 = (bf16[320,2048]{1,0:T(8,128)(2,1)}, bf16[320,2048]{1,0:T(8,128)(2,1)S(1)}, u32[]{:S(2)}, u32[]{:S(2)}) collective-permute-start(bf16[320,2048]{1,0:T(8,128)(2,1)} %get-tuple-element.600), channel_id=1, source_target_pairs={{16,0},{24,8},{0,16},{8,24},{17,1},{25,9},{1,17},{9,25},{18,2},{26... | collective-permute-start | bytes 3932168 | tf_op jit(solution)/shard_map/ppermute | solution.py:54
  455.7 34.3 %collective-permute-start.55 = (bf16[320,2048]{1,0:T(8,128)(2,1)S(1)}, bf16[320,2048]{1,0:T(8,128)(2,1)S(1)}, u32[]{:S(2)}, u32[]{:S(2)}) collective-permute-start(bf16[320,2048]{1,0:T(8,128)(2,1)S(1)} %get-tuple-element.599), channel_id=1, source_target_pairs={{1,0},{0,1},{3,2},{2,3},{5,4},{4,5},{7,6},{6,7},{9,8},{8,9},{11,10... | collective-permute-start | bytes 3932168 | tf_op jit(solution)/shard_map/ppermute | solution.py:54
  513.3 43.7 %collective-permute-start.62 = (bf16[640,2048]{1,0:T(8,128)(2,1)}, bf16[640,2048]{1,0:T(8,128)(2,1)}, u32[]{:S(2)}, u32[]{:S(2)}) collective-permute-start(bf16[640,2048]{1,0:T(8,128)(2,1)} %convolution_convert_fusion.6), channel_id=1, source_target_pairs={{8,0},{0,8},{24,16},{16,24},{9,1},{1,9},{25,17},{17,25},{10,2},{2,... | collective-permute-start | bytes 7864328 | tf_op jit(solution)/shard_map/ppermute | solution.py:54
  525.7 30.1 %collective-permute-start.60 = (bf16[320,2048]{1,0:T(8,128)(2,1)}, bf16[320,2048]{1,0:T(8,128)(2,1)S(1)}, u32[]{:S(2)}, u32[]{:S(2)}) collective-permute-start(bf16[320,2048]{1,0:T(8,128)(2,1)} %fusion.10), channel_id=1, source_target_pairs={{16,0},{24,8},{0,16},{8,24},{17,1},{25,9},{1,17},{9,25},{18,2},{26... | collective-permute-start | bytes 3932168 | tf_op jit(solution)/shard_map/ppermute | solution.py:54
  527.2 29.8 %collective-permute-start.61 = (bf16[320,2048]{1,0:T(8,128)(2,1)}, bf16[320,2048]{1,0:T(8,128)(2,1)}, u32[]{:S(2)}, u32[]{:S(2)}) collective-permute-start(bf16[320,2048]{1,0:T(8,128)(2,1)} %fusion.11), channel_id=1, source_target_pairs={{1,0},{0,1},{3,2},{2,3},{5,4},{4,5},{7,6},{6,7},{9,8},{8,9},{11,10... | collective-permute-start | bytes 3932168 | tf_op jit(solution)/shard_map/ppermute | solution.py:54
  579.5 20.5 %all-to-all-start.3 = ((bf16[4,2,64,1024]{3,2,1,0:T(8,128)(2,1)}), bf16[4,2,64,1024]{3,2,1,0:T(8,128)(2,1)S(1)}, u32[]{:S(2)}, u32[]{:S(2)}) async-start(bf16[4,2,64,1024]{3,2,1,0:T(8,128)(2,1)} %shard_map.202), calls=%async_computation.6 | async-start | bytes 2097152 | tf_op jit(solution)/shard_map/all_to_all | solution.py:163
  583.1 46.9 %reduce-scatter.11.cloned.1.call-start = ((), (), s32[]{:S(2)}) async-start(), calls=%async_computation.16 | async-start | bytes 1310720 | tf_op jit(solution)/shard_map/reduce_scatter | solution.py:79
  (143 other events, 1702.8 us)
Sparse Core Ops, SparseCore 0:
  40.0 71.4 all-gather.3
  113.1 81.1 all-gather.5
  195.9 79.2 all-gather.7
  347.2 74.2 reduce-scatter.4
  436.0 74.4 reduce-scatter.6
  512.6 60.7 reduce-scatter.8
  586.2 28.1 reduce-scatter.10

commit v7 on v6

--- a/solution.py
+++ b/solution.py
@@ -246,17 +246,19 @@
 
 
 def sum_dp(parts, hidden):
-    dp = lax.axis_size("dp")
-    count = parts.shape[0]
-    parts = parts.reshape(count, dp, -1).transpose(1, 0, 2)
-    share = parts.shape[2]
-    hidden = jnp.repeat(hidden.reshape(dp // 2, -1), 2, axis=0)
-    both = jnp.concatenate([parts.reshape(dp, -1), hidden], axis=1)
-    both = lax.all_to_all(both, "dp", 0, 0)
-    mine = jnp.arange(dp) % 2 == lax.axis_index("dp") % 2
+    dp, d = lax.axis_size("dp"), lax.axis_index("dp")
+    count, columns = parts.shape
+    parts = parts + flip_y(parts)
+    both = jnp.concatenate([parts.reshape(-1), hidden])
+    bits = 2
+    while bits < dp:
+        both = both + flip("dp", bits, both)
+        bits *= 2
+    units = hidden.shape[0] // (dp // 2)
+    parts, hidden = both[: count * columns].reshape(count, columns), both[count * columns :]
     return (
-        jnp.sum(both[:, : count * share], axis=0).reshape(count, share),
-        jnp.sum(jnp.where(mine[:, None], both[:, count * share :], 0.0), axis=0),
+        lax.dynamic_slice_in_dim(parts, d * (columns // dp), columns // dp, 1),
+        lax.dynamic_slice_in_dim(hidden, (d // 2) * units, units),
     )
 
 
@@ -707,9 +709,8 @@
     qkv_got = exchange(*enter(*qkv_pair))
     out_sum = scatter_z(after(out_term, qkv_sum), 0)
     grad_up = merge_columns(enter(up_got), *up_cut)
-    norms, qkv_got, grad_up = seal(norms, qkv_got, grad_up)
-    norms, hidden_sum = sum_dp(enter(norms), hidden_sum)
-    grad_qkv = merge_columns(enter(qkv_got), *qkv_cut)
+    norms, hidden_sum = sum_dp(norms, hidden_sum)
+    grad_qkv = merge_columns(qkv_got, *qkv_cut)
     out_sum = after(out_sum, norms)
     grad_out = lax.ppermute(out_sum, "dp", [(j, i) for i, j in route]).astype(F32)
     return (

time: 652 us -> 647 us (level)
    ppermute x67 -> x70, starting transfers between devices: 53.5 us -> 57.5 us  [flip(): return lax.ppermute(block, axis, [(i ^ bits, i) for i in range(count)])]
    ppermute x67 -> x70, waiting for transfers between devices: 206 us -> 205 us  [flip(): return lax.ppermute(block, axis, [(i ^ bits, i) for i in range(count)])]
  transfers between devices with their start and end apart: 82 -> 84, of which waited for: 50 -> 52; matrix products, arithmetic and copies ran while one was open for 32% -> 32% of each run, Pallas kernels for 11% -> 12%
where the time goes in v7:
time: 647 us; the launch traced here: 639 us
  waiting for transfers between devices  218 us (34%)
  matrix products  148 us (23%)
  Pallas kernels  102 us (16%)
  starting transfers between devices  82.7 us (13%)
  other arithmetic  44.3 us (7%)
  local copies, waits for them, and re-layouts  28.7 us (4%)
  between operations  16 us (2%)
    ppermute x70, waiting for transfers between devices, flip(): return lax.ppermute(block, axis, [(i ^ bits, i) for i in range(count)])  205 us
    dot_general x12, matrix products, contract_last(): lax.dot_general(left, right, (((1,), (1,)), ((), ())), preferred_element_...  63.9 us
    ppermute x70, starting transfers between devices, flip(): return lax.ppermute(block, axis, [(i ^ bits, i) for i in range(count)])  57.5 us
    dot_general x4, matrix products, contract_first(): lax.dot_general(left, right, (((0,), (0,)), ((), ())), preferred_element_...  47.1 us
    pallas_call x8, Pallas kernels, assemble(): pl.pallas_call(kernel, in_specs=[pl.BlockSpec(memory_space=pl.ANY)] * len...  37.1 us
    dot_general x9, matrix products, times(): return jnp.dot(left, right, preferred_element_type=F32)  37 us
    pallas_call x2, Pallas kernels, attention_call(): pl.pallas_call(kernel, grid_spec=pltpu.PrefetchScalarGridSpec(num_scalar_...  29.2 us
    pallas_call x1, Pallas kernels, hidden_call(): pl.pallas_call(kernel, grid=(count // step,), in_specs=[rows(width), whol...  21.3 us
  transfers between devices with their start and end apart: 84, of which 52 were waited for; matrix products, arithmetic and copies ran while one was open for 32% of the time, Pallas kernels for 12%

profile of v7, /device:TPU:0, one launch (start us, length us, event | category | flops | bytes accessed | tf_op | source)
XLA Modules:
  0.0 639.3 jit_solution(1268508029451692506)
XLA Ops:
  29.5 8.9 %collective-permute-done.4.other_ref = bf16[4,64,768]{2,1,0:T(8,128)(2,1)S(1)} collective-permute-done((bf16[4,64,768]{2,1,0:T(8,128)(2,1)S(1)}, bf16[4,64,768]{2,1,0:T(8,128)(2,1)S(1)}, u32[]{:S(2)}, u32[]{:S(2)}) %collective-permute-start.4) | collective-permute-done | bytes 393248 | tf_op jit(solution)/shard_map/ppermute | solution.py:54
  43.1 26.7 %collective-permute-done.1.refs_1_ = bf16[320,2048]{1,0:T(8,128)(2,1)S(1)} collective-permute-done((bf16[320,2048]{1,0:T(8,128)(2,1)S(1)}, bf16[320,2048]{1,0:T(8,128)(2,1)S(1)}, u32[]{:S(2)}, u32[]{:S(2)}) %collective-permute-start.1) | collective-permute-done | bytes 1310752 | tf_op jit(solution)/shard_map/ppermute | solution.py:54
  76.5 6.4 %shard_map.190.refs_4_ = bf16[2560,2048]{1,0:T(8,128)(2,1)} custom-call(bf16[320,2048]{1,0:T(8,128)(2,1)} %copy-done.25, bf16[320,2048]{1,0:T(8,128)(2,1)} %copy-done.33, bf16[320,2048]{1,0:T(8,128)(2,1)} %copy-done.35, bf16[320,2048]{1,0:T(8,128)(2,1)} %copy-done.42, bf16[320,2048]{1,0:T(8,128)(2,1)} %copy-done.44, ...), custom_call_target="tpu_custom_call" | custom-call | bytes 15728640 | tf_op jit(solution)/shard_map/pallas_call | solution.py:208
  83.0 6.7 %collective-permute-done.5.refs_0_ = bf16[160,2048]{1,0:T(8,128)(2,1)S(1)} collective-permute-done((bf16[160,2048]{1,0:T(8,128)(2,1)}, bf16[160,2048]{1,0:T(8,128)(2,1)S(1)}, u32[]{:S(2)}, u32[]{:S(2)}) %collective-permute-start.5) | collective-permute-done | bytes 655392 | tf_op jit(solution)/shard_map/ppermute | solution.py:54
  106.3 20.5 %collective-permute-done.10.refs_2_ = bf16[320,2048]{1,0:T(8,128)(2,1)} collective-permute-done((bf16[320,2048]{1,0:T(8,128)(2,1)S(1)}, bf16[320,2048]{1,0:T(8,128)(2,1)}, u32[]{:S(2)}, u32[]{:S(2)}) %collective-permute-start.10) | collective-permute-done | bytes 1310752 | tf_op jit(solution)/shard_map/ppermute | solution.py:54
  140.5 13.3 %convolution_convert_fusion.1 = bf16[2560,768]{1,0:T(8,128)(2,1)} fusion(bf16[2560,2048]{1,0:T(8,128)(2,1)} %shard_map.191, bf16[2048,768]{1,0:T(8,128)(2,1)} %bitcast.178), kind=kOutput, calls=%fused_computation.2 | convolution fusion | flops 8055029760 | bytes 17563648 | tf_op jit(solution)/shard_map/dot_general | solution.py:508
  160.1 10.4 %shard_map.192 = (bf16[16,160,256]{2,1,0:T(8,128)(2,1)S(1)}, f32[16,160,256]{2,1,0:T(8,128)S(1)}) custom-call(s32[2,2,8]{2,1,0:T(2,128)S(1)} %reshape.167.places_ref, s32[2,2]{1,0:T(2,128)S(1)} %pad_add_fusion.1.lengths_ref, bf16[16,160,768]{2,1,0:T(8,128)(2,1)} %bitcast.184), custom_call_target="tpu_custom_call" | custom-call | flops 2147483648 | bytes 5242880 | tf_op jit(solution)/shard_map/pallas_call | solution.py:395
  182.0 7.4 %collective-permute-done.23.other_ref = bf16[4,64,1024]{2,1,0:T(8,128)(2,1)S(1)} collective-permute-done((bf16[4,64,1024]{2,1,0:T(8,128)(2,1)S(1)}, bf16[4,64,1024]{2,1,0:T(8,128)(2,1)S(1)}, u32[]{:S(2)}, u32[]{:S(2)}) %collective-permute-start.23) | collective-permute-done | bytes 524320 | tf_op jit(solution)/shard_map/ppermute | solution.py:54
  192.6 6.4 %shard_map.193.refs_4_ = bf16[2560,2048]{1,0:T(8,128)(2,1)} custom-call(bf16[320,2048]{1,0:T(8,128)(2,1)} %bitcast.144, bf16[320,2048]{1,0:T(8,128)(2,1)} %collective-permute-done.9.refs_1_, bf16[320,2048]{1,0:T(8,128)(2,1)} %collective-permute-done.10.refs_2_, bf16[320,2048]{1,0:T(8,128)(2,1)} %collective-permute-done.11.refs_3_, ...), custom_call_target="tpu_custom_call" | custom-call | bytes 15728640 | tf_op jit(solution)/shard_map/pallas_call | solution.py:208
  204.8 14.8 %collective-permute-done.25 = bf16[320,2048]{1,0:T(8,128)(2,1)} collective-permute-done((bf16[320,2048]{1,0:T(8,128)(2,1)}, bf16[320,2048]{1,0:T(8,128)(2,1)}, u32[]{:S(2)}, u32[]{:S(2)}) %collective-permute-start.25) | collective-permute-done | bytes 1310752 | tf_op jit(solution)/shard_map/ppermute | solution.py:54
  229.1 8.9 %collective-permute-done.26 = bf16[160,2048]{1,0:T(8,128)(2,1)S(1)} collective-permute-done((bf16[160,2048]{1,0:T(8,128)(2,1)S(1)}, bf16[160,2048]{1,0:T(8,128)(2,1)S(1)}, u32[]{:S(2)}, u32[]{:S(2)}) %collective-permute-start.26) | collective-permute-done | bytes 655392 | tf_op jit(solution)/shard_map/ppermute | solution.py:54
  243.6 14.5 %fusion.60.grad_ref = f32[2560,1024]{1,0:T(8,128)} fusion(bf16[2560,2048]{1,0:T(8,128)(2,1)S(1)} %bitcast.135, bf16[1024,2048]{1,0:T(8,128)(2,1)S(1)} %copy-done.75), kind=kOutput, calls=%fused_computation.138 | convolution fusion | flops 10737418240 | bytes 25165824 | tf_op jit(solution)/shard_map/dot_general | solution.py:41
  258.1 10.9 %collective-permute-done.28.refs_1_ = bf16[320,2048]{1,0:T(8,128)(2,1)S(1)} collective-permute-done((bf16[320,2048]{1,0:T(8,128)(2,1)S(1)}, bf16[320,2048]{1,0:T(8,128)(2,1)S(1)}, u32[]{:S(2)}, u32[]{:S(2)}) %collective-permute-start.28) | collective-permute-done | bytes 1310752 | tf_op jit(solution)/shard_map/ppermute | solution.py:54
  274.9 6.4 %shard_map.195.refs_4_ = bf16[2560,2048]{1,0:T(8,128)(2,1)} custom-call(bf16[320,2048]{1,0:T(8,128)(2,1)} %copy-done.26, bf16[320,2048]{1,0:T(8,128)(2,1)} %copy-done.32, bf16[320,2048]{1,0:T(8,128)(2,1)} %copy-done.34, bf16[320,2048]{1,0:T(8,128)(2,1)} %copy-done.41, bf16[320,2048]{1,0:T(8,128)(2,1)} %copy-done.45, ...), custom_call_target="tpu_custom_call" | custom-call | bytes 15728640 | tf_op jit(solution)/shard_map/pallas_call | solution.py:208
  281.3 6.5 %collective-permute-done.31.refs_0_ = bf16[160,2048]{1,0:T(8,128)(2,1)S(1)} collective-permute-done((bf16[160,2048]{1,0:T(8,128)(2,1)}, bf16[160,2048]{1,0:T(8,128)(2,1)S(1)}, u32[]{:S(2)}, u32[]{:S(2)}) %collective-permute-start.31) | collective-permute-done | bytes 655392 | tf_op jit(solution)/shard_map/ppermute | solution.py:54
  294.7 21.3 %shard_map.198 = (bf16[2560,1024]{1,0:T(8,128)(2,1)S(1)}, bf16[2560,1024]{1,0:T(8,128)(2,1)}) custom-call(bf16[2560,2048]{1,0:T(8,128)(2,1)} %shard_map.197.second_ref, bf16[2048,1024]{1,0:T(8,128)(2,1)S(1)} %bitcast.124, f32[1,1024]{1,0:T(1,128)S(1)} %bitcast.122, f32[2560,1024]{1,0:T(8,128)} %fusion.60.grad_ref), custom_call_target="tpu_custom_call" | custom-call | flops 10737418240 | bytes 35651584 | tf_op jit(solution)/shard_map/pallas_call | solution.py:435
  316.0 5.6 convolution_convert_fusion.13
  334.2 12.8 %convolution_convert_fusion.3 = bf16[1024,2048]{1,0:T(8,128)(2,1)} fusion(bf16[2560,1024]{1,0:T(8,128)(2,1)S(1)} %get-tuple-element.459, bf16[2560,2048]{1,0:T(8,128)(2,1)S(1)} %bitcast.137), kind=kOutput, calls=%fused_computation.6 | convolution fusion | flops 10739515392 | bytes 19922944 | tf_op jit(solution)/shard_map/dot_general | solution.py:47
  347.0 5.5 fusion.23
  352.5 10.6 %collective-permute-done.40 = bf16[320,2048]{1,0:T(8,128)(2,1)} collective-permute-done((bf16[320,2048]{1,0:T(8,128)(2,1)}, bf16[320,2048]{1,0:T(8,128)(2,1)}, u32[]{:S(2)}, u32[]{:S(2)}) %collective-permute-start.40) | collective-permute-done | bytes 1310752 | tf_op jit(solution)/shard_map/ppermute | solution.py:54
  368.7 7.3 %convolution_convert_fusion = bf16[1280,2048]{1,0:T(8,128)(2,1)} fusion(bf16[1024,2048]{1,0:T(8,128)(2,1)S(1)} %copy-done.76, bf16[2560,1024]{1,0:T(8,128)(2,1)S(1)} %copy-done.10), kind=kOutput, calls=%fused_computation.1 | convolution fusion | flops 5371330560 | bytes 12058624 | tf_op jit(solution)/shard_map/dot_general | solution.py:508
  388.9 15.4 %convolution_convert_fusion.4 = bf16[2048,1024]{1,0:T(8,128)(2,1)} fusion(bf16[2560,2048]{1,0:T(8,128)(2,1)S(1)} %bitcast.133, bf16[2560,1024]{1,0:T(8,128)(2,1)} %get-tuple-element.512), kind=kOutput, calls=%fused_computation.7 | convolution fusion | flops 10739515392 | bytes 19922944 | tf_op jit(solution)/shard_map/dot_general | solution.py:47
  408.5 7.2 %collective-permute-done.43.refs_1_ = bf16[320,2048]{1,0:T(8,128)(2,1)S(1)} collective-permute-done((bf16[320,2048]{1,0:T(8,128)(2,1)S(1)}, bf16[320,2048]{1,0:T(8,128)(2,1)S(1)}, u32[]{:S(2)}, u32[]{:S(2)}) %collective-permute-start.43) | collective-permute-done | bytes 1310752 | tf_op jit(solution)/shard_map/ppermute | solution.py:54
  425.8 6.4 %shard_map.199.refs_4_ = bf16[2560,2048]{1,0:T(8,128)(2,1)} custom-call(bf16[320,2048]{1,0:T(8,128)(2,1)} %copy-done.27, bf16[320,2048]{1,0:T(8,128)(2,1)} %copy-done.30, bf16[320,2048]{1,0:T(8,128)(2,1)} %copy-done.31, bf16[320,2048]{1,0:T(8,128)(2,1)} %copy-done.40, bf16[320,2048]{1,0:T(8,128)(2,1)} %copy-done.43, ...), custom_call_target="tpu_custom_call" | custom-call | bytes 15728640 | tf_op jit(solution)/shard_map/pallas_call | solution.py:208
  445.1 7.9 %convolution_convert_fusion.2 = bf16[2560,256]{1,0:T(8,128)(2,1)S(1)} fusion(bf16[2560,2048]{1,0:T(8,128)(2,1)} %shard_map.200, bf16[256,2048]{1,0:T(8,128)(2,1)S(1)} %bitcast.143), kind=kOutput, calls=%fused_computation.5 | convolution fusion | flops 2685009920 | bytes 12845056 | tf_op jit(solution)/shard_map/dot_general | solution.py:41
  456.8 18.7 %shard_map.201 = bf16[16,160,768]{2,1,0:T(8,128)(2,1)} custom-call(s32[2,2,8]{2,1,0:T(2,128)S(1)} %reshape.167.places_ref, s32[2,2]{1,0:T(2,128)S(1)} %copy-done.5, bf16[16,160,768]{2,1,0:T(8,128)(2,1)} %bitcast.185, bf16[16,160,256]{2,1,0:T(8,128)(2,1)S(1)} %bitcast.129, f32[16,160,256]{2,1,0:T(8,128)S(1)} %copy-done.8), custom_call_target="tpu_custom_call" | custom-call | flops 5368709120 | bytes 5242880 | tf_op jit(solution)/shard_map/pallas_call | solution.py:395
  475.5 15.1 %convolution_convert_fusion.5 = bf16[2048,768]{1,0:T(8,128)(2,1)} fusion(bf16[2560,2048]{1,0:T(8,128)(2,1)} %shard_map.191, bf16[2560,768]{1,0:T(8,128)(2,1)} %bitcast.186), kind=kOutput, calls=%fused_computation.8 | convolution fusion | flops 8054636544 | bytes 17563648 | tf_op jit(solution)/shard_map/dot_general | solution.py:47
  502.0 6.5 %collective-permute-done.56 = bf16[160,2048]{1,0:T(8,128)(2,1)S(1)} collective-permute-done((bf16[160,2048]{1,0:T(8,128)(2,1)S(1)}, bf16[160,2048]{1,0:T(8,128)(2,1)S(1)}, u32[]{:S(2)}, u32[]{:S(2)}) %collective-permute-start.56) | collective-permute-done | bytes 655392 | tf_op jit(solution)/shard_map/ppermute | solution.py:54
  542.7 13.7 %collective-permute-done.60 = bf16[320,2048]{1,0:T(8,128)(2,1)S(1)} collective-permute-done((bf16[320,2048]{1,0:T(8,128)(2,1)}, bf16[320,2048]{1,0:T(8,128)(2,1)S(1)}, u32[]{:S(2)}, u32[]{:S(2)}) %collective-permute-start.60) | collective-permute-done | bytes 1310752 | tf_op jit(solution)/shard_map/ppermute | solution.py:54
  567.5 7.8 %collective-permute-done.63 = bf16[160,2048]{1,0:T(8,128)(2,1)S(1)} collective-permute-done((bf16[160,2048]{1,0:T(8,128)(2,1)S(1)}, bf16[160,2048]{1,0:T(8,128)(2,1)S(1)}, u32[]{:S(2)}, u32[]{:S(2)}) %collective-permute-start.63) | collective-permute-done | bytes 655392 | tf_op jit(solution)/shard_map/ppermute | solution.py:54
  589.7 5.0 add_convert_fusion
  594.8 5.0 collective-permute-done.65.other_ref
  (467 shorter events, 282.8 us)
Async XLA Ops:
  15.3 118.1 %all-gather.4.cloned.1.call-start = ((), (), s32[]{:S(2)}) async-start(), calls=%async_computation.9 | async-start | bytes 3932160 | tf_op jit(solution)/shard_map/all_gather | solution.py:75
  39.9 29.8 %collective-permute-start.1 = (bf16[320,2048]{1,0:T(8,128)(2,1)S(1)}, bf16[320,2048]{1,0:T(8,128)(2,1)S(1)}, u32[]{:S(2)}, u32[]{:S(2)}) collective-permute-start(bf16[320,2048]{1,0:T(8,128)(2,1)S(1)} %fusion.15.refs_0_), channel_id=1, source_target_pairs={{16,0},{24,8},{0,16},{8,24},{17,1},{25,9},{1,17},{9,25},{18,2},{26... | collective-permute-start | bytes 3932168 | tf_op jit(solution)/shard_map/ppermute | solution.py:54
  41.3 29.1 %collective-permute-start.2 = (bf16[320,2048]{1,0:T(8,128)(2,1)S(1)}, bf16[320,2048]{1,0:T(8,128)(2,1)S(1)}, u32[]{:S(2)}, u32[]{:S(2)}) collective-permute-start(bf16[320,2048]{1,0:T(8,128)(2,1)S(1)} %fusion.15.refs_0_), channel_id=1, source_target_pairs={{1,0},{0,1},{3,2},{2,3},{5,4},{4,5},{7,6},{6,7},{9,8},{8,9},{11,10... | collective-permute-start | bytes 3932168 | tf_op jit(solution)/shard_map/ppermute | solution.py:54
  43.1 27.4 %collective-permute-start.3 = (bf16[320,2048]{1,0:T(8,128)(2,1)S(1)}, bf16[320,2048]{1,0:T(8,128)(2,1)S(1)}, u32[]{:S(2)}, u32[]{:S(2)}) collective-permute-start(bf16[320,2048]{1,0:T(8,128)(2,1)S(1)} %fusion.15.refs_0_), channel_id=1, source_target_pairs={{8,0},{0,8},{24,16},{16,24},{9,1},{1,9},{25,17},{17,25},{10,2},{2,... | collective-permute-start | bytes 3932168 | tf_op jit(solution)/shard_map/ppermute | solution.py:54
  93.0 40.4 %all-to-all-start.1 = ((bf16[4,64,2048]{2,1,0:T(8,128)(2,1)}), bf16[4,64,2048]{2,1,0:T(8,128)(2,1)S(1)}, u32[]{:S(2)}, u32[]{:S(2)}) async-start(bf16[4,64,2048]{2,1,0:T(8,128)(2,1)} %broadcast_in_dim.52), calls=%async_computation.1 | async-start | bytes 2097152 | tf_op jit(solution)/shard_map/all_to_all | solution.py:535
  97.7 107.2 %all-gather.6.cloned.1.call-start = ((), (), s32[]{:S(2)}) async-start(), calls=%async_computation.10 | async-start | bytes 5242880 | tf_op jit(solution)/shard_map/all_gather | solution.py:75
  97.7 29.2 %collective-permute-start.10 = (bf16[320,2048]{1,0:T(8,128)(2,1)S(1)}, bf16[320,2048]{1,0:T(8,128)(2,1)}, u32[]{:S(2)}, u32[]{:S(2)}) collective-permute-start(bf16[320,2048]{1,0:T(8,128)(2,1)S(1)} %bitcast.146), channel_id=1, source_target_pairs={{1,0},{0,1},{3,2},{2,3},{5,4},{4,5},{7,6},{6,7},{9,8},{8,9},{11,10... | collective-permute-start | bytes 3932168 | tf_op jit(solution)/shard_map/ppermute | solution.py:54
  98.5 28.4 %collective-permute-start.11 = (bf16[320,2048]{1,0:T(8,128)(2,1)S(1)}, bf16[320,2048]{1,0:T(8,128)(2,1)}, u32[]{:S(2)}, u32[]{:S(2)}) collective-permute-start(bf16[320,2048]{1,0:T(8,128)(2,1)S(1)} %bitcast.147), channel_id=1, source_target_pairs={{8,0},{0,8},{24,16},{16,24},{9,1},{1,9},{25,17},{17,25},{10,2},{2,... | collective-permute-start | bytes 3932168 | tf_op jit(solution)/shard_map/ppermute | solution.py:54
  98.5 31.3 %collective-permute-start.9 = (bf16[320,2048]{1,0:T(8,128)(2,1)S(1)}, bf16[320,2048]{1,0:T(8,128)(2,1)}, u32[]{:S(2)}, u32[]{:S(2)}) collective-permute-start(bf16[320,2048]{1,0:T(8,128)(2,1)S(1)} %bitcast.148), channel_id=1, source_target_pairs={{16,0},{24,8},{0,16},{8,24},{17,1},{25,9},{1,17},{9,25},{18,2},{26... | collective-permute-start | bytes 3932168 | tf_op jit(solution)/shard_map/ppermute | solution.py:54
  134.9 20.1 %collective-permute-start.16 = (bf16[320,2048]{1,0:T(8,128)(2,1)}, bf16[320,2048]{1,0:T(8,128)(2,1)}, u32[]{:S(2)}, u32[]{:S(2)}) collective-permute-start(bf16[320,2048]{1,0:T(8,128)(2,1)} %collective-permute-done.9.refs_1_), channel_id=1, source_target_pairs={{8,0},{0,8},{24,16},{16,24},{9,1},{1,9},{25,17},{17,25},{10,2},{2,... | collective-permute-start | bytes 3932168 | tf_op jit(solution)/shard_map/ppermute | solution.py:54
  158.6 130.1 %all-gather.8.cloned.1.call-start = ((), (), s32[]{:S(2)}) async-start(), calls=%async_computation.11 | async-start | bytes 5242880 | tf_op jit(solution)/shard_map/all_gather | solution.py:75
  189.4 30.3 %collective-permute-start.25 = (bf16[320,2048]{1,0:T(8,128)(2,1)}, bf16[320,2048]{1,0:T(8,128)(2,1)}, u32[]{:S(2)}, u32[]{:S(2)}) collective-permute-start(bf16[320,2048]{1,0:T(8,128)(2,1)} %fusion.13), channel_id=1, source_target_pairs={{1,0},{0,1},{3,2},{2,3},{5,4},{4,5},{7,6},{6,7},{9,8},{8,9},{11,10... | collective-permute-start | bytes 3932168 | tf_op jit(solution)/shard_map/ppermute | solution.py:54
  189.7 30.0 %collective-permute-start.24 = (bf16[320,2048]{1,0:T(8,128)(2,1)}, bf16[320,2048]{1,0:T(8,128)(2,1)}, u32[]{:S(2)}, u32[]{:S(2)}) collective-permute-start(bf16[320,2048]{1,0:T(8,128)(2,1)} %fusion.12), channel_id=1, source_target_pairs={{16,0},{24,8},{0,16},{8,24},{17,1},{25,9},{1,17},{9,25},{18,2},{26... | collective-permute-start | bytes 3932168 | tf_op jit(solution)/shard_map/ppermute | solution.py:54
  192.5 243.3 %reduce-scatter.5.cloned.1.call-start = ((), (), s32[]{:S(2)}) async-start(), calls=%async_computation.12 | async-start | bytes 5242880 | tf_op jit(solution)/shard_map/reduce_scatter | solution.py:79
  240.9 28.1 %collective-permute-start.28 = (bf16[320,2048]{1,0:T(8,128)(2,1)S(1)}, bf16[320,2048]{1,0:T(8,128)(2,1)S(1)}, u32[]{:S(2)}, u32[]{:S(2)}) collective-permute-start(bf16[320,2048]{1,0:T(8,128)(2,1)S(1)} %add_convert_fusion.3.refs_0_), channel_id=1, source_target_pairs={{16,0},{24,8},{0,16},{8,24},{17,1},{25,9},{1,17},{9,25},{18,2},{26... | collective-permute-start | bytes 3932168 | tf_op jit(solution)/shard_map/ppermute | solution.py:54
  241.5 27.8 %collective-permute-start.29 = (bf16[320,2048]{1,0:T(8,128)(2,1)S(1)}, bf16[320,2048]{1,0:T(8,128)(2,1)S(1)}, u32[]{:S(2)}, u32[]{:S(2)}) collective-permute-start(bf16[320,2048]{1,0:T(8,128)(2,1)S(1)} %add_convert_fusion.3.refs_0_), channel_id=1, source_target_pairs={{1,0},{0,1},{3,2},{2,3},{5,4},{4,5},{7,6},{6,7},{9,8},{8,9},{11,10... | collective-permute-start | bytes 3932168 | tf_op jit(solution)/shard_map/ppermute | solution.py:54
  242.9 26.3 %collective-permute-start.30 = (bf16[320,2048]{1,0:T(8,128)(2,1)S(1)}, bf16[320,2048]{1,0:T(8,128)(2,1)S(1)}, u32[]{:S(2)}, u32[]{:S(2)}) collective-permute-start(bf16[320,2048]{1,0:T(8,128)(2,1)S(1)} %add_convert_fusion.3.refs_0_), channel_id=1, source_target_pairs={{8,0},{0,8},{24,16},{16,24},{9,1},{1,9},{25,17},{17,25},{10,2},{2,... | collective-permute-start | bytes 3932168 | tf_op jit(solution)/shard_map/ppermute | solution.py:54
  332.0 31.1 %collective-permute-start.40 = (bf16[320,2048]{1,0:T(8,128)(2,1)}, bf16[320,2048]{1,0:T(8,128)(2,1)}, u32[]{:S(2)}, u32[]{:S(2)}) collective-permute-start(bf16[320,2048]{1,0:T(8,128)(2,1)} %fusion.9), channel_id=1, source_target_pairs={{1,0},{0,1},{3,2},{2,3},{5,4},{4,5},{7,6},{6,7},{9,8},{8,9},{11,10... | collective-permute-start | bytes 3932168 | tf_op jit(solution)/shard_map/ppermute | solution.py:54
  332.7 30.8 %collective-permute-start.39 = (bf16[320,2048]{1,0:T(8,128)(2,1)}, bf16[320,2048]{1,0:T(8,128)(2,1)}, u32[]{:S(2)}, u32[]{:S(2)}) collective-permute-start(bf16[320,2048]{1,0:T(8,128)(2,1)} %fusion.8), channel_id=1, source_target_pairs={{16,0},{24,8},{0,16},{8,24},{17,1},{25,9},{1,17},{9,25},{18,2},{26... | collective-permute-start | bytes 3932168 | tf_op jit(solution)/shard_map/ppermute | solution.py:54
  347.0 164.1 %reduce-scatter.7.cloned.1.call-start = ((), (), s32[]{:S(2)}) async-start(), calls=%async_computation.13 | async-start | bytes 5242880 | tf_op jit(solution)/shard_map/reduce_scatter | solution.py:79
  387.1 28.6 %collective-permute-start.43 = (bf16[320,2048]{1,0:T(8,128)(2,1)S(1)}, bf16[320,2048]{1,0:T(8,128)(2,1)S(1)}, u32[]{:S(2)}, u32[]{:S(2)}) collective-permute-start(bf16[320,2048]{1,0:T(8,128)(2,1)S(1)} %fusion.20.refs_0_), channel_id=1, source_target_pairs={{16,0},{24,8},{0,16},{8,24},{17,1},{25,9},{1,17},{9,25},{18,2},{26... | collective-permute-start | bytes 3932168 | tf_op jit(solution)/shard_map/ppermute | solution.py:54
  387.7 28.3 %collective-permute-start.44 = (bf16[320,2048]{1,0:T(8,128)(2,1)S(1)}, bf16[320,2048]{1,0:T(8,128)(2,1)S(1)}, u32[]{:S(2)}, u32[]{:S(2)}) collective-permute-start(bf16[320,2048]{1,0:T(8,128)(2,1)S(1)} %fusion.20.refs_0_), channel_id=1, source_target_pairs={{1,0},{0,1},{3,2},{2,3},{5,4},{4,5},{7,6},{6,7},{9,8},{8,9},{11,10... | collective-permute-start | bytes 3932168 | tf_op jit(solution)/shard_map/ppermute | solution.py:54
  388.9 27.1 %collective-permute-start.45 = (bf16[320,2048]{1,0:T(8,128)(2,1)S(1)}, bf16[320,2048]{1,0:T(8,128)(2,1)S(1)}, u32[]{:S(2)}, u32[]{:S(2)}) collective-permute-start(bf16[320,2048]{1,0:T(8,128)(2,1)S(1)} %fusion.20.refs_0_), channel_id=1, source_target_pairs={{8,0},{0,8},{24,16},{16,24},{9,1},{1,9},{25,17},{17,25},{10,2},{2,... | collective-permute-start | bytes 3932168 | tf_op jit(solution)/shard_map/ppermute | solution.py:54
  416.0 19.8 %collective-permute-start.50 = (bf16[640,2048]{1,0:T(8,128)(2,1)}, bf16[640,2048]{1,0:T(8,128)(2,1)S(1)}, u32[]{:S(2)}, u32[]{:S(2)}) collective-permute-start(bf16[640,2048]{1,0:T(8,128)(2,1)} %convolution_convert_fusion.11), channel_id=1, source_target_pairs={{8,0},{0,8},{24,16},{16,24},{9,1},{1,9},{25,17},{17,25},{10,2},{2,... | collective-permute-start | bytes 7864328 | tf_op jit(solution)/shard_map/ppermute | solution.py:54
  436.4 139.3 %reduce-scatter.9.cloned.1.call-start = ((), (), s32[]{:S(2)}) async-start(), calls=%async_computation.14 | async-start | bytes 3932160 | tf_op jit(solution)/shard_map/reduce_scatter | solution.py:79
  455.1 35.4 %collective-permute-start.54 = (bf16[320,2048]{1,0:T(8,128)(2,1)}, bf16[320,2048]{1,0:T(8,128)(2,1)S(1)}, u32[]{:S(2)}, u32[]{:S(2)}) collective-permute-start(bf16[320,2048]{1,0:T(8,128)(2,1)} %get-tuple-element.588), channel_id=1, source_target_pairs={{16,0},{24,8},{0,16},{8,24},{17,1},{25,9},{1,17},{9,25},{18,2},{26... | collective-permute-start | bytes 3932168 | tf_op jit(solution)/shard_map/ppermute | solution.py:54
  456.1 34.5 %collective-permute-start.55 = (bf16[320,2048]{1,0:T(8,128)(2,1)S(1)}, bf16[320,2048]{1,0:T(8,128)(2,1)S(1)}, u32[]{:S(2)}, u32[]{:S(2)}) collective-permute-start(bf16[320,2048]{1,0:T(8,128)(2,1)S(1)} %get-tuple-element.587), channel_id=1, source_target_pairs={{1,0},{0,1},{3,2},{2,3},{5,4},{4,5},{7,6},{6,7},{9,8},{8,9},{11,10... | collective-permute-start | bytes 3932168 | tf_op jit(solution)/shard_map/ppermute | solution.py:54
  509.2 113.6 %reduce-scatter.11.cloned.1.call-start = ((), (), s32[]{:S(2)}) async-start(), calls=%async_computation.15 | async-start | bytes 1310720 | tf_op jit(solution)/shard_map/reduce_scatter | solution.py:79
  514.0 43.7 %collective-permute-start.62 = (bf16[640,2048]{1,0:T(8,128)(2,1)}, bf16[640,2048]{1,0:T(8,128)(2,1)}, u32[]{:S(2)}, u32[]{:S(2)}) collective-permute-start(bf16[640,2048]{1,0:T(8,128)(2,1)} %convolution_convert_fusion.6), channel_id=1, source_target_pairs={{8,0},{0,8},{24,16},{16,24},{9,1},{1,9},{25,17},{17,25},{10,2},{2,... | collective-permute-start | bytes 7864328 | tf_op jit(solution)/shard_map/ppermute | solution.py:54
  526.3 30.1 %collective-permute-start.60 = (bf16[320,2048]{1,0:T(8,128)(2,1)}, bf16[320,2048]{1,0:T(8,128)(2,1)S(1)}, u32[]{:S(2)}, u32[]{:S(2)}) collective-permute-start(bf16[320,2048]{1,0:T(8,128)(2,1)} %fusion.10), channel_id=1, source_target_pairs={{16,0},{24,8},{0,16},{8,24},{17,1},{25,9},{1,17},{9,25},{18,2},{26... | collective-permute-start | bytes 3932168 | tf_op jit(solution)/shard_map/ppermute | solution.py:54
  527.9 29.8 %collective-permute-start.61 = (bf16[320,2048]{1,0:T(8,128)(2,1)}, bf16[320,2048]{1,0:T(8,128)(2,1)}, u32[]{:S(2)}, u32[]{:S(2)}) collective-permute-start(bf16[320,2048]{1,0:T(8,128)(2,1)} %fusion.11), channel_id=1, source_target_pairs={{1,0},{0,1},{3,2},{2,3},{5,4},{4,5},{7,6},{6,7},{9,8},{8,9},{11,10... | collective-permute-start | bytes 3932168 | tf_op jit(solution)/shard_map/ppermute | solution.py:54
  610.7 19.1 %all-to-all-start.4 = ((bf16[4,2,64,768]{3,2,1,0:T(8,128)(2,1)}), bf16[4,2,64,768]{3,2,1,0:T(8,128)(2,1)S(1)}, u32[]{:S(2)}, u32[]{:S(2)}) async-start(bf16[4,2,64,768]{3,2,1,0:T(8,128)(2,1)} %shard_map.203), calls=%async_computation.7 | async-start | bytes 1572864 | tf_op jit(solution)/shard_map/all_to_all | solution.py:163
  (149 other events, 1753.2 us)
Sparse Core Ops, SparseCore 0:
  40.0 71.4 all-gather.3
  113.1 81.1 all-gather.5
  195.9 79.2 all-gather.7
  347.1 74.2 reduce-scatter.4
  436.5 74.5 reduce-scatter.6
  513.3 60.7 reduce-scatter.8
  578.5 27.6 reduce-scatter.10

commit v8 on v7

--- a/solution.py
+++ b/solution.py
@@ -542,13 +542,15 @@
     cot_across = diagonal_of(cot_x, cot_y)
     cot_others = cot_core, flip_core(cot_x), flip_core(cot_y)
     projected = times(normed_all, qkv_full).astype(BF16)
-    cot_across, cot_others, projected, lengths = seal(
-        cot_across, cot_others, projected, flip_y(enter(seq_lengths))
+    up_pair = enter(up_pair)
+    cot_across, cot_others, projected, up_other, lengths = seal(
+        cot_across, cot_others, projected, flip_y(up_pair[:, 0]), flip_y(enter(seq_lengths))
     )
     lengths = jnp.concatenate([seq_lengths, lengths], axis=0)
 
-    projected, up_pair, cot_across = enter(projected, up_pair, cot_across)
-    up_pair = lax.all_to_all(up_pair, "blk", 0, 0)
+    projected, up_own, up_other, cot_across = enter(projected, up_pair[:, 1], up_other, cot_across)
+    up_part = exchange(up_own, up_other).reshape(blk, 2 * shard, lanes * units)
+    up_full = gather_z(after(up_part, qkv_full), 1).reshape(width, lanes * units)
     attended_low, log_total = attention_call(
         attention_forward_kernel,
         [projected],
@@ -559,8 +561,7 @@
         2,
     )
     cot_others = [*cot_others, *[flip_core(piece) for piece in cot_across]]
-    attended_low, up_pair, cot_others = seal(attended_low, up_pair, cot_others)
-    up_pair = enter(up_pair)
+    attended_low, up_part, cot_others = seal(attended_low, up_part, cot_others)
 
     def start_sum(left, multiply, *beside):
         left = enter(left)
@@ -573,11 +574,7 @@
         to_x, to_y, near, beside = seal(to_x, to_y, near, beside)
         return enter(to_x), enter(to_y), near, beside
 
-    to_x, to_y, near, (up_other,) = start_sum(
-        attended_low, lambda v: times(v, out_full), flip_y(up_pair[:, 0])
-    )
-    up_part = join_y(*enter(up_pair[:, 1], up_other)).reshape(blk, 2 * shard, lanes * units)
-    up_full = gather_z(after(up_part, qkv_full), 1).reshape(width, lanes * units)
+    to_x, to_y, near, _ = start_sum(attended_low, lambda v: times(v, out_full))
     own = times(rows_of(enter(attended_low), 0, 4), out_full)
     cot_all = assemble(enter(*[cot_low, cot_x, cot_y, *cot_others[:3]]), MOST)
     cot_all = assemble(enter(*[*cot_across, *cot_others[3:]]), REST, cot_all)

time: 647 us -> 675 us (1.043)
  waiting for transfers between devices: 218 us -> 243 us
    ppermute x70, waiting for transfers between devices: 205 us -> 231 us  [flip(): return lax.ppermute(block, axis, [(i ^ bits, i) for i in range(count)])]
  transfers between devices with their start and end apart: 84 -> 84, of which waited for: 52 -> 53; matrix products, arithmetic and copies ran while one was open for 32% -> 31% of each run, Pallas kernels for 12% -> 11%
where the time goes in v8:
time: 675 us; the launch traced here: 667 us
  waiting for transfers between devices  243 us (36%)
  matrix products  148 us (22%)
  Pallas kernels  98.9 us (15%)
  starting transfers between devices  83.1 us (12%)
  other arithmetic  45.4 us (7%)
  local copies, waits for them, and re-layouts  33.4 us (5%)
  between operations  16 us (2%)
    ppermute x70, waiting for transfers between devices, flip(): return lax.ppermute(block, axis, [(i ^ bits, i) for i in range(count)])  231 us
    dot_general x12, matrix products, contract_last(): lax.dot_general(left, right, (((1,), (1,)), ((), ())), preferred_element_...  64.4 us
    ppermute x70, starting transfers between devices, flip(): return lax.ppermute(block, axis, [(i ^ bits, i) for i in range(count)])  57.7 us
    dot_general x4, matrix products, contract_first(): lax.dot_general(left, right, (((0,), (0,)), ((), ())), preferred_element_...  47 us
    pallas_call x8, Pallas kernels, assemble(): pl.pallas_call(kernel, in_specs=[pl.BlockSpec(memory_space=pl.ANY)] * len...  36.8 us
    dot_general x9, matrix products, times(): return jnp.dot(left, right, preferred_element_type=F32)  36.1 us
    pallas_call x2, Pallas kernels, attention_call(): pl.pallas_call(kernel, grid_spec=pltpu.PrefetchScalarGridSpec(num_scalar_...  29 us
    pallas_call x1, Pallas kernels, hidden_call(): pl.pallas_call(kernel, grid=(count // step,), in_specs=[rows(width), whol...  21.3 us
  transfers between devices with their start and end apart: 84, of which 53 were waited for; matrix products, arithmetic and copies ran while one was open for 31% of the time, Pallas kernels for 11%

profile of v8, /device:TPU:0, one launch (start us, length us, event | category | flops | bytes accessed | tf_op | source)
XLA Modules:
  0.0 667.4 jit_solution(16454276876126791480)
XLA Ops:
  22.3 5.3 all-to-all-done
  31.3 8.9 %collective-permute-done.4.other_ref = bf16[4,64,768]{2,1,0:T(8,128)(2,1)S(1)} collective-permute-done((bf16[4,64,768]{2,1,0:T(8,128)(2,1)S(1)}, bf16[4,64,768]{2,1,0:T(8,128)(2,1)S(1)}, u32[]{:S(2)}, u32[]{:S(2)}) %collective-permute-start.4) | collective-permute-done | bytes 393248 | tf_op jit(solution)/shard_map/ppermute | solution.py:54
  44.8 26.7 %collective-permute-done.1.refs_1_ = bf16[320,2048]{1,0:T(8,128)(2,1)S(1)} collective-permute-done((bf16[320,2048]{1,0:T(8,128)(2,1)S(1)}, bf16[320,2048]{1,0:T(8,128)(2,1)S(1)}, u32[]{:S(2)}, u32[]{:S(2)}) %collective-permute-start.1) | collective-permute-done | bytes 1310752 | tf_op jit(solution)/shard_map/ppermute | solution.py:54
  79.4 6.4 shard_map.190.refs_4_
  85.9 5.8 collective-permute-done.5.refs_0_
  108.2 20.6 %collective-permute-done.10.refs_2_ = bf16[320,2048]{1,0:T(8,128)(2,1)} collective-permute-done((bf16[320,2048]{1,0:T(8,128)(2,1)S(1)}, bf16[320,2048]{1,0:T(8,128)(2,1)}, u32[]{:S(2)}, u32[]{:S(2)}) %collective-permute-start.10) | collective-permute-done | bytes 1310752 | tf_op jit(solution)/shard_map/ppermute | solution.py:54
  142.2 24.2 %collective-permute-done.19 = s32[1,2]{1,0:T(1,128)S(1)} collective-permute-done((s32[1,2]{1,0:T(1,128)S(1)}, s32[1,2]{1,0:T(1,128)S(1)}, u32[]{:S(2)}, u32[]{:S(2)}) %collective-permute-start.19) | collective-permute-done | bytes 40 | tf_op jit(solution)/shard_map/ppermute | solution.py:54
  168.1 12.4 %convolution_convert_fusion.1 = bf16[2560,768]{1,0:T(8,128)(2,1)} fusion(bf16[2560,2048]{1,0:T(8,128)(2,1)} %shard_map.191, bf16[2048,768]{1,0:T(8,128)(2,1)S(1)} %bitcast.180), kind=kOutput, calls=%fused_computation.2 | convolution fusion | flops 8055029760 | bytes 17563648 | tf_op jit(solution)/shard_map/dot_general | solution.py:508
  189.3 10.5 %shard_map.192 = (bf16[16,160,256]{2,1,0:T(8,128)(2,1)S(1)}, f32[16,160,256]{2,1,0:T(8,128)S(1)}) custom-call(s32[2,2,8]{2,1,0:T(2,128)S(1)} %reshape.167.places_ref, s32[2,2]{1,0:T(2,128)S(1)} %pad_add_fusion.1.lengths_ref, bf16[16,160,768]{2,1,0:T(8,128)(2,1)} %bitcast.185), custom_call_target="tpu_custom_call" | custom-call | flops 2147483648 | bytes 5242880 | tf_op jit(solution)/shard_map/pallas_call | solution.py:395
  215.8 6.7 %shard_map.194.refs_4_ = bf16[2560,2048]{1,0:T(8,128)(2,1)} custom-call(bf16[320,2048]{1,0:T(8,128)(2,1)} %bitcast.144, bf16[320,2048]{1,0:T(8,128)(2,1)} %collective-permute-done.9.refs_1_, bf16[320,2048]{1,0:T(8,128)(2,1)} %collective-permute-done.10.refs_2_, bf16[320,2048]{1,0:T(8,128)(2,1)} %collective-permute-done.11.refs_3_, ...), custom_call_target="tpu_custom_call" | custom-call | bytes 15728640 | tf_op jit(solution)/shard_map/pallas_call | solution.py:208
  228.7 15.7 %collective-permute-done.25 = bf16[320,2048]{1,0:T(8,128)(2,1)} collective-permute-done((bf16[320,2048]{1,0:T(8,128)(2,1)}, bf16[320,2048]{1,0:T(8,128)(2,1)}, u32[]{:S(2)}, u32[]{:S(2)}) %collective-permute-start.25) | collective-permute-done | bytes 1310752 | tf_op jit(solution)/shard_map/ppermute | solution.py:54
  253.6 10.9 %collective-permute-done.26 = bf16[160,2048]{1,0:T(8,128)(2,1)S(1)} collective-permute-done((bf16[160,2048]{1,0:T(8,128)(2,1)S(1)}, bf16[160,2048]{1,0:T(8,128)(2,1)S(1)}, u32[]{:S(2)}, u32[]{:S(2)}) %collective-permute-start.26) | collective-permute-done | bytes 655392 | tf_op jit(solution)/shard_map/ppermute | solution.py:54
  269.7 14.6 %fusion.60.grad_ref = f32[2560,1024]{1,0:T(8,128)} fusion(bf16[2560,2048]{1,0:T(8,128)(2,1)S(1)} %bitcast.135, bf16[1024,2048]{1,0:T(8,128)(2,1)S(1)} %copy-done.76), kind=kOutput, calls=%fused_computation.138 | convolution fusion | flops 10737418240 | bytes 25165824 | tf_op jit(solution)/shard_map/dot_general | solution.py:41
  284.3 11.4 %collective-permute-done.28.refs_1_ = bf16[320,2048]{1,0:T(8,128)(2,1)S(1)} collective-permute-done((bf16[320,2048]{1,0:T(8,128)(2,1)S(1)}, bf16[320,2048]{1,0:T(8,128)(2,1)S(1)}, u32[]{:S(2)}, u32[]{:S(2)}) %collective-permute-start.28) | collective-permute-done | bytes 1310752 | tf_op jit(solution)/shard_map/ppermute | solution.py:54
  301.8 6.4 shard_map.196.refs_4_
  308.2 7.5 %collective-permute-done.31.refs_0_ = bf16[160,2048]{1,0:T(8,128)(2,1)S(1)} collective-permute-done((bf16[160,2048]{1,0:T(8,128)(2,1)}, bf16[160,2048]{1,0:T(8,128)(2,1)S(1)}, u32[]{:S(2)}, u32[]{:S(2)}) %collective-permute-start.31) | collective-permute-done | bytes 655392 | tf_op jit(solution)/shard_map/ppermute | solution.py:54
  322.1 21.3 %shard_map.198 = (bf16[2560,1024]{1,0:T(8,128)(2,1)S(1)}, bf16[2560,1024]{1,0:T(8,128)(2,1)}) custom-call(bf16[2560,2048]{1,0:T(8,128)(2,1)} %shard_map.197.second_ref, bf16[2048,1024]{1,0:T(8,128)(2,1)S(1)} %bitcast.124, f32[1,1024]{1,0:T(1,128)S(1)} %bitcast.122, f32[2560,1024]{1,0:T(8,128)} %fusion.60.grad_ref), custom_call_target="tpu_custom_call" | custom-call | flops 10737418240 | bytes 35651584 | tf_op jit(solution)/shard_map/pallas_call | solution.py:435
  343.4 5.6 convolution_convert_fusion.13
  361.9 12.8 %convolution_convert_fusion.3 = bf16[1024,2048]{1,0:T(8,128)(2,1)} fusion(bf16[2560,1024]{1,0:T(8,128)(2,1)S(1)} %get-tuple-element.455, bf16[2560,2048]{1,0:T(8,128)(2,1)S(1)} %bitcast.137), kind=kOutput, calls=%fused_computation.6 | convolution fusion | flops 10739515392 | bytes 19922944 | tf_op jit(solution)/shard_map/dot_general | solution.py:47
  374.8 5.5 fusion.23
  380.3 10.2 %collective-permute-done.40 = bf16[320,2048]{1,0:T(8,128)(2,1)} collective-permute-done((bf16[320,2048]{1,0:T(8,128)(2,1)}, bf16[320,2048]{1,0:T(8,128)(2,1)}, u32[]{:S(2)}, u32[]{:S(2)}) %collective-permute-start.40) | collective-permute-done | bytes 1310752 | tf_op jit(solution)/shard_map/ppermute | solution.py:54
  395.7 7.3 %convolution_convert_fusion = bf16[1280,2048]{1,0:T(8,128)(2,1)} fusion(bf16[1024,2048]{1,0:T(8,128)(2,1)S(1)} %copy-done.77, bf16[2560,1024]{1,0:T(8,128)(2,1)S(1)} %copy-done.10), kind=kOutput, calls=%fused_computation.1 | convolution fusion | flops 5371330560 | bytes 12058624 | tf_op jit(solution)/shard_map/dot_general | solution.py:508
  416.4 15.4 %convolution_convert_fusion.4 = bf16[2048,1024]{1,0:T(8,128)(2,1)} fusion(bf16[2560,2048]{1,0:T(8,128)(2,1)S(1)} %bitcast.133, bf16[2560,1024]{1,0:T(8,128)(2,1)} %get-tuple-element.508), kind=kOutput, calls=%fused_computation.7 | convolution fusion | flops 10739515392 | bytes 19922944 | tf_op jit(solution)/shard_map/dot_general | solution.py:47
  436.0 7.4 %collective-permute-done.43.refs_1_ = bf16[320,2048]{1,0:T(8,128)(2,1)S(1)} collective-permute-done((bf16[320,2048]{1,0:T(8,128)(2,1)S(1)}, bf16[320,2048]{1,0:T(8,128)(2,1)S(1)}, u32[]{:S(2)}, u32[]{:S(2)}) %collective-permute-start.43) | collective-permute-done | bytes 1310752 | tf_op jit(solution)/shard_map/ppermute | solution.py:54
  453.5 6.4 shard_map.199.refs_4_
  471.8 7.9 %convolution_convert_fusion.2 = bf16[2560,256]{1,0:T(8,128)(2,1)S(1)} fusion(bf16[2560,2048]{1,0:T(8,128)(2,1)} %shard_map.200, bf16[256,2048]{1,0:T(8,128)(2,1)S(1)} %bitcast.143), kind=kOutput, calls=%fused_computation.5 | convolution fusion | flops 2685009920 | bytes 12845056 | tf_op jit(solution)/shard_map/dot_general | solution.py:41
  484.5 18.6 %shard_map.201 = bf16[16,160,768]{2,1,0:T(8,128)(2,1)} custom-call(s32[2,2,8]{2,1,0:T(2,128)S(1)} %reshape.167.places_ref, s32[2,2]{1,0:T(2,128)S(1)} %copy-done.5, bf16[16,160,768]{2,1,0:T(8,128)(2,1)} %bitcast.186, bf16[16,160,256]{2,1,0:T(8,128)(2,1)S(1)} %bitcast.129, f32[16,160,256]{2,1,0:T(8,128)S(1)} %copy-done.8), custom_call_target="tpu_custom_call" | custom-call | flops 5368709120 | bytes 5242880 | tf_op jit(solution)/shard_map/pallas_call | solution.py:395
  503.1 15.0 %convolution_convert_fusion.5 = bf16[2048,768]{1,0:T(8,128)(2,1)} fusion(bf16[2560,2048]{1,0:T(8,128)(2,1)} %shard_map.191, bf16[2560,768]{1,0:T(8,128)(2,1)} %bitcast.187), kind=kOutput, calls=%fused_computation.8 | convolution fusion | flops 8054636544 | bytes 17563648 | tf_op jit(solution)/shard_map/dot_general | solution.py:47
  528.5 7.3 %collective-permute-done.56 = bf16[160,2048]{1,0:T(8,128)(2,1)S(1)} collective-permute-done((bf16[160,2048]{1,0:T(8,128)(2,1)S(1)}, bf16[160,2048]{1,0:T(8,128)(2,1)S(1)}, u32[]{:S(2)}, u32[]{:S(2)}) %collective-permute-start.56) | collective-permute-done | bytes 655392 | tf_op jit(solution)/shard_map/ppermute | solution.py:54
  542.0 5.2 fusion.11
  570.8 13.7 %collective-permute-done.60 = bf16[320,2048]{1,0:T(8,128)(2,1)S(1)} collective-permute-done((bf16[320,2048]{1,0:T(8,128)(2,1)}, bf16[320,2048]{1,0:T(8,128)(2,1)S(1)}, u32[]{:S(2)}, u32[]{:S(2)}) %collective-permute-start.60) | collective-permute-done | bytes 1310752 | tf_op jit(solution)/shard_map/ppermute | solution.py:54
  595.5 7.8 %collective-permute-done.63 = bf16[160,2048]{1,0:T(8,128)(2,1)S(1)} collective-permute-done((bf16[160,2048]{1,0:T(8,128)(2,1)S(1)}, bf16[160,2048]{1,0:T(8,128)(2,1)S(1)}, u32[]{:S(2)}, u32[]{:S(2)}) %collective-permute-start.63) | collective-permute-done | bytes 655392 | tf_op jit(solution)/shard_map/ppermute | solution.py:54
  (471 shorter events, 290.1 us)
Async XLA Ops:
  15.3 117.2 %all-gather.4.cloned.1.call-start = ((), (), s32[]{:S(2)}) async-start(), calls=%async_computation.9 | async-start | bytes 3932160 | tf_op jit(solution)/shard_map/all_gather | solution.py:75
  41.7 29.8 %collective-permute-start.1 = (bf16[320,2048]{1,0:T(8,128)(2,1)S(1)}, bf16[320,2048]{1,0:T(8,128)(2,1)S(1)}, u32[]{:S(2)}, u32[]{:S(2)}) collective-permute-start(bf16[320,2048]{1,0:T(8,128)(2,1)S(1)} %copy-done.25), channel_id=1, source_target_pairs={{16,0},{24,8},{0,16},{8,24},{17,1},{25,9},{1,17},{9,25},{18,2},{26... | collective-permute-start | bytes 3932168 | tf_op jit(solution)/shard_map/ppermute | solution.py:54
  43.1 29.1 %collective-permute-start.2 = (bf16[320,2048]{1,0:T(8,128)(2,1)S(1)}, bf16[320,2048]{1,0:T(8,128)(2,1)S(1)}, u32[]{:S(2)}, u32[]{:S(2)}) collective-permute-start(bf16[320,2048]{1,0:T(8,128)(2,1)S(1)} %copy-done.25), channel_id=1, source_target_pairs={{1,0},{0,1},{3,2},{2,3},{5,4},{4,5},{7,6},{6,7},{9,8},{8,9},{11,10... | collective-permute-start | bytes 3932168 | tf_op jit(solution)/shard_map/ppermute | solution.py:54
  94.8 37.7 %all-to-all-start.1 = ((bf16[4,64,2048]{2,1,0:T(8,128)(2,1)}), bf16[4,64,2048]{2,1,0:T(8,128)(2,1)S(1)}, u32[]{:S(2)}, u32[]{:S(2)}) async-start(bf16[4,64,2048]{2,1,0:T(8,128)(2,1)} %broadcast_in_dim.52), calls=%async_computation.1 | async-start | bytes 2097152 | tf_op jit(solution)/shard_map/all_to_all | solution.py:535
  99.5 129.1 %all-gather.6.cloned.1.call-start = ((), (), s32[]{:S(2)}) async-start(), calls=%async_computation.10 | async-start | bytes 5242880 | tf_op jit(solution)/shard_map/all_gather | solution.py:75
  99.5 29.2 %collective-permute-start.10 = (bf16[320,2048]{1,0:T(8,128)(2,1)S(1)}, bf16[320,2048]{1,0:T(8,128)(2,1)}, u32[]{:S(2)}, u32[]{:S(2)}) collective-permute-start(bf16[320,2048]{1,0:T(8,128)(2,1)S(1)} %bitcast.146), channel_id=1, source_target_pairs={{1,0},{0,1},{3,2},{2,3},{5,4},{4,5},{7,6},{6,7},{9,8},{8,9},{11,10... | collective-permute-start | bytes 3932168 | tf_op jit(solution)/shard_map/ppermute | solution.py:54
  100.3 28.5 %collective-permute-start.11 = (bf16[320,2048]{1,0:T(8,128)(2,1)S(1)}, bf16[320,2048]{1,0:T(8,128)(2,1)}, u32[]{:S(2)}, u32[]{:S(2)}) collective-permute-start(bf16[320,2048]{1,0:T(8,128)(2,1)S(1)} %bitcast.147), channel_id=1, source_target_pairs={{8,0},{0,8},{24,16},{16,24},{9,1},{1,9},{25,17},{17,25},{10,2},{2,... | collective-permute-start | bytes 3932168 | tf_op jit(solution)/shard_map/ppermute | solution.py:54
  100.3 31.3 %collective-permute-start.9 = (bf16[320,2048]{1,0:T(8,128)(2,1)S(1)}, bf16[320,2048]{1,0:T(8,128)(2,1)}, u32[]{:S(2)}, u32[]{:S(2)}) collective-permute-start(bf16[320,2048]{1,0:T(8,128)(2,1)S(1)} %bitcast.148), channel_id=1, source_target_pairs={{16,0},{24,8},{0,16},{8,24},{17,1},{25,9},{1,17},{9,25},{18,2},{26... | collective-permute-start | bytes 3932168 | tf_op jit(solution)/shard_map/ppermute | solution.py:54
  134.1 48.6 %collective-permute-start.16 = (bf16[320,2048]{1,0:T(8,128)(2,1)}, bf16[320,2048]{1,0:T(8,128)(2,1)}, u32[]{:S(2)}, u32[]{:S(2)}) collective-permute-start(bf16[320,2048]{1,0:T(8,128)(2,1)} %collective-permute-done.9.refs_1_), channel_id=1, source_target_pairs={{8,0},{0,8},{24,16},{16,24},{9,1},{1,9},{25,17},{17,25},{10,2},{2,... | collective-permute-start | bytes 3932168 | tf_op jit(solution)/shard_map/ppermute | solution.py:54
  135.3 47.4 %collective-permute-start.17 = (bf16[320,2048]{1,0:T(8,128)(2,1)}, bf16[320,2048]{1,0:T(8,128)(2,1)}, u32[]{:S(2)}, u32[]{:S(2)}) collective-permute-start(bf16[320,2048]{1,0:T(8,128)(2,1)} %collective-permute-done.10.refs_2_), channel_id=1, source_target_pairs={{8,0},{0,8},{24,16},{16,24},{9,1},{1,9},{25,17},{17,25},{10,2},{2,... | collective-permute-start | bytes 3932168 | tf_op jit(solution)/shard_map/ppermute | solution.py:54
  136.0 44.6 %collective-permute-start.18 = (bf16[4,64,1024]{2,1,0:T(8,128)(2,1)S(1)}, bf16[4,64,1024]{2,1,0:T(8,128)(2,1)S(1)}, u32[]{:S(2)}, u32[]{:S(2)}) collective-permute-start(bf16[4,64,1024]{2,1,0:T(8,128)(2,1)S(1)} %get-tuple-element.594), channel_id=1, source_target_pairs={{1,0},{0,1},{3,2},{2,3},{5,4},{4,5},{7,6},{6,7},{9,8},{8,9},{11,10... | collective-permute-start | bytes 1572872 | tf_op jit(solution)/shard_map/ppermute | solution.py:54
  140.2 40.3 %collective-permute-start.14 = (bf16[160,2048]{1,0:T(8,128)(2,1)S(1)}, bf16[160,2048]{1,0:T(8,128)(2,1)}, u32[]{:S(2)}, u32[]{:S(2)}) collective-permute-start(bf16[160,2048]{1,0:T(8,128)(2,1)S(1)} %slice.283), channel_id=1, source_target_pairs={{1,0},{0,1},{3,2},{2,3},{5,4},{4,5},{7,6},{6,7},{9,8},{8,9},{11,10... | collective-permute-start | bytes 1966088 | tf_op jit(solution)/shard_map/ppermute | solution.py:54
  187.8 120.4 %all-gather.8.cloned.1.call-start = ((), (), s32[]{:S(2)}) async-start(), calls=%async_computation.11 | async-start | bytes 5242880 | tf_op jit(solution)/shard_map/all_gather | solution.py:75
  213.3 31.1 %collective-permute-start.25 = (bf16[320,2048]{1,0:T(8,128)(2,1)}, bf16[320,2048]{1,0:T(8,128)(2,1)}, u32[]{:S(2)}, u32[]{:S(2)}) collective-permute-start(bf16[320,2048]{1,0:T(8,128)(2,1)} %fusion.13), channel_id=1, source_target_pairs={{1,0},{0,1},{3,2},{2,3},{5,4},{4,5},{7,6},{6,7},{9,8},{8,9},{11,10... | collective-permute-start | bytes 3932168 | tf_op jit(solution)/shard_map/ppermute | solution.py:54
  214.7 30.9 %collective-permute-start.24 = (bf16[320,2048]{1,0:T(8,128)(2,1)}, bf16[320,2048]{1,0:T(8,128)(2,1)}, u32[]{:S(2)}, u32[]{:S(2)}) collective-permute-start(bf16[320,2048]{1,0:T(8,128)(2,1)} %fusion.12), channel_id=1, source_target_pairs={{16,0},{24,8},{0,16},{8,24},{17,1},{25,9},{1,17},{9,25},{18,2},{26... | collective-permute-start | bytes 3932168 | tf_op jit(solution)/shard_map/ppermute | solution.py:54
  215.8 247.5 %reduce-scatter.5.cloned.1.call-start = ((), (), s32[]{:S(2)}) async-start(), calls=%async_computation.12 | async-start | bytes 5242880 | tf_op jit(solution)/shard_map/reduce_scatter | solution.py:79
  267.1 28.7 %collective-permute-start.28 = (bf16[320,2048]{1,0:T(8,128)(2,1)S(1)}, bf16[320,2048]{1,0:T(8,128)(2,1)S(1)}, u32[]{:S(2)}, u32[]{:S(2)}) collective-permute-start(bf16[320,2048]{1,0:T(8,128)(2,1)S(1)} %add_convert_fusion.3.refs_0_), channel_id=1, source_target_pairs={{16,0},{24,8},{0,16},{8,24},{17,1},{25,9},{1,17},{9,25},{18,2},{26... | collective-permute-start | bytes 3932168 | tf_op jit(solution)/shard_map/ppermute | solution.py:54
  268.1 28.3 %collective-permute-start.29 = (bf16[320,2048]{1,0:T(8,128)(2,1)S(1)}, bf16[320,2048]{1,0:T(8,128)(2,1)S(1)}, u32[]{:S(2)}, u32[]{:S(2)}) collective-permute-start(bf16[320,2048]{1,0:T(8,128)(2,1)S(1)} %add_convert_fusion.3.refs_0_), channel_id=1, source_target_pairs={{1,0},{0,1},{3,2},{2,3},{5,4},{4,5},{7,6},{6,7},{9,8},{8,9},{11,10... | collective-permute-start | bytes 3932168 | tf_op jit(solution)/shard_map/ppermute | solution.py:54
  268.7 27.7 %collective-permute-start.30 = (bf16[320,2048]{1,0:T(8,128)(2,1)S(1)}, bf16[320,2048]{1,0:T(8,128)(2,1)S(1)}, u32[]{:S(2)}, u32[]{:S(2)}) collective-permute-start(bf16[320,2048]{1,0:T(8,128)(2,1)S(1)} %add_convert_fusion.3.refs_0_), channel_id=1, source_target_pairs={{8,0},{0,8},{24,16},{16,24},{9,1},{1,9},{25,17},{17,25},{10,2},{2,... | collective-permute-start | bytes 3932168 | tf_op jit(solution)/shard_map/ppermute | solution.py:54
  359.3 31.2 %collective-permute-start.40 = (bf16[320,2048]{1,0:T(8,128)(2,1)}, bf16[320,2048]{1,0:T(8,128)(2,1)}, u32[]{:S(2)}, u32[]{:S(2)}) collective-permute-start(bf16[320,2048]{1,0:T(8,128)(2,1)} %fusion.9), channel_id=1, source_target_pairs={{1,0},{0,1},{3,2},{2,3},{5,4},{4,5},{7,6},{6,7},{9,8},{8,9},{11,10... | collective-permute-start | bytes 3932168 | tf_op jit(solution)/shard_map/ppermute | solution.py:54
  360.8 30.9 %collective-permute-start.39 = (bf16[320,2048]{1,0:T(8,128)(2,1)}, bf16[320,2048]{1,0:T(8,128)(2,1)}, u32[]{:S(2)}, u32[]{:S(2)}) collective-permute-start(bf16[320,2048]{1,0:T(8,128)(2,1)} %fusion.8), channel_id=1, source_target_pairs={{16,0},{24,8},{0,16},{8,24},{17,1},{25,9},{1,17},{9,25},{18,2},{26... | collective-permute-start | bytes 3932168 | tf_op jit(solution)/shard_map/ppermute | solution.py:54
  374.7 164.4 %reduce-scatter.7.cloned.1.call-start = ((), (), s32[]{:S(2)}) async-start(), calls=%async_computation.13 | async-start | bytes 5242880 | tf_op jit(solution)/shard_map/reduce_scatter | solution.py:79
  414.8 28.6 %collective-permute-start.43 = (bf16[320,2048]{1,0:T(8,128)(2,1)S(1)}, bf16[320,2048]{1,0:T(8,128)(2,1)S(1)}, u32[]{:S(2)}, u32[]{:S(2)}) collective-permute-start(bf16[320,2048]{1,0:T(8,128)(2,1)S(1)} %fusion.20.refs_0_), channel_id=1, source_target_pairs={{16,0},{24,8},{0,16},{8,24},{17,1},{25,9},{1,17},{9,25},{18,2},{26... | collective-permute-start | bytes 3932168 | tf_op jit(solution)/shard_map/ppermute | solution.py:54
  415.7 28.3 %collective-permute-start.44 = (bf16[320,2048]{1,0:T(8,128)(2,1)S(1)}, bf16[320,2048]{1,0:T(8,128)(2,1)S(1)}, u32[]{:S(2)}, u32[]{:S(2)}) collective-permute-start(bf16[320,2048]{1,0:T(8,128)(2,1)S(1)} %fusion.20.refs_0_), channel_id=1, source_target_pairs={{1,0},{0,1},{3,2},{2,3},{5,4},{4,5},{7,6},{6,7},{9,8},{8,9},{11,10... | collective-permute-start | bytes 3932168 | tf_op jit(solution)/shard_map/ppermute | solution.py:54
  416.4 27.7 %collective-permute-start.45 = (bf16[320,2048]{1,0:T(8,128)(2,1)S(1)}, bf16[320,2048]{1,0:T(8,128)(2,1)S(1)}, u32[]{:S(2)}, u32[]{:S(2)}) collective-permute-start(bf16[320,2048]{1,0:T(8,128)(2,1)S(1)} %fusion.20.refs_0_), channel_id=1, source_target_pairs={{8,0},{0,8},{24,16},{16,24},{9,1},{1,9},{25,17},{17,25},{10,2},{2,... | collective-permute-start | bytes 3932168 | tf_op jit(solution)/shard_map/ppermute | solution.py:54
  463.9 139.9 %reduce-scatter.9.cloned.1.call-start = ((), (), s32[]{:S(2)}) async-start(), calls=%async_computation.14 | async-start | bytes 3932160 | tf_op jit(solution)/shard_map/reduce_scatter | solution.py:79
  481.8 36.2 %collective-permute-start.54 = (bf16[320,2048]{1,0:T(8,128)(2,1)}, bf16[320,2048]{1,0:T(8,128)(2,1)S(1)}, u32[]{:S(2)}, u32[]{:S(2)}) collective-permute-start(bf16[320,2048]{1,0:T(8,128)(2,1)} %get-tuple-element.584), channel_id=1, source_target_pairs={{16,0},{24,8},{0,16},{8,24},{17,1},{25,9},{1,17},{9,25},{18,2},{26... | collective-permute-start | bytes 3932168 | tf_op jit(solution)/shard_map/ppermute | solution.py:54
  483.0 35.1 %collective-permute-start.55 = (bf16[320,2048]{1,0:T(8,128)(2,1)S(1)}, bf16[320,2048]{1,0:T(8,128)(2,1)S(1)}, u32[]{:S(2)}, u32[]{:S(2)}) collective-permute-start(bf16[320,2048]{1,0:T(8,128)(2,1)S(1)} %get-tuple-element.583), channel_id=1, source_target_pairs={{1,0},{0,1},{3,2},{2,3},{5,4},{4,5},{7,6},{6,7},{9,8},{8,9},{11,10... | collective-permute-start | bytes 3932168 | tf_op jit(solution)/shard_map/ppermute | solution.py:54
  536.7 114.2 %reduce-scatter.11.cloned.1.call-start = ((), (), s32[]{:S(2)}) async-start(), calls=%async_computation.15 | async-start | bytes 1310720 | tf_op jit(solution)/shard_map/reduce_scatter | solution.py:79
  542.0 43.7 %collective-permute-start.62 = (bf16[640,2048]{1,0:T(8,128)(2,1)}, bf16[640,2048]{1,0:T(8,128)(2,1)}, u32[]{:S(2)}, u32[]{:S(2)}) collective-permute-start(bf16[640,2048]{1,0:T(8,128)(2,1)} %convolution_convert_fusion.6), channel_id=1, source_target_pairs={{8,0},{0,8},{24,16},{16,24},{9,1},{1,9},{25,17},{17,25},{10,2},{2,... | collective-permute-start | bytes 7864328 | tf_op jit(solution)/shard_map/ppermute | solution.py:54
  554.3 30.1 %collective-permute-start.60 = (bf16[320,2048]{1,0:T(8,128)(2,1)}, bf16[320,2048]{1,0:T(8,128)(2,1)S(1)}, u32[]{:S(2)}, u32[]{:S(2)}) collective-permute-start(bf16[320,2048]{1,0:T(8,128)(2,1)} %fusion.10), channel_id=1, source_target_pairs={{16,0},{24,8},{0,16},{8,24},{17,1},{25,9},{1,17},{9,25},{18,2},{26... | collective-permute-start | bytes 3932168 | tf_op jit(solution)/shard_map/ppermute | solution.py:54
  555.9 29.8 %collective-permute-start.61 = (bf16[320,2048]{1,0:T(8,128)(2,1)}, bf16[320,2048]{1,0:T(8,128)(2,1)}, u32[]{:S(2)}, u32[]{:S(2)}) collective-permute-start(bf16[320,2048]{1,0:T(8,128)(2,1)} %fusion.11), channel_id=1, source_target_pairs={{1,0},{0,1},{3,2},{2,3},{5,4},{4,5},{7,6},{6,7},{9,8},{8,9},{11,10... | collective-permute-start | bytes 3932168 | tf_op jit(solution)/shard_map/ppermute | solution.py:54
  (151 other events, 1751.2 us)
Sparse Core Ops, SparseCore 0:
  41.8 71.5 all-gather.3
  115.0 81.2 all-gather.5
  215.9 78.1 all-gather.7
  374.8 74.3 reduce-scatter.4
  464.0 75.0 reduce-scatter.6
  541.3 60.7 reduce-scatter.8
  606.5 27.6 reduce-scatter.10
